TPU v7x, 32 devices: a whole 2x2x4 slice. The times are simulated.
32 devices in a mesh: gx: 4 (over y, core), gy: 2 (over x), gz: 4 (over z).
Axes of the slice: x: 2, y: 2, z: 4, core: 2. Of those that a mesh axis runs over, the one named last changes fastest.
Arguments:
- rhs: float32 [4, 2, 4, 2, 64, 256], P('gx', 'gy', 'gz'), may hold values from -6 to 6
- viscosity: float32 [4, 2, 4, 64], P('gx', 'gy', 'gz'), may hold values from 0.3 to 3
- counts: int32 [4, 2, 4], P('gx', 'gy', 'gz'), may hold values from 8 to 64, as said below
- neighbours: int32 [4, 2, 4, 16], P('gx', 'gy', 'gz'), may hold values from -1 to 3, as said below
- face_index: int32 [4, 2, 4, 16, 512], P('gx', 'gy', 'gz'), may hold values from 0 to 16383, as said below
- k_matrix: float32 [256, 256], replicated, may hold values from -0.04 to 1.04, as said below
- p_matrix: float32 [256, 256], replicated, may hold values from -0.04 to 1.04, as said below
Outputs:
- solution: float32 [4, 2, 4, 2, 64, 256], P('gx', 'gy', 'gz')
Inputs may be any that keep to these rules, and one draw needn't show every extreme that they name: `counts`: in every gz group some partition has exactly 64 live elements. `neighbours`: each list names distinct partitions of the same gz group in increasing order, followed by -1 entries; the relation is symmetric and no partition names itself. `face_index`: every index lies within the live elements of its partition, that is below 256 times counts. `k_matrix`: the identity plus independent entries. `p_matrix`: the identity plus independent entries.
All inputs are finite; a program needn't handle non-finite values.
Results may differ from a plain program's by a relative error of at most 0.0003.
Values sent between devices are 32-bit elements; how exact they have to be, the bound alone decides.
No kernel may reach another device: no remote copies, remote signals or barrier semaphores. Data moves between devices by JAX's collectives and lax.ppermute only.
A program may use at most 64 MiB of HBM per device.

v0:
```python
import jax
import jax.numpy as jnp
from jax import lax
from jax.sharding import PartitionSpec as P

coupling = 0.5
largest_rank = lax.Precision.HIGHEST


def per_element(vector, matrix):
    shaped = vector.shape
    product = jnp.dot(
        vector.reshape(-1, shaped[-1]),
        matrix,
        precision=largest_rank,
        preferred_element_type=jnp.float32,
    )
    return product.reshape(shaped)


def shared_faces(departing_rows, links, probes, slots, width):
    flat_rows = departing_rows.reshape(slots, probes * width)
    my_index = lax.axis_index("gz")
    face_vals = lax.all_gather(flat_rows[None], "gz", axis=0, tiled=True)
    link_rows = lax.all_gather(links[None], "gz", axis=0, tiled=True)
    count_src = link_rows.shape[0]
    sources = jnp.arange(count_src, dtype=jnp.int32)
    pick_rows = (links[:, None] == sources[None, :]).astype(jnp.float32)
    to_self = (link_rows == my_index).astype(jnp.float32)
    selection = (pick_rows[:, :, None] * to_self[None, :, :]).reshape(slots, count_src * slots)
    gathered_rows = face_vals.reshape(count_src * slots, probes * width)
    return jnp.dot(
        selection, gathered_rows, precision=largest_rank, preferred_element_type=jnp.float32
    )


def operate(vector, k_matrix, visc_col, live_mask, links, blocks):
    probes, elements, dofs = vector.shape
    slots, width = blocks.shape
    flat_vec = vector.reshape(probes, elements * dofs)
    flat_index = blocks.reshape(-1)
    departing_rows = flat_vec[:, flat_index].reshape(probes, slots, width).transpose(1, 0, 2)
    received_rows = shared_faces(departing_rows, links, probes, slots, width)
    received_rows = (
        received_rows.reshape(slots, probes, width).transpose(1, 0, 2).reshape(probes, -1)
    )
    placed = jnp.zeros((probes, elements * dofs), jnp.float32).at[:, flat_index].add(received_rows)
    return (
        per_element(vector, k_matrix) * visc_col - coupling * placed.reshape(vector.shape)
    ) * live_mask


def inner_prod(left_vec, right_vec):
    return jnp.sum(left_vec * right_vec, axis=(1, 2))


def per_device(rhs, viscosity, counts, neighbours, face_index, k_matrix, p_matrix):
    vector = rhs[0, 0, 0]
    elements = vector.shape[1]
    live_count = counts[0, 0, 0]
    live_mask = (jnp.arange(elements, dtype=jnp.int32) < live_count).astype(jnp.float32)[
        None, :, None
    ]
    visc_col = viscosity[0, 0, 0][None, :, None]
    links = neighbours[0, 0, 0]
    blocks = face_index[0, 0, 0]
    source = vector * live_mask

    def smooth(field_in):
        return per_element(field_in, p_matrix) / visc_col * live_mask

    def apply_op(field_in):
        return operate(field_in, k_matrix, visc_col, live_mask, links, blocks)

    first_pre = smooth(source)
    first_img = apply_op(first_pre)
    second_pre = smooth(first_img)
    second_img = apply_op(second_pre)
    self_one, cross_mid, self_two, load_one, load_two = lax.psum(
        (
            inner_prod(first_img, first_img),
            inner_prod(first_img, second_img),
            inner_prod(second_img, second_img),
            inner_prod(first_img, source),
            inner_prod(second_img, source),
        ),
        ("gx", "gy", "gz"),
    )
    determinant = self_one * self_two - cross_mid * cross_mid
    weight_one = (self_two * load_one - cross_mid * load_two) / determinant
    weight_two = (self_one * load_two - cross_mid * load_one) / determinant
    solution = weight_one[:, None, None] * first_pre + weight_two[:, None, None] * second_pre
    return solution[None, None, None]


def solution(mesh):
    return jax.shard_map(
        per_device,
        mesh=mesh,
        in_specs=(
            P("gx", "gy", "gz", None, None, None),
            P("gx", "gy", "gz", None),
            P("gx", "gy", "gz"),
            P("gx", "gy", "gz", None),
            P("gx", "gy", "gz", None, None),
            P(),
            P(),
        ),
        out_specs=P("gx", "gy", "gz", None, None, None),
        check_vma=False,
    )
```

profile of v0, /device:TPU:0, one launch (start us, length us, event | category | flops | bytes accessed | tf_op | source)
XLA Modules:
  0.0 286.2 jit_solution(179358773577575300)
XLA Ops:
  0.0 0.0 copy-start
  0.7 12.7 %all-gather = s32[4,1,1,16]{3,2,1,0:T(1,128)S(1)} all-gather(s32[1,1,1,16]{3,2,1,0:T(1,128)} %param.10), channel_id=2, replica_groups=mesh['gx'=4,'gy'=2,'gz'=4] {'gz'}, dimensions={0}, use_global_device_ids=true | all-gather | bytes 320 | tf_op jit(solution)/shard_map/all_gather | solution.py:25
  13.4 0.7 fusion.19
  14.2 0.1 broadcast_multiply_fusion.2
  14.2 0.1 reshape.224
  14.3 0.8 copy.50
  15.2 0.0 copy-done
  15.2 1.2 fusion.9
  16.4 4.6 %copy.44 = f32[2,64,256]{0,2,1:T(8,128)} copy(f32[2,64,256]{2,1,0:T(8,128)S(1)} %fusion.9) | data formatting | bytes 262144 | tf_op jit(solution)/shard_map/reshape | solution.py:40
  21.1 31.1 %gather_fusion = f32[8192,2]{1,0:T(8,128)} fusion(f32[2,16384]{0,1:T(8,128)} %bitcast.77, s32[8192]{0:T(1024)S(1)} %broadcast_clamp_fusion), kind=kCustom, calls=%fused_computation | custom fusion | bytes 163840 | tf_op jit(solution)/shard_map/gather | solution.py:42
  52.2 2.8 copy.35
  55.0 0.1 broadcast_in_dim_reshape.6
  55.1 13.9 %all_gather.11 = f32[4,16,1024]{2,1,0:T(8,128)S(1)} all-gather(f32[1,16,1024]{2,1,0:T(8,128)S(1)} %broadcast_in_dim_reshape.6), channel_id=1, replica_groups=mesh['gx'=4,'gy'=2,'gz'=4] {'gz'}, dimensions={0}, use_global_device_ids=true | all-gather | bytes 327680 | tf_op jit(solution)/shard_map/all_gather | solution.py:24
  69.0 0.2 convolution_bitcast_fusion.1
  69.2 2.6 copy.45
  71.9 48.0 %scatter_custom_fusion = f32[2,16384]{0,1:T(8,128)} fusion(s32[8192]{0:T(1024)S(1)} %bitcast.89, f32[8192,2]{1,0:T(8,128)} %bitcast.81, f32[]{:T(128)} %constant.5.clone.1), kind=kCustom, calls=%fused_computation.8 | custom fusion | flops 16384 | bytes 131584 | tf_op jit(solution)/shard_map/scatter-add | solution.py:47
  119.9 5.7 %broadcast_multiply_fusion.1 = f32[2,16384]{0,1:T(8,128)} fusion(f32[2,16384]{0,1:T(8,128)} %scatter_custom_fusion), kind=kLoop, calls=%fused_computation.5 | loop fusion | flops 32768 | bytes 262144 | tf_op jit(solution)/shard_map/mul | solution.py:49
  125.6 0.0 copy-start.2
  125.6 0.0 copy-start.4
  125.6 5.4 %copy.53 = f32[2,16384]{1,0:T(2,128)S(1)} copy(f32[2,16384]{0,1:T(8,128)} %broadcast_multiply_fusion.1) | data formatting | bytes 262144
  131.0 0.0 copy-done.2
  131.0 0.0 copy-done.4
  131.0 0.3 fusion.8
  131.3 0.3 fusion.6
  131.6 4.6 %copy.46 = f32[2,64,256]{0,2,1:T(8,128)} copy(f32[2,64,256]{2,1,0:T(8,128)S(1)} %fusion.6) | data formatting | bytes 262144 | tf_op jit(solution)/shard_map/reshape | solution.py:40
  136.2 31.1 %gather_fusion.1 = f32[8192,2]{1,0:T(8,128)} fusion(f32[2,16384]{0,1:T(8,128)} %bitcast.76, s32[8192]{0:T(1024)S(1)} %broadcast_clamp_fusion), kind=kCustom, calls=%fused_computation.1 | custom fusion | bytes 163840 | tf_op jit(solution)/shard_map/gather | solution.py:42
  167.3 2.8 copy.40
  170.1 0.1 broadcast_in_dim_reshape.7
  170.2 14.2 %all_gather.12 = f32[4,16,1024]{2,1,0:T(8,128)S(1)} all-gather(f32[1,16,1024]{2,1,0:T(8,128)S(1)} %broadcast_in_dim_reshape.7), channel_id=1, replica_groups=mesh['gx'=4,'gy'=2,'gz'=4] {'gz'}, dimensions={0}, use_global_device_ids=true | all-gather | bytes 327680 | tf_op jit(solution)/shard_map/all_gather | solution.py:24
  184.4 0.2 convolution_bitcast_fusion
  184.6 2.6 copy.47
  187.3 48.0 %scatter_custom_fusion.1 = f32[2,16384]{0,1:T(8,128)} fusion(s32[8192]{0:T(1024)S(1)} %bitcast.90, f32[8192,2]{1,0:T(8,128)} %bitcast.80, f32[]{:T(128)} %constant.5.clone.1), kind=kCustom, calls=%fused_computation.6 | custom fusion | flops 16384 | bytes 131584 | tf_op jit(solution)/shard_map/scatter-add | solution.py:47
  235.3 0.0 copy-start.1
  235.3 5.7 %broadcast_multiply_fusion = f32[2,16384]{0,1:T(8,128)} fusion(f32[2,16384]{0,1:T(8,128)} %scatter_custom_fusion.1), kind=kLoop, calls=%fused_computation.4 | loop fusion | flops 32768 | bytes 262144 | tf_op jit(solution)/shard_map/mul | solution.py:49
  241.0 0.0 copy-start.3
  241.1 5.4 %copy.54 = f32[2,16384]{1,0:T(2,128)S(1)} copy(f32[2,16384]{0,1:T(8,128)} %broadcast_multiply_fusion) | data formatting | bytes 262144
  246.4 0.0 copy-done.3
  246.4 0.4 multiply_reduce_fusion.1
  246.8 38.6 %all-reduce = (f32[2]{0:T(128)S(1)}, f32[2]{0:T(128)S(1)}, f32[2]{0:T(128)S(1)}, f32[2]{0:T(128)S(1)}, f32[2]{0:T(128)S(1)}) all-reduce(f32[2]{0:T(128)S(1)} %get-tuple-element.7, f32[2]{0:T(128)S(1)} %get-tuple-element.6, f32[2]{0:T(128)S(1)} %get-tuple-element.8, ...), channel_id=1, replica_groups=mesh['gx'=4,'gy'=2,'gz'=4] {'gx','gy','gz'}, use_global_device_ids=true, to_apply=%region_7.0 | all-reduce | flops 10 | bytes 80 | tf_op jit(solution)/shard_map/psum | solution.py:79
  285.5 0.7 add_bitcast_fusion
  286.2 0.0 copy-done.1
  (5 shorter events, 0.1 us)
Async XLA Ops:
  0.0 15.2 %copy-start = (f32[256,256]{1,0:T(8,128)S(1)}, f32[256,256]{1,0:T(8,128)}, u32[]{:S(2)}) copy-start(f32[256,256]{1,0:T(8,128)} %param.13) | copy-start | bytes 786436
  125.6 5.4 %copy-start.2 = (f32[256,256]{1,0:T(8,128)S(1)}, f32[256,256]{1,0:T(8,128)}, u32[]{:S(2)}) copy-start(f32[256,256]{1,0:T(8,128)} %param.12) | copy-start | bytes 786436
  125.6 5.4 %copy-start.4 = (f32[1,1,1,64]{3,2,1,0:T(1,128)S(1)}, f32[1,1,1,64]{3,2,1,0:T(1,128)}, u32[]{:S(2)}) copy-start(f32[1,1,1,64]{3,2,1,0:T(1,128)} %param.8) | copy-start | bytes 772
  235.3 50.9 %copy-start.1 = (f32[256,256]{1,0:T(8,128)S(1)}, f32[256,256]{1,0:T(8,128)}, u32[]{:S(2)}) copy-start(f32[256,256]{1,0:T(8,128)} %param.13) | copy-start | bytes 786436
  241.0 5.4 %copy-start.3 = (f32[1,1,1,2,64,256]{5,4,3,2,1,0:T(8,128)S(1)}, f32[1,1,1,2,64,256]{5,4,3,2,1,0:T(8,128)}, u32[]{:S(2)}) copy-start(f32[1,1,1,2,64,256]{5,4,3,2,1,0:T(8,128)} %param.7) | copy-start | bytes 393220
where the time goes:
time: 287 us; the launch traced here: 286 us
  other arithmetic  109 us (38%)
  local copies, waits for them, and re-layouts  94.2 us (33%)
  blocking collectives  79.4 us (28%)
    scatter-add x2, other arithmetic, operate(): jnp.zeros((probes, elements * dofs), jnp.float32).at[:, flat_index]  96 us
    gather x2, local copies, waits for them, and re-layouts, operate(): flat_vec[:, flat_index].reshape(probes, slots, width).transpose(1, 0, 2)  62.2 us
    psum x1, blocking collectives, per_device(): lax.psum((inner_prod(first_img, first_img), inner_prod(first_img, second_...  38.6 us
    all_gather x2, blocking collectives, shared_faces(): face_vals = lax.all_gather(flat_rows[None], 'gz', axis=0, tiled=True)  28.1 us
    all_gather x1, blocking collectives, shared_faces(): link_rows = lax.all_gather(links[None], 'gz', axis=0, tiled=True)  12.7 us
    unnamed x13, local copies, waits for them, and re-layouts  11.5 us
    mul x2, other arithmetic, operate(): coupling * placed.reshape(vector.shape)  11.4 us
    reshape x2, local copies, waits for them, and re-layouts, operate(): flat_vec = vector.reshape(probes, elements * dofs)  9.28 us

commit v1 on v0

v1 whole, which is shorter than its diff:
```python
import functools

import jax
import jax.numpy as jnp
from jax import lax
from jax.experimental import pallas as pl
from jax.experimental.pallas import tpu as pltpu
from jax.sharding import PartitionSpec as P

coupling = 0.5
vmem_grant = 48 * 1024 * 1024
f32 = jnp.float32
bf16 = jnp.bfloat16
vmem_spec = pl.BlockSpec(memory_space=pltpu.VMEM)
smem_spec = pl.BlockSpec(memory_space=pltpu.SMEM)


def two_parts(value):
    high = value.astype(bf16)
    return high, (value - high.astype(f32)).astype(bf16)


def dot(left, right):
    return jnp.dot(left, right, preferred_element_type=f32)


def dot_transposed(left, right):
    return lax.dot_general(left, right, (((1,), (1,)), ((), ())), preferred_element_type=f32)


def times_matrix(rows, matrix):
    count = rows.shape[0]
    row_high, row_low = two_parts(rows)
    mat_high, mat_low = two_parts(matrix)
    both = dot(jnp.concatenate([row_high, row_low], axis=0), mat_high)
    return both[:count] + (both[count:] + dot(row_high, mat_low))


def split_index(index, dofs):
    if dofs & (dofs - 1) == 0:
        return lax.shift_right_arithmetic(index, dofs.bit_length() - 1), index & (dofs - 1)
    element = jnp.floor_divide(index, dofs)
    return element, index - element * dofs


def shift_slot(links_ref, index_ref, shift, members):
    target = lax.rem(lax.axis_index("gz") + shift, members)
    slot = jnp.int32(-1)
    for position in range(links_ref.shape[0]):
        slot = jnp.where(links_ref[position] == target, jnp.int32(position), slot)
    row = index_ref[pl.ds(jnp.maximum(slot, 0), 1), :]
    return jnp.where(slot >= 0, row, -1)


def hot_columns(flat_row, elements, dofs):
    element, dof = split_index(flat_row, dofs)
    width = flat_row.shape[1]
    over_elements = lax.broadcasted_iota(jnp.int32, (elements, width), 0) == element
    over_dofs = (lax.broadcasted_iota(jnp.int32, (dofs, width), 0) == dof).astype(f32).astype(bf16)
    return over_elements, over_dofs


def viscosity_rows(visc_ref, probes):
    elements = visc_ref.shape[1]
    line = lax.broadcasted_iota(jnp.int32, (elements, elements), 0)
    column = lax.broadcasted_iota(jnp.int32, (elements, elements), 1)
    diagonal = jnp.where(line == column, jnp.broadcast_to(visc_ref[...], (elements, elements)), 0.0)
    visc_col = jnp.sum(diagonal, axis=1, keepdims=True)
    return jnp.concatenate([visc_col] * probes, axis=0)


def live_rows(count_ref, elements, probes):
    slot = lax.broadcasted_iota(jnp.int32, (elements, 1), 0)
    live = (slot < count_ref[0]).astype(f32)
    return jnp.concatenate([live] * probes, axis=0)


def send_faces(field, probes, links_ref, index_ref, face_refs):
    rows, dofs = field.shape
    elements = rows // probes
    high, low = two_parts(field)
    parts = jnp.concatenate([high, low], axis=0)
    members = len(face_refs) + 1
    for shift in range(1, members):
        flat_row = shift_slot(links_ref, index_ref, shift, members)
        over_elements, over_dofs = hot_columns(flat_row, elements, dofs)
        picked = dot(parts, over_dofs)
        picked = picked[:rows] + picked[rows:]
        for probe in range(probes):
            block = picked[probe * elements : (probe + 1) * elements]
            face_refs[shift - 1][pl.ds(probe, 1), :] = jnp.sum(
                jnp.where(over_elements, block, 0.0), axis=0, keepdims=True
            )


def placed_faces(shape, probes, links_ref, index_ref, face_refs):
    rows, dofs = shape
    elements = rows // probes
    members = len(face_refs) + 1
    total = jnp.zeros((2 * rows, dofs), f32)
    for shift in range(1, members):
        flat_row = shift_slot(links_ref, index_ref, shift, members)
        over_elements, over_dofs = hot_columns(flat_row, elements, dofs)
        came = face_refs[members - shift - 1]
        spread = jnp.concatenate(
            [
                jnp.where(over_elements, came[pl.ds(probe, 1), :], 0.0)
                for probe in range(probes)
            ],
            axis=0,
        )
        high, low = two_parts(spread)
        total += dot_transposed(jnp.concatenate([high, low], axis=0), over_dofs)
    return total[:rows] + total[rows:]


def first_kernel(probes, count_ref, links_ref, index_ref, visc_ref, rhs_ref, p_ref, first_ref, *face_refs):
    rows, _ = rhs_ref.shape
    live = live_rows(count_ref, rows // probes, probes)
    visc = viscosity_rows(visc_ref, probes)
    first_pre = times_matrix(rhs_ref[...] * live, p_ref[...]) / visc * live
    first_ref[...] = first_pre
    send_faces(first_pre, probes, links_ref, index_ref, face_refs)


def second_kernel(
    probes, members, count_ref, links_ref, index_ref, visc_ref, first_ref, k_ref, p_ref, *refs
):
    came_refs = refs[: members - 1]
    image_ref, second_ref = refs[members - 1 : members + 1]
    face_refs = refs[members + 1 :]
    rows, _ = first_ref.shape
    live = live_rows(count_ref, rows // probes, probes)
    visc = viscosity_rows(visc_ref, probes)
    placed = placed_faces(first_ref.shape, probes, links_ref, index_ref, came_refs)
    image = (times_matrix(first_ref[...], k_ref[...]) * visc - coupling * placed) * live
    image_ref[...] = image
    second_pre = times_matrix(image, p_ref[...]) / visc * live
    second_ref[...] = second_pre
    send_faces(second_pre, probes, links_ref, index_ref, face_refs)


def third_kernel(
    probes, count_ref, links_ref, index_ref, visc_ref, rhs_ref, image_ref, second_ref, k_ref, *refs
):
    came_refs, products_ref = refs[:-1], refs[-1]
    rows, dofs = rhs_ref.shape
    elements = rows // probes
    live = live_rows(count_ref, elements, probes)
    visc = viscosity_rows(visc_ref, probes)
    placed = placed_faces(rhs_ref.shape, probes, links_ref, index_ref, came_refs)
    second_img = (times_matrix(second_ref[...], k_ref[...]) * visc - coupling * placed) * live
    first_img = image_ref[...]
    source = rhs_ref[...] * live
    pairs = (
        (first_img, first_img),
        (first_img, second_img),
        (second_img, second_img),
        (first_img, source),
        (second_img, source),
    )
    products_ref[...] = jnp.zeros(products_ref.shape, f32)
    for place, (left, right) in enumerate(pairs):
        product = left * right
        for probe in range(probes):
            products_ref[pl.ds(place * probes + probe, 1), :] = jnp.sum(
                product[probe * elements : (probe + 1) * elements], axis=0, keepdims=True
            )


def last_kernel(probes, first_ref, second_ref, *refs):
    part_refs, out_ref = refs[:-1], refs[-1]
    rows, _ = first_ref.shape
    elements = rows // probes
    total = part_refs[0][...]
    for part in part_refs[1:]:
        total = total + part[...]
    sums = jnp.sum(total, axis=1, keepdims=True)
    for probe in range(probes):
        self_one, cross_mid, self_two, load_one, load_two = (
            sums[place * probes + probe : place * probes + probe + 1, :] for place in range(5)
        )
        determinant = self_one * self_two - cross_mid * cross_mid
        weight_one = (self_two * load_one - cross_mid * load_two) / determinant
        weight_two = (self_one * load_two - cross_mid * load_one) / determinant
        block = pl.ds(probe * elements, elements)
        out_ref[block, :] = weight_one * first_ref[block, :] + weight_two * second_ref[block, :]


def shifted(array, axis, size, shift):
    return lax.ppermute(array, axis, [(source, (source + shift) % size) for source in range(size)])


def call(kernel, in_specs, out_shapes, flops, *args):
    return pl.pallas_call(
        kernel,
        out_shape=out_shapes,
        in_specs=in_specs,
        out_specs=jax.tree.map(lambda _: vmem_spec, out_shapes),
        compiler_params=pltpu.CompilerParams(vmem_limit_bytes=vmem_grant),
        cost_estimate=pl.CostEstimate(flops=flops, bytes_accessed=1 << 20, transcendentals=0),
    )(*args)


def per_device(mesh, rhs, viscosity, counts, neighbours, face_index, k_matrix, p_matrix):
    probes, elements, dofs = rhs.shape[3:]
    slots, width = face_index.shape[3:]
    members = mesh.shape["gz"]
    rows = probes * elements
    flat_rhs = rhs.reshape(rows, dofs)
    shared = (
        counts.reshape(1),
        neighbours.reshape(slots),
        face_index.reshape(slots, width),
        viscosity.reshape(1, elements),
    )
    shared_specs = [smem_spec, smem_spec, vmem_spec, vmem_spec]
    field = jax.ShapeDtypeStruct((rows, dofs), f32)
    faces = [jax.ShapeDtypeStruct((probes, width), f32)] * (members - 1)
    flops = 8 * rows * dofs * (members - 1) * width

    def exchange(values):
        return [shifted(value, "gz", members, shift + 1) for shift, value in enumerate(values)]

    first_pre, *leaving = call(
        functools.partial(first_kernel, probes),
        shared_specs + [vmem_spec] * 2,
        [field] + faces,
        flops,
        *shared,
        flat_rhs,
        p_matrix,
    )
    came = exchange(leaving)
    first_img, second_pre, *leaving = call(
        functools.partial(second_kernel, probes, members),
        shared_specs + [vmem_spec] * (2 + members),
        [field, field] + faces,
        2 * flops,
        *shared,
        first_pre,
        k_matrix,
        p_matrix,
        *came,
    )
    came = exchange(leaving)
    products = call(
        functools.partial(third_kernel, probes),
        shared_specs + [vmem_spec] * (3 + members),
        jax.ShapeDtypeStruct((-(-5 * probes // 8) * 8, dofs), f32),
        flops,
        *shared,
        flat_rhs,
        first_img,
        second_pre,
        k_matrix,
        *came,
    )
    parts = [products]
    for axis in ("gz", "gx", "gy"):
        total = functools.reduce(jnp.add, parts)
        size = mesh.shape[axis]
        parts = [total] + [shifted(total, axis, size, shift) for shift in range(1, size)]
    result = call(
        functools.partial(last_kernel, probes),
        [vmem_spec] * (2 + len(parts)),
        field,
        rows * dofs,
        first_pre,
        second_pre,
        *parts,
    )
    return result.reshape(rhs.shape)


def solution(mesh):
    return jax.shard_map(
        functools.partial(per_device, mesh),
        mesh=mesh,
        in_specs=(
            P("gx", "gy", "gz", None, None, None),
            P("gx", "gy", "gz", None),
            P("gx", "gy", "gz"),
            P("gx", "gy", "gz", None),
            P("gx", "gy", "gz", None, None),
            P(),
            P(),
        ),
        out_specs=P("gx", "gy", "gz", None, None, None),
        check_vma=False,
    )
```

time: 287 us -> 42.1 us (0.15)
  other arithmetic: 109 us -> 0.01 us
  local copies, waits for them, and re-layouts: 94.2 us -> 3.27 us
  blocking collectives: 79.4 us -> 0 us
  starting transfers between devices: 0 us -> 17.1 us
  waiting for transfers between devices: 0 us -> 15.8 us
  Pallas kernels: 0 us -> 4.97 us
    scatter-add x2 -> x0, other arithmetic: 96 us -> none  [operate(): jnp.zeros((probes, elements * dofs), jnp.float32).at[:, flat_index]]
    gather x2 -> x0, local copies, waits for them, and re-layouts: 62.2 us -> none  [operate(): flat_vec[:, flat_index].reshape(probes, slots, width).transpose(1, 0, 2)]
    all_gather x3 -> x0, blocking collectives: 40.8 us -> none  [the longest x2 28.1 us: shared_faces(): face_vals = lax.all_gather(flat_rows[None], 'gz', axis=0, tiled=True)]
    psum x1 -> x0, blocking collectives: 38.6 us -> none  [per_device(): lax.psum((inner_prod(first_img, first_img), inner_prod(first_img, second_...]
    reshape x6 -> x0, local copies, waits for them, and re-layouts: 20.2 us -> none  [the longest x2 9.28 us: operate(): flat_vec = vector.reshape(probes, elements * dofs)]
    ppermute x0 -> x13, starting transfers between devices: none -> 17.1 us  [shifted(): lax.ppermute(array, axis, [(source, (source + shift) % size) for source i...]
    ppermute x0 -> x13, waiting for transfers between devices: none -> 15.8 us  [shifted(): lax.ppermute(array, axis, [(source, (source + shift) % size) for source i...]
    mul x3 -> x0, other arithmetic: 11.5 us -> none  [the longest x2 11.4 us: operate(): coupling * placed.reshape(vector.shape)]
  transfers between devices with their start and end apart: 0 -> 13, of which waited for: 0 -> 10; matrix products, arithmetic and copies ran while one was open for 0% -> 0% of each run, Pallas kernels for 0% -> 0%
where the time goes in v1:
time: 42.1 us; the launch traced here: 41.8 us
  starting transfers between devices  17.1 us (41%)
  waiting for transfers between devices  15.8 us (38%)
  Pallas kernels  4.97 us (12%)
  local copies, waits for them, and re-layouts  3.27 us (8%)
  between operations  0.71 us (2%)
    ppermute x13, starting transfers between devices, shifted(): lax.ppermute(array, axis, [(source, (source + shift) % size) for source i...  17.1 us
    ppermute x13, waiting for transfers between devices, shifted(): lax.ppermute(array, axis, [(source, (source + shift) % size) for source i...  15.8 us
    pallas_call x4, Pallas kernels, call(): pl.pallas_call(kernel, out_shape=out_shapes, in_specs=in_specs, out_specs...  4.97 us
    unnamed x12, local copies, waits for them, and re-layouts  3.27 us
  transfers between devices with their start and end apart: 13, of which 10 were waited for; matrix products, arithmetic and copies ran while one was open for 0% of the time, Pallas kernels for 0%

profile of v1, /device:TPU:0, one launch (start us, length us, event | category | flops | bytes accessed | tf_op | source)
XLA Modules:
  0.0 41.8 jit_solution(7423683377175975287)
XLA Ops:
  0.7 0.0 copy-start.4
  0.7 0.0 copy-start.5
  0.7 0.6 %copy-done.4 = s32[1,1,1,16]{3,2,1,0:T(1,128)S(1)} copy-done((s32[1,1,1,16]{3,2,1,0:T(1,128)S(1)}, s32[1,1,1,16]{3,2,1,0:T(1,128)}, u32[]{:S(2)}) %copy-start.4) | copy-done | bytes 88
  1.3 0.0 copy-done.5
  1.3 0.0 copy-start
  1.3 0.9 %copy-done = f32[256,256]{1,0:T(8,128)S(1)} copy-done((f32[256,256]{1,0:T(8,128)S(1)}, f32[256,256]{1,0:T(8,128)}, u32[]{:S(2)}) %copy-start) | copy-done | bytes 262168
  2.3 0.0 copy-start.2
  2.3 0.9 %copy-done.2 = f32[1,1,1,2,64,256]{5,4,3,2,1,0:T(8,128)S(1)} copy-done((f32[1,1,1,2,64,256]{5,4,3,2,1,0:T(8,128)S(1)}, f32[1,1,1,2,64,256]{5,4,3,2,1,0:T(8,128)}, u32[]{:S(2)}) %copy-start.2) | copy-done | bytes 131096
  3.2 0.0 copy-start.3
  3.2 0.8 %copy-done.3 = s32[1,1,1,16,512]{4,3,2,1,0:T(8,128)S(1)} copy-done((s32[1,1,1,16,512]{4,3,2,1,0:T(8,128)S(1)}, s32[1,1,1,16,512]{4,3,2,1,0:T(8,128)}, u32[]{:S(2)}) %copy-start.3) | copy-done | bytes 32792
  3.9 0.0 copy-start.1
  3.9 1.2 %shard_map.73 = (f32[128,256]{1,0:T(8,128)S(1)}, f32[2,512]{1,0:T(2,128)S(1)}, f32[2,512]{1,0:T(2,128)S(1)}, f32[2,512]{1,0:T(2,128)S(1)}) custom-call(s32[1]{0:T(128)} %bitcast.6.count_ref, s32[16]{0:T(128)S(1)} %bitcast.14, s32[16,512]{1,0:T(8,128)S(1)} %bitcast.11, f32[1,64]{1,0:T(1,128)S(1)} %bitcast.17, f32[128,256]{1,0:T(8,128)S(1)} %bitcast.9, ...), custom_call_target="tpu_custom_call" | custom-call | flops 402653184 | bytes 1048576 | tf_op jit(solution)/shard_map/pallas_call | solution.py:195
  5.2 3.1 %collective-permute-start = (f32[2,512]{1,0:T(2,128)S(1)}, f32[2,512]{1,0:T(2,128)S(1)}, u32[]{:S(2)}, u32[]{:S(2)}) collective-permute-start(f32[2,512]{1,0:T(2,128)S(1)} %get-tuple-element.15), channel_id=1, source_target_pairs={{0,1},{1,2},{2,3},{3,0},{4,5},{5,6},{6,7},{7,4},{8,9},{9,10},{10,1... | collective-permute-start | bytes 12296 | tf_op jit(solution)/shard_map/ppermute | solution.py:191
  8.2 2.6 %collective-permute-start.1 = (f32[2,512]{1,0:T(2,128)S(1)}, f32[2,512]{1,0:T(2,128)S(1)}, u32[]{:S(2)}, u32[]{:S(2)}) collective-permute-start(f32[2,512]{1,0:T(2,128)S(1)} %get-tuple-element.16), channel_id=1, source_target_pairs={{0,2},{1,3},{2,0},{3,1},{4,6},{5,7},{6,4},{7,5},{8,10},{9,11},{10,... | collective-permute-start | bytes 12296 | tf_op jit(solution)/shard_map/ppermute | solution.py:191
  10.8 1.3 %collective-permute-start.2 = (f32[2,512]{1,0:T(2,128)S(1)}, f32[2,512]{1,0:T(2,128)S(1)}, u32[]{:S(2)}, u32[]{:S(2)}) collective-permute-start(f32[2,512]{1,0:T(2,128)S(1)} %get-tuple-element.17), channel_id=1, source_target_pairs={{0,3},{1,0},{2,1},{3,2},{4,7},{5,4},{6,5},{7,6},{8,11},{9,8},{10,9... | collective-permute-start | bytes 12296 | tf_op jit(solution)/shard_map/ppermute | solution.py:191
  12.2 0.0 collective-permute-done.refs_0_
  12.2 0.6 %collective-permute-done.1.refs_1_ = f32[2,512]{1,0:T(2,128)S(1)} collective-permute-done((f32[2,512]{1,0:T(2,128)S(1)}, f32[2,512]{1,0:T(2,128)S(1)}, u32[]{:S(2)}, u32[]{:S(2)}) %collective-permute-start.1) | collective-permute-done | bytes 4128 | tf_op jit(solution)/shard_map/ppermute | solution.py:191
  12.8 1.7 %collective-permute-done.2.refs_2_ = f32[2,512]{1,0:T(2,128)S(1)} collective-permute-done((f32[2,512]{1,0:T(2,128)S(1)}, f32[2,512]{1,0:T(2,128)S(1)}, u32[]{:S(2)}, u32[]{:S(2)}) %collective-permute-start.2) | collective-permute-done | bytes 4128 | tf_op jit(solution)/shard_map/ppermute | solution.py:191
  14.5 0.0 copy-done.1
  14.5 1.8 %shard_map.74 = (f32[128,256]{1,0:T(8,128)S(1)}, f32[128,256]{1,0:T(8,128)S(1)}, f32[2,512]{1,0:T(2,128)S(1)}, f32[2,512]{1,0:T(2,128)S(1)}, f32[2,512]{1,0:T(2,128)S(1)}) custom-call(s32[1]{0:T(128)} %bitcast.7.count_ref, s32[16]{0:T(128)S(1)} %bitcast.15, s32[16,512]{1,0:T(8,128)S(1)} %bitcast.12, f32[1,64]{1,0:T(1,128)S(1)} %bitcast.18, ...), custom_call_target="tpu_custom_call" | custom-call | flops 805306368 | bytes 1048576 | tf_op jit(solution)/shard_map/pallas_call | solution.py:195
  16.3 0.1 collective-permute-start.3
  16.4 3.6 %collective-permute-start.4 = (f32[2,512]{1,0:T(2,128)S(1)}, f32[2,512]{1,0:T(2,128)S(1)}, u32[]{:S(2)}, u32[]{:S(2)}) collective-permute-start(f32[2,512]{1,0:T(2,128)S(1)} %get-tuple-element.21), channel_id=1, source_target_pairs={{0,2},{1,3},{2,0},{3,1},{4,6},{5,7},{6,4},{7,5},{8,10},{9,11},{10,... | collective-permute-start | bytes 12296 | tf_op jit(solution)/shard_map/ppermute | solution.py:191
  20.1 0.1 collective-permute-start.5
  20.2 1.6 %collective-permute-done.3.refs_0_ = f32[2,512]{1,0:T(2,128)S(1)} collective-permute-done((f32[2,512]{1,0:T(2,128)S(1)}, f32[2,512]{1,0:T(2,128)S(1)}, u32[]{:S(2)}, u32[]{:S(2)}) %collective-permute-start.3) | collective-permute-done | bytes 4128 | tf_op jit(solution)/shard_map/ppermute | solution.py:191
  21.8 0.0 collective-permute-done.4.refs_1_
  21.8 1.9 %collective-permute-done.5.refs_2_ = f32[2,512]{1,0:T(2,128)S(1)} collective-permute-done((f32[2,512]{1,0:T(2,128)S(1)}, f32[2,512]{1,0:T(2,128)S(1)}, u32[]{:S(2)}, u32[]{:S(2)}) %collective-permute-start.5) | collective-permute-done | bytes 4128 | tf_op jit(solution)/shard_map/ppermute | solution.py:191
  23.7 1.1 %shard_map.75 = f32[16,256]{1,0:T(8,128)S(1)} custom-call(s32[1]{0:T(128)} %bitcast.8.count_ref, s32[16]{0:T(128)S(1)} %bitcast.16, s32[16,512]{1,0:T(8,128)S(1)} %bitcast.13, f32[1,64]{1,0:T(1,128)S(1)} %bitcast.19, f32[128,256]{1,0:T(8,128)S(1)} %bitcast.10, f32[128,256]{1,0:T(8,128)S(1)} %get-tuple-element.19.image_ref, ...), custom_call_target="tpu_custom_call" | custom-call | flops 402653184 | bytes 1048576 | tf_op jit(solution)/shard_map/pallas_call | solution.py:195
  24.8 2.0 %collective-permute-start.8 = (f32[16,256]{1,0:T(8,128)S(1)}, f32[16,256]{1,0:T(8,128)S(1)}, u32[]{:S(2)}, u32[]{:S(2)}) collective-permute-start(f32[16,256]{1,0:T(8,128)S(1)} %shard_map.75), channel_id=1, source_target_pairs={{0,3},{1,0},{2,1},{3,2},{4,7},{5,4},{6,5},{7,6},{8,11},{9,8},{10,9... | collective-permute-start | bytes 49160 | tf_op jit(solution)/shard_map/ppermute | solution.py:191
  26.8 0.2 collective-permute-start.7
  27.0 0.8 %collective-permute-start.6 = (f32[16,256]{1,0:T(8,128)S(1)}, f32[16,256]{1,0:T(8,128)S(1)}, u32[]{:S(2)}, u32[]{:S(2)}) collective-permute-start(f32[16,256]{1,0:T(8,128)S(1)} %shard_map.75), channel_id=1, source_target_pairs={{0,1},{1,2},{2,3},{3,0},{4,5},{5,6},{6,7},{7,4},{8,9},{9,10},{10,1... | collective-permute-start | bytes 49160 | tf_op jit(solution)/shard_map/ppermute | solution.py:191
  27.8 0.8 %collective-permute-done.8 = f32[16,256]{1,0:T(8,128)S(1)} collective-permute-done((f32[16,256]{1,0:T(8,128)S(1)}, f32[16,256]{1,0:T(8,128)S(1)}, u32[]{:S(2)}, u32[]{:S(2)}) %collective-permute-start.8) | collective-permute-done | bytes 16416 | tf_op jit(solution)/shard_map/ppermute | solution.py:191
  28.6 2.8 %collective-permute-done.7 = f32[16,256]{1,0:T(8,128)S(1)} collective-permute-done((f32[16,256]{1,0:T(8,128)S(1)}, f32[16,256]{1,0:T(8,128)S(1)}, u32[]{:S(2)}, u32[]{:S(2)}) %collective-permute-start.7) | collective-permute-done | bytes 16416 | tf_op jit(solution)/shard_map/ppermute | solution.py:191
  31.4 1.1 %collective-permute-done.6 = f32[16,256]{1,0:T(8,128)S(1)} collective-permute-done((f32[16,256]{1,0:T(8,128)S(1)}, f32[16,256]{1,0:T(8,128)S(1)}, u32[]{:S(2)}, u32[]{:S(2)}) %collective-permute-start.6) | collective-permute-done | bytes 16416 | tf_op jit(solution)/shard_map/ppermute | solution.py:191
  32.5 0.0 collective-permute-start.11
  32.5 1.6 %collective-permute-start.10 = (f32[16,256]{1,0:T(8,128)S(1)}, f32[16,256]{1,0:T(8,128)S(1)}, u32[]{:S(2)}, u32[]{:S(2)}) collective-permute-start(f32[16,256]{1,0:T(8,128)S(1)} %add_add_fusion.1), channel_id=1, source_target_pairs={{0,16},{8,24},{16,0},{24,8},{1,17},{9,25},{17,1},{25,9},{2,18},{10... | collective-permute-start | bytes 49160 | tf_op jit(solution)/shard_map/ppermute | solution.py:191
  34.1 0.2 collective-permute-start.9
  34.3 0.0 collective-permute-done.11
  34.3 2.1 %collective-permute-done.10 = f32[16,256]{1,0:T(8,128)S(1)} collective-permute-done((f32[16,256]{1,0:T(8,128)S(1)}, f32[16,256]{1,0:T(8,128)S(1)}, u32[]{:S(2)}, u32[]{:S(2)}) %collective-permute-start.10) | collective-permute-done | bytes 16416 | tf_op jit(solution)/shard_map/ppermute | solution.py:191
  36.3 0.9 %collective-permute-done.9 = f32[16,256]{1,0:T(8,128)S(1)} collective-permute-done((f32[16,256]{1,0:T(8,128)S(1)}, f32[16,256]{1,0:T(8,128)S(1)}, u32[]{:S(2)}, u32[]{:S(2)}) %collective-permute-start.9) | collective-permute-done | bytes 16416 | tf_op jit(solution)/shard_map/ppermute | solution.py:191
  37.3 1.5 %collective-permute-start.12 = (f32[16,256]{1,0:T(8,128)S(1)}, f32[16,256]{1,0:T(8,128)S(1)}, u32[]{:S(2)}, u32[]{:S(2)}) collective-permute-start(f32[16,256]{1,0:T(8,128)S(1)} %add_add_fusion.refs_0_), channel_id=1, source_target_pairs={{0,4},{4,0},{1,5},{5,1},{2,6},{6,2},{3,7},{7,3},{8,12},{12,8},{9,1... | collective-permute-start | bytes 49160 | tf_op jit(solution)/shard_map/ppermute | solution.py:191
  38.8 2.3 %collective-permute-done.12.refs_1_ = f32[16,256]{1,0:T(8,128)S(1)} collective-permute-done((f32[16,256]{1,0:T(8,128)S(1)}, f32[16,256]{1,0:T(8,128)S(1)}, u32[]{:S(2)}, u32[]{:S(2)}) %collective-permute-start.12) | collective-permute-done | bytes 16416 | tf_op jit(solution)/shard_map/ppermute | solution.py:191
  41.0 0.8 %shard_map.76 = f32[128,256]{1,0:T(8,128)} custom-call(f32[128,256]{1,0:T(8,128)S(1)} %get-tuple-element.14.first_ref, f32[128,256]{1,0:T(8,128)S(1)} %get-tuple-element.18.second_ref, f32[16,256]{1,0:T(8,128)S(1)} %add_add_fusion.refs_0_, f32[16,256]{1,0:T(8,128)S(1)} %collective-permute-done.12.refs_1_), custom_call_target="tpu_custom_call" | custom-call | flops 32768 | bytes 1048576 | tf_op jit(solution)/shard_map/pallas_call | solution.py:195
  (2 shorter events, 0.0 us)
Async XLA Ops:
  0.7 0.7 %copy-start.4 = (s32[1,1,1,16]{3,2,1,0:T(1,128)S(1)}, s32[1,1,1,16]{3,2,1,0:T(1,128)}, u32[]{:S(2)}) copy-start(s32[1,1,1,16]{3,2,1,0:T(1,128)} %param.10) | copy-start | bytes 196
  0.7 0.7 %copy-start.5 = (f32[1,1,1,64]{3,2,1,0:T(1,128)S(1)}, f32[1,1,1,64]{3,2,1,0:T(1,128)}, u32[]{:S(2)}) copy-start(f32[1,1,1,64]{3,2,1,0:T(1,128)} %param.8) | copy-start | bytes 772
  1.3 0.9 %copy-start = (f32[256,256]{1,0:T(8,128)S(1)}, f32[256,256]{1,0:T(8,128)}, u32[]{:S(2)}) copy-start(f32[256,256]{1,0:T(8,128)} %p_ref.3) | copy-start | bytes 786436
  2.3 0.9 %copy-start.2 = (f32[1,1,1,2,64,256]{5,4,3,2,1,0:T(8,128)S(1)}, f32[1,1,1,2,64,256]{5,4,3,2,1,0:T(8,128)}, u32[]{:S(2)}) copy-start(f32[1,1,1,2,64,256]{5,4,3,2,1,0:T(8,128)} %param.7) | copy-start | bytes 393220
  3.2 0.8 %copy-start.3 = (s32[1,1,1,16,512]{4,3,2,1,0:T(8,128)S(1)}, s32[1,1,1,16,512]{4,3,2,1,0:T(8,128)}, u32[]{:S(2)}) copy-start(s32[1,1,1,16,512]{4,3,2,1,0:T(8,128)} %param.11) | copy-start | bytes 98308
  3.9 10.5 %copy-start.1 = (f32[256,256]{1,0:T(8,128)S(1)}, f32[256,256]{1,0:T(8,128)}, u32[]{:S(2)}) copy-start(f32[256,256]{1,0:T(8,128)} %k_ref.3) | copy-start | bytes 786436
  5.2 7.0 %collective-permute-start = (f32[2,512]{1,0:T(2,128)S(1)}, f32[2,512]{1,0:T(2,128)S(1)}, u32[]{:S(2)}, u32[]{:S(2)}) collective-permute-start(f32[2,512]{1,0:T(2,128)S(1)} %get-tuple-element.15), channel_id=1, source_target_pairs={{0,1},{1,2},{2,3},{3,0},{4,5},{5,6},{6,7},{7,4},{8,9},{9,10},{10,1... | collective-permute-start | bytes 12296 | tf_op jit(solution)/shard_map/ppermute | solution.py:191
  8.2 4.5 %collective-permute-start.1 = (f32[2,512]{1,0:T(2,128)S(1)}, f32[2,512]{1,0:T(2,128)S(1)}, u32[]{:S(2)}, u32[]{:S(2)}) collective-permute-start(f32[2,512]{1,0:T(2,128)S(1)} %get-tuple-element.16), channel_id=1, source_target_pairs={{0,2},{1,3},{2,0},{3,1},{4,6},{5,7},{6,4},{7,5},{8,10},{9,11},{10,... | collective-permute-start | bytes 12296 | tf_op jit(solution)/shard_map/ppermute | solution.py:191
  10.8 3.6 %collective-permute-start.2 = (f32[2,512]{1,0:T(2,128)S(1)}, f32[2,512]{1,0:T(2,128)S(1)}, u32[]{:S(2)}, u32[]{:S(2)}) collective-permute-start(f32[2,512]{1,0:T(2,128)S(1)} %get-tuple-element.17), channel_id=1, source_target_pairs={{0,3},{1,0},{2,1},{3,2},{4,7},{5,4},{6,5},{7,6},{8,11},{9,8},{10,9... | collective-permute-start | bytes 12296 | tf_op jit(solution)/shard_map/ppermute | solution.py:191
  16.3 5.5 %collective-permute-start.3 = (f32[2,512]{1,0:T(2,128)S(1)}, f32[2,512]{1,0:T(2,128)S(1)}, u32[]{:S(2)}, u32[]{:S(2)}) collective-permute-start(f32[2,512]{1,0:T(2,128)S(1)} %get-tuple-element.20), channel_id=1, source_target_pairs={{0,1},{1,2},{2,3},{3,0},{4,5},{5,6},{6,7},{7,4},{8,9},{9,10},{10,1... | collective-permute-start | bytes 12296 | tf_op jit(solution)/shard_map/ppermute | solution.py:191
  16.4 5.3 %collective-permute-start.4 = (f32[2,512]{1,0:T(2,128)S(1)}, f32[2,512]{1,0:T(2,128)S(1)}, u32[]{:S(2)}, u32[]{:S(2)}) collective-permute-start(f32[2,512]{1,0:T(2,128)S(1)} %get-tuple-element.21), channel_id=1, source_target_pairs={{0,2},{1,3},{2,0},{3,1},{4,6},{5,7},{6,4},{7,5},{8,10},{9,11},{10,... | collective-permute-start | bytes 12296 | tf_op jit(solution)/shard_map/ppermute | solution.py:191
  20.1 3.6 %collective-permute-start.5 = (f32[2,512]{1,0:T(2,128)S(1)}, f32[2,512]{1,0:T(2,128)S(1)}, u32[]{:S(2)}, u32[]{:S(2)}) collective-permute-start(f32[2,512]{1,0:T(2,128)S(1)} %get-tuple-element.22), channel_id=1, source_target_pairs={{0,3},{1,0},{2,1},{3,2},{4,7},{5,4},{6,5},{7,6},{8,11},{9,8},{10,9... | collective-permute-start | bytes 12296 | tf_op jit(solution)/shard_map/ppermute | solution.py:191
  24.8 3.8 %collective-permute-start.8 = (f32[16,256]{1,0:T(8,128)S(1)}, f32[16,256]{1,0:T(8,128)S(1)}, u32[]{:S(2)}, u32[]{:S(2)}) collective-permute-start(f32[16,256]{1,0:T(8,128)S(1)} %shard_map.75), channel_id=1, source_target_pairs={{0,3},{1,0},{2,1},{3,2},{4,7},{5,4},{6,5},{7,6},{8,11},{9,8},{10,9... | collective-permute-start | bytes 49160 | tf_op jit(solution)/shard_map/ppermute | solution.py:191
  26.8 4.6 %collective-permute-start.7 = (f32[16,256]{1,0:T(8,128)S(1)}, f32[16,256]{1,0:T(8,128)S(1)}, u32[]{:S(2)}, u32[]{:S(2)}) collective-permute-start(f32[16,256]{1,0:T(8,128)S(1)} %shard_map.75), channel_id=1, source_target_pairs={{0,2},{1,3},{2,0},{3,1},{4,6},{5,7},{6,4},{7,5},{8,10},{9,11},{10,... | collective-permute-start | bytes 49160 | tf_op jit(solution)/shard_map/ppermute | solution.py:191
  27.0 5.5 %collective-permute-start.6 = (f32[16,256]{1,0:T(8,128)S(1)}, f32[16,256]{1,0:T(8,128)S(1)}, u32[]{:S(2)}, u32[]{:S(2)}) collective-permute-start(f32[16,256]{1,0:T(8,128)S(1)} %shard_map.75), channel_id=1, source_target_pairs={{0,1},{1,2},{2,3},{3,0},{4,5},{5,6},{6,7},{7,4},{8,9},{9,10},{10,1... | collective-permute-start | bytes 49160 | tf_op jit(solution)/shard_map/ppermute | solution.py:191
  32.5 1.8 %collective-permute-start.11 = (f32[16,256]{1,0:T(8,128)S(1)}, f32[16,256]{1,0:T(8,128)S(1)}, u32[]{:S(2)}, u32[]{:S(2)}) collective-permute-start(f32[16,256]{1,0:T(8,128)S(1)} %add_add_fusion.1), channel_id=1, source_target_pairs={{0,24},{8,0},{16,8},{24,16},{1,25},{9,1},{17,9},{25,17},{2,26},{10... | collective-permute-start | bytes 49160 | tf_op jit(solution)/shard_map/ppermute | solution.py:191
  32.5 3.8 %collective-permute-start.10 = (f32[16,256]{1,0:T(8,128)S(1)}, f32[16,256]{1,0:T(8,128)S(1)}, u32[]{:S(2)}, u32[]{:S(2)}) collective-permute-start(f32[16,256]{1,0:T(8,128)S(1)} %add_add_fusion.1), channel_id=1, source_target_pairs={{0,16},{8,24},{16,0},{24,8},{1,17},{9,25},{17,1},{25,9},{2,18},{10... | collective-permute-start | bytes 49160 | tf_op jit(solution)/shard_map/ppermute | solution.py:191
  34.1 3.2 %collective-permute-start.9 = (f32[16,256]{1,0:T(8,128)S(1)}, f32[16,256]{1,0:T(8,128)S(1)}, u32[]{:S(2)}, u32[]{:S(2)}) collective-permute-start(f32[16,256]{1,0:T(8,128)S(1)} %add_add_fusion.1), channel_id=1, source_target_pairs={{0,8},{8,16},{16,24},{24,0},{1,9},{9,17},{17,25},{25,1},{2,10},{10... | collective-permute-start | bytes 49160 | tf_op jit(solution)/shard_map/ppermute | solution.py:191
  37.3 3.7 %collective-permute-start.12 = (f32[16,256]{1,0:T(8,128)S(1)}, f32[16,256]{1,0:T(8,128)S(1)}, u32[]{:S(2)}, u32[]{:S(2)}) collective-permute-start(f32[16,256]{1,0:T(8,128)S(1)} %add_add_fusion.refs_0_), channel_id=1, source_target_pairs={{0,4},{4,0},{1,5},{5,1},{2,6},{6,2},{3,7},{7,3},{8,12},{12,8},{9,1... | collective-permute-start | bytes 49160 | tf_op jit(solution)/shard_map/ppermute | solution.py:191

commit v2 on v1

v2 whole, which is shorter than its diff:
```python
import functools

import jax
import jax.numpy as jnp
from jax import lax
from jax.experimental import pallas as pl
from jax.experimental.pallas import tpu as pltpu
from jax.sharding import PartitionSpec as P

coupling = 0.5
vmem_grant = 48 * 1024 * 1024
f32 = jnp.float32
bf16 = jnp.bfloat16
vmem_spec = pl.BlockSpec(memory_space=pltpu.VMEM)
smem_spec = pl.BlockSpec(memory_space=pltpu.SMEM)
hbm_spec = pl.BlockSpec(memory_space=pltpu.HBM)


def two_parts(value):
    high = value.astype(bf16)
    return high, (value - high.astype(f32)).astype(bf16)


def dot(left, right):
    return jnp.dot(left, right, preferred_element_type=f32)


def dot_transposed(left, right):
    return lax.dot_general(left, right, (((1,), (1,)), ((), ())), preferred_element_type=f32)


def times_matrix(rows, matrix):
    count = rows.shape[0]
    row_high, row_low = two_parts(rows)
    mat_high, mat_low = two_parts(matrix)
    both = dot(jnp.concatenate([row_high, row_low], axis=0), mat_high)
    return both[:count] + (both[count:] + dot(row_high, mat_low))


def split_index(index, dofs):
    if dofs & (dofs - 1) == 0:
        return lax.shift_right_arithmetic(index, dofs.bit_length() - 1), index & (dofs - 1)
    element = jnp.floor_divide(index, dofs)
    return element, index - element * dofs


def shift_slot(links_ref, index_ref, shift, members):
    target = lax.rem(lax.axis_index("gz") + shift, members)
    slot = jnp.int32(-1)
    for position in range(links_ref.shape[-1]):
        slot = jnp.where(links_ref[0, 0, 0, position] == target, jnp.int32(position), slot)
    row = index_ref[0, 0, 0, pl.ds(jnp.maximum(slot, 0), 1), :]
    return jnp.where(slot >= 0, row, -1)


def hot_columns(flat_row, elements, dofs):
    element, dof = split_index(flat_row, dofs)
    width = flat_row.shape[1]
    over_elements = lax.broadcasted_iota(jnp.int32, (elements, width), 0) == element
    over_dofs = (lax.broadcasted_iota(jnp.int32, (dofs, width), 0) == dof).astype(f32).astype(bf16)
    return over_elements, over_dofs


def viscosity_column(visc_row):
    elements = visc_row.shape[1]
    line = lax.broadcasted_iota(jnp.int32, (elements, elements), 0)
    column = lax.broadcasted_iota(jnp.int32, (elements, elements), 1)
    spread = jnp.where(line == column, jnp.broadcast_to(visc_row, (elements, elements)), 0.0)
    return jnp.sum(spread, axis=1, keepdims=True)


def wide(column, dofs):
    return jnp.broadcast_to(column, (column.shape[0], dofs))


def send_faces(field, probes, slots_ref, leave_ref):
    rows, dofs = field.shape
    elements = rows // probes
    members = slots_ref.shape[0] + 1
    high, low = two_parts(field)
    parts = jnp.concatenate([high, low], axis=0)
    me = lax.axis_index("gz")
    for shift in range(1, members):
        over_elements, over_dofs = hot_columns(slots_ref[pl.ds(shift - 1, 1), :], elements, dofs)
        picked = dot(parts, over_dofs)
        picked = picked[:rows] + picked[rows:]
        target = lax.rem(me + shift, members)
        for probe in range(probes):
            block = picked[probe * elements : (probe + 1) * elements]
            leave_ref[target, pl.ds(probe, 1), :] = jnp.sum(
                jnp.where(over_elements, block, 0.0), axis=0, keepdims=True
            )
    leave_ref[me] = jnp.zeros(leave_ref.shape[1:], f32)


def placed_faces(shape, probes, slots_ref, came_ref):
    rows, dofs = shape
    elements = rows // probes
    members = slots_ref.shape[0] + 1
    me = lax.axis_index("gz")
    total = jnp.zeros((2 * rows, dofs), f32)
    for shift in range(1, members):
        over_elements, over_dofs = hot_columns(slots_ref[pl.ds(shift - 1, 1), :], elements, dofs)
        came = came_ref[lax.rem(me + shift, members)]
        spread = jnp.concatenate(
            [
                jnp.where(over_elements, came[probe : probe + 1, :], 0.0)
                for probe in range(probes)
            ],
            axis=0,
        )
        high, low = two_parts(spread)
        total += dot_transposed(jnp.concatenate([high, low], axis=0), over_dofs)
    return total[:rows] + total[rows:]


def first_kernel(
    count_ref, links_hbm, index_hbm, visc_hbm, rhs_hbm, p_hbm,
    first_ref, source_ref, up_ref, down_ref, slots_ref, leave_ref,
    links_ref, index_ref, visc_ref, rhs_ref, p_ref, arrived,
):
    pairs = (
        (links_hbm, links_ref),
        (index_hbm, index_ref),
        (visc_hbm, visc_ref),
        (rhs_hbm, rhs_ref),
        (p_hbm, p_ref),
    )
    copies = [
        pltpu.make_async_copy(held, here, arrived.at[place])
        for place, (held, here) in enumerate(pairs)
    ]
    for copy in copies:
        copy.start()
    copies[0].wait()
    copies[1].wait()
    members = slots_ref.shape[0] + 1
    for shift in range(1, members):
        slots_ref[pl.ds(shift - 1, 1), :] = shift_slot(links_ref, index_ref, shift, members)
    copies[2].wait()
    probes, elements, dofs = rhs_ref.shape[3:]
    slot = lax.broadcasted_iota(jnp.int32, (elements, 1), 0)
    live = (slot < count_ref[0, 0, 0]).astype(f32)
    visc = viscosity_column(visc_ref[0, 0])
    up = wide(jnp.concatenate([live * visc] * probes, axis=0), dofs)
    down = wide(jnp.concatenate([live / visc] * probes, axis=0), dofs)
    up_ref[...] = up
    down_ref[...] = down
    copies[3].wait()
    source = rhs_ref[...].reshape(probes * elements, dofs)
    source = source * wide(jnp.concatenate([live] * probes, axis=0), dofs)
    source_ref[...] = source
    copies[4].wait()
    first_pre = times_matrix(source, p_ref[...]) * down
    first_ref[...] = first_pre
    send_faces(first_pre, probes, slots_ref, leave_ref)


def masked(placed, up):
    return jnp.where(up > 0.0, placed, 0.0)


def second_kernel(
    probes, slots_ref, up_ref, down_ref, first_ref, k_ref, p_ref, came_ref,
    image_ref, second_ref, leave_ref,
):
    up = up_ref[...]
    placed = placed_faces(first_ref.shape, probes, slots_ref, came_ref)
    image = times_matrix(first_ref[...], k_ref[...]) * up - masked(coupling * placed, up)
    image_ref[...] = image
    second_pre = times_matrix(image, p_ref[...]) * down_ref[...]
    second_ref[...] = second_pre
    send_faces(second_pre, probes, slots_ref, leave_ref)


def as_row(lines, lanes):
    count = -(-len(lines) // 8) * 8
    spare = jnp.zeros((count - len(lines), lines[0].shape[1]), f32)
    sums = jnp.sum(jnp.concatenate(lines + [spare], axis=0), axis=1, keepdims=True)
    line = lax.broadcasted_iota(jnp.int32, (count, lanes), 0)
    lane = lax.broadcasted_iota(jnp.int32, (count, lanes), 1)
    return jnp.sum(jnp.where(line == lane, sums, 0.0), axis=0, keepdims=True)


def third_kernel(
    probes, slots_ref, up_ref, source_ref, image_ref, second_ref, k_ref, came_ref, products_ref
):
    rows, dofs = source_ref.shape
    elements = rows // probes
    up = up_ref[...]
    placed = placed_faces(source_ref.shape, probes, slots_ref, came_ref)
    second_img = times_matrix(second_ref[...], k_ref[...]) * up - masked(coupling * placed, up)
    first_img = image_ref[...]
    source = source_ref[...]
    pairs = (
        (first_img, first_img),
        (first_img, second_img),
        (second_img, second_img),
        (first_img, source),
        (second_img, source),
    )
    lines = []
    for left, right in pairs:
        product = left * right
        for probe in range(probes):
            lines.append(
                jnp.sum(product[probe * elements : (probe + 1) * elements], axis=0, keepdims=True)
            )
    products_ref[...] = jnp.broadcast_to(as_row(lines, products_ref.shape[-1]), products_ref.shape)


def last_kernel(probes, first_ref, second_ref, parts_ref, out_ref):
    rows, _ = first_ref.shape
    elements = rows // probes
    total = jnp.sum(parts_ref[...], axis=0)
    for probe in range(probes):
        self_one, cross_mid, self_two, load_one, load_two = (
            total[:, place * probes + probe : place * probes + probe + 1] for place in range(5)
        )
        determinant = self_one * self_two - cross_mid * cross_mid
        weight_one = (self_two * load_one - cross_mid * load_two) / determinant
        weight_two = (self_one * load_two - cross_mid * load_one) / determinant
        block = pl.ds(probe * elements, elements)
        out_ref[block, :] = weight_one * first_ref[block, :] + weight_two * second_ref[block, :]


def call(kernel, in_specs, out_shapes, flops, *args, scratch=()):
    return pl.pallas_call(
        kernel,
        out_shape=out_shapes,
        in_specs=in_specs,
        out_specs=jax.tree.map(lambda _: vmem_spec, out_shapes),
        scratch_shapes=scratch,
        compiler_params=pltpu.CompilerParams(vmem_limit_bytes=vmem_grant),
        cost_estimate=pl.CostEstimate(flops=flops, bytes_accessed=1 << 20, transcendentals=0),
    )(*args)


def per_device(mesh, rhs, viscosity, counts, neighbours, face_index, k_matrix, p_matrix):
    probes, elements, dofs = rhs.shape[3:]
    width = face_index.shape[-1]
    members = mesh.shape["gz"]
    rows = probes * elements
    field = jax.ShapeDtypeStruct((rows, dofs), f32)
    slots_shape = jax.ShapeDtypeStruct((members - 1, width), jnp.int32)
    faces = jax.ShapeDtypeStruct((members, probes, width), f32)
    flops = 8 * rows * dofs * (members - 1) * width

    def exchange(value):
        return lax.all_to_all(value, "gz", split_axis=0, concat_axis=0)

    first_pre, source, up, down, slots, leaving = call(
        first_kernel,
        [smem_spec] + [hbm_spec] * 5,
        [field] * 4 + [slots_shape, faces],
        flops,
        counts,
        *(
            pltpu.with_memory_space_constraint(value, pltpu.HBM)
            for value in (neighbours, face_index, viscosity, rhs, p_matrix)
        ),
        scratch=[
            pltpu.SMEM(neighbours.shape, jnp.int32),
            pltpu.VMEM(face_index.shape, jnp.int32),
            pltpu.VMEM(viscosity.shape, f32),
            pltpu.VMEM(rhs.shape, f32),
            pltpu.VMEM(p_matrix.shape, f32),
            pltpu.SemaphoreType.DMA((5,)),
        ],
    )
    came = exchange(leaving)
    first_img, second_pre, leaving = call(
        functools.partial(second_kernel, probes),
        [vmem_spec] * 7,
        [field, field, faces],
        2 * flops,
        slots,
        up,
        down,
        first_pre,
        k_matrix,
        p_matrix,
        came,
    )
    came = exchange(leaving)
    devices = mesh.size
    lanes = -(-5 * probes // 128) * 128
    products = call(
        functools.partial(third_kernel, probes),
        [vmem_spec] * 7,
        jax.ShapeDtypeStruct((devices, 1, lanes), f32),
        flops,
        slots,
        up,
        source,
        first_img,
        second_pre,
        k_matrix,
        came,
    )
    parts = lax.all_to_all(products, ("gx", "gy", "gz"), split_axis=0, concat_axis=0)
    result = call(
        functools.partial(last_kernel, probes),
        [vmem_spec] * 3,
        field,
        rows * dofs,
        first_pre,
        second_pre,
        parts,
    )
    return result.reshape(rhs.shape)


def solution(mesh):
    return jax.shard_map(
        functools.partial(per_device, mesh),
        mesh=mesh,
        in_specs=(
            P("gx", "gy", "gz", None, None, None),
            P("gx", "gy", "gz", None),
            P("gx", "gy", "gz"),
            P("gx", "gy", "gz", None),
            P("gx", "gy", "gz", None, None),
            P(),
            P(),
        ),
        out_specs=P("gx", "gy", "gz", None, None, None),
        check_vma=False,
    )
```

time: 42.1 us -> 35.2 us (0.84)
  blocking collectives: 0 us -> 29.5 us
  starting transfers between devices: 17.1 us -> 0 us
  waiting for transfers between devices: 15.8 us -> 0 us
  local copies, waits for them, and re-layouts: 3.27 us -> 0.01 us
    all_to_all x0 -> x3, blocking collectives: none -> 29.5 us  [the longest x2 19.7 us: exchange(): return lax.all_to_all(value, 'gz', split_axis=0, concat_axis=0)]
    ppermute x13 -> x0, starting transfers between devices: 17.1 us -> none  [shifted(): lax.ppermute(array, axis, [(source, (source + shift) % size) for source i...]
    ppermute x13 -> x0, waiting for transfers between devices: 15.8 us -> none  [shifted(): lax.ppermute(array, axis, [(source, (source + shift) % size) for source i...]
    unnamed x12 -> x4, local copies, waits for them, and re-layouts: 3.27 us -> 0.01 us
  transfers between devices with their start and end apart: 13 -> 0, of which waited for: 10 -> 0; matrix products, arithmetic and copies ran while one was open for 0% -> 0% of each run, Pallas kernels for 0% -> 0%
where the time goes in v2:
time: 35.2 us; the launch traced here: 34.9 us
  blocking collectives  29.5 us (84%)
  Pallas kernels  4.71 us (13%)
  between operations  0.69 us (2%)
    all_to_all x2, blocking collectives, exchange(): return lax.all_to_all(value, 'gz', split_axis=0, concat_axis=0)  19.7 us
    all_to_all x1, blocking collectives, per_device(): lax.all_to_all(products, ('gx', 'gy', 'gz'), split_axis=0, concat_axis=0)  9.83 us
    pallas_call x4, Pallas kernels, call(): pl.pallas_call(kernel, out_shape=out_shapes, in_specs=in_specs, out_specs...  4.71 us

profile of v2, /device:TPU:0, one launch (start us, length us, event | category | flops | bytes accessed | tf_op | source)
XLA Modules:
  0.0 34.9 jit_solution(10609484054763218234)
XLA Ops:
  0.7 0.0 copy-start
  0.7 0.0 copy-start.1
  0.7 1.8 %shard_map.73 = (f32[128,256]{1,0:T(8,128)S(1)}, f32[128,256]{1,0:T(8,128)S(1)}, f32[128,256]{1,0:T(8,128)S(1)}, f32[128,256]{1,0:T(8,128)S(1)}, s32[3,512]{1,0:T(4,128)S(1)}, /*index=5*/f32[4,2,512]{2,1,0:T(2,128)S(1)}) custom-call(s32[1,1,1]{2,1,0:T(1,128)S(6)} %copy.8.count_ref, s32[1,1,1,16]{3,2,1,0:T(1,128)} %links_hbm.1, ...), custom_call_target="tpu_custom_call" | custom-call | flops 402653184 | bytes 1048576 | tf_op jit(solution)/shard_map/pallas_call | solution.py:228
  2.5 11.7 %all_to_all.15.came_ref = f32[4,2,512]{2,1,0:T(2,128)S(1)} all-to-all(f32[4,2,512]{2,1,0:T(2,128)S(1)} %get-tuple-element.18), channel_id=1, replica_groups=mesh['gx'=4,'gy'=2,'gz'=4] {'gz'}, dimensions={0} | all-to-all | bytes 32768 | tf_op jit(solution)/shard_map/all_to_all | solution.py:250
  14.2 0.0 copy-done
  14.2 0.0 copy-done.1
  14.2 1.3 %shard_map.74 = (f32[128,256]{1,0:T(8,128)S(1)}, f32[128,256]{1,0:T(8,128)S(1)}, f32[4,2,512]{2,1,0:T(2,128)S(1)}) custom-call(s32[3,512]{1,0:T(4,128)S(1)} %get-tuple-element.15.slots_ref, f32[128,256]{1,0:T(8,128)S(1)} %get-tuple-element.16.up_ref, f32[128,256]{1,0:T(8,128)S(1)} %get-tuple-element.17.down_ref, f32[128,256]{1,0:T(8,128)S(1)} %get-tuple-element.14.first_ref, ...), custom_call_target="tpu_custom_call" | custom-call | flops 805306368 | bytes 1048576 | tf_op jit(solution)/shard_map/pallas_call | solution.py:228
  15.5 8.0 %all_to_all.16.came_ref = f32[4,2,512]{2,1,0:T(2,128)S(1)} all-to-all(f32[4,2,512]{2,1,0:T(2,128)S(1)} %get-tuple-element.22), channel_id=1, replica_groups=mesh['gx'=4,'gy'=2,'gz'=4] {'gz'}, dimensions={0} | all-to-all | bytes 32768 | tf_op jit(solution)/shard_map/all_to_all | solution.py:250
  23.5 0.6 %shard_map.75 = f32[32,1,128]{2,1,0:T(1,128)S(1)} custom-call(s32[3,512]{1,0:T(4,128)S(1)} %get-tuple-element.15.slots_ref, f32[128,256]{1,0:T(8,128)S(1)} %get-tuple-element.16.up_ref, f32[128,256]{1,0:T(8,128)S(1)} %get-tuple-element.20.source_ref, f32[128,256]{1,0:T(8,128)S(1)} %get-tuple-element.21.image_ref, ...), custom_call_target="tpu_custom_call" | custom-call | flops 402653184 | bytes 1048576 | tf_op jit(solution)/shard_map/pallas_call | solution.py:228
  24.2 9.8 %all_to_all.17.parts_ref = f32[32,1,128]{2,1,0:T(1,128)S(1)} all-to-all(f32[32,1,128]{2,1,0:T(1,128)S(1)} %shard_map.75), channel_id=1, replica_groups=mesh['gx'=4,'gy'=2,'gz'=4] {'gx','gy','gz'}, dimensions={0} | all-to-all | bytes 32768 | tf_op jit(solution)/shard_map/all_to_all | solution.py:301
  34.0 1.0 %shard_map.76 = f32[128,256]{1,0:T(8,128)} custom-call(f32[128,256]{1,0:T(8,128)S(1)} %get-tuple-element.14.first_ref, f32[128,256]{1,0:T(8,128)S(1)} %get-tuple-element.19.second_ref, f32[32,1,128]{2,1,0:T(1,128)S(1)} %all_to_all.17.parts_ref), custom_call_target="tpu_custom_call" | custom-call | flops 32768 | bytes 1048576 | tf_op jit(solution)/shard_map/pallas_call | solution.py:228
Async XLA Ops:
  0.7 13.6 %copy-start = (f32[256,256]{1,0:T(8,128)S(1)}, f32[256,256]{1,0:T(8,128)}, u32[]{:S(2)}) copy-start(f32[256,256]{1,0:T(8,128)} %p_ref.1) | copy-start | bytes 786436
  0.7 13.6 %copy-start.1 = (f32[256,256]{1,0:T(8,128)S(1)}, f32[256,256]{1,0:T(8,128)}, u32[]{:S(2)}) copy-start(f32[256,256]{1,0:T(8,128)} %k_ref.3) | copy-start | bytes 786436

commit v3 on v2

v3 whole, which is shorter than its diff:
```python
import functools

import jax
import jax.numpy as jnp
from jax import lax
from jax.experimental import pallas as pl
from jax.experimental.pallas import tpu as pltpu
from jax.sharding import PartitionSpec as P

coupling = 0.5
vmem_grant = 48 * 1024 * 1024
short_group = 4
f32 = jnp.float32
bf16 = jnp.bfloat16
vmem_spec = pl.BlockSpec(memory_space=pltpu.VMEM)
smem_spec = pl.BlockSpec(memory_space=pltpu.SMEM)
hbm_spec = pl.BlockSpec(memory_space=pltpu.HBM)


def two_parts(value):
    high = value.astype(bf16)
    return high, (value - high.astype(f32)).astype(bf16)


def dot(left, right):
    return jnp.dot(left, right, preferred_element_type=f32)


def dot_transposed(left, right):
    return lax.dot_general(left, right, (((1,), (1,)), ((), ())), preferred_element_type=f32)


def times_matrix(rows, matrix):
    count = rows.shape[0]
    row_high, row_low = two_parts(rows)
    mat_high, mat_low = two_parts(matrix)
    both = dot(jnp.concatenate([row_high, row_low], axis=0), mat_high)
    return both[:count] + (both[count:] + dot(row_high, mat_low))


def split_index(index, dofs):
    if dofs & (dofs - 1) == 0:
        return lax.shift_right_arithmetic(index, dofs.bit_length() - 1), index & (dofs - 1)
    element = jnp.floor_divide(index, dofs)
    return element, index - element * dofs


def shift_slot(links_ref, index_ref, shift, members):
    target = lax.rem(lax.axis_index("gz") + shift, members)
    slot = jnp.int32(-1)
    for position in range(links_ref.shape[-1]):
        slot = jnp.where(links_ref[0, 0, 0, position] == target, jnp.int32(position), slot)
    row = index_ref[0, 0, 0, pl.ds(jnp.maximum(slot, 0), 1), :]
    return jnp.where(slot >= 0, row, -1)


def hot_elements(flat_row, elements, dofs):
    element, _ = split_index(flat_row, dofs)
    return lax.broadcasted_iota(jnp.int32, (elements, flat_row.shape[1]), 0) == element


def hot_dofs(flat_row, dofs):
    _, dof = split_index(flat_row, dofs)
    line = lax.broadcasted_iota(jnp.int32, (dofs, flat_row.shape[1]), 0)
    return (line == dof).astype(f32).astype(bf16)


def as_column(row):
    elements = row.shape[1]
    line = lax.broadcasted_iota(jnp.int32, (elements, elements), 0)
    column = lax.broadcasted_iota(jnp.int32, (elements, elements), 1)
    spread = jnp.where(line == column, jnp.broadcast_to(row, (elements, elements)), 0.0)
    return jnp.sum(spread, axis=1, keepdims=True)


def wide(column, probes, dofs):
    return jnp.broadcast_to(jnp.concatenate([column] * probes, axis=0), (probes * column.shape[0], dofs))


def stacked(value):
    return jnp.concatenate(two_parts(value), axis=0)


def take_faces(parts, over_elements, over_dofs):
    elements = over_elements.shape[0]
    rows = parts.shape[0] // 2
    picked = dot(parts, over_dofs)
    picked = picked[:rows] + picked[rows:]
    return [
        jnp.sum(jnp.where(over_elements, picked[low : low + elements], 0.0), axis=0, keepdims=True)
        for low in range(0, rows, elements)
    ]


def add_faces(values, over_elements, over_dofs):
    highs = [value.astype(bf16).astype(f32) for value in values]
    lows = [value - high for value, high in zip(values, highs)]
    spread = jnp.concatenate(
        [jnp.where(over_elements, part, 0.0).astype(bf16) for part in highs + lows], axis=0
    )
    return dot_transposed(spread, over_dofs)


def folded(parts):
    rows = parts.shape[0] // 2
    return parts[:rows] + parts[rows:]


def as_row(lines, lanes):
    count = -(-len(lines) // 8) * 8
    spare = jnp.zeros((count - len(lines), lines[0].shape[1]), f32)
    sums = jnp.sum(jnp.concatenate(lines + [spare], axis=0), axis=1, keepdims=True)
    line = lax.broadcasted_iota(jnp.int32, (count, lanes), 0)
    lane = lax.broadcasted_iota(jnp.int32, (count, lanes), 1)
    return jnp.sum(jnp.where(line == lane, sums, 0.0), axis=0, keepdims=True)


def inner_products(first_img, second_img, source, probes, products_ref):
    elements = source.shape[0] // probes
    pairs = (
        (first_img, first_img),
        (first_img, second_img),
        (second_img, second_img),
        (first_img, source),
        (second_img, source),
    )
    lines = []
    for left, right in pairs:
        product = left * right
        for probe in range(probes):
            lines.append(
                jnp.sum(product[probe * elements : (probe + 1) * elements], axis=0, keepdims=True)
            )
    products_ref[...] = jnp.broadcast_to(as_row(lines, products_ref.shape[-1]), products_ref.shape)


def begin(refs):
    count_ref, links_hbm, index_hbm, visc_hbm, rhs_hbm, *matrices_hbm = refs["operands"]
    links_ref, index_ref, visc_ref, rhs_ref, *matrix_refs, arrived = refs["scratch"]
    pairs = (
        (links_hbm, links_ref),
        (index_hbm, index_ref),
        (visc_hbm, visc_ref),
        (rhs_hbm, rhs_ref),
        *zip(matrices_hbm, matrix_refs),
    )
    copies = [
        pltpu.make_async_copy(held, here, arrived.at[place])
        for place, (held, here) in enumerate(pairs)
    ]
    for copy in copies:
        copy.start()
    copies[0].wait()
    copies[1].wait()
    slots_ref = refs["slots"]
    members = slots_ref.shape[0] + 1
    for shift in range(1, members):
        slots_ref[shift - 1] = shift_slot(links_ref, index_ref, shift, members)
    copies[2].wait()
    probes, elements, dofs = rhs_ref.shape[3:]
    slot = lax.broadcasted_iota(jnp.int32, (elements, 1), 0)
    live = (slot < count_ref[0, 0, 0]).astype(f32)
    visc = as_column(visc_ref[0, 0])
    up = wide(live * visc, probes, dofs)
    down = wide(live / visc, probes, dofs)
    refs["up"][...] = up
    refs["down"][...] = down
    copies[3].wait()
    source = rhs_ref[...].reshape(probes * elements, dofs) * wide(live, probes, dofs)
    refs["source"][...] = source
    for copy in copies[4:]:
        copy.wait()
    first_pre = times_matrix(source, matrix_refs[0][...]) * down
    refs["first"][...] = first_pre
    return first_pre, up, down


def message_places(shifts, probes):
    values = shifts * probes
    return values, values + probes, values + probes + shifts


def near_first_kernel(*refs):
    operands, refs = refs[:7], refs[7:]
    first_ref, source_ref, up_ref, down_ref, base_ref, slots_ref, hot_ref = refs[:7]
    shifts, _, width = slots_ref.shape
    leave_refs, scratch = refs[7 : 7 + shifts], refs[7 + shifts :]
    visc_ref, rhs_ref, p_ref, k_ref = scratch[2:6]
    probes, elements, dofs = rhs_ref.shape[3:]
    first_pre, up, down = begin(
        {
            "operands": operands,
            "scratch": scratch,
            "slots": slots_ref,
            "up": up_ref,
            "down": down_ref,
            "source": source_ref,
            "first": first_ref,
        }
    )
    base = times_matrix(first_pre, k_ref[...]) * up
    base_ref[...] = base
    first_parts = stacked(first_pre)
    second_parts = stacked(times_matrix(base, p_ref[...]) * down)
    second_at, index_at, visc_at = message_places(shifts, probes)
    slot = lax.broadcasted_iota(jnp.int32, (1, elements), 1)
    live_visc = jnp.where(slot < operands[0][0, 0, 0], visc_ref[0, 0], 0.0)
    for shift in range(1, shifts + 1):
        flat_row = slots_ref[shift - 1]
        over_elements = hot_elements(flat_row, elements, dofs)
        over_dofs = hot_dofs(flat_row, dofs)
        hot_ref[:, (shift - 1) * width : shift * width] = over_dofs
        first_rows = take_faces(first_parts, over_elements, over_dofs)
        second_rows = take_faces(second_parts, over_elements, over_dofs)
        for probe in range(probes):
            leave_refs[shift - 1][second_at + probe] = second_rows[probe]
            for leave_ref in leave_refs:
                leave_ref[(shift - 1) * probes + probe] = first_rows[probe]
        for leave_ref in leave_refs:
            leave_ref[index_at + shift - 1] = flat_row.astype(f32)
    for leave_ref in leave_refs:
        leave_ref[visc_at, :, :elements] = live_visc


def near_second_kernel(
    source_ref, up_ref, down_ref, base_ref, slots_ref, hot_ref, k_ref, p_ref, mine_ref, *refs
):
    came_refs = refs[:-3]
    image_ref, second_ref, products_ref = refs[-3:]
    shifts, _, width = slots_ref.shape
    members = shifts + 1
    rows, dofs = source_ref.shape
    second_at, index_at, visc_at = message_places(shifts, 0)
    probes = (mine_ref.shape[0] - visc_at - 1) // members
    elements = rows // probes
    second_at, index_at, visc_at = message_places(shifts, probes)

    def message(ahead):
        ahead = ahead % members
        return mine_ref if ahead == 0 else came_refs[members - ahead - 1]

    def inbound_first(ahead, shift):
        row = (members - shift - 1) * probes
        sent = message(ahead + shift)
        return [sent[row + probe] for probe in range(probes)]

    own_elements = [hot_elements(slots_ref[shift], elements, dofs) for shift in range(shifts)]
    own_dofs = [hot_ref[:, shift * width : (shift + 1) * width] for shift in range(shifts)]

    def placed_here(values):
        return folded(
            sum(add_faces(values[i], own_elements[i], own_dofs[i]) for i in range(shifts))
        )

    up, down = up_ref[...], down_ref[...]
    live = up > 0.0
    placed = placed_here([inbound_first(0, shift) for shift in range(1, members)])
    image = base_ref[...] - jnp.where(live, coupling * placed, 0.0)
    image_ref[...] = image
    images, back = [image], []
    for ahead in range(1, members):
        total = 0.0
        for shift in range(1, members):
            flat_row = message(ahead)[index_at + shift - 1].astype(jnp.int32)
            over_elements = hot_elements(flat_row, elements, dofs)
            over_dofs = hot_dofs(flat_row, dofs)
            total = total + add_faces(inbound_first(ahead, shift), over_elements, over_dofs)
            if shift + ahead == members:
                back.append((over_elements, over_dofs))
        images.append(-coupling * folded(total))
    smooth = times_matrix(jnp.concatenate(images, axis=0), p_ref[...])
    second_pre = smooth[:rows] * down
    second_ref[...] = second_pre
    values = []
    for ahead in range(1, members):
        sent = message(ahead)
        visc = as_column(sent[visc_at, :, :elements])
        scale = wide(jnp.where(visc > 0.0, 1.0 / visc, 0.0), probes, dofs)
        change = smooth[ahead * rows : (ahead + 1) * rows] * scale
        taken = take_faces(stacked(change), *back[ahead - 1])
        values.append([taken[probe] + sent[second_at + probe] for probe in range(probes)])
    placed = placed_here(values)
    second_img = times_matrix(second_pre, k_ref[...]) * up - jnp.where(live, coupling * placed, 0.0)
    inner_products(image, second_img, source_ref[...], probes, products_ref)


def leave_faces(field, probes, slots_ref, leave_ref):
    elements, dofs = field.shape[0] // probes, field.shape[1]
    members = slots_ref.shape[0] + 1
    parts = stacked(field)
    me = lax.axis_index("gz")
    for shift in range(1, members):
        flat_row = slots_ref[shift - 1]
        taken = take_faces(parts, hot_elements(flat_row, elements, dofs), hot_dofs(flat_row, dofs))
        target = lax.rem(me + shift, members)
        for probe in range(probes):
            leave_ref[target, pl.ds(probe, 1), :] = taken[probe]
    leave_ref[me] = jnp.zeros(leave_ref.shape[1:], f32)


def placed_faces(shape, probes, slots_ref, came_ref):
    rows, dofs = shape
    elements = rows // probes
    members = slots_ref.shape[0] + 1
    me = lax.axis_index("gz")
    total = jnp.zeros((2 * rows, dofs), f32)
    for shift in range(1, members):
        flat_row = slots_ref[shift - 1]
        came = came_ref[lax.rem(me + shift, members)]
        total += add_faces(
            [came[probe : probe + 1, :] for probe in range(probes)],
            hot_elements(flat_row, elements, dofs),
            hot_dofs(flat_row, dofs),
        )
    return folded(total)


def far_first_kernel(*refs):
    operands, refs = refs[:6], refs[6:]
    first_ref, source_ref, up_ref, down_ref, slots_ref, leave_ref = refs[:6]
    first_pre, _, _ = begin(
        {
            "operands": operands,
            "scratch": refs[6:],
            "slots": slots_ref,
            "up": up_ref,
            "down": down_ref,
            "source": source_ref,
            "first": first_ref,
        }
    )
    leave_faces(first_pre, leave_ref.shape[1], slots_ref, leave_ref)


def far_second_kernel(
    slots_ref, up_ref, down_ref, first_ref, k_ref, p_ref, came_ref,
    image_ref, second_ref, leave_ref,
):
    probes = came_ref.shape[1]
    up = up_ref[...]
    placed = placed_faces(first_ref.shape, probes, slots_ref, came_ref)
    image = times_matrix(first_ref[...], k_ref[...]) * up - jnp.where(up > 0.0, coupling * placed, 0.0)
    image_ref[...] = image
    second_pre = times_matrix(image, p_ref[...]) * down_ref[...]
    second_ref[...] = second_pre
    leave_faces(second_pre, probes, slots_ref, leave_ref)


def far_third_kernel(
    slots_ref, up_ref, source_ref, image_ref, second_ref, k_ref, came_ref, products_ref
):
    probes = came_ref.shape[1]
    up = up_ref[...]
    placed = placed_faces(source_ref.shape, probes, slots_ref, came_ref)
    second_img = times_matrix(second_ref[...], k_ref[...]) * up - jnp.where(up > 0.0, coupling * placed, 0.0)
    inner_products(image_ref[...], second_img, source_ref[...], probes, products_ref)


def last_kernel(probes, first_ref, second_ref, parts_ref, out_ref):
    rows, _ = first_ref.shape
    elements = rows // probes
    total = jnp.sum(parts_ref[...], axis=0)
    for probe in range(probes):
        self_one, cross_mid, self_two, load_one, load_two = (
            total[:, place * probes + probe : place * probes + probe + 1] for place in range(5)
        )
        determinant = self_one * self_two - cross_mid * cross_mid
        weight_one = (self_two * load_one - cross_mid * load_two) / determinant
        weight_two = (self_one * load_two - cross_mid * load_one) / determinant
        block = pl.ds(probe * elements, elements)
        out_ref[block, :] = weight_one * first_ref[block, :] + weight_two * second_ref[block, :]


def call(kernel, in_specs, out_shapes, flops, *args, scratch=()):
    return pl.pallas_call(
        kernel,
        out_shape=out_shapes,
        in_specs=in_specs,
        out_specs=jax.tree.map(lambda _: vmem_spec, out_shapes),
        scratch_shapes=scratch,
        compiler_params=pltpu.CompilerParams(vmem_limit_bytes=vmem_grant),
        cost_estimate=pl.CostEstimate(flops=flops, bytes_accessed=1 << 20, transcendentals=0),
    )(*args)


def begin_call(kernel, out_shapes, flops, counts, *fetched):
    links, *others = fetched
    scratch = [pltpu.SMEM(links.shape, links.dtype)]
    scratch += [pltpu.VMEM(value.shape, value.dtype) for value in others]
    return call(
        kernel,
        [smem_spec] + [hbm_spec] * len(fetched),
        out_shapes,
        flops,
        counts,
        *(pltpu.with_memory_space_constraint(value, pltpu.HBM) for value in fetched),
        scratch=scratch + [pltpu.SemaphoreType.DMA((len(fetched),))],
    )


def near_steps(members, shapes, arguments):
    rhs, viscosity, counts, neighbours, face_index, k_matrix, p_matrix = arguments
    field, slots_shape, products_shape = shapes
    rows, dofs = field.shape
    shifts, _, width = slots_shape.shape
    probes = rhs.shape[3]
    flops = 8 * rows * dofs * shifts * width
    hot = jax.ShapeDtypeStruct((dofs, shifts * width), bf16)
    length = message_places(shifts, probes)[2] + 1
    messages = [jax.ShapeDtypeStruct((length, 1, width), f32)] * shifts
    first_pre, source, up, down, base, slots, hot_own, *leaving = begin_call(
        near_first_kernel,
        [field] * 5 + [slots_shape, hot] + messages,
        2 * flops,
        counts,
        neighbours,
        face_index,
        viscosity,
        rhs,
        p_matrix,
        k_matrix,
    )
    came = [
        lax.ppermute(
            value, "gz", [(source, (source + shift) % members) for source in range(members)]
        )
        for shift, value in enumerate(leaving, 1)
    ]
    _, second_pre, products = call(
        near_second_kernel,
        [vmem_spec] * (9 + shifts),
        [field, field, products_shape],
        6 * flops,
        source,
        up,
        down,
        base,
        slots,
        hot_own,
        k_matrix,
        p_matrix,
        leaving[0],
        *came,
    )
    return first_pre, second_pre, products


def far_steps(members, shapes, arguments):
    rhs, viscosity, counts, neighbours, face_index, k_matrix, p_matrix = arguments
    field, slots_shape, products_shape = shapes
    rows, dofs = field.shape
    shifts, _, width = slots_shape.shape
    flops = 8 * rows * dofs * shifts * width
    faces = jax.ShapeDtypeStruct((members, rhs.shape[3], width), f32)

    def exchange(value):
        return lax.all_to_all(value, "gz", split_axis=0, concat_axis=0)

    first_pre, source, up, down, slots, leaving = begin_call(
        far_first_kernel,
        [field] * 4 + [slots_shape, faces],
        flops,
        counts,
        neighbours,
        face_index,
        viscosity,
        rhs,
        p_matrix,
    )
    first_img, second_pre, leaving = call(
        far_second_kernel,
        [vmem_spec] * 7,
        [field, field, faces],
        2 * flops,
        slots,
        up,
        down,
        first_pre,
        k_matrix,
        p_matrix,
        exchange(leaving),
    )
    products = call(
        far_third_kernel,
        [vmem_spec] * 7,
        products_shape,
        flops,
        slots,
        up,
        source,
        first_img,
        second_pre,
        k_matrix,
        exchange(leaving),
    )
    return first_pre, second_pre, products


def per_device(mesh, *arguments):
    rhs, face_index = arguments[0], arguments[4]
    probes, elements, dofs = rhs.shape[3:]
    members = mesh.shape["gz"]
    lanes = -(-5 * probes // 128) * 128
    shapes = (
        jax.ShapeDtypeStruct((probes * elements, dofs), f32),
        jax.ShapeDtypeStruct((members - 1, 1, face_index.shape[-1]), jnp.int32),
        jax.ShapeDtypeStruct((mesh.size, 1, lanes), f32),
    )
    near = 1 < members <= short_group and elements <= face_index.shape[-1]
    near = near and elements * dofs < 1 << 24
    steps = near_steps if near else far_steps
    first_pre, second_pre, products = steps(members, shapes, arguments)
    result = call(
        functools.partial(last_kernel, probes),
        [vmem_spec] * 3,
        shapes[0],
        probes * elements * dofs,
        first_pre,
        second_pre,
        lax.all_to_all(products, ("gx", "gy", "gz"), split_axis=0, concat_axis=0),
    )
    return result.reshape(rhs.shape)


def solution(mesh):
    return jax.shard_map(
        functools.partial(per_device, mesh),
        mesh=mesh,
        in_specs=(
            P("gx", "gy", "gz", None, None, None),
            P("gx", "gy", "gz", None),
            P("gx", "gy", "gz"),
            P("gx", "gy", "gz", None),
            P("gx", "gy", "gz", None, None),
            P(),
            P(),
        ),
        out_specs=P("gx", "gy", "gz", None, None, None),
        check_vma=False,
    )
```

time: 35.2 us -> 27.9 us (0.79)
  blocking collectives: 29.5 us -> 9.73 us
  starting transfers between devices: 0 us -> 6.13 us
  waiting for transfers between devices: 0 us -> 4.94 us
  Pallas kernels: 4.71 us -> 6.23 us
    all_to_all x2 -> x0, blocking collectives: 19.7 us -> none  [exchange(): return lax.all_to_all(value, 'gz', split_axis=0, concat_axis=0)]
    ppermute x0 -> x3, starting transfers between devices: none -> 6.13 us  [near_steps(): lax.ppermute(value, 'gz', [(source, (source + shift) % members) for sourc...]
    ppermute x0 -> x3, waiting for transfers between devices: none -> 4.94 us  [near_steps(): lax.ppermute(value, 'gz', [(source, (source + shift) % members) for sourc...]
    pallas_call x4 -> x3, Pallas kernels: 4.71 us -> 6.23 us  [call(): pl.pallas_call(kernel, out_shape=out_shapes, in_specs=in_specs, out_specs...]
  transfers between devices with their start and end apart: 0 -> 3, of which waited for: 0 -> 2; matrix products, arithmetic and copies ran while one was open for 0% -> 0% of each run, Pallas kernels for 0% -> 0%
where the time goes in v3:
time: 27.9 us; the launch traced here: 27.7 us
  blocking collectives  9.73 us (35%)
  Pallas kernels  6.23 us (22%)
  starting transfers between devices  6.13 us (22%)
  waiting for transfers between devices  4.94 us (18%)
  between operations  0.68 us (2%)
    all_to_all x1, blocking collectives, per_device(): lax.all_to_all(products, ('gx', 'gy', 'gz'), split_axis=0, concat_axis=0)  9.73 us
    pallas_call x3, Pallas kernels, call(): pl.pallas_call(kernel, out_shape=out_shapes, in_specs=in_specs, out_specs...  6.23 us
    ppermute x3, starting transfers between devices, near_steps(): lax.ppermute(value, 'gz', [(source, (source + shift) % members) for sourc...  6.13 us
    ppermute x3, waiting for transfers between devices, near_steps(): lax.ppermute(value, 'gz', [(source, (source + shift) % members) for sourc...  4.94 us
  transfers between devices with their start and end apart: 3, of which 2 were waited for; matrix products, arithmetic and copies ran while one was open for 0% of the time, Pallas kernels for 0%

profile of v3, /device:TPU:0, one launch (start us, length us, event | category | flops | bytes accessed | tf_op | source)
XLA Modules:
  0.0 27.7 jit_solution(13053510761324867619)
XLA Ops:
  0.7 0.0 copy-start
  0.7 0.0 copy-start.1
  0.7 2.5 %shard_map.73 = (f32[128,256]{1,0:T(8,128)S(1)}, f32[128,256]{1,0:T(8,128)S(1)}, f32[128,256]{1,0:T(8,128)S(1)}, f32[128,256]{1,0:T(8,128)S(1)}, f32[128,256]{1,...) custom-call(s32[1,1,1]{2,1,0:T(1,128)S(6)} %copy.8.refs_0_, ...), custom_call_target="tpu_custom_call" | custom-call | flops 805306368 | bytes 1048576 | tf_op jit(solution)/shard_map/pallas_call | solution.py:375
  3.2 4.1 %collective-permute-start.1 = (f32[12,1,512]{2,1,0:T(1,128)S(1)}, f32[12,1,512]{2,1,0:T(1,128)S(1)}, u32[]{:S(2)}, u32[]{:S(2)}) collective-permute-start(f32[12,1,512]{2,1,0:T(1,128)S(1)} %get-tuple-element.25), channel_id=1, source_target_pairs={{0,2},{1,3},{2,0},{3,1},{4,6},{5,7},{6,4},{7,5},{8,10},{9,11},{10,... | collective-permute-start | bytes 73736 | tf_op jit(solution)/shard_map/ppermute | solution.py:424
  7.3 1.3 %collective-permute-start.2 = (f32[12,1,512]{2,1,0:T(1,128)S(1)}, f32[12,1,512]{2,1,0:T(1,128)S(1)}, u32[]{:S(2)}, u32[]{:S(2)}) collective-permute-start(f32[12,1,512]{2,1,0:T(1,128)S(1)} %get-tuple-element.26), channel_id=1, source_target_pairs={{0,3},{1,0},{2,1},{3,2},{4,7},{5,4},{6,5},{7,6},{8,11},{9,8},{10,9... | collective-permute-start | bytes 73736 | tf_op jit(solution)/shard_map/ppermute | solution.py:424
  8.6 0.7 %collective-permute-start = (f32[12,1,512]{2,1,0:T(1,128)S(1)}, f32[12,1,512]{2,1,0:T(1,128)S(1)}, u32[]{:S(2)}, u32[]{:S(2)}) collective-permute-start(f32[12,1,512]{2,1,0:T(1,128)S(1)} %get-tuple-element.24.mine_ref), channel_id=1, source_target_pairs={{0,1},{1,2},{2,3},{3,0},{4,5},{5,6},{6,7},{7,4},{8,9},{9,10},{10,1... | collective-permute-start | bytes 73736 | tf_op jit(solution)/shard_map/ppermute | solution.py:424
  9.3 0.0 collective-permute-done.1.refs_1_
  9.3 1.8 %collective-permute-done.2.refs_2_ = f32[12,1,512]{2,1,0:T(1,128)S(1)} collective-permute-done((f32[12,1,512]{2,1,0:T(1,128)S(1)}, f32[12,1,512]{2,1,0:T(1,128)S(1)}, u32[]{:S(2)}, u32[]{:S(2)}) %collective-permute-start.2) | collective-permute-done | bytes 24608 | tf_op jit(solution)/shard_map/ppermute | solution.py:424
  11.1 3.1 %collective-permute-done.refs_0_ = f32[12,1,512]{2,1,0:T(1,128)S(1)} collective-permute-done((f32[12,1,512]{2,1,0:T(1,128)S(1)}, f32[12,1,512]{2,1,0:T(1,128)S(1)}, u32[]{:S(2)}, u32[]{:S(2)}) %collective-permute-start) | collective-permute-done | bytes 24608 | tf_op jit(solution)/shard_map/ppermute | solution.py:424
  14.2 0.0 copy-done
  14.2 0.0 copy-done.1
  14.3 2.8 %shard_map.74 = (f32[128,256]{1,0:T(8,128)}, f32[128,256]{1,0:T(8,128)S(1)}, f32[32,1,128]{2,1,0:T(1,128)S(1)}) custom-call(f32[128,256]{1,0:T(8,128)S(1)} %get-tuple-element.18.source_ref, f32[128,256]{1,0:T(8,128)S(1)} %get-tuple-element.19.up_ref, f32[128,256]{1,0:T(8,128)S(1)} %get-tuple-element.20.down_ref, f32[128,256]{1,0:T(8,128)S(1)} %get-tuple-element.21.base_ref, ...), custom_call_target="tpu_custom_call" | custom-call | flops 2415919104 | bytes 1048576 | tf_op jit(solution)/shard_map/pallas_call | solution.py:375
  17.0 9.7 %all_to_all.5.parts_ref = f32[32,1,128]{2,1,0:T(1,128)S(1)} all-to-all(f32[32,1,128]{2,1,0:T(1,128)S(1)} %get-tuple-element.28), channel_id=1, replica_groups=mesh['gx'=4,'gy'=2,'gz'=4] {'gx','gy','gz'}, dimensions={0} | all-to-all | bytes 32768 | tf_op jit(solution)/shard_map/all_to_all | solution.py:520
  26.8 1.0 %shard_map.75 = f32[128,256]{1,0:T(8,128)} custom-call(f32[128,256]{1,0:T(8,128)S(1)} %get-tuple-element.17.first_ref, f32[128,256]{1,0:T(8,128)S(1)} %get-tuple-element.27.second_ref, f32[32,1,128]{2,1,0:T(1,128)S(1)} %all_to_all.5.parts_ref), custom_call_target="tpu_custom_call" | custom-call | flops 32768 | bytes 1048576 | tf_op jit(solution)/shard_map/pallas_call | solution.py:375
Async XLA Ops:
  0.7 13.6 %copy-start = (f32[256,256]{1,0:T(8,128)S(1)}, f32[256,256]{1,0:T(8,128)}, u32[]{:S(2)}) copy-start(f32[256,256]{1,0:T(8,128)} %p_ref.1) | copy-start | bytes 786436
  0.7 13.6 %copy-start.1 = (f32[256,256]{1,0:T(8,128)S(1)}, f32[256,256]{1,0:T(8,128)}, u32[]{:S(2)}) copy-start(f32[256,256]{1,0:T(8,128)} %k_ref.1) | copy-start | bytes 786436
  3.2 6.1 %collective-permute-start.1 = (f32[12,1,512]{2,1,0:T(1,128)S(1)}, f32[12,1,512]{2,1,0:T(1,128)S(1)}, u32[]{:S(2)}, u32[]{:S(2)}) collective-permute-start(f32[12,1,512]{2,1,0:T(1,128)S(1)} %get-tuple-element.25), channel_id=1, source_target_pairs={{0,2},{1,3},{2,0},{3,1},{4,6},{5,7},{6,4},{7,5},{8,10},{9,11},{10,... | collective-permute-start | bytes 73736 | tf_op jit(solution)/shard_map/ppermute | solution.py:424
  7.3 3.8 %collective-permute-start.2 = (f32[12,1,512]{2,1,0:T(1,128)S(1)}, f32[12,1,512]{2,1,0:T(1,128)S(1)}, u32[]{:S(2)}, u32[]{:S(2)}) collective-permute-start(f32[12,1,512]{2,1,0:T(1,128)S(1)} %get-tuple-element.26), channel_id=1, source_target_pairs={{0,3},{1,0},{2,1},{3,2},{4,7},{5,4},{6,5},{7,6},{8,11},{9,8},{10,9... | collective-permute-start | bytes 73736 | tf_op jit(solution)/shard_map/ppermute | solution.py:424
  8.6 5.6 %collective-permute-start = (f32[12,1,512]{2,1,0:T(1,128)S(1)}, f32[12,1,512]{2,1,0:T(1,128)S(1)}, u32[]{:S(2)}, u32[]{:S(2)}) collective-permute-start(f32[12,1,512]{2,1,0:T(1,128)S(1)} %get-tuple-element.24.mine_ref), channel_id=1, source_target_pairs={{0,1},{1,2},{2,3},{3,0},{4,5},{5,6},{6,7},{7,4},{8,9},{9,10},{10,1... | collective-permute-start | bytes 73736 | tf_op jit(solution)/shard_map/ppermute | solution.py:424

commit v4 on v3

--- a/solution.py
+++ b/solution.py
@@ -45,8 +45,7 @@
     return element, index - element * dofs
 
 
-def shift_slot(links_ref, index_ref, shift, members):
-    target = lax.rem(lax.axis_index("gz") + shift, members)
+def slot_of(target, links_ref, index_ref):
     slot = jnp.int32(-1)
     for position in range(links_ref.shape[-1]):
         slot = jnp.where(links_ref[0, 0, 0, position] == target, jnp.int32(position), slot)
@@ -134,7 +133,7 @@
     products_ref[...] = jnp.broadcast_to(as_row(lines, products_ref.shape[-1]), products_ref.shape)
 
 
-def begin(refs):
+def begin(refs, partner):
     count_ref, links_hbm, index_hbm, visc_hbm, rhs_hbm, *matrices_hbm = refs["operands"]
     links_ref, index_ref, visc_ref, rhs_ref, *matrix_refs, arrived = refs["scratch"]
     pairs = (
@@ -153,9 +152,9 @@
     copies[0].wait()
     copies[1].wait()
     slots_ref = refs["slots"]
-    members = slots_ref.shape[0] + 1
-    for shift in range(1, members):
-        slots_ref[shift - 1] = shift_slot(links_ref, index_ref, shift, members)
+    me = lax.axis_index("gz")
+    for step in range(1, slots_ref.shape[0] + 1):
+        slots_ref[step - 1] = slot_of(partner(me, step), links_ref, index_ref)
     copies[2].wait()
     probes, elements, dofs = rhs_ref.shape[3:]
     slot = lax.broadcasted_iota(jnp.int32, (elements, 1), 0)
@@ -175,16 +174,16 @@
     return first_pre, up, down
 
 
-def message_places(shifts, probes):
-    values = shifts * probes
-    return values, values + probes, values + probes + shifts
+def message_places(steps, probes):
+    values = steps * probes
+    return values, values + probes, values + probes + steps
 
 
 def near_first_kernel(*refs):
     operands, refs = refs[:7], refs[7:]
     first_ref, source_ref, up_ref, down_ref, base_ref, slots_ref, hot_ref = refs[:7]
-    shifts, _, width = slots_ref.shape
-    leave_refs, scratch = refs[7 : 7 + shifts], refs[7 + shifts :]
+    steps, _, width = slots_ref.shape
+    leave_refs, scratch = refs[7 : 7 + steps], refs[7 + steps :]
     visc_ref, rhs_ref, p_ref, k_ref = scratch[2:6]
     probes, elements, dofs = rhs_ref.shape[3:]
     first_pre, up, down = begin(
@@ -196,28 +195,29 @@
             "down": down_ref,
             "source": source_ref,
             "first": first_ref,
-        }
+        },
+        lambda me, step: me ^ step,
     )
     base = times_matrix(first_pre, k_ref[...]) * up
     base_ref[...] = base
     first_parts = stacked(first_pre)
     second_parts = stacked(times_matrix(base, p_ref[...]) * down)
-    second_at, index_at, visc_at = message_places(shifts, probes)
+    second_at, index_at, visc_at = message_places(steps, probes)
     slot = lax.broadcasted_iota(jnp.int32, (1, elements), 1)
     live_visc = jnp.where(slot < operands[0][0, 0, 0], visc_ref[0, 0], 0.0)
-    for shift in range(1, shifts + 1):
-        flat_row = slots_ref[shift - 1]
+    for step in range(1, steps + 1):
+        flat_row = slots_ref[step - 1]
         over_elements = hot_elements(flat_row, elements, dofs)
         over_dofs = hot_dofs(flat_row, dofs)
-        hot_ref[:, (shift - 1) * width : shift * width] = over_dofs
+        hot_ref[:, (step - 1) * width : step * width] = over_dofs
         first_rows = take_faces(first_parts, over_elements, over_dofs)
         second_rows = take_faces(second_parts, over_elements, over_dofs)
         for probe in range(probes):
-            leave_refs[shift - 1][second_at + probe] = second_rows[probe]
+            leave_refs[step - 1][second_at + probe] = second_rows[probe]
             for leave_ref in leave_refs:
-                leave_ref[(shift - 1) * probes + probe] = first_rows[probe]
+                leave_ref[(step - 1) * probes + probe] = first_rows[probe]
         for leave_ref in leave_refs:
-            leave_ref[index_at + shift - 1] = flat_row.astype(f32)
+            leave_ref[index_at + step - 1] = flat_row.astype(f32)
     for leave_ref in leave_refs:
         leave_ref[visc_at, :, :elements] = live_visc
 
@@ -225,59 +225,56 @@
 def near_second_kernel(
     source_ref, up_ref, down_ref, base_ref, slots_ref, hot_ref, k_ref, p_ref, mine_ref, *refs
 ):
-    came_refs = refs[:-3]
-    image_ref, second_ref, products_ref = refs[-3:]
-    shifts, _, width = slots_ref.shape
-    members = shifts + 1
+    came_refs = refs[:-2]
+    second_ref, products_ref = refs[-2:]
+    steps, _, width = slots_ref.shape
+    members = steps + 1
     rows, dofs = source_ref.shape
-    second_at, index_at, visc_at = message_places(shifts, 0)
+    second_at, index_at, visc_at = message_places(steps, 0)
     probes = (mine_ref.shape[0] - visc_at - 1) // members
     elements = rows // probes
-    second_at, index_at, visc_at = message_places(shifts, probes)
-
-    def message(ahead):
-        ahead = ahead % members
-        return mine_ref if ahead == 0 else came_refs[members - ahead - 1]
-
-    def inbound_first(ahead, shift):
-        row = (members - shift - 1) * probes
-        sent = message(ahead + shift)
-        return [sent[row + probe] for probe in range(probes)]
-
-    own_elements = [hot_elements(slots_ref[shift], elements, dofs) for shift in range(shifts)]
-    own_dofs = [hot_ref[:, shift * width : (shift + 1) * width] for shift in range(shifts)]
+    second_at, index_at, visc_at = message_places(steps, probes)
+
+    def message(step):
+        return mine_ref if step == 0 else came_refs[steps - step]
+
+    def inbound_first(member, step):
+        sent = message(member ^ step)
+        return [sent[(step - 1) * probes + probe] for probe in range(probes)]
+
+    own_elements = [hot_elements(slots_ref[step], elements, dofs) for step in range(steps)]
+    own_dofs = [hot_ref[:, step * width : (step + 1) * width] for step in range(steps)]
 
     def placed_here(values):
         return folded(
-            sum(add_faces(values[i], own_elements[i], own_dofs[i]) for i in range(shifts))
+            sum(add_faces(values[i], own_elements[i], own_dofs[i]) for i in range(steps))
         )
 
     up, down = up_ref[...], down_ref[...]
     live = up > 0.0
-    placed = placed_here([inbound_first(0, shift) for shift in range(1, members)])
+    placed = placed_here([inbound_first(0, step) for step in range(1, members)])
     image = base_ref[...] - jnp.where(live, coupling * placed, 0.0)
-    image_ref[...] = image
     images, back = [image], []
-    for ahead in range(1, members):
+    for member in range(1, members):
         total = 0.0
-        for shift in range(1, members):
-            flat_row = message(ahead)[index_at + shift - 1].astype(jnp.int32)
+        for step in range(1, members):
+            flat_row = message(member)[index_at + step - 1].astype(jnp.int32)
             over_elements = hot_elements(flat_row, elements, dofs)
             over_dofs = hot_dofs(flat_row, dofs)
-            total = total + add_faces(inbound_first(ahead, shift), over_elements, over_dofs)
-            if shift + ahead == members:
+            total = total + add_faces(inbound_first(member, step), over_elements, over_dofs)
+            if step == member:
                 back.append((over_elements, over_dofs))
         images.append(-coupling * folded(total))
     smooth = times_matrix(jnp.concatenate(images, axis=0), p_ref[...])
     second_pre = smooth[:rows] * down
     second_ref[...] = second_pre
     values = []
-    for ahead in range(1, members):
-        sent = message(ahead)
+    for member in range(1, members):
+        sent = message(member)
         visc = as_column(sent[visc_at, :, :elements])
         scale = wide(jnp.where(visc > 0.0, 1.0 / visc, 0.0), probes, dofs)
-        change = smooth[ahead * rows : (ahead + 1) * rows] * scale
-        taken = take_faces(stacked(change), *back[ahead - 1])
+        change = smooth[member * rows : (member + 1) * rows] * scale
+        taken = take_faces(stacked(change), *back[member - 1])
         values.append([taken[probe] + sent[second_at + probe] for probe in range(probes)])
     placed = placed_here(values)
     second_img = times_matrix(second_pre, k_ref[...]) * up - jnp.where(live, coupling * placed, 0.0)
@@ -318,6 +315,7 @@
 def far_first_kernel(*refs):
     operands, refs = refs[:6], refs[6:]
     first_ref, source_ref, up_ref, down_ref, slots_ref, leave_ref = refs[:6]
+    members = slots_ref.shape[0] + 1
     first_pre, _, _ = begin(
         {
             "operands": operands,
@@ -327,7 +325,8 @@
             "down": down_ref,
             "source": source_ref,
             "first": first_ref,
-        }
+        },
+        lambda me, step: lax.rem(me + step, members),
     )
     leave_faces(first_pre, leave_ref.shape[1], slots_ref, leave_ref)
 
@@ -402,12 +401,12 @@
     rhs, viscosity, counts, neighbours, face_index, k_matrix, p_matrix = arguments
     field, slots_shape, products_shape = shapes
     rows, dofs = field.shape
-    shifts, _, width = slots_shape.shape
+    steps, _, width = slots_shape.shape
     probes = rhs.shape[3]
-    flops = 8 * rows * dofs * shifts * width
-    hot = jax.ShapeDtypeStruct((dofs, shifts * width), bf16)
-    length = message_places(shifts, probes)[2] + 1
-    messages = [jax.ShapeDtypeStruct((length, 1, width), f32)] * shifts
+    flops = 8 * rows * dofs * steps * width
+    hot = jax.ShapeDtypeStruct((dofs, steps * width), bf16)
+    length = message_places(steps, probes)[2] + 1
+    messages = [jax.ShapeDtypeStruct((length, 1, width), f32)] * steps
     first_pre, source, up, down, base, slots, hot_own, *leaving = begin_call(
         near_first_kernel,
         [field] * 5 + [slots_shape, hot] + messages,
@@ -422,14 +421,14 @@
     )
     came = [
         lax.ppermute(
-            value, "gz", [(source, (source + shift) % members) for source in range(members)]
+            leaving[step - 1], "gz", [(source, source ^ step) for source in range(members)]
         )
-        for shift, value in enumerate(leaving, 1)
+        for step in range(steps, 0, -1)
     ]
-    _, second_pre, products = call(
+    second_pre, products = call(
         near_second_kernel,
-        [vmem_spec] * (9 + shifts),
-        [field, field, products_shape],
+        [vmem_spec] * (9 + steps),
+        [field, products_shape],
         6 * flops,
         source,
         up,

time: 27.9 us -> 27.6 us (0.989)
  blocking collectives: 9.73 us -> 11.2 us
  waiting for transfers between devices: 4.94 us -> 4.08 us
  Pallas kernels: 6.23 us -> 5.66 us
  starting transfers between devices: 6.13 us -> 5.76 us
    all_to_all x1, blocking collectives: 9.73 us -> 11.2 us  [per_device(): lax.all_to_all(products, ('gx', 'gy', 'gz'), split_axis=0, concat_axis=0)]
    ppermute x3, waiting for transfers between devices: 4.94 us -> 4.08 us  [near_steps(): lax.ppermute(leaving[step - 1], 'gz', [(source, source ^ step) for source...]
    pallas_call x3, Pallas kernels: 6.23 us -> 5.66 us  [call(): pl.pallas_call(kernel, out_shape=out_shapes, in_specs=in_specs, out_specs...]
    ppermute x3, starting transfers between devices: 6.13 us -> 5.76 us  [near_steps(): lax.ppermute(leaving[step - 1], 'gz', [(source, source ^ step) for source...]
where the time goes in v4:
time: 27.6 us; the launch traced here: 27.4 us
  blocking collectives  11.2 us (41%)
  starting transfers between devices  5.76 us (21%)
  Pallas kernels  5.66 us (21%)
  waiting for transfers between devices  4.08 us (15%)
  between operations  0.69 us (2%)
    all_to_all x1, blocking collectives, per_device(): lax.all_to_all(products, ('gx', 'gy', 'gz'), split_axis=0, concat_axis=0)  11.2 us
    ppermute x3, starting transfers between devices, near_steps(): lax.ppermute(leaving[step - 1], 'gz', [(source, source ^ step) for source...  5.76 us
    pallas_call x3, Pallas kernels, call(): pl.pallas_call(kernel, out_shape=out_shapes, in_specs=in_specs, out_specs...  5.66 us
    ppermute x3, waiting for transfers between devices, near_steps(): lax.ppermute(leaving[step - 1], 'gz', [(source, source ^ step) for source...  4.08 us
  transfers between devices with their start and end apart: 3, of which 2 were waited for; matrix products, arithmetic and copies ran while one was open for 0% of the time, Pallas kernels for 0%

profile of v4, /device:TPU:0, one launch (start us, length us, event | category | flops | bytes accessed | tf_op | source)
XLA Modules:
  0.0 27.4 jit_solution(9165339178389470208)
XLA Ops:
  0.7 0.0 copy-start
  0.7 0.0 copy-start.1
  0.7 2.5 %shard_map.73 = (f32[128,256]{1,0:T(8,128)S(1)}, f32[128,256]{1,0:T(8,128)S(1)}, f32[128,256]{1,0:T(8,128)S(1)}, f32[128,256]{1,0:T(8,128)S(1)}, f32[128,256]{1,...) custom-call(s32[1,1,1]{2,1,0:T(1,128)S(6)} %copy.8.refs_0_, ...), custom_call_target="tpu_custom_call" | custom-call | flops 805306368 | bytes 1048576 | tf_op jit(solution)/shard_map/pallas_call | solution.py:374
  3.2 5.1 %collective-permute-start = (f32[12,1,512]{2,1,0:T(1,128)S(1)}, f32[12,1,512]{2,1,0:T(1,128)S(1)}, u32[]{:S(2)}, u32[]{:S(2)}) collective-permute-start(f32[12,1,512]{2,1,0:T(1,128)S(1)} %get-tuple-element.25), channel_id=1, source_target_pairs={{0,3},{1,2},{2,1},{3,0},{4,7},{5,6},{6,5},{7,4},{8,11},{9,10},{10,... | collective-permute-start | bytes 73736 | tf_op jit(solution)/shard_map/ppermute | solution.py:423
  8.3 0.0 collective-permute-start.1
  8.3 0.6 %collective-permute-start.2 = (f32[12,1,512]{2,1,0:T(1,128)S(1)}, f32[12,1,512]{2,1,0:T(1,128)S(1)}, u32[]{:S(2)}, u32[]{:S(2)}) collective-permute-start(f32[12,1,512]{2,1,0:T(1,128)S(1)} %get-tuple-element.24.mine_ref), channel_id=1, source_target_pairs={{0,1},{1,0},{2,3},{3,2},{4,5},{5,4},{6,7},{7,6},{8,9},{9,8},{10,11... | collective-permute-start | bytes 73736 | tf_op jit(solution)/shard_map/ppermute | solution.py:423
  8.9 1.2 %collective-permute-done.refs_0_ = f32[12,1,512]{2,1,0:T(1,128)S(1)} collective-permute-done((f32[12,1,512]{2,1,0:T(1,128)S(1)}, f32[12,1,512]{2,1,0:T(1,128)S(1)}, u32[]{:S(2)}, u32[]{:S(2)}) %collective-permute-start) | collective-permute-done | bytes 24608 | tf_op jit(solution)/shard_map/ppermute | solution.py:423
  10.1 2.9 %collective-permute-done.1.refs_1_ = f32[12,1,512]{2,1,0:T(1,128)S(1)} collective-permute-done((f32[12,1,512]{2,1,0:T(1,128)S(1)}, f32[12,1,512]{2,1,0:T(1,128)S(1)}, u32[]{:S(2)}, u32[]{:S(2)}) %collective-permute-start.1) | collective-permute-done | bytes 24608 | tf_op jit(solution)/shard_map/ppermute | solution.py:423
  13.0 0.0 collective-permute-done.2.refs_2_
  13.0 0.0 copy-done
  13.0 0.0 copy-done.1
  13.0 2.2 %shard_map.74 = (f32[128,256]{1,0:T(8,128)S(1)}, f32[32,1,128]{2,1,0:T(1,128)S(1)}) custom-call(f32[128,256]{1,0:T(8,128)S(1)} %get-tuple-element.18.source_ref, f32[128,256]{1,0:T(8,128)S(1)} %get-tuple-element.19.up_ref, f32[128,256]{1,0:T(8,128)S(1)} %get-tuple-element.20.down_ref, f32[128,256]{1,0:T(8,128)S(1)} %get-tuple-element.21.base_ref, ...), custom_call_target="tpu_custom_call" | custom-call | flops 2415919104 | bytes 1048576 | tf_op jit(solution)/shard_map/pallas_call | solution.py:374
  15.2 11.2 %all_to_all.5.parts_ref = f32[32,1,128]{2,1,0:T(1,128)S(1)} all-to-all(f32[32,1,128]{2,1,0:T(1,128)S(1)} %get-tuple-element.28), channel_id=1, replica_groups=mesh['gx'=4,'gy'=2,'gz'=4] {'gx','gy','gz'}, dimensions={0} | all-to-all | bytes 32768 | tf_op jit(solution)/shard_map/all_to_all | solution.py:519
  26.4 1.0 %shard_map.75 = f32[128,256]{1,0:T(8,128)} custom-call(f32[128,256]{1,0:T(8,128)S(1)} %get-tuple-element.17.first_ref, f32[128,256]{1,0:T(8,128)S(1)} %get-tuple-element.27.second_ref, f32[32,1,128]{2,1,0:T(1,128)S(1)} %all_to_all.5.parts_ref), custom_call_target="tpu_custom_call" | custom-call | flops 32768 | bytes 1048576 | tf_op jit(solution)/shard_map/pallas_call | solution.py:374
Async XLA Ops:
  0.7 12.4 %copy-start = (f32[256,256]{1,0:T(8,128)S(1)}, f32[256,256]{1,0:T(8,128)}, u32[]{:S(2)}) copy-start(f32[256,256]{1,0:T(8,128)} %p_ref.1) | copy-start | bytes 786436
  0.7 12.4 %copy-start.1 = (f32[256,256]{1,0:T(8,128)S(1)}, f32[256,256]{1,0:T(8,128)}, u32[]{:S(2)}) copy-start(f32[256,256]{1,0:T(8,128)} %k_ref.1) | copy-start | bytes 786436
  3.2 6.9 %collective-permute-start = (f32[12,1,512]{2,1,0:T(1,128)S(1)}, f32[12,1,512]{2,1,0:T(1,128)S(1)}, u32[]{:S(2)}, u32[]{:S(2)}) collective-permute-start(f32[12,1,512]{2,1,0:T(1,128)S(1)} %get-tuple-element.25), channel_id=1, source_target_pairs={{0,3},{1,2},{2,1},{3,0},{4,7},{5,6},{6,5},{7,4},{8,11},{9,10},{10,... | collective-permute-start | bytes 73736 | tf_op jit(solution)/shard_map/ppermute | solution.py:423
  8.3 4.7 %collective-permute-start.1 = (f32[12,1,512]{2,1,0:T(1,128)S(1)}, f32[12,1,512]{2,1,0:T(1,128)S(1)}, u32[]{:S(2)}, u32[]{:S(2)}) collective-permute-start(f32[12,1,512]{2,1,0:T(1,128)S(1)} %get-tuple-element.26), channel_id=1, source_target_pairs={{0,2},{1,3},{2,0},{3,1},{4,6},{5,7},{6,4},{7,5},{8,10},{9,11},{10,... | collective-permute-start | bytes 73736 | tf_op jit(solution)/shard_map/ppermute | solution.py:423
  8.3 4.7 %collective-permute-start.2 = (f32[12,1,512]{2,1,0:T(1,128)S(1)}, f32[12,1,512]{2,1,0:T(1,128)S(1)}, u32[]{:S(2)}, u32[]{:S(2)}) collective-permute-start(f32[12,1,512]{2,1,0:T(1,128)S(1)} %get-tuple-element.24.mine_ref), channel_id=1, source_target_pairs={{0,1},{1,0},{2,3},{3,2},{4,5},{5,4},{6,7},{7,6},{8,9},{9,8},{10,11... | collective-permute-start | bytes 73736 | tf_op jit(solution)/shard_map/ppermute | solution.py:423

commit v5 on v4

--- a/solution.py
+++ b/solution.py
@@ -10,6 +10,7 @@
 coupling = 0.5
 vmem_grant = 48 * 1024 * 1024
 short_group = 4
+lane_count = 128
 f32 = jnp.float32
 bf16 = jnp.bfloat16
 vmem_spec = pl.BlockSpec(memory_space=pltpu.VMEM)
@@ -60,8 +61,10 @@
 
 def hot_dofs(flat_row, dofs):
     _, dof = split_index(flat_row, dofs)
-    line = lax.broadcasted_iota(jnp.int32, (dofs, flat_row.shape[1]), 0)
-    return (line == dof).astype(f32).astype(bf16)
+    shape = (dofs, flat_row.shape[1])
+    line = lax.broadcasted_iota(jnp.int32, shape, 0).astype(jnp.int16)
+    hit = line == jnp.broadcast_to(dof.astype(jnp.int16), shape)
+    return jnp.where(hit, jnp.ones(shape, bf16), jnp.zeros(shape, bf16))
 
 
 def as_column(row):
@@ -179,6 +182,23 @@
     return values, values + probes, values + probes + steps
 
 
+def message_length(steps, probes, width):
+    return -(-(message_places(steps, probes)[2] * (width // lane_count) + 1) // 8) * 8
+
+
+def write_row(message_ref, place, row):
+    pieces = row.shape[1] // lane_count
+    for piece in range(pieces):
+        line = place * pieces + piece
+        message_ref[line : line + 1, :] = row[:, piece * lane_count : (piece + 1) * lane_count]
+
+
+def read_row(message_ref, place, width):
+    pieces = width // lane_count
+    lines = range(place * pieces, (place + 1) * pieces)
+    return jnp.concatenate([message_ref[line : line + 1, :] for line in lines], axis=1)
+
+
 def near_first_kernel(*refs):
     operands, refs = refs[:7], refs[7:]
     first_ref, source_ref, up_ref, down_ref, base_ref, slots_ref, hot_ref = refs[:7]
@@ -213,34 +233,35 @@
         first_rows = take_faces(first_parts, over_elements, over_dofs)
         second_rows = take_faces(second_parts, over_elements, over_dofs)
         for probe in range(probes):
-            leave_refs[step - 1][second_at + probe] = second_rows[probe]
+            write_row(leave_refs[step - 1], second_at + probe, second_rows[probe])
             for leave_ref in leave_refs:
-                leave_ref[(step - 1) * probes + probe] = first_rows[probe]
+                write_row(leave_ref, (step - 1) * probes + probe, first_rows[probe])
         for leave_ref in leave_refs:
-            leave_ref[index_at + step - 1] = flat_row.astype(f32)
+            write_row(leave_ref, index_at + step - 1, flat_row.astype(f32))
+    visc_line = visc_at * (width // lane_count)
     for leave_ref in leave_refs:
-        leave_ref[visc_at, :, :elements] = live_visc
+        leave_ref[visc_line : visc_line + 1, :elements] = live_visc
 
 
 def near_second_kernel(
-    source_ref, up_ref, down_ref, base_ref, slots_ref, hot_ref, k_ref, p_ref, mine_ref, *refs
+    probes, source_ref, up_ref, down_ref, base_ref, slots_ref, hot_ref, k_ref, p_ref, mine_ref, *refs
 ):
     came_refs = refs[:-2]
     second_ref, products_ref = refs[-2:]
     steps, _, width = slots_ref.shape
     members = steps + 1
     rows, dofs = source_ref.shape
-    second_at, index_at, visc_at = message_places(steps, 0)
-    probes = (mine_ref.shape[0] - visc_at - 1) // members
     elements = rows // probes
     second_at, index_at, visc_at = message_places(steps, probes)
 
     def message(step):
-        return mine_ref if step == 0 else came_refs[steps - step]
+        return mine_ref if step == 0 else came_refs[step - 1]
 
     def inbound_first(member, step):
         sent = message(member ^ step)
-        return [sent[(step - 1) * probes + probe] for probe in range(probes)]
+        return [
+            read_row(sent, (step - 1) * probes + probe, width) for probe in range(probes)
+        ]
 
     own_elements = [hot_elements(slots_ref[step], elements, dofs) for step in range(steps)]
     own_dofs = [hot_ref[:, step * width : (step + 1) * width] for step in range(steps)]
@@ -258,7 +279,7 @@
     for member in range(1, members):
         total = 0.0
         for step in range(1, members):
-            flat_row = message(member)[index_at + step - 1].astype(jnp.int32)
+            flat_row = read_row(message(member), index_at + step - 1, width).astype(jnp.int32)
             over_elements = hot_elements(flat_row, elements, dofs)
             over_dofs = hot_dofs(flat_row, dofs)
             total = total + add_faces(inbound_first(member, step), over_elements, over_dofs)
@@ -269,13 +290,16 @@
     second_pre = smooth[:rows] * down
     second_ref[...] = second_pre
     values = []
+    visc_line = visc_at * (width // lane_count)
     for member in range(1, members):
         sent = message(member)
-        visc = as_column(sent[visc_at, :, :elements])
+        visc = as_column(sent[visc_line : visc_line + 1, :elements])
         scale = wide(jnp.where(visc > 0.0, 1.0 / visc, 0.0), probes, dofs)
         change = smooth[member * rows : (member + 1) * rows] * scale
         taken = take_faces(stacked(change), *back[member - 1])
-        values.append([taken[probe] + sent[second_at + probe] for probe in range(probes)])
+        values.append(
+            [taken[probe] + read_row(sent, second_at + probe, width) for probe in range(probes)]
+        )
     placed = placed_here(values)
     second_img = times_matrix(second_pre, k_ref[...]) * up - jnp.where(live, coupling * placed, 0.0)
     inner_products(image, second_img, source_ref[...], probes, products_ref)
@@ -405,11 +429,10 @@
     probes = rhs.shape[3]
     flops = 8 * rows * dofs * steps * width
     hot = jax.ShapeDtypeStruct((dofs, steps * width), bf16)
-    length = message_places(steps, probes)[2] + 1
-    messages = [jax.ShapeDtypeStruct((length, 1, width), f32)] * steps
+    message = jax.ShapeDtypeStruct((message_length(steps, probes, width), lane_count), f32)
     first_pre, source, up, down, base, slots, hot_own, *leaving = begin_call(
         near_first_kernel,
-        [field] * 5 + [slots_shape, hot] + messages,
+        [field] * 5 + [slots_shape, hot] + [message] * steps,
         2 * flops,
         counts,
         neighbours,
@@ -423,10 +446,10 @@
         lax.ppermute(
             leaving[step - 1], "gz", [(source, source ^ step) for source in range(members)]
         )
-        for step in range(steps, 0, -1)
+        for step in range(1, members)
     ]
     second_pre, products = call(
-        near_second_kernel,
+        functools.partial(near_second_kernel, probes),
         [vmem_spec] * (9 + steps),
         [field, products_shape],
         6 * flops,

time: 27.6 us -> 27.3 us (0.989)
  no operation moved by 1% of the time
where the time goes in v5:
time: 27.3 us; the launch traced here: 27.1 us
  blocking collectives  11.2 us (41%)
  starting transfers between devices  5.68 us (21%)
  Pallas kernels  5.46 us (20%)
  waiting for transfers between devices  4.05 us (15%)
  between operations  0.69 us (3%)
    all_to_all x1, blocking collectives, per_device(): lax.all_to_all(products, ('gx', 'gy', 'gz'), split_axis=0, concat_axis=0)  11.2 us
    ppermute x3, starting transfers between devices, near_steps(): lax.ppermute(leaving[step - 1], 'gz', [(source, source ^ step) for source...  5.68 us
    pallas_call x3, Pallas kernels, call(): pl.pallas_call(kernel, out_shape=out_shapes, in_specs=in_specs, out_specs...  5.46 us
    ppermute x3, waiting for transfers between devices, near_steps(): lax.ppermute(leaving[step - 1], 'gz', [(source, source ^ step) for source...  4.05 us
  transfers between devices with their start and end apart: 3, of which 2 were waited for; matrix products, arithmetic and copies ran while one was open for 0% of the time, Pallas kernels for 0%

profile of v5, /device:TPU:0, one launch (start us, length us, event | category | flops | bytes accessed | tf_op | source)
XLA Modules:
  0.0 27.1 jit_solution(13344526212600770338)
XLA Ops:
  0.7 0.0 copy-start
  0.7 0.0 copy-start.1
  0.7 2.4 %shard_map.73 = (f32[128,256]{1,0:T(8,128)S(1)}, f32[128,256]{1,0:T(8,128)S(1)}, f32[128,256]{1,0:T(8,128)S(1)}, f32[128,256]{1,0:T(8,128)S(1)}, f32[128,256]{1,...) custom-call(s32[1,1,1]{2,1,0:T(1,128)S(6)} %copy.8.refs_0_, ...), custom_call_target="tpu_custom_call" | custom-call | flops 805306368 | bytes 1048576 | tf_op jit(solution)/shard_map/pallas_call | solution.py:398
  3.0 4.1 %collective-permute-start.1 = (f32[48,128]{1,0:T(8,128)S(1)}, f32[48,128]{1,0:T(8,128)S(1)}, u32[]{:S(2)}, u32[]{:S(2)}) collective-permute-start(f32[48,128]{1,0:T(8,128)S(1)} %get-tuple-element.25), channel_id=1, source_target_pairs={{0,2},{1,3},{2,0},{3,1},{4,6},{5,7},{6,4},{7,5},{8,10},{9,11},{10,... | collective-permute-start | bytes 73736 | tf_op jit(solution)/shard_map/ppermute | solution.py:446
  7.1 1.3 %collective-permute-start.2 = (f32[48,128]{1,0:T(8,128)S(1)}, f32[48,128]{1,0:T(8,128)S(1)}, u32[]{:S(2)}, u32[]{:S(2)}) collective-permute-start(f32[48,128]{1,0:T(8,128)S(1)} %get-tuple-element.26), channel_id=1, source_target_pairs={{0,3},{1,2},{2,1},{3,0},{4,7},{5,6},{6,5},{7,4},{8,11},{9,10},{10,... | collective-permute-start | bytes 73736 | tf_op jit(solution)/shard_map/ppermute | solution.py:446
  8.5 0.2 collective-permute-start
  8.7 0.2 collective-permute-done.1.refs_1_
  9.0 3.8 %collective-permute-done.2.refs_2_ = f32[48,128]{1,0:T(8,128)S(1)} collective-permute-done((f32[48,128]{1,0:T(8,128)S(1)}, f32[48,128]{1,0:T(8,128)S(1)}, u32[]{:S(2)}, u32[]{:S(2)}) %collective-permute-start.2) | collective-permute-done | bytes 24608 | tf_op jit(solution)/shard_map/ppermute | solution.py:446
  12.8 0.0 collective-permute-done.refs_0_
  12.8 0.0 copy-done
  12.8 0.0 copy-done.1
  12.8 2.2 %shard_map.74 = (f32[128,256]{1,0:T(8,128)S(1)}, f32[32,1,128]{2,1,0:T(1,128)S(1)}) custom-call(f32[128,256]{1,0:T(8,128)S(1)} %get-tuple-element.18.source_ref, f32[128,256]{1,0:T(8,128)S(1)} %get-tuple-element.19.up_ref, f32[128,256]{1,0:T(8,128)S(1)} %get-tuple-element.20.down_ref, f32[128,256]{1,0:T(8,128)S(1)} %get-tuple-element.21.base_ref, ...), custom_call_target="tpu_custom_call" | custom-call | flops 2415919104 | bytes 1048576 | tf_op jit(solution)/shard_map/pallas_call | solution.py:398
  14.9 11.2 %all_to_all.5.parts_ref = f32[32,1,128]{2,1,0:T(1,128)S(1)} all-to-all(f32[32,1,128]{2,1,0:T(1,128)S(1)} %get-tuple-element.28), channel_id=1, replica_groups=mesh['gx'=4,'gy'=2,'gz'=4] {'gx','gy','gz'}, dimensions={0} | all-to-all | bytes 32768 | tf_op jit(solution)/shard_map/all_to_all | solution.py:542
  26.1 1.0 %shard_map.75 = f32[128,256]{1,0:T(8,128)} custom-call(f32[128,256]{1,0:T(8,128)S(1)} %get-tuple-element.17.first_ref, f32[128,256]{1,0:T(8,128)S(1)} %get-tuple-element.27.second_ref, f32[32,1,128]{2,1,0:T(1,128)S(1)} %all_to_all.5.parts_ref), custom_call_target="tpu_custom_call" | custom-call | flops 32768 | bytes 1048576 | tf_op jit(solution)/shard_map/pallas_call | solution.py:398
Async XLA Ops:
  0.7 12.1 %copy-start = (f32[256,256]{1,0:T(8,128)S(1)}, f32[256,256]{1,0:T(8,128)}, u32[]{:S(2)}) copy-start(f32[256,256]{1,0:T(8,128)} %p_ref.1) | copy-start | bytes 786436
  0.7 12.1 %copy-start.1 = (f32[256,256]{1,0:T(8,128)S(1)}, f32[256,256]{1,0:T(8,128)}, u32[]{:S(2)}) copy-start(f32[256,256]{1,0:T(8,128)} %k_ref.1) | copy-start | bytes 786436
  3.0 5.9 %collective-permute-start.1 = (f32[48,128]{1,0:T(8,128)S(1)}, f32[48,128]{1,0:T(8,128)S(1)}, u32[]{:S(2)}, u32[]{:S(2)}) collective-permute-start(f32[48,128]{1,0:T(8,128)S(1)} %get-tuple-element.25), channel_id=1, source_target_pairs={{0,2},{1,3},{2,0},{3,1},{4,6},{5,7},{6,4},{7,5},{8,10},{9,11},{10,... | collective-permute-start | bytes 73736 | tf_op jit(solution)/shard_map/ppermute | solution.py:446
  7.1 5.6 %collective-permute-start.2 = (f32[48,128]{1,0:T(8,128)S(1)}, f32[48,128]{1,0:T(8,128)S(1)}, u32[]{:S(2)}, u32[]{:S(2)}) collective-permute-start(f32[48,128]{1,0:T(8,128)S(1)} %get-tuple-element.26), channel_id=1, source_target_pairs={{0,3},{1,2},{2,1},{3,0},{4,7},{5,6},{6,5},{7,4},{8,11},{9,10},{10,... | collective-permute-start | bytes 73736 | tf_op jit(solution)/shard_map/ppermute | solution.py:446
  8.5 4.3 %collective-permute-start = (f32[48,128]{1,0:T(8,128)S(1)}, f32[48,128]{1,0:T(8,128)S(1)}, u32[]{:S(2)}, u32[]{:S(2)}) collective-permute-start(f32[48,128]{1,0:T(8,128)S(1)} %get-tuple-element.24.mine_ref), channel_id=1, source_target_pairs={{0,1},{1,0},{2,3},{3,2},{4,5},{5,4},{6,7},{7,6},{8,9},{9,8},{10,11... | collective-permute-start | bytes 73736 | tf_op jit(solution)/shard_map/ppermute | solution.py:446

commit v6 on v5

--- a/solution.py
+++ b/solution.py
@@ -133,7 +133,7 @@
             lines.append(
                 jnp.sum(product[probe * elements : (probe + 1) * elements], axis=0, keepdims=True)
             )
-    products_ref[...] = jnp.broadcast_to(as_row(lines, products_ref.shape[-1]), products_ref.shape)
+    products_ref[...] = as_row(lines, products_ref.shape[-1])
 
 
 def begin(refs, partner):
@@ -379,10 +379,10 @@
     inner_products(image_ref[...], second_img, source_ref[...], probes, products_ref)
 
 
-def last_kernel(probes, first_ref, second_ref, parts_ref, out_ref):
+def last_kernel(probes, first_ref, second_ref, total_ref, out_ref):
     rows, _ = first_ref.shape
     elements = rows // probes
-    total = jnp.sum(parts_ref[...], axis=0)
+    total = total_ref[...]
     for probe in range(probes):
         self_one, cross_mid, self_two, load_one, load_two = (
             total[:, place * probes + probe : place * probes + probe + 1] for place in range(5)
@@ -526,7 +526,7 @@
     shapes = (
         jax.ShapeDtypeStruct((probes * elements, dofs), f32),
         jax.ShapeDtypeStruct((members - 1, 1, face_index.shape[-1]), jnp.int32),
-        jax.ShapeDtypeStruct((mesh.size, 1, lanes), f32),
+        jax.ShapeDtypeStruct((1, lanes), f32),
     )
     near = 1 < members <= short_group and elements <= face_index.shape[-1]
     near = near and elements * dofs < 1 << 24
@@ -539,7 +539,7 @@
         probes * elements * dofs,
         first_pre,
         second_pre,
-        lax.all_to_all(products, ("gx", "gy", "gz"), split_axis=0, concat_axis=0),
+        lax.psum(products, ("gx", "gy", "gz")),
     )
     return result.reshape(rhs.shape)
 

time: 27.3 us -> 55.1 us (2.02)
  blocking collectives: 11.2 us -> 39.1 us
    psum x0 -> x1, blocking collectives: none -> 39.1 us  [per_device(): lax.psum(products, ('gx', 'gy', 'gz'))]
    all_to_all x1 -> x0, blocking collectives: 11.2 us -> none  [per_device(): lax.all_to_all(products, ('gx', 'gy', 'gz'), split_axis=0, concat_axis=0)]
where the time goes in v6:
time: 55.1 us; the launch traced here: 54.9 us
  blocking collectives  39.1 us (71%)
  starting transfers between devices  5.68 us (10%)
  Pallas kernels  5.41 us (10%)
  waiting for transfers between devices  4.05 us (7%)
  between operations  0.68 us (1%)
    psum x1, blocking collectives, per_device(): lax.psum(products, ('gx', 'gy', 'gz'))  39.1 us
    ppermute x3, starting transfers between devices, near_steps(): lax.ppermute(leaving[step - 1], 'gz', [(source, source ^ step) for source...  5.68 us
    pallas_call x3, Pallas kernels, call(): pl.pallas_call(kernel, out_shape=out_shapes, in_specs=in_specs, out_specs...  5.41 us
    ppermute x3, waiting for transfers between devices, near_steps(): lax.ppermute(leaving[step - 1], 'gz', [(source, source ^ step) for source...  4.05 us
  transfers between devices with their start and end apart: 3, of which 2 were waited for; matrix products, arithmetic and copies ran while one was open for 0% of the time, Pallas kernels for 0%

profile of v6, /device:TPU:0, one launch (start us, length us, event | category | flops | bytes accessed | tf_op | source)
XLA Modules:
  0.0 54.9 jit_solution(5045807260200336908)
XLA Ops:
  0.7 0.0 copy-start
  0.7 0.0 copy-start.1
  0.7 2.4 %shard_map.73 = (f32[128,256]{1,0:T(8,128)S(1)}, f32[128,256]{1,0:T(8,128)S(1)}, f32[128,256]{1,0:T(8,128)S(1)}, f32[128,256]{1,0:T(8,128)S(1)}, f32[128,256]{1,...) custom-call(s32[1,1,1]{2,1,0:T(1,128)S(6)} %copy.8.refs_0_, ...), custom_call_target="tpu_custom_call" | custom-call | flops 805306368 | bytes 1048576 | tf_op jit(solution)/shard_map/pallas_call | solution.py:398
  3.0 4.1 %collective-permute-start.1 = (f32[48,128]{1,0:T(8,128)S(1)}, f32[48,128]{1,0:T(8,128)S(1)}, u32[]{:S(2)}, u32[]{:S(2)}) collective-permute-start(f32[48,128]{1,0:T(8,128)S(1)} %get-tuple-element.25), channel_id=1, source_target_pairs={{0,2},{1,3},{2,0},{3,1},{4,6},{5,7},{6,4},{7,5},{8,10},{9,11},{10,... | collective-permute-start | bytes 73736 | tf_op jit(solution)/shard_map/ppermute | solution.py:446
  7.1 1.3 %collective-permute-start.2 = (f32[48,128]{1,0:T(8,128)S(1)}, f32[48,128]{1,0:T(8,128)S(1)}, u32[]{:S(2)}, u32[]{:S(2)}) collective-permute-start(f32[48,128]{1,0:T(8,128)S(1)} %get-tuple-element.26), channel_id=1, source_target_pairs={{0,3},{1,2},{2,1},{3,0},{4,7},{5,6},{6,5},{7,4},{8,11},{9,10},{10,... | collective-permute-start | bytes 73736 | tf_op jit(solution)/shard_map/ppermute | solution.py:446
  8.5 0.2 collective-permute-start
  8.7 0.2 collective-permute-done.1.refs_1_
  9.0 3.8 %collective-permute-done.2.refs_2_ = f32[48,128]{1,0:T(8,128)S(1)} collective-permute-done((f32[48,128]{1,0:T(8,128)S(1)}, f32[48,128]{1,0:T(8,128)S(1)}, u32[]{:S(2)}, u32[]{:S(2)}) %collective-permute-start.2) | collective-permute-done | bytes 24608 | tf_op jit(solution)/shard_map/ppermute | solution.py:446
  12.8 0.0 collective-permute-done.refs_0_
  12.8 0.0 copy-done
  12.8 0.0 copy-done.1
  12.8 2.2 %shard_map.74 = (f32[128,256]{1,0:T(8,128)S(1)}, f32[1,128]{1,0:T(1,128)S(1)}) custom-call(f32[128,256]{1,0:T(8,128)S(1)} %get-tuple-element.18.source_ref, f32[128,256]{1,0:T(8,128)S(1)} %get-tuple-element.19.up_ref, f32[128,256]{1,0:T(8,128)S(1)} %get-tuple-element.20.down_ref, f32[128,256]{1,0:T(8,128)S(1)} %get-tuple-element.21.base_ref, ...), custom_call_target="tpu_custom_call" | custom-call | flops 2415919104 | bytes 1048576 | tf_op jit(solution)/shard_map/pallas_call | solution.py:398
  14.9 39.1 %psum.7.total_ref = f32[1,128]{1,0:T(1,128)S(1)} all-reduce(f32[1,128]{1,0:T(1,128)S(1)} %get-tuple-element.28), channel_id=1, replica_groups=mesh['gx'=4,'gy'=2,'gz'=4] {'gx','gy','gz'}, use_global_device_ids=true, to_apply=%region_0.0 | all-reduce | flops 128 | bytes 1024 | tf_op jit(solution)/shard_map/psum | solution.py:542
  54.0 0.9 %shard_map.75 = f32[128,256]{1,0:T(8,128)} custom-call(f32[128,256]{1,0:T(8,128)S(1)} %get-tuple-element.17.first_ref, f32[128,256]{1,0:T(8,128)S(1)} %get-tuple-element.27.second_ref, f32[1,128]{1,0:T(1,128)S(1)} %psum.7.total_ref), custom_call_target="tpu_custom_call" | custom-call | flops 32768 | bytes 1048576 | tf_op jit(solution)/shard_map/pallas_call | solution.py:398
Async XLA Ops:
  0.7 12.1 %copy-start = (f32[256,256]{1,0:T(8,128)S(1)}, f32[256,256]{1,0:T(8,128)}, u32[]{:S(2)}) copy-start(f32[256,256]{1,0:T(8,128)} %p_ref.1) | copy-start | bytes 786436
  0.7 12.1 %copy-start.1 = (f32[256,256]{1,0:T(8,128)S(1)}, f32[256,256]{1,0:T(8,128)}, u32[]{:S(2)}) copy-start(f32[256,256]{1,0:T(8,128)} %k_ref.1) | copy-start | bytes 786436
  3.0 5.9 %collective-permute-start.1 = (f32[48,128]{1,0:T(8,128)S(1)}, f32[48,128]{1,0:T(8,128)S(1)}, u32[]{:S(2)}, u32[]{:S(2)}) collective-permute-start(f32[48,128]{1,0:T(8,128)S(1)} %get-tuple-element.25), channel_id=1, source_target_pairs={{0,2},{1,3},{2,0},{3,1},{4,6},{5,7},{6,4},{7,5},{8,10},{9,11},{10,... | collective-permute-start | bytes 73736 | tf_op jit(solution)/shard_map/ppermute | solution.py:446
  7.1 5.6 %collective-permute-start.2 = (f32[48,128]{1,0:T(8,128)S(1)}, f32[48,128]{1,0:T(8,128)S(1)}, u32[]{:S(2)}, u32[]{:S(2)}) collective-permute-start(f32[48,128]{1,0:T(8,128)S(1)} %get-tuple-element.26), channel_id=1, source_target_pairs={{0,3},{1,2},{2,1},{3,0},{4,7},{5,6},{6,5},{7,4},{8,11},{9,10},{10,... | collective-permute-start | bytes 73736 | tf_op jit(solution)/shard_map/ppermute | solution.py:446
  8.5 4.3 %collective-permute-start = (f32[48,128]{1,0:T(8,128)S(1)}, f32[48,128]{1,0:T(8,128)S(1)}, u32[]{:S(2)}, u32[]{:S(2)}) collective-permute-start(f32[48,128]{1,0:T(8,128)S(1)} %get-tuple-element.24.mine_ref), channel_id=1, source_target_pairs={{0,1},{1,0},{2,3},{3,2},{4,5},{5,4},{6,7},{7,6},{8,9},{9,8},{10,11... | collective-permute-start | bytes 73736 | tf_op jit(solution)/shard_map/ppermute | solution.py:446

commit v7 on v6

--- a/solution.py
+++ b/solution.py
@@ -379,10 +379,10 @@
     inner_products(image_ref[...], second_img, source_ref[...], probes, products_ref)
 
 
-def last_kernel(probes, first_ref, second_ref, total_ref, out_ref):
+def last_kernel(probes, first_ref, second_ref, parts_ref, out_ref):
     rows, _ = first_ref.shape
     elements = rows // probes
-    total = total_ref[...]
+    total = jnp.sum(parts_ref[...], axis=0)
     for probe in range(probes):
         self_one, cross_mid, self_two, load_one, load_two = (
             total[:, place * probes + probe : place * probes + probe + 1] for place in range(5)
@@ -518,6 +518,23 @@
     return first_pre, second_pre, products
 
 
+def all_rows(row, mesh):
+    axes = ("gx", "gy", "gz")
+    size = mesh.shape["gx"]
+    groups = None
+    rows = mesh.size
+    if size % 2 == 0:
+        row = row + lax.ppermute(row, "gx", [(place, place ^ 1) for place in range(size)])
+        rest = mesh.size // size
+        groups = [
+            [place * rest + other for place in range(half, size, 2) for other in range(rest)]
+            for half in range(2)
+        ]
+        rows //= 2
+    copies = jnp.broadcast_to(row[None], (rows,) + row.shape)
+    return lax.all_to_all(copies, axes, split_axis=0, concat_axis=0, axis_index_groups=groups)
+
+
 def per_device(mesh, *arguments):
     rhs, face_index = arguments[0], arguments[4]
     probes, elements, dofs = rhs.shape[3:]
@@ -539,7 +556,7 @@
         probes * elements * dofs,
         first_pre,
         second_pre,
-        lax.psum(products, ("gx", "gy", "gz")),
+        all_rows(products, mesh),
     )
     return result.reshape(rhs.shape)
 

time: 55.1 us -> 29.5 us (0.54)
  blocking collectives: 39.1 us -> 12.3 us
  waiting for transfers between devices: 4.05 us -> 5.16 us
    psum x1 -> x0, blocking collectives: 39.1 us -> none  [per_device(): lax.psum(products, ('gx', 'gy', 'gz'))]
    all_to_all x0 -> x1, blocking collectives: none -> 12.3 us  [all_rows(): lax.all_to_all(copies, axes, split_axis=0, concat_axis=0, axis_index_grou...]
    ppermute x0 -> x1, waiting for transfers between devices: none -> 1.12 us  [all_rows(): lax.ppermute(row, 'gx', [(place, place ^ 1) for place in range(size)])]
  transfers between devices with their start and end apart: 3 -> 4, of which waited for: 2 -> 3; matrix products, arithmetic and copies ran while one was open for 0% -> 0% of each run, Pallas kernels for 0% -> 0%
where the time goes in v7:
time: 29.5 us; the launch traced here: 29.4 us
  blocking collectives  12.3 us (42%)
  starting transfers between devices  5.68 us (19%)
  Pallas kernels  5.46 us (19%)
  waiting for transfers between devices  5.16 us (17%)
  between operations  0.69 us (2%)
    all_to_all x1, blocking collectives, all_rows(): lax.all_to_all(copies, axes, split_axis=0, concat_axis=0, axis_index_grou...  12.3 us
    ppermute x3, starting transfers between devices, near_steps(): lax.ppermute(leaving[step - 1], 'gz', [(source, source ^ step) for source...  5.68 us
    pallas_call x3, Pallas kernels, call(): pl.pallas_call(kernel, out_shape=out_shapes, in_specs=in_specs, out_specs...  5.46 us
    ppermute x3, waiting for transfers between devices, near_steps(): lax.ppermute(leaving[step - 1], 'gz', [(source, source ^ step) for source...  4.05 us
    ppermute x1, waiting for transfers between devices, all_rows(): lax.ppermute(row, 'gx', [(place, place ^ 1) for place in range(size)])  1.12 us
  transfers between devices with their start and end apart: 4, of which 3 were waited for; matrix products, arithmetic and copies ran while one was open for 0% of the time, Pallas kernels for 0%

profile of v7, /device:TPU:0, one launch (start us, length us, event | category | flops | bytes accessed | tf_op | source)
XLA Modules:
  0.0 29.4 jit_solution(10021179796062520077)
XLA Ops:
  0.7 0.0 copy-start
  0.7 0.0 copy-start.1
  0.7 2.4 %shard_map.73 = (f32[128,256]{1,0:T(8,128)S(1)}, f32[128,256]{1,0:T(8,128)S(1)}, f32[128,256]{1,0:T(8,128)S(1)}, f32[128,256]{1,0:T(8,128)S(1)}, f32[128,256]{1,...) custom-call(s32[1,1,1]{2,1,0:T(1,128)S(6)} %copy.8.refs_0_, ...), custom_call_target="tpu_custom_call" | custom-call | flops 805306368 | bytes 1048576 | tf_op jit(solution)/shard_map/pallas_call | solution.py:398
  3.0 4.1 %collective-permute-start.1 = (f32[48,128]{1,0:T(8,128)S(1)}, f32[48,128]{1,0:T(8,128)S(1)}, u32[]{:S(2)}, u32[]{:S(2)}) collective-permute-start(f32[48,128]{1,0:T(8,128)S(1)} %get-tuple-element.25), channel_id=1, source_target_pairs={{0,2},{1,3},{2,0},{3,1},{4,6},{5,7},{6,4},{7,5},{8,10},{9,11},{10,... | collective-permute-start | bytes 73736 | tf_op jit(solution)/shard_map/ppermute | solution.py:446
  7.1 1.3 %collective-permute-start.2 = (f32[48,128]{1,0:T(8,128)S(1)}, f32[48,128]{1,0:T(8,128)S(1)}, u32[]{:S(2)}, u32[]{:S(2)}) collective-permute-start(f32[48,128]{1,0:T(8,128)S(1)} %get-tuple-element.26), channel_id=1, source_target_pairs={{0,3},{1,2},{2,1},{3,0},{4,7},{5,6},{6,5},{7,4},{8,11},{9,10},{10,... | collective-permute-start | bytes 73736 | tf_op jit(solution)/shard_map/ppermute | solution.py:446
  8.5 0.2 collective-permute-start
  8.7 0.2 collective-permute-done.1.refs_1_
  9.0 3.8 %collective-permute-done.2.refs_2_ = f32[48,128]{1,0:T(8,128)S(1)} collective-permute-done((f32[48,128]{1,0:T(8,128)S(1)}, f32[48,128]{1,0:T(8,128)S(1)}, u32[]{:S(2)}, u32[]{:S(2)}) %collective-permute-start.2) | collective-permute-done | bytes 24608 | tf_op jit(solution)/shard_map/ppermute | solution.py:446
  12.8 0.0 collective-permute-done.refs_0_
  12.8 0.0 copy-done
  12.8 0.0 copy-done.1
  12.8 2.2 %shard_map.74 = (f32[128,256]{1,0:T(8,128)S(1)}, f32[1,128]{1,0:T(1,128)S(1)}) custom-call(f32[128,256]{1,0:T(8,128)S(1)} %get-tuple-element.18.source_ref, f32[128,256]{1,0:T(8,128)S(1)} %get-tuple-element.19.up_ref, f32[128,256]{1,0:T(8,128)S(1)} %get-tuple-element.20.down_ref, f32[128,256]{1,0:T(8,128)S(1)} %get-tuple-element.21.base_ref, ...), custom_call_target="tpu_custom_call" | custom-call | flops 2415919104 | bytes 1048576 | tf_op jit(solution)/shard_map/pallas_call | solution.py:398
  14.9 0.0 collective-permute-start.3
  15.0 1.1 %collective-permute-done.3 = f32[1,128]{1,0:T(1,128)S(1)} collective-permute-done((f32[1,128]{1,0:T(1,128)S(1)}, f32[1,128]{1,0:T(1,128)S(1)}, u32[]{:S(2)}, u32[]{:S(2)}) %collective-permute-start.3) | collective-permute-done | bytes 544 | tf_op jit(solution)/shard_map/ppermute | solution.py:527
  16.1 12.3 %all_to_all.5.parts_ref = f32[16,1,128]{2,1,0:T(1,128)S(1)} all-to-all(f32[16,1,128]{2,1,0:T(1,128)S(1)} %broadcast_in_dim.9), channel_id=1, replica_groups={{0,1,2,3,4,5,6,7,16,17,18,19,20,21,22,23},{8,9,10,11,12,13,14,15,24,25,..., dimensions={0} | all-to-all | bytes 16384 | tf_op jit(solution)/shard_map/all_to_all | solution.py:535
  28.4 0.9 %shard_map.75 = f32[128,256]{1,0:T(8,128)} custom-call(f32[128,256]{1,0:T(8,128)S(1)} %get-tuple-element.17.first_ref, f32[128,256]{1,0:T(8,128)S(1)} %get-tuple-element.27.second_ref, f32[16,1,128]{2,1,0:T(1,128)S(1)} %all_to_all.5.parts_ref), custom_call_target="tpu_custom_call" | custom-call | flops 32768 | bytes 1048576 | tf_op jit(solution)/shard_map/pallas_call | solution.py:398
  (2 shorter events, 0.0 us)
Async XLA Ops:
  0.7 12.1 %copy-start = (f32[256,256]{1,0:T(8,128)S(1)}, f32[256,256]{1,0:T(8,128)}, u32[]{:S(2)}) copy-start(f32[256,256]{1,0:T(8,128)} %p_ref.1) | copy-start | bytes 786436
  0.7 12.1 %copy-start.1 = (f32[256,256]{1,0:T(8,128)S(1)}, f32[256,256]{1,0:T(8,128)}, u32[]{:S(2)}) copy-start(f32[256,256]{1,0:T(8,128)} %k_ref.1) | copy-start | bytes 786436
  3.0 5.9 %collective-permute-start.1 = (f32[48,128]{1,0:T(8,128)S(1)}, f32[48,128]{1,0:T(8,128)S(1)}, u32[]{:S(2)}, u32[]{:S(2)}) collective-permute-start(f32[48,128]{1,0:T(8,128)S(1)} %get-tuple-element.25), channel_id=1, source_target_pairs={{0,2},{1,3},{2,0},{3,1},{4,6},{5,7},{6,4},{7,5},{8,10},{9,11},{10,... | collective-permute-start | bytes 73736 | tf_op jit(solution)/shard_map/ppermute | solution.py:446
  7.1 5.6 %collective-permute-start.2 = (f32[48,128]{1,0:T(8,128)S(1)}, f32[48,128]{1,0:T(8,128)S(1)}, u32[]{:S(2)}, u32[]{:S(2)}) collective-permute-start(f32[48,128]{1,0:T(8,128)S(1)} %get-tuple-element.26), channel_id=1, source_target_pairs={{0,3},{1,2},{2,1},{3,0},{4,7},{5,6},{6,5},{7,4},{8,11},{9,10},{10,... | collective-permute-start | bytes 73736 | tf_op jit(solution)/shard_map/ppermute | solution.py:446
  8.5 4.3 %collective-permute-start = (f32[48,128]{1,0:T(8,128)S(1)}, f32[48,128]{1,0:T(8,128)S(1)}, u32[]{:S(2)}, u32[]{:S(2)}) collective-permute-start(f32[48,128]{1,0:T(8,128)S(1)} %get-tuple-element.24.mine_ref), channel_id=1, source_target_pairs={{0,1},{1,0},{2,3},{3,2},{4,5},{5,4},{6,7},{7,6},{8,9},{9,8},{10,11... | collective-permute-start | bytes 73736 | tf_op jit(solution)/shard_map/ppermute | solution.py:446
  14.9 1.1 %collective-permute-start.3 = (f32[1,128]{1,0:T(1,128)S(1)}, f32[1,128]{1,0:T(1,128)S(1)}, u32[]{:S(2)}, u32[]{:S(2)}) collective-permute-start(f32[1,128]{1,0:T(1,128)S(1)} %get-tuple-element.28), channel_id=1, source_target_pairs={{0,8},{8,0},{16,24},{24,16},{1,9},{9,1},{17,25},{25,17},{2,10},{10... | collective-permute-start | bytes 1544 | tf_op jit(solution)/shard_map/ppermute | solution.py:527

commit v8 on v6

--- a/solution.py
+++ b/solution.py
@@ -2,6 +2,7 @@
 
 import jax
 import jax.numpy as jnp
+import numpy as np
 from jax import lax
 from jax.experimental import pallas as pl
 from jax.experimental.pallas import tpu as pltpu
@@ -518,6 +519,46 @@
     return first_pre, second_pre, products
 
 
+def tree_levels(line):
+    levels = []
+    while len(line) > 1:
+        count = next((n for n in range(short_group, 1, -1) if len(line) % n == 0), len(line))
+        groups = [line[low : low + count] for low in range(0, len(line), count)]
+        middle = (count - 1) // 2
+        line = [group[middle] for group in groups]
+        levels.append([(group[middle], group[:middle] + group[middle + 1 :]) for group in groups])
+    return levels, line[0]
+
+
+def tree_sum(row, mesh):
+    axes = ("gx", "gy", "gz")
+    ids = np.arange(mesh.size).reshape([mesh.shape[axis] for axis in axes])
+    levels = []
+    if ids.shape[0] % 2 == 0:
+        pairs = zip(ids[1::2].ravel().tolist(), ids[::2].ravel().tolist())
+        levels.append([(root, [other]) for root, other in pairs])
+        ids = ids[1::2]
+    trees = [tree_levels(line) for line in ids.reshape(-1, ids.shape[2]).tolist()]
+    levels += [sum(parts, []) for parts in zip(*(tree for tree, _ in trees))]
+    upper, top = tree_levels([root for _, root in trees])
+    levels += upper
+
+    def one_way(value, level, down):
+        came = []
+        for place in range(len(level[0][1])):
+            pairs = [(others[place], root) for root, others in level]
+            pairs = [pair[::-1] for pair in pairs] if down else pairs
+            came.append(lax.ppermute(value, axes, pairs))
+        return functools.reduce(jnp.add, came, value)
+
+    for level in levels:
+        row = one_way(row, level, False)
+    row = jnp.where(lax.axis_index(axes) == top, row, 0.0)
+    for level in reversed(levels):
+        row = one_way(row, level, True)
+    return row
+
+
 def per_device(mesh, *arguments):
     rhs, face_index = arguments[0], arguments[4]
     probes, elements, dofs = rhs.shape[3:]
@@ -539,7 +580,7 @@
         probes * elements * dofs,
         first_pre,
         second_pre,
-        lax.psum(products, ("gx", "gy", "gz")),
+        tree_sum(products, mesh),
     )
     return result.reshape(rhs.shape)
 

time: 55.1 us -> 45 us (0.82)
  blocking collectives: 39.1 us -> 0 us
  waiting for transfers between devices: 4.05 us -> 22 us
  starting transfers between devices: 5.68 us -> 16.2 us
    psum x1 -> x0, blocking collectives: 39.1 us -> none  [per_device(): lax.psum(products, ('gx', 'gy', 'gz'))]
    ppermute x0 -> x14, waiting for transfers between devices: none -> 16.4 us  [one_way(): came.append(lax.ppermute(value, axes, pairs))]
    ppermute x0 -> x14, starting transfers between devices: none -> 10.5 us  [one_way(): came.append(lax.ppermute(value, axes, pairs))]
    ppermute x3, waiting for transfers between devices: 4.05 us -> 5.62 us  [near_steps(): lax.ppermute(leaving[step - 1], 'gz', [(source, source ^ step) for source...]
  transfers between devices with their start and end apart: 3 -> 17, of which waited for: 2 -> 4; matrix products, arithmetic and copies ran while one was open for 0% -> 0% of each run, Pallas kernels for 0% -> 0%
where the time goes in v8:
time: 45 us; the launch traced here: 44.6 us
  waiting for transfers between devices  22 us (49%)
  starting transfers between devices  16.2 us (36%)
  Pallas kernels  5.41 us (12%)
  between operations  0.94 us (2%)
    ppermute x14, waiting for transfers between devices, one_way(): came.append(lax.ppermute(value, axes, pairs))  16.4 us
    ppermute x14, starting transfers between devices, one_way(): came.append(lax.ppermute(value, axes, pairs))  10.5 us
    ppermute x3, starting transfers between devices, near_steps(): lax.ppermute(leaving[step - 1], 'gz', [(source, source ^ step) for source...  5.68 us
    ppermute x3, waiting for transfers between devices, near_steps(): lax.ppermute(leaving[step - 1], 'gz', [(source, source ^ step) for source...  5.62 us
    pallas_call x3, Pallas kernels, call(): pl.pallas_call(kernel, out_shape=out_shapes, in_specs=in_specs, out_specs...  5.41 us
  transfers between devices with their start and end apart: 17, of which 4 were waited for; matrix products, arithmetic and copies ran while one was open for 0% of the time, Pallas kernels for 0%

profile of v8, /device:TPU:0, one launch (start us, length us, event | category | flops | bytes accessed | tf_op | source)
XLA Modules:
  0.0 44.6 jit_solution(11888985724673902123)
XLA Ops:
  0.7 0.0 copy-start
  0.7 0.0 copy-start.1
  0.7 2.4 %shard_map.73 = (f32[128,256]{1,0:T(8,128)S(1)}, f32[128,256]{1,0:T(8,128)S(1)}, f32[128,256]{1,0:T(8,128)S(1)}, f32[128,256]{1,0:T(8,128)S(1)}, f32[128,256]{1,...) custom-call(s32[1,1,1]{2,1,0:T(1,128)S(6)} %copy.8.refs_0_, ...), custom_call_target="tpu_custom_call" | custom-call | flops 805306368 | bytes 1048576 | tf_op jit(solution)/shard_map/pallas_call | solution.py:399
  3.0 3.1 %collective-permute-start = (f32[48,128]{1,0:T(8,128)S(1)}, f32[48,128]{1,0:T(8,128)S(1)}, u32[]{:S(2)}, u32[]{:S(2)}) collective-permute-start(f32[48,128]{1,0:T(8,128)S(1)} %get-tuple-element.24.mine_ref), channel_id=1, source_target_pairs={{0,1},{1,0},{2,3},{3,2},{4,5},{5,4},{6,7},{7,6},{8,9},{9,8},{10,11... | collective-permute-start | bytes 73736 | tf_op jit(solution)/shard_map/ppermute | solution.py:447
  6.1 2.6 %collective-permute-start.1 = (f32[48,128]{1,0:T(8,128)S(1)}, f32[48,128]{1,0:T(8,128)S(1)}, u32[]{:S(2)}, u32[]{:S(2)}) collective-permute-start(f32[48,128]{1,0:T(8,128)S(1)} %get-tuple-element.25), channel_id=1, source_target_pairs={{0,2},{1,3},{2,0},{3,1},{4,6},{5,7},{6,4},{7,5},{8,10},{9,11},{10,... | collective-permute-start | bytes 73736 | tf_op jit(solution)/shard_map/ppermute | solution.py:447
  8.7 0.0 collective-permute-start.2
  8.7 0.0 collective-permute-done.refs_0_
  8.7 2.5 %collective-permute-done.1.refs_1_ = f32[48,128]{1,0:T(8,128)S(1)} collective-permute-done((f32[48,128]{1,0:T(8,128)S(1)}, f32[48,128]{1,0:T(8,128)S(1)}, u32[]{:S(2)}, u32[]{:S(2)}) %collective-permute-start.1) | collective-permute-done | bytes 24608 | tf_op jit(solution)/shard_map/ppermute | solution.py:447
  11.2 3.1 %collective-permute-done.2.refs_2_ = f32[48,128]{1,0:T(8,128)S(1)} collective-permute-done((f32[48,128]{1,0:T(8,128)S(1)}, f32[48,128]{1,0:T(8,128)S(1)}, u32[]{:S(2)}, u32[]{:S(2)}) %collective-permute-start.2) | collective-permute-done | bytes 24608 | tf_op jit(solution)/shard_map/ppermute | solution.py:447
  14.3 0.0 copy-done
  14.3 0.0 copy-done.1
  14.3 2.2 %shard_map.74 = (f32[128,256]{1,0:T(8,128)S(1)}, f32[1,128]{1,0:T(1,128)S(1)}) custom-call(f32[128,256]{1,0:T(8,128)S(1)} %get-tuple-element.18.source_ref, f32[128,256]{1,0:T(8,128)S(1)} %get-tuple-element.19.up_ref, f32[128,256]{1,0:T(8,128)S(1)} %get-tuple-element.20.down_ref, f32[128,256]{1,0:T(8,128)S(1)} %get-tuple-element.21.base_ref, ...), custom_call_target="tpu_custom_call" | custom-call | flops 2415919104 | bytes 1048576 | tf_op jit(solution)/shard_map/pallas_call | solution.py:399
  16.5 1.3 %collective-permute-start.3 = (f32[1,128]{1,0:T(1,128)S(1)}, f32[1,128]{1,0:T(1,128)S(1)}, u32[]{:S(2)}, u32[]{:S(2)}) collective-permute-start(f32[1,128]{1,0:T(1,128)S(1)} %get-tuple-element.28), channel_id=1, source_target_pairs={{0,8},{1,9},{2,10},{3,11},{4,12},{5,13},{6,14},{7,15},{16,24},{17,... | collective-permute-start | bytes 1544 | tf_op jit(solution)/shard_map/ppermute | solution.py:551
  17.8 0.8 %collective-permute-done.3 = f32[1,128]{1,0:T(1,128)S(1)} collective-permute-done((f32[1,128]{1,0:T(1,128)S(1)}, f32[1,128]{1,0:T(1,128)S(1)}, u32[]{:S(2)}, u32[]{:S(2)}) %collective-permute-start.3) | collective-permute-done | bytes 544 | tf_op jit(solution)/shard_map/ppermute | solution.py:551
  18.6 0.6 %collective-permute-start.6 = (f32[1,128]{1,0:T(1,128)S(1)}, f32[1,128]{1,0:T(1,128)S(1)}, u32[]{:S(2)}, u32[]{:S(2)}) collective-permute-start(f32[1,128]{1,0:T(1,128)S(1)} %add.50), channel_id=1, source_target_pairs={{11,9},{15,13},{27,25},{31,29}} | collective-permute-start | bytes 1544 | tf_op jit(solution)/shard_map/ppermute | solution.py:551
  19.3 0.7 %collective-permute-start.5 = (f32[1,128]{1,0:T(1,128)S(1)}, f32[1,128]{1,0:T(1,128)S(1)}, u32[]{:S(2)}, u32[]{:S(2)}) collective-permute-start(f32[1,128]{1,0:T(1,128)S(1)} %add.50), channel_id=1, source_target_pairs={{10,9},{14,13},{26,25},{30,29}} | collective-permute-start | bytes 1544 | tf_op jit(solution)/shard_map/ppermute | solution.py:551
  19.9 0.7 %collective-permute-start.4 = (f32[1,128]{1,0:T(1,128)S(1)}, f32[1,128]{1,0:T(1,128)S(1)}, u32[]{:S(2)}, u32[]{:S(2)}) collective-permute-start(f32[1,128]{1,0:T(1,128)S(1)} %add.50), channel_id=1, source_target_pairs={{8,9},{12,13},{24,25},{28,29}} | collective-permute-start | bytes 1544 | tf_op jit(solution)/shard_map/ppermute | solution.py:551
  20.6 0.0 collective-permute-done.6
  20.6 0.0 collective-permute-done.5
  20.6 0.0 collective-permute-done.4
  20.7 0.7 %collective-permute-start.9 = (f32[1,128]{1,0:T(1,128)S(1)}, f32[1,128]{1,0:T(1,128)S(1)}, u32[]{:S(2)}, u32[]{:S(2)}) collective-permute-start(f32[1,128]{1,0:T(1,128)S(1)} %add_add_fusion.2), channel_id=1, source_target_pairs={{29,13}} | collective-permute-start | bytes 1544 | tf_op jit(solution)/shard_map/ppermute | solution.py:551
  21.3 0.7 %collective-permute-start.8 = (f32[1,128]{1,0:T(1,128)S(1)}, f32[1,128]{1,0:T(1,128)S(1)}, u32[]{:S(2)}, u32[]{:S(2)}) collective-permute-start(f32[1,128]{1,0:T(1,128)S(1)} %add_add_fusion.2), channel_id=1, source_target_pairs={{25,13}} | collective-permute-start | bytes 1544 | tf_op jit(solution)/shard_map/ppermute | solution.py:551
  22.0 0.7 %collective-permute-start.7 = (f32[1,128]{1,0:T(1,128)S(1)}, f32[1,128]{1,0:T(1,128)S(1)}, u32[]{:S(2)}, u32[]{:S(2)}) collective-permute-start(f32[1,128]{1,0:T(1,128)S(1)} %add_add_fusion.2), channel_id=1, source_target_pairs={{9,13}} | collective-permute-start | bytes 1544 | tf_op jit(solution)/shard_map/ppermute | solution.py:551
  22.7 0.0 collective-permute-done.9
  22.7 0.0 collective-permute-done.8
  22.7 0.0 collective-permute-done.7
  22.7 0.7 %collective-permute-start.12 = (f32[1,128]{1,0:T(1,128)S(1)}, f32[1,128]{1,0:T(1,128)S(1)}, u32[]{:S(2)}, u32[]{:S(2)}) collective-permute-start(f32[1,128]{1,0:T(1,128)S(1)} %broadcast_select_fusion), channel_id=1, source_target_pairs={{13,29}} | collective-permute-start | bytes 1544 | tf_op jit(solution)/shard_map/ppermute | solution.py:551
  23.4 0.7 %collective-permute-start.11 = (f32[1,128]{1,0:T(1,128)S(1)}, f32[1,128]{1,0:T(1,128)S(1)}, u32[]{:S(2)}, u32[]{:S(2)}) collective-permute-start(f32[1,128]{1,0:T(1,128)S(1)} %broadcast_select_fusion), channel_id=1, source_target_pairs={{13,25}} | collective-permute-start | bytes 1544 | tf_op jit(solution)/shard_map/ppermute | solution.py:551
  24.1 0.7 %collective-permute-start.10 = (f32[1,128]{1,0:T(1,128)S(1)}, f32[1,128]{1,0:T(1,128)S(1)}, u32[]{:S(2)}, u32[]{:S(2)}) collective-permute-start(f32[1,128]{1,0:T(1,128)S(1)} %broadcast_select_fusion), channel_id=1, source_target_pairs={{13,9}} | collective-permute-start | bytes 1544 | tf_op jit(solution)/shard_map/ppermute | solution.py:551
  24.7 0.0 collective-permute-done.12
  24.7 0.0 collective-permute-done.11
  24.7 0.0 collective-permute-done.10
  24.8 0.7 %collective-permute-start.15 = (f32[1,128]{1,0:T(1,128)S(1)}, f32[1,128]{1,0:T(1,128)S(1)}, u32[]{:S(2)}, u32[]{:S(2)}) collective-permute-start(f32[1,128]{1,0:T(1,128)S(1)} %add_add_fusion.1), channel_id=1, source_target_pairs={{9,11},{13,15},{25,27},{29,31}} | collective-permute-start | bytes 1544 | tf_op jit(solution)/shard_map/ppermute | solution.py:551
  25.4 0.7 %collective-permute-start.14 = (f32[1,128]{1,0:T(1,128)S(1)}, f32[1,128]{1,0:T(1,128)S(1)}, u32[]{:S(2)}, u32[]{:S(2)}) collective-permute-start(f32[1,128]{1,0:T(1,128)S(1)} %add_add_fusion.1), channel_id=1, source_target_pairs={{9,10},{13,14},{25,26},{29,30}} | collective-permute-start | bytes 1544 | tf_op jit(solution)/shard_map/ppermute | solution.py:551
  26.1 0.7 %collective-permute-start.13 = (f32[1,128]{1,0:T(1,128)S(1)}, f32[1,128]{1,0:T(1,128)S(1)}, u32[]{:S(2)}, u32[]{:S(2)}) collective-permute-start(f32[1,128]{1,0:T(1,128)S(1)} %add_add_fusion.1), channel_id=1, source_target_pairs={{9,8},{13,12},{25,24},{29,28}} | collective-permute-start | bytes 1544 | tf_op jit(solution)/shard_map/ppermute | solution.py:551
  26.8 0.0 collective-permute-done.15
  26.8 0.0 collective-permute-done.14
  26.8 0.0 collective-permute-done.13
  26.8 1.3 %collective-permute-start.16 = (f32[1,128]{1,0:T(1,128)S(1)}, f32[1,128]{1,0:T(1,128)S(1)}, u32[]{:S(2)}, u32[]{:S(2)}) collective-permute-start(f32[1,128]{1,0:T(1,128)S(1)} %add_add_fusion), channel_id=1, source_target_pairs={{8,0},{9,1},{10,2},{11,3},{12,4},{13,5},{14,6},{15,7},{24,16},{25,... | collective-permute-start | bytes 1544 | tf_op jit(solution)/shard_map/ppermute | solution.py:551
  28.1 15.6 %collective-permute-done.16 = f32[1,128]{1,0:T(1,128)S(1)} collective-permute-done((f32[1,128]{1,0:T(1,128)S(1)}, f32[1,128]{1,0:T(1,128)S(1)}, u32[]{:S(2)}, u32[]{:S(2)}) %collective-permute-start.16) | collective-permute-done | bytes 544 | tf_op jit(solution)/shard_map/ppermute | solution.py:551
  43.7 0.9 %shard_map.75 = f32[128,256]{1,0:T(8,128)} custom-call(f32[128,256]{1,0:T(8,128)S(1)} %get-tuple-element.17.first_ref, f32[128,256]{1,0:T(8,128)S(1)} %get-tuple-element.27.second_ref, f32[1,128]{1,0:T(1,128)S(1)} %add.63.total_ref), custom_call_target="tpu_custom_call" | custom-call | flops 32768 | bytes 1048576 | tf_op jit(solution)/shard_map/pallas_call | solution.py:399
  (6 shorter events, 0.0 us)
Async XLA Ops:
  0.7 13.7 %copy-start = (f32[256,256]{1,0:T(8,128)S(1)}, f32[256,256]{1,0:T(8,128)}, u32[]{:S(2)}) copy-start(f32[256,256]{1,0:T(8,128)} %p_ref.1) | copy-start | bytes 786436
  0.7 13.7 %copy-start.1 = (f32[256,256]{1,0:T(8,128)S(1)}, f32[256,256]{1,0:T(8,128)}, u32[]{:S(2)}) copy-start(f32[256,256]{1,0:T(8,128)} %k_ref.1) | copy-start | bytes 786436
  3.0 5.7 %collective-permute-start = (f32[48,128]{1,0:T(8,128)S(1)}, f32[48,128]{1,0:T(8,128)S(1)}, u32[]{:S(2)}, u32[]{:S(2)}) collective-permute-start(f32[48,128]{1,0:T(8,128)S(1)} %get-tuple-element.24.mine_ref), channel_id=1, source_target_pairs={{0,1},{1,0},{2,3},{3,2},{4,5},{5,4},{6,7},{7,6},{8,9},{9,8},{10,11... | collective-permute-start | bytes 73736 | tf_op jit(solution)/shard_map/ppermute | solution.py:447
  6.1 5.1 %collective-permute-start.1 = (f32[48,128]{1,0:T(8,128)S(1)}, f32[48,128]{1,0:T(8,128)S(1)}, u32[]{:S(2)}, u32[]{:S(2)}) collective-permute-start(f32[48,128]{1,0:T(8,128)S(1)} %get-tuple-element.25), channel_id=1, source_target_pairs={{0,2},{1,3},{2,0},{3,1},{4,6},{5,7},{6,4},{7,5},{8,10},{9,11},{10,... | collective-permute-start | bytes 73736 | tf_op jit(solution)/shard_map/ppermute | solution.py:447
  8.7 5.6 %collective-permute-start.2 = (f32[48,128]{1,0:T(8,128)S(1)}, f32[48,128]{1,0:T(8,128)S(1)}, u32[]{:S(2)}, u32[]{:S(2)}) collective-permute-start(f32[48,128]{1,0:T(8,128)S(1)} %get-tuple-element.26), channel_id=1, source_target_pairs={{0,3},{1,2},{2,1},{3,0},{4,7},{5,6},{6,5},{7,4},{8,11},{9,10},{10,... | collective-permute-start | bytes 73736 | tf_op jit(solution)/shard_map/ppermute | solution.py:447
  16.5 2.1 %collective-permute-start.3 = (f32[1,128]{1,0:T(1,128)S(1)}, f32[1,128]{1,0:T(1,128)S(1)}, u32[]{:S(2)}, u32[]{:S(2)}) collective-permute-start(f32[1,128]{1,0:T(1,128)S(1)} %get-tuple-element.28), channel_id=1, source_target_pairs={{0,8},{1,9},{2,10},{3,11},{4,12},{5,13},{6,14},{7,15},{16,24},{17,... | collective-permute-start | bytes 1544 | tf_op jit(solution)/shard_map/ppermute | solution.py:551
  18.6 2.0 %collective-permute-start.6 = (f32[1,128]{1,0:T(1,128)S(1)}, f32[1,128]{1,0:T(1,128)S(1)}, u32[]{:S(2)}, u32[]{:S(2)}) collective-permute-start(f32[1,128]{1,0:T(1,128)S(1)} %add.50), channel_id=1, source_target_pairs={{11,9},{15,13},{27,25},{31,29}} | collective-permute-start | bytes 1544 | tf_op jit(solution)/shard_map/ppermute | solution.py:551
  19.3 1.4 %collective-permute-start.5 = (f32[1,128]{1,0:T(1,128)S(1)}, f32[1,128]{1,0:T(1,128)S(1)}, u32[]{:S(2)}, u32[]{:S(2)}) collective-permute-start(f32[1,128]{1,0:T(1,128)S(1)} %add.50), channel_id=1, source_target_pairs={{10,9},{14,13},{26,25},{30,29}} | collective-permute-start | bytes 1544 | tf_op jit(solution)/shard_map/ppermute | solution.py:551
  19.9 0.7 %collective-permute-start.4 = (f32[1,128]{1,0:T(1,128)S(1)}, f32[1,128]{1,0:T(1,128)S(1)}, u32[]{:S(2)}, u32[]{:S(2)}) collective-permute-start(f32[1,128]{1,0:T(1,128)S(1)} %add.50), channel_id=1, source_target_pairs={{8,9},{12,13},{24,25},{28,29}} | collective-permute-start | bytes 1544 | tf_op jit(solution)/shard_map/ppermute | solution.py:551
  20.7 2.0 %collective-permute-start.9 = (f32[1,128]{1,0:T(1,128)S(1)}, f32[1,128]{1,0:T(1,128)S(1)}, u32[]{:S(2)}, u32[]{:S(2)}) collective-permute-start(f32[1,128]{1,0:T(1,128)S(1)} %add_add_fusion.2), channel_id=1, source_target_pairs={{29,13}} | collective-permute-start | bytes 1544 | tf_op jit(solution)/shard_map/ppermute | solution.py:551
  21.3 1.4 %collective-permute-start.8 = (f32[1,128]{1,0:T(1,128)S(1)}, f32[1,128]{1,0:T(1,128)S(1)}, u32[]{:S(2)}, u32[]{:S(2)}) collective-permute-start(f32[1,128]{1,0:T(1,128)S(1)} %add_add_fusion.2), channel_id=1, source_target_pairs={{25,13}} | collective-permute-start | bytes 1544 | tf_op jit(solution)/shard_map/ppermute | solution.py:551
  22.0 0.7 %collective-permute-start.7 = (f32[1,128]{1,0:T(1,128)S(1)}, f32[1,128]{1,0:T(1,128)S(1)}, u32[]{:S(2)}, u32[]{:S(2)}) collective-permute-start(f32[1,128]{1,0:T(1,128)S(1)} %add_add_fusion.2), channel_id=1, source_target_pairs={{9,13}} | collective-permute-start | bytes 1544 | tf_op jit(solution)/shard_map/ppermute | solution.py:551
  22.7 2.0 %collective-permute-start.12 = (f32[1,128]{1,0:T(1,128)S(1)}, f32[1,128]{1,0:T(1,128)S(1)}, u32[]{:S(2)}, u32[]{:S(2)}) collective-permute-start(f32[1,128]{1,0:T(1,128)S(1)} %broadcast_select_fusion), channel_id=1, source_target_pairs={{13,29}} | collective-permute-start | bytes 1544 | tf_op jit(solution)/shard_map/ppermute | solution.py:551
  23.4 1.4 %collective-permute-start.11 = (f32[1,128]{1,0:T(1,128)S(1)}, f32[1,128]{1,0:T(1,128)S(1)}, u32[]{:S(2)}, u32[]{:S(2)}) collective-permute-start(f32[1,128]{1,0:T(1,128)S(1)} %broadcast_select_fusion), channel_id=1, source_target_pairs={{13,25}} | collective-permute-start | bytes 1544 | tf_op jit(solution)/shard_map/ppermute | solution.py:551
  24.1 0.7 %collective-permute-start.10 = (f32[1,128]{1,0:T(1,128)S(1)}, f32[1,128]{1,0:T(1,128)S(1)}, u32[]{:S(2)}, u32[]{:S(2)}) collective-permute-start(f32[1,128]{1,0:T(1,128)S(1)} %broadcast_select_fusion), channel_id=1, source_target_pairs={{13,9}} | collective-permute-start | bytes 1544 | tf_op jit(solution)/shard_map/ppermute | solution.py:551
  24.8 2.0 %collective-permute-start.15 = (f32[1,128]{1,0:T(1,128)S(1)}, f32[1,128]{1,0:T(1,128)S(1)}, u32[]{:S(2)}, u32[]{:S(2)}) collective-permute-start(f32[1,128]{1,0:T(1,128)S(1)} %add_add_fusion.1), channel_id=1, source_target_pairs={{9,11},{13,15},{25,27},{29,31}} | collective-permute-start | bytes 1544 | tf_op jit(solution)/shard_map/ppermute | solution.py:551
  25.4 1.4 %collective-permute-start.14 = (f32[1,128]{1,0:T(1,128)S(1)}, f32[1,128]{1,0:T(1,128)S(1)}, u32[]{:S(2)}, u32[]{:S(2)}) collective-permute-start(f32[1,128]{1,0:T(1,128)S(1)} %add_add_fusion.1), channel_id=1, source_target_pairs={{9,10},{13,14},{25,26},{29,30}} | collective-permute-start | bytes 1544 | tf_op jit(solution)/shard_map/ppermute | solution.py:551
  26.1 0.7 %collective-permute-start.13 = (f32[1,128]{1,0:T(1,128)S(1)}, f32[1,128]{1,0:T(1,128)S(1)}, u32[]{:S(2)}, u32[]{:S(2)}) collective-permute-start(f32[1,128]{1,0:T(1,128)S(1)} %add_add_fusion.1), channel_id=1, source_target_pairs={{9,8},{13,12},{25,24},{29,28}} | collective-permute-start | bytes 1544 | tf_op jit(solution)/shard_map/ppermute | solution.py:551
  26.8 16.9 %collective-permute-start.16 = (f32[1,128]{1,0:T(1,128)S(1)}, f32[1,128]{1,0:T(1,128)S(1)}, u32[]{:S(2)}, u32[]{:S(2)}) collective-permute-start(f32[1,128]{1,0:T(1,128)S(1)} %add_add_fusion), channel_id=1, source_target_pairs={{8,0},{9,1},{10,2},{11,3},{12,4},{13,5},{14,6},{15,7},{24,16},{25,... | collective-permute-start | bytes 1544 | tf_op jit(solution)/shard_map/ppermute | solution.py:551

commit v9 on v5

--- a/solution.py
+++ b/solution.py
@@ -136,8 +136,12 @@
     products_ref[...] = jnp.broadcast_to(as_row(lines, products_ref.shape[-1]), products_ref.shape)
 
 
-def begin(refs, partner):
-    count_ref, links_hbm, index_hbm, visc_hbm, rhs_hbm, *matrices_hbm = refs["operands"]
+def live_column(count_ref, elements):
+    return lax.broadcasted_iota(jnp.int32, (elements, 1), 0) < count_ref[0, 0, 0]
+
+
+def begin(refs, partner, count_ref, prepare):
+    links_hbm, index_hbm, visc_hbm, rhs_hbm, *matrices_hbm = refs["operands"]
     links_ref, index_ref, visc_ref, rhs_ref, *matrix_refs, arrived = refs["scratch"]
     pairs = (
         (links_hbm, links_ref),
@@ -158,17 +162,21 @@
     me = lax.axis_index("gz")
     for step in range(1, slots_ref.shape[0] + 1):
         slots_ref[step - 1] = slot_of(partner(me, step), links_ref, index_ref)
+    prepare()
     copies[2].wait()
     probes, elements, dofs = rhs_ref.shape[3:]
-    slot = lax.broadcasted_iota(jnp.int32, (elements, 1), 0)
-    live = (slot < count_ref[0, 0, 0]).astype(f32)
+    live = jnp.ones((elements, 1), f32)
+    if count_ref is not None:
+        live = live_column(count_ref, elements).astype(f32)
     visc = as_column(visc_ref[0, 0])
     up = wide(live * visc, probes, dofs)
     down = wide(live / visc, probes, dofs)
     refs["up"][...] = up
     refs["down"][...] = down
     copies[3].wait()
-    source = rhs_ref[...].reshape(probes * elements, dofs) * wide(live, probes, dofs)
+    source = rhs_ref[...].reshape(probes * elements, dofs)
+    if count_ref is not None:
+        source = source * wide(live, probes, dofs)
     refs["source"][...] = source
     for copy in copies[4:]:
         copy.wait()
@@ -200,12 +208,17 @@
 
 
 def near_first_kernel(*refs):
-    operands, refs = refs[:7], refs[7:]
+    operands, refs = refs[:6], refs[6:]
     first_ref, source_ref, up_ref, down_ref, base_ref, slots_ref, hot_ref = refs[:7]
     steps, _, width = slots_ref.shape
     leave_refs, scratch = refs[7 : 7 + steps], refs[7 + steps :]
     visc_ref, rhs_ref, p_ref, k_ref = scratch[2:6]
     probes, elements, dofs = rhs_ref.shape[3:]
+
+    def prepare():
+        for step in range(steps):
+            hot_ref[:, step * width : (step + 1) * width] = hot_dofs(slots_ref[step], dofs)
+
     first_pre, up, down = begin(
         {
             "operands": operands,
@@ -217,19 +230,18 @@
             "first": first_ref,
         },
         lambda me, step: me ^ step,
+        None,
+        prepare,
     )
     base = times_matrix(first_pre, k_ref[...]) * up
     base_ref[...] = base
     first_parts = stacked(first_pre)
     second_parts = stacked(times_matrix(base, p_ref[...]) * down)
     second_at, index_at, visc_at = message_places(steps, probes)
-    slot = lax.broadcasted_iota(jnp.int32, (1, elements), 1)
-    live_visc = jnp.where(slot < operands[0][0, 0, 0], visc_ref[0, 0], 0.0)
     for step in range(1, steps + 1):
         flat_row = slots_ref[step - 1]
         over_elements = hot_elements(flat_row, elements, dofs)
-        over_dofs = hot_dofs(flat_row, dofs)
-        hot_ref[:, (step - 1) * width : step * width] = over_dofs
+        over_dofs = hot_ref[:, (step - 1) * width : step * width]
         first_rows = take_faces(first_parts, over_elements, over_dofs)
         second_rows = take_faces(second_parts, over_elements, over_dofs)
         for probe in range(probes):
@@ -240,11 +252,11 @@
             write_row(leave_ref, index_at + step - 1, flat_row.astype(f32))
     visc_line = visc_at * (width // lane_count)
     for leave_ref in leave_refs:
-        leave_ref[visc_line : visc_line + 1, :elements] = live_visc
+        leave_ref[visc_line : visc_line + 1, :elements] = visc_ref[0, 0]
 
 
 def near_second_kernel(
-    probes, source_ref, up_ref, down_ref, base_ref, slots_ref, hot_ref, k_ref, p_ref, mine_ref, *refs
+    probes, count_ref, source_ref, up_ref, down_ref, base_ref, slots_ref, hot_ref, k_ref, p_ref, mine_ref, *refs
 ):
     came_refs = refs[:-2]
     second_ref, products_ref = refs[-2:]
@@ -272,9 +284,9 @@
         )
 
     up, down = up_ref[...], down_ref[...]
-    live = up > 0.0
+    live = wide(live_column(count_ref, elements).astype(f32), probes, dofs) > 0.0
     placed = placed_here([inbound_first(0, step) for step in range(1, members)])
-    image = base_ref[...] - jnp.where(live, coupling * placed, 0.0)
+    image = jnp.where(live, base_ref[...] - coupling * placed, 0.0)
     images, back = [image], []
     for member in range(1, members):
         total = 0.0
@@ -294,15 +306,17 @@
     for member in range(1, members):
         sent = message(member)
         visc = as_column(sent[visc_line : visc_line + 1, :elements])
-        scale = wide(jnp.where(visc > 0.0, 1.0 / visc, 0.0), probes, dofs)
+        scale = wide(1.0 / visc, probes, dofs)
         change = smooth[member * rows : (member + 1) * rows] * scale
         taken = take_faces(stacked(change), *back[member - 1])
         values.append(
             [taken[probe] + read_row(sent, second_at + probe, width) for probe in range(probes)]
         )
     placed = placed_here(values)
-    second_img = times_matrix(second_pre, k_ref[...]) * up - jnp.where(live, coupling * placed, 0.0)
-    inner_products(image, second_img, source_ref[...], probes, products_ref)
+    second_img = times_matrix(second_pre, k_ref[...]) * up - coupling * placed
+    second_img = jnp.where(live, second_img, 0.0)
+    source = jnp.where(live, source_ref[...], 0.0)
+    inner_products(image, second_img, source, probes, products_ref)
 
 
 def leave_faces(field, probes, slots_ref, leave_ref):
@@ -337,7 +351,8 @@
 
 
 def far_first_kernel(*refs):
-    operands, refs = refs[:6], refs[6:]
+    count_ref, *operands = refs[:6]
+    refs = refs[6:]
     first_ref, source_ref, up_ref, down_ref, slots_ref, leave_ref = refs[:6]
     members = slots_ref.shape[0] + 1
     first_pre, _, _ = begin(
@@ -351,6 +366,8 @@
             "first": first_ref,
         },
         lambda me, step: lax.rem(me + step, members),
+        count_ref,
+        lambda: None,
     )
     leave_faces(first_pre, leave_ref.shape[1], slots_ref, leave_ref)
 
@@ -379,10 +396,11 @@
     inner_products(image_ref[...], second_img, source_ref[...], probes, products_ref)
 
 
-def last_kernel(probes, first_ref, second_ref, parts_ref, out_ref):
+def last_kernel(probes, count_ref, first_ref, second_ref, parts_ref, out_ref):
     rows, _ = first_ref.shape
     elements = rows // probes
     total = jnp.sum(parts_ref[...], axis=0)
+    live = live_column(count_ref, elements)
     for probe in range(probes):
         self_one, cross_mid, self_two, load_one, load_two = (
             total[:, place * probes + probe : place * probes + probe + 1] for place in range(5)
@@ -391,7 +409,8 @@
         weight_one = (self_two * load_one - cross_mid * load_two) / determinant
         weight_two = (self_one * load_two - cross_mid * load_one) / determinant
         block = pl.ds(probe * elements, elements)
-        out_ref[block, :] = weight_one * first_ref[block, :] + weight_two * second_ref[block, :]
+        value = weight_one * first_ref[block, :] + weight_two * second_ref[block, :]
+        out_ref[block, :] = jnp.where(live, value, 0.0)
 
 
 def call(kernel, in_specs, out_shapes, flops, *args, scratch=()):
@@ -406,16 +425,16 @@
     )(*args)
 
 
-def begin_call(kernel, out_shapes, flops, counts, *fetched):
+def begin_call(kernel, out_shapes, flops, scalars, *fetched):
     links, *others = fetched
     scratch = [pltpu.SMEM(links.shape, links.dtype)]
     scratch += [pltpu.VMEM(value.shape, value.dtype) for value in others]
     return call(
         kernel,
-        [smem_spec] + [hbm_spec] * len(fetched),
+        [smem_spec] * len(scalars) + [hbm_spec] * len(fetched),
         out_shapes,
         flops,
-        counts,
+        *scalars,
         *(pltpu.with_memory_space_constraint(value, pltpu.HBM) for value in fetched),
         scratch=scratch + [pltpu.SemaphoreType.DMA((len(fetched),))],
     )
@@ -434,7 +453,7 @@
         near_first_kernel,
         [field] * 5 + [slots_shape, hot] + [message] * steps,
         2 * flops,
-        counts,
+        (),
         neighbours,
         face_index,
         viscosity,
@@ -450,9 +469,10 @@
     ]
     second_pre, products = call(
         functools.partial(near_second_kernel, probes),
-        [vmem_spec] * (9 + steps),
+        [smem_spec] + [vmem_spec] * (9 + steps),
         [field, products_shape],
         6 * flops,
+        counts,
         source,
         up,
         down,
@@ -482,7 +502,7 @@
         far_first_kernel,
         [field] * 4 + [slots_shape, faces],
         flops,
-        counts,
+        (counts,),
         neighbours,
         face_index,
         viscosity,
@@ -534,9 +554,10 @@
     first_pre, second_pre, products = steps(members, shapes, arguments)
     result = call(
         functools.partial(last_kernel, probes),
-        [vmem_spec] * 3,
+        [smem_spec] + [vmem_spec] * 3,
         shapes[0],
         probes * elements * dofs,
+        arguments[2],
         first_pre,
         second_pre,
         lax.all_to_all(products, ("gx", "gy", "gz"), split_axis=0, concat_axis=0),

time: 27.3 us -> 26.6 us (0.974)
  waiting for transfers between devices: 4.05 us -> 3.39 us
    ppermute x3, waiting for transfers between devices: 4.05 us -> 3.39 us  [near_steps(): lax.ppermute(leaving[step - 1], 'gz', [(source, source ^ step) for source...]
  transfers between devices with their start and end apart: 3 -> 3, of which waited for: 2 -> 1; matrix products, arithmetic and copies ran while one was open for 0% -> 0% of each run, Pallas kernels for 0% -> 0%
where the time goes in v9:
time: 26.6 us; the launch traced here: 26.4 us
  blocking collectives  11.2 us (42%)
  starting transfers between devices  5.68 us (21%)
  Pallas kernels  5.47 us (21%)
  waiting for transfers between devices  3.39 us (13%)
  between operations  0.68 us (3%)
    all_to_all x1, blocking collectives, per_device(): lax.all_to_all(products, ('gx', 'gy', 'gz'), split_axis=0, concat_axis=0)  11.2 us
    ppermute x3, starting transfers between devices, near_steps(): lax.ppermute(leaving[step - 1], 'gz', [(source, source ^ step) for source...  5.68 us
    pallas_call x3, Pallas kernels, call(): pl.pallas_call(kernel, out_shape=out_shapes, in_specs=in_specs, out_specs...  5.47 us
    ppermute x3, waiting for transfers between devices, near_steps(): lax.ppermute(leaving[step - 1], 'gz', [(source, source ^ step) for source...  3.39 us
  transfers between devices with their start and end apart: 3, of which 1 were waited for; matrix products, arithmetic and copies ran while one was open for 0% of the time, Pallas kernels for 0%

profile of v9, /device:TPU:0, one launch (start us, length us, event | category | flops | bytes accessed | tf_op | source)
XLA Modules:
  0.0 26.4 jit_solution(17795652011487355966)
XLA Ops:
  0.0 0.0 copy-start
  0.0 0.0 copy-start.1
  0.0 2.3 %shard_map.73 = (f32[128,256]{1,0:T(8,128)S(1)}, f32[128,256]{1,0:T(8,128)S(1)}, f32[128,256]{1,0:T(8,128)S(1)}, f32[128,256]{1,0:T(8,128)S(1)}, f32[128,256]{1,...) custom-call(s32[1,1,1,16]{3,2,1,0:T(1,128)} %refs_0_.1, ...), custom_call_target="tpu_custom_call" | custom-call | flops 805306368 | bytes 1048576 | tf_op jit(solution)/shard_map/pallas_call | solution.py:417
  2.4 4.1 %collective-permute-start.1 = (f32[48,128]{1,0:T(8,128)S(1)}, f32[48,128]{1,0:T(8,128)S(1)}, u32[]{:S(2)}, u32[]{:S(2)}) collective-permute-start(f32[48,128]{1,0:T(8,128)S(1)} %get-tuple-element.25), channel_id=1, source_target_pairs={{0,2},{1,3},{2,0},{3,1},{4,6},{5,7},{6,4},{7,5},{8,10},{9,11},{10,... | collective-permute-start | bytes 73736 | tf_op jit(solution)/shard_map/ppermute | solution.py:465
  6.5 1.3 %collective-permute-start.2 = (f32[48,128]{1,0:T(8,128)S(1)}, f32[48,128]{1,0:T(8,128)S(1)}, u32[]{:S(2)}, u32[]{:S(2)}) collective-permute-start(f32[48,128]{1,0:T(8,128)S(1)} %get-tuple-element.26), channel_id=1, source_target_pairs={{0,3},{1,2},{2,1},{3,0},{4,7},{5,6},{6,5},{7,4},{8,11},{9,10},{10,... | collective-permute-start | bytes 73736 | tf_op jit(solution)/shard_map/ppermute | solution.py:465
  7.8 0.2 collective-permute-start
  8.7 0.0 collective-permute-done.1.refs_1_
  8.7 3.4 %collective-permute-done.2.refs_2_ = f32[48,128]{1,0:T(8,128)S(1)} collective-permute-done((f32[48,128]{1,0:T(8,128)S(1)}, f32[48,128]{1,0:T(8,128)S(1)}, u32[]{:S(2)}, u32[]{:S(2)}) %collective-permute-start.2) | collective-permute-done | bytes 24608 | tf_op jit(solution)/shard_map/ppermute | solution.py:465
  12.1 0.0 collective-permute-done.refs_0_
  12.1 0.0 copy-done
  12.1 0.0 copy-done.1
  12.1 2.2 %shard_map.74 = (f32[128,256]{1,0:T(8,128)S(1)}, f32[32,1,128]{2,1,0:T(1,128)S(1)}) custom-call(s32[1,1,1]{2,1,0:T(1,128)S(6)} %copy.8.count_ref, f32[128,256]{1,0:T(8,128)S(1)} %get-tuple-element.18.source_ref, f32[128,256]{1,0:T(8,128)S(1)} %get-tuple-element.19.up_ref, f32[128,256]{1,0:T(8,128)S(1)} %get-tuple-element.20.down_ref, ...), custom_call_target="tpu_custom_call" | custom-call | flops 2415919104 | bytes 1048576 | tf_op jit(solution)/shard_map/pallas_call | solution.py:417
  14.3 11.2 %all_to_all.5.parts_ref = f32[32,1,128]{2,1,0:T(1,128)S(1)} all-to-all(f32[32,1,128]{2,1,0:T(1,128)S(1)} %get-tuple-element.28), channel_id=1, replica_groups=mesh['gx'=4,'gy'=2,'gz'=4] {'gx','gy','gz'}, dimensions={0} | all-to-all | bytes 32768 | tf_op jit(solution)/shard_map/all_to_all | solution.py:563
  25.5 1.0 %shard_map.75 = f32[128,256]{1,0:T(8,128)} custom-call(s32[1,1,1]{2,1,0:T(1,128)S(6)} %copy.8.count_ref, f32[128,256]{1,0:T(8,128)S(1)} %get-tuple-element.17.first_ref, f32[128,256]{1,0:T(8,128)S(1)} %get-tuple-element.27.second_ref, f32[32,1,128]{2,1,0:T(1,128)S(1)} %all_to_all.5.parts_ref), custom_call_target="tpu_custom_call" | custom-call | flops 32768 | bytes 1048576 | tf_op jit(solution)/shard_map/pallas_call | solution.py:417
Async XLA Ops:
  0.0 12.1 %copy-start = (f32[256,256]{1,0:T(8,128)S(1)}, f32[256,256]{1,0:T(8,128)}, u32[]{:S(2)}) copy-start(f32[256,256]{1,0:T(8,128)} %p_ref.1) | copy-start | bytes 786436
  0.0 12.1 %copy-start.1 = (f32[256,256]{1,0:T(8,128)S(1)}, f32[256,256]{1,0:T(8,128)}, u32[]{:S(2)}) copy-start(f32[256,256]{1,0:T(8,128)} %k_ref.1) | copy-start | bytes 786436
  2.4 6.3 %collective-permute-start.1 = (f32[48,128]{1,0:T(8,128)S(1)}, f32[48,128]{1,0:T(8,128)S(1)}, u32[]{:S(2)}, u32[]{:S(2)}) collective-permute-start(f32[48,128]{1,0:T(8,128)S(1)} %get-tuple-element.25), channel_id=1, source_target_pairs={{0,2},{1,3},{2,0},{3,1},{4,6},{5,7},{6,4},{7,5},{8,10},{9,11},{10,... | collective-permute-start | bytes 73736 | tf_op jit(solution)/shard_map/ppermute | solution.py:465
  6.5 5.6 %collective-permute-start.2 = (f32[48,128]{1,0:T(8,128)S(1)}, f32[48,128]{1,0:T(8,128)S(1)}, u32[]{:S(2)}, u32[]{:S(2)}) collective-permute-start(f32[48,128]{1,0:T(8,128)S(1)} %get-tuple-element.26), channel_id=1, source_target_pairs={{0,3},{1,2},{2,1},{3,0},{4,7},{5,6},{6,5},{7,4},{8,11},{9,10},{10,... | collective-permute-start | bytes 73736 | tf_op jit(solution)/shard_map/ppermute | solution.py:465
  7.8 4.3 %collective-permute-start = (f32[48,128]{1,0:T(8,128)S(1)}, f32[48,128]{1,0:T(8,128)S(1)}, u32[]{:S(2)}, u32[]{:S(2)}) collective-permute-start(f32[48,128]{1,0:T(8,128)S(1)} %get-tuple-element.24.mine_ref), channel_id=1, source_target_pairs={{0,1},{1,0},{2,3},{3,2},{4,5},{5,4},{6,7},{7,6},{8,9},{9,8},{10,11... | collective-permute-start | bytes 73736 | tf_op jit(solution)/shard_map/ppermute | solution.py:465

commit v10 on v9

--- a/solution.py
+++ b/solution.py
@@ -32,9 +32,12 @@
 
 
 def times_matrix(rows, matrix):
+    return times_parts(rows, *two_parts(matrix))
+
+
+def times_parts(rows, mat_high, mat_low):
     count = rows.shape[0]
     row_high, row_low = two_parts(rows)
-    mat_high, mat_low = two_parts(matrix)
     both = dot(jnp.concatenate([row_high, row_low], axis=0), mat_high)
     return both[:count] + (both[count:] + dot(row_high, mat_low))
 
@@ -146,9 +149,10 @@
     pairs = (
         (links_hbm, links_ref),
         (index_hbm, index_ref),
+        (rhs_hbm, rhs_ref),
+        (matrices_hbm[0], matrix_refs[0]),
         (visc_hbm, visc_ref),
-        (rhs_hbm, rhs_ref),
-        *zip(matrices_hbm, matrix_refs),
+        *zip(matrices_hbm[1:], matrix_refs[1:]),
     )
     copies = [
         pltpu.make_async_copy(held, here, arrived.at[place])
@@ -163,7 +167,7 @@
     for step in range(1, slots_ref.shape[0] + 1):
         slots_ref[step - 1] = slot_of(partner(me, step), links_ref, index_ref)
     prepare()
-    copies[2].wait()
+    copies[4].wait()
     probes, elements, dofs = rhs_ref.shape[3:]
     live = jnp.ones((elements, 1), f32)
     if count_ref is not None:
@@ -173,16 +177,18 @@
     down = wide(live / visc, probes, dofs)
     refs["up"][...] = up
     refs["down"][...] = down
-    copies[3].wait()
+    copies[2].wait()
     source = rhs_ref[...].reshape(probes * elements, dofs)
     if count_ref is not None:
         source = source * wide(live, probes, dofs)
     refs["source"][...] = source
-    for copy in copies[4:]:
+    copies[3].wait()
+    smoother = two_parts(matrix_refs[0][...])
+    first_pre = times_parts(source, *smoother) * down
+    refs["first"][...] = first_pre
+    for copy in copies[5:]:
         copy.wait()
-    first_pre = times_matrix(source, matrix_refs[0][...]) * down
-    refs["first"][...] = first_pre
-    return first_pre, up, down
+    return first_pre, up, down, smoother
 
 
 def message_places(steps, probes):
@@ -210,16 +216,17 @@
 def near_first_kernel(*refs):
     operands, refs = refs[:6], refs[6:]
     first_ref, source_ref, up_ref, down_ref, base_ref, slots_ref, hot_ref = refs[:7]
+    part_refs, refs = refs[7:11], refs[11:]
     steps, _, width = slots_ref.shape
-    leave_refs, scratch = refs[7 : 7 + steps], refs[7 + steps :]
-    visc_ref, rhs_ref, p_ref, k_ref = scratch[2:6]
+    leave_refs, scratch = refs[:steps], refs[steps:]
+    visc_ref, rhs_ref, _, k_ref = scratch[2:6]
     probes, elements, dofs = rhs_ref.shape[3:]
 
     def prepare():
         for step in range(steps):
             hot_ref[:, step * width : (step + 1) * width] = hot_dofs(slots_ref[step], dofs)
 
-    first_pre, up, down = begin(
+    first_pre, up, down, smoother = begin(
         {
             "operands": operands,
             "scratch": scratch,
@@ -233,10 +240,13 @@
         None,
         prepare,
     )
-    base = times_matrix(first_pre, k_ref[...]) * up
+    stiffness = two_parts(k_ref[...])
+    base = times_parts(first_pre, *stiffness) * up
     base_ref[...] = base
     first_parts = stacked(first_pre)
-    second_parts = stacked(times_matrix(base, p_ref[...]) * down)
+    second_parts = stacked(times_parts(base, *smoother) * down)
+    for part_ref, part in zip(part_refs, smoother + stiffness):
+        part_ref[...] = part
     second_at, index_at, visc_at = message_places(steps, probes)
     for step in range(1, steps + 1):
         flat_row = slots_ref[step - 1]
@@ -256,7 +266,8 @@
 
 
 def near_second_kernel(
-    probes, count_ref, source_ref, up_ref, down_ref, base_ref, slots_ref, hot_ref, k_ref, p_ref, mine_ref, *refs
+    probes, count_ref, source_ref, up_ref, down_ref, base_ref, slots_ref, hot_ref,
+    p_high_ref, p_low_ref, k_high_ref, k_low_ref, mine_ref, *refs
 ):
     came_refs = refs[:-2]
     second_ref, products_ref = refs[-2:]
@@ -298,7 +309,7 @@
             if step == member:
                 back.append((over_elements, over_dofs))
         images.append(-coupling * folded(total))
-    smooth = times_matrix(jnp.concatenate(images, axis=0), p_ref[...])
+    smooth = times_parts(jnp.concatenate(images, axis=0), p_high_ref[...], p_low_ref[...])
     second_pre = smooth[:rows] * down
     second_ref[...] = second_pre
     values = []
@@ -313,7 +324,7 @@
             [taken[probe] + read_row(sent, second_at + probe, width) for probe in range(probes)]
         )
     placed = placed_here(values)
-    second_img = times_matrix(second_pre, k_ref[...]) * up - coupling * placed
+    second_img = times_parts(second_pre, k_high_ref[...], k_low_ref[...]) * up - coupling * placed
     second_img = jnp.where(live, second_img, 0.0)
     source = jnp.where(live, source_ref[...], 0.0)
     inner_products(image, second_img, source, probes, products_ref)
@@ -355,7 +366,7 @@
     refs = refs[6:]
     first_ref, source_ref, up_ref, down_ref, slots_ref, leave_ref = refs[:6]
     members = slots_ref.shape[0] + 1
-    first_pre, _, _ = begin(
+    first_pre, *_ = begin(
         {
             "operands": operands,
             "scratch": refs[6:],
@@ -449,9 +460,10 @@
     flops = 8 * rows * dofs * steps * width
     hot = jax.ShapeDtypeStruct((dofs, steps * width), bf16)
     message = jax.ShapeDtypeStruct((message_length(steps, probes, width), lane_count), f32)
-    first_pre, source, up, down, base, slots, hot_own, *leaving = begin_call(
+    part = jax.ShapeDtypeStruct(p_matrix.shape, bf16)
+    first_pre, source, up, down, base, slots, hot_own, *rest = begin_call(
         near_first_kernel,
-        [field] * 5 + [slots_shape, hot] + [message] * steps,
+        [field] * 5 + [slots_shape, hot] + [part] * 4 + [message] * steps,
         2 * flops,
         (),
         neighbours,
@@ -461,6 +473,7 @@
         p_matrix,
         k_matrix,
     )
+    parts, leaving = rest[:4], rest[4:]
     came = [
         lax.ppermute(
             leaving[step - 1], "gz", [(source, source ^ step) for source in range(members)]
@@ -469,7 +482,7 @@
     ]
     second_pre, products = call(
         functools.partial(near_second_kernel, probes),
-        [smem_spec] + [vmem_spec] * (9 + steps),
+        [smem_spec] + [vmem_spec] * (11 + steps),
         [field, products_shape],
         6 * flops,
         counts,
@@ -479,8 +492,7 @@
         base,
         slots,
         hot_own,
-        k_matrix,
-        p_matrix,
+        *parts,
         leaving[0],
         *came,
     )

time: 26.6 us -> 26.6 us (level)
  no operation moved by 1% of the time
where the time goes in v10:
time: 26.6 us; the launch traced here: 26.4 us
  blocking collectives  11.2 us (42%)
  starting transfers between devices  5.7 us (21%)
  Pallas kernels  5.46 us (21%)
  waiting for transfers between devices  3.37 us (13%)
  between operations  0.68 us (3%)
    all_to_all x1, blocking collectives, per_device(): lax.all_to_all(products, ('gx', 'gy', 'gz'), split_axis=0, concat_axis=0)  11.2 us
    ppermute x3, starting transfers between devices, near_steps(): lax.ppermute(leaving[step - 1], 'gz', [(source, source ^ step) for source...  5.7 us
    pallas_call x3, Pallas kernels, call(): pl.pallas_call(kernel, out_shape=out_shapes, in_specs=in_specs, out_specs...  5.46 us
    ppermute x3, waiting for transfers between devices, near_steps(): lax.ppermute(leaving[step - 1], 'gz', [(source, source ^ step) for source...  3.37 us
  transfers between devices with their start and end apart: 3, of which 1 were waited for; matrix products, arithmetic and copies ran while one was open for 0% of the time, Pallas kernels for 0%

profile of v10, /device:TPU:0, one launch (start us, length us, event | category | flops | bytes accessed | tf_op | source)
XLA Modules:
  0.0 26.4 jit_solution(12291649484431016121)
XLA Ops:
  0.0 2.3 %shard_map.73 = (f32[128,256]{1,0:T(8,128)S(1)}, f32[128,256]{1,0:T(8,128)S(1)}, f32[128,256]{1,0:T(8,128)S(1)}, f32[128,256]{1,0:T(8,128)S(1)}, f32[128,256]{1,...) custom-call(s32[1,1,1,16]{3,2,1,0:T(1,128)} %refs_0_.1, ...), custom_call_target="tpu_custom_call" | custom-call | flops 805306368 | bytes 1048576 | tf_op jit(solution)/shard_map/pallas_call | solution.py:428
  2.3 4.1 %collective-permute-start.1 = (f32[48,128]{1,0:T(8,128)S(1)}, f32[48,128]{1,0:T(8,128)S(1)}, u32[]{:S(2)}, u32[]{:S(2)}) collective-permute-start(f32[48,128]{1,0:T(8,128)S(1)} %get-tuple-element.33), channel_id=1, source_target_pairs={{0,2},{1,3},{2,0},{3,1},{4,6},{5,7},{6,4},{7,5},{8,10},{9,11},{10,... | collective-permute-start | bytes 73736 | tf_op jit(solution)/shard_map/ppermute | solution.py:478
  6.4 1.3 %collective-permute-start.2 = (f32[48,128]{1,0:T(8,128)S(1)}, f32[48,128]{1,0:T(8,128)S(1)}, u32[]{:S(2)}, u32[]{:S(2)}) collective-permute-start(f32[48,128]{1,0:T(8,128)S(1)} %get-tuple-element.34), channel_id=1, source_target_pairs={{0,3},{1,2},{2,1},{3,0},{4,7},{5,6},{6,5},{7,4},{8,11},{9,10},{10,... | collective-permute-start | bytes 73736 | tf_op jit(solution)/shard_map/ppermute | solution.py:478
  7.8 0.2 collective-permute-start
  8.7 0.0 collective-permute-done.1.refs_1_
  8.7 3.4 %collective-permute-done.2.refs_2_ = f32[48,128]{1,0:T(8,128)S(1)} collective-permute-done((f32[48,128]{1,0:T(8,128)S(1)}, f32[48,128]{1,0:T(8,128)S(1)}, u32[]{:S(2)}, u32[]{:S(2)}) %collective-permute-start.2) | collective-permute-done | bytes 24608 | tf_op jit(solution)/shard_map/ppermute | solution.py:478
  12.1 0.0 collective-permute-done.refs_0_
  12.1 2.2 %shard_map.74 = (f32[128,256]{1,0:T(8,128)S(1)}, f32[32,1,128]{2,1,0:T(1,128)S(1)}) custom-call(s32[1,1,1]{2,1,0:T(1,128)S(6)} %copy.8.count_ref, f32[128,256]{1,0:T(8,128)S(1)} %get-tuple-element.22.source_ref, f32[128,256]{1,0:T(8,128)S(1)} %get-tuple-element.23.up_ref, f32[128,256]{1,0:T(8,128)S(1)} %get-tuple-element.24.down_ref, ...), custom_call_target="tpu_custom_call" | custom-call | flops 2415919104 | bytes 1048576 | tf_op jit(solution)/shard_map/pallas_call | solution.py:428
  14.3 11.2 %all_to_all.5.parts_ref = f32[32,1,128]{2,1,0:T(1,128)S(1)} all-to-all(f32[32,1,128]{2,1,0:T(1,128)S(1)} %get-tuple-element.36), channel_id=1, replica_groups=mesh['gx'=4,'gy'=2,'gz'=4] {'gx','gy','gz'}, dimensions={0} | all-to-all | bytes 32768 | tf_op jit(solution)/shard_map/all_to_all | solution.py:575
  25.5 1.0 %shard_map.75 = f32[128,256]{1,0:T(8,128)} custom-call(s32[1,1,1]{2,1,0:T(1,128)S(6)} %copy.8.count_ref, f32[128,256]{1,0:T(8,128)S(1)} %get-tuple-element.21.first_ref, f32[128,256]{1,0:T(8,128)S(1)} %get-tuple-element.35.second_ref, f32[32,1,128]{2,1,0:T(1,128)S(1)} %all_to_all.5.parts_ref), custom_call_target="tpu_custom_call" | custom-call | flops 32768 | bytes 1048576 | tf_op jit(solution)/shard_map/pallas_call | solution.py:428
Async XLA Ops:
  2.3 6.4 %collective-permute-start.1 = (f32[48,128]{1,0:T(8,128)S(1)}, f32[48,128]{1,0:T(8,128)S(1)}, u32[]{:S(2)}, u32[]{:S(2)}) collective-permute-start(f32[48,128]{1,0:T(8,128)S(1)} %get-tuple-element.33), channel_id=1, source_target_pairs={{0,2},{1,3},{2,0},{3,1},{4,6},{5,7},{6,4},{7,5},{8,10},{9,11},{10,... | collective-permute-start | bytes 73736 | tf_op jit(solution)/shard_map/ppermute | solution.py:478
  6.4 5.6 %collective-permute-start.2 = (f32[48,128]{1,0:T(8,128)S(1)}, f32[48,128]{1,0:T(8,128)S(1)}, u32[]{:S(2)}, u32[]{:S(2)}) collective-permute-start(f32[48,128]{1,0:T(8,128)S(1)} %get-tuple-element.34), channel_id=1, source_target_pairs={{0,3},{1,2},{2,1},{3,0},{4,7},{5,6},{6,5},{7,4},{8,11},{9,10},{10,... | collective-permute-start | bytes 73736 | tf_op jit(solution)/shard_map/ppermute | solution.py:478
  7.8 4.3 %collective-permute-start = (f32[48,128]{1,0:T(8,128)S(1)}, f32[48,128]{1,0:T(8,128)S(1)}, u32[]{:S(2)}, u32[]{:S(2)}) collective-permute-start(f32[48,128]{1,0:T(8,128)S(1)} %get-tuple-element.32.mine_ref), channel_id=1, source_target_pairs={{0,1},{1,0},{2,3},{3,2},{4,5},{5,4},{6,7},{7,6},{8,9},{9,8},{10,11... | collective-permute-start | bytes 73736 | tf_op jit(solution)/shard_map/ppermute | solution.py:478

commit v11 on v10

--- a/solution.py
+++ b/solution.py
@@ -36,10 +36,11 @@
 
 
 def times_parts(rows, mat_high, mat_low):
-    count = rows.shape[0]
     row_high, row_low = two_parts(rows)
-    both = dot(jnp.concatenate([row_high, row_low], axis=0), mat_high)
-    return both[:count] + (both[count:] + dot(row_high, mat_low))
+    return dot(
+        jnp.concatenate([row_high, row_low, row_high], axis=1),
+        jnp.concatenate([mat_high, mat_high, mat_low], axis=0),
+    )
 
 
 def split_index(index, dofs):
@@ -82,31 +83,27 @@
     return jnp.broadcast_to(jnp.concatenate([column] * probes, axis=0), (probes * column.shape[0], dofs))
 
 
-def stacked(value):
-    return jnp.concatenate(two_parts(value), axis=0)
-
-
-def take_faces(parts, over_elements, over_dofs):
+def take_faces(fields, over_elements, over_dofs):
     elements = over_elements.shape[0]
-    rows = parts.shape[0] // 2
-    picked = dot(parts, over_dofs)
-    picked = picked[:rows] + picked[rows:]
+    picked = dot(
+        jnp.concatenate(two_parts(fields), axis=1), jnp.concatenate([over_dofs, over_dofs], axis=0)
+    )
     return [
         jnp.sum(jnp.where(over_elements, picked[low : low + elements], 0.0), axis=0, keepdims=True)
-        for low in range(0, rows, elements)
+        for low in range(0, fields.shape[0], elements)
     ]
 
 
-def add_faces(values, over_elements, over_dofs):
+def spread_faces(values, over_elements):
     highs = [value.astype(bf16).astype(f32) for value in values]
     lows = [value - high for value, high in zip(values, highs)]
-    spread = jnp.concatenate(
+    return jnp.concatenate(
         [jnp.where(over_elements, part, 0.0).astype(bf16) for part in highs + lows], axis=0
     )
-    return dot_transposed(spread, over_dofs)
-
-
-def folded(parts):
+
+
+def add_faces(spreads, over_dofs):
+    parts = dot_transposed(jnp.concatenate(spreads, axis=1), over_dofs)
     rows = parts.shape[0] // 2
     return parts[:rows] + parts[rows:]
 
@@ -243,8 +240,7 @@
     stiffness = two_parts(k_ref[...])
     base = times_parts(first_pre, *stiffness) * up
     base_ref[...] = base
-    first_parts = stacked(first_pre)
-    second_parts = stacked(times_parts(base, *smoother) * down)
+    fields = jnp.concatenate([first_pre, times_parts(base, *smoother) * down], axis=0)
     for part_ref, part in zip(part_refs, smoother + stiffness):
         part_ref[...] = part
     second_at, index_at, visc_at = message_places(steps, probes)
@@ -252,12 +248,11 @@
         flat_row = slots_ref[step - 1]
         over_elements = hot_elements(flat_row, elements, dofs)
         over_dofs = hot_ref[:, (step - 1) * width : step * width]
-        first_rows = take_faces(first_parts, over_elements, over_dofs)
-        second_rows = take_faces(second_parts, over_elements, over_dofs)
+        taken = take_faces(fields, over_elements, over_dofs)
         for probe in range(probes):
-            write_row(leave_refs[step - 1], second_at + probe, second_rows[probe])
+            write_row(leave_refs[step - 1], second_at + probe, taken[probes + probe])
             for leave_ref in leave_refs:
-                write_row(leave_ref, (step - 1) * probes + probe, first_rows[probe])
+                write_row(leave_ref, (step - 1) * probes + probe, taken[probe])
         for leave_ref in leave_refs:
             write_row(leave_ref, index_at + step - 1, flat_row.astype(f32))
     visc_line = visc_at * (width // lane_count)
@@ -287,11 +282,10 @@
         ]
 
     own_elements = [hot_elements(slots_ref[step], elements, dofs) for step in range(steps)]
-    own_dofs = [hot_ref[:, step * width : (step + 1) * width] for step in range(steps)]
 
     def placed_here(values):
-        return folded(
-            sum(add_faces(values[i], own_elements[i], own_dofs[i]) for i in range(steps))
+        return add_faces(
+            [spread_faces(values[step], own_elements[step]) for step in range(steps)], hot_ref[...]
         )
 
     up, down = up_ref[...], down_ref[...]
@@ -300,15 +294,18 @@
     image = jnp.where(live, base_ref[...] - coupling * placed, 0.0)
     images, back = [image], []
     for member in range(1, members):
-        total = 0.0
-        for step in range(1, members):
-            flat_row = read_row(message(member), index_at + step - 1, width).astype(jnp.int32)
-            over_elements = hot_elements(flat_row, elements, dofs)
-            over_dofs = hot_dofs(flat_row, dofs)
-            total = total + add_faces(inbound_first(member, step), over_elements, over_dofs)
-            if step == member:
-                back.append((over_elements, over_dofs))
-        images.append(-coupling * folded(total))
+        rows_of = [
+            read_row(message(member), index_at + step, width).astype(jnp.int32)
+            for step in range(steps)
+        ]
+        over_elements = [hot_elements(flat_row, elements, dofs) for flat_row in rows_of]
+        over_dofs = [hot_dofs(flat_row, dofs) for flat_row in rows_of]
+        spreads = [
+            spread_faces(inbound_first(member, step + 1), over_elements[step])
+            for step in range(steps)
+        ]
+        images.append(-coupling * add_faces(spreads, jnp.concatenate(over_dofs, axis=1)))
+        back.append((over_elements[member - 1], over_dofs[member - 1]))
     smooth = times_parts(jnp.concatenate(images, axis=0), p_high_ref[...], p_low_ref[...])
     second_pre = smooth[:rows] * down
     second_ref[...] = second_pre
@@ -319,7 +316,7 @@
         visc = as_column(sent[visc_line : visc_line + 1, :elements])
         scale = wide(1.0 / visc, probes, dofs)
         change = smooth[member * rows : (member + 1) * rows] * scale
-        taken = take_faces(stacked(change), *back[member - 1])
+        taken = take_faces(change, *back[member - 1])
         values.append(
             [taken[probe] + read_row(sent, second_at + probe, width) for probe in range(probes)]
         )
@@ -333,11 +330,10 @@
 def leave_faces(field, probes, slots_ref, leave_ref):
     elements, dofs = field.shape[0] // probes, field.shape[1]
     members = slots_ref.shape[0] + 1
-    parts = stacked(field)
     me = lax.axis_index("gz")
     for shift in range(1, members):
         flat_row = slots_ref[shift - 1]
-        taken = take_faces(parts, hot_elements(flat_row, elements, dofs), hot_dofs(flat_row, dofs))
+        taken = take_faces(field, hot_elements(flat_row, elements, dofs), hot_dofs(flat_row, dofs))
         target = lax.rem(me + shift, members)
         for probe in range(probes):
             leave_ref[target, pl.ds(probe, 1), :] = taken[probe]
@@ -349,16 +345,14 @@
     elements = rows // probes
     members = slots_ref.shape[0] + 1
     me = lax.axis_index("gz")
-    total = jnp.zeros((2 * rows, dofs), f32)
+    total = jnp.zeros(shape, f32)
     for shift in range(1, members):
         flat_row = slots_ref[shift - 1]
         came = came_ref[lax.rem(me + shift, members)]
-        total += add_faces(
-            [came[probe : probe + 1, :] for probe in range(probes)],
-            hot_elements(flat_row, elements, dofs),
-            hot_dofs(flat_row, dofs),
-        )
-    return folded(total)
+        values = [came[probe : probe + 1, :] for probe in range(probes)]
+        spread = spread_faces(values, hot_elements(flat_row, elements, dofs))
+        total += add_faces([spread], hot_dofs(flat_row, dofs))
+    return total
 
 
 def far_first_kernel(*refs):

time: 26.6 us -> 26.5 us (level)
  no operation moved by 1% of the time
where the time goes in v11:
time: 26.5 us; the launch traced here: 26.4 us
  blocking collectives  11.2 us (42%)
  starting transfers between devices  5.68 us (21%)
  Pallas kernels  5.42 us (20%)
  waiting for transfers between devices  3.39 us (13%)
  between operations  0.68 us (3%)
    all_to_all x1, blocking collectives, per_device(): lax.all_to_all(products, ('gx', 'gy', 'gz'), split_axis=0, concat_axis=0)  11.2 us
    ppermute x3, starting transfers between devices, near_steps(): lax.ppermute(leaving[step - 1], 'gz', [(source, source ^ step) for source...  5.68 us
    pallas_call x3, Pallas kernels, call(): pl.pallas_call(kernel, out_shape=out_shapes, in_specs=in_specs, out_specs...  5.42 us
    ppermute x3, waiting for transfers between devices, near_steps(): lax.ppermute(leaving[step - 1], 'gz', [(source, source ^ step) for source...  3.39 us
  transfers between devices with their start and end apart: 3, of which 1 were waited for; matrix products, arithmetic and copies ran while one was open for 0% of the time, Pallas kernels for 0%

profile of v11, /device:TPU:0, one launch (start us, length us, event | category | flops | bytes accessed | tf_op | source)
XLA Modules:
  0.0 26.4 jit_solution(13546073562346733963)
XLA Ops:
  0.0 2.4 %shard_map.73 = (f32[128,256]{1,0:T(8,128)S(1)}, f32[128,256]{1,0:T(8,128)S(1)}, f32[128,256]{1,0:T(8,128)S(1)}, f32[128,256]{1,0:T(8,128)S(1)}, f32[128,256]{1,...) custom-call(s32[1,1,1,16]{3,2,1,0:T(1,128)} %refs_0_.1, ...), custom_call_target="tpu_custom_call" | custom-call | flops 805306368 | bytes 1048576 | tf_op jit(solution)/shard_map/pallas_call | solution.py:422
  2.4 4.1 %collective-permute-start.1 = (f32[48,128]{1,0:T(8,128)S(1)}, f32[48,128]{1,0:T(8,128)S(1)}, u32[]{:S(2)}, u32[]{:S(2)}) collective-permute-start(f32[48,128]{1,0:T(8,128)S(1)} %get-tuple-element.33), channel_id=1, source_target_pairs={{0,2},{1,3},{2,0},{3,1},{4,6},{5,7},{6,4},{7,5},{8,10},{9,11},{10,... | collective-permute-start | bytes 73736 | tf_op jit(solution)/shard_map/ppermute | solution.py:472
  6.5 1.3 %collective-permute-start.2 = (f32[48,128]{1,0:T(8,128)S(1)}, f32[48,128]{1,0:T(8,128)S(1)}, u32[]{:S(2)}, u32[]{:S(2)}) collective-permute-start(f32[48,128]{1,0:T(8,128)S(1)} %get-tuple-element.34), channel_id=1, source_target_pairs={{0,3},{1,2},{2,1},{3,0},{4,7},{5,6},{6,5},{7,4},{8,11},{9,10},{10,... | collective-permute-start | bytes 73736 | tf_op jit(solution)/shard_map/ppermute | solution.py:472
  7.9 0.2 collective-permute-start
  8.8 0.0 collective-permute-done.1.refs_1_
  8.8 3.4 %collective-permute-done.2.refs_2_ = f32[48,128]{1,0:T(8,128)S(1)} collective-permute-done((f32[48,128]{1,0:T(8,128)S(1)}, f32[48,128]{1,0:T(8,128)S(1)}, u32[]{:S(2)}, u32[]{:S(2)}) %collective-permute-start.2) | collective-permute-done | bytes 24608 | tf_op jit(solution)/shard_map/ppermute | solution.py:472
  12.2 0.0 collective-permute-done.refs_0_
  12.2 2.0 %shard_map.74 = (f32[128,256]{1,0:T(8,128)S(1)}, f32[32,1,128]{2,1,0:T(1,128)S(1)}) custom-call(s32[1,1,1]{2,1,0:T(1,128)S(6)} %copy.8.count_ref, f32[128,256]{1,0:T(8,128)S(1)} %get-tuple-element.22.source_ref, f32[128,256]{1,0:T(8,128)S(1)} %get-tuple-element.23.up_ref, f32[128,256]{1,0:T(8,128)S(1)} %get-tuple-element.24.down_ref, ...), custom_call_target="tpu_custom_call" | custom-call | flops 2415919104 | bytes 1048576 | tf_op jit(solution)/shard_map/pallas_call | solution.py:422
  14.2 11.2 %all_to_all.5.parts_ref = f32[32,1,128]{2,1,0:T(1,128)S(1)} all-to-all(f32[32,1,128]{2,1,0:T(1,128)S(1)} %get-tuple-element.36), channel_id=1, replica_groups=mesh['gx'=4,'gy'=2,'gz'=4] {'gx','gy','gz'}, dimensions={0} | all-to-all | bytes 32768 | tf_op jit(solution)/shard_map/all_to_all | solution.py:569
  25.4 1.0 %shard_map.75 = f32[128,256]{1,0:T(8,128)} custom-call(s32[1,1,1]{2,1,0:T(1,128)S(6)} %copy.8.count_ref, f32[128,256]{1,0:T(8,128)S(1)} %get-tuple-element.21.first_ref, f32[128,256]{1,0:T(8,128)S(1)} %get-tuple-element.35.second_ref, f32[32,1,128]{2,1,0:T(1,128)S(1)} %all_to_all.5.parts_ref), custom_call_target="tpu_custom_call" | custom-call | flops 32768 | bytes 1048576 | tf_op jit(solution)/shard_map/pallas_call | solution.py:422
Async XLA Ops:
  2.4 6.3 %collective-permute-start.1 = (f32[48,128]{1,0:T(8,128)S(1)}, f32[48,128]{1,0:T(8,128)S(1)}, u32[]{:S(2)}, u32[]{:S(2)}) collective-permute-start(f32[48,128]{1,0:T(8,128)S(1)} %get-tuple-element.33), channel_id=1, source_target_pairs={{0,2},{1,3},{2,0},{3,1},{4,6},{5,7},{6,4},{7,5},{8,10},{9,11},{10,... | collective-permute-start | bytes 73736 | tf_op jit(solution)/shard_map/ppermute | solution.py:472
  6.5 5.6 %collective-permute-start.2 = (f32[48,128]{1,0:T(8,128)S(1)}, f32[48,128]{1,0:T(8,128)S(1)}, u32[]{:S(2)}, u32[]{:S(2)}) collective-permute-start(f32[48,128]{1,0:T(8,128)S(1)} %get-tuple-element.34), channel_id=1, source_target_pairs={{0,3},{1,2},{2,1},{3,0},{4,7},{5,6},{6,5},{7,4},{8,11},{9,10},{10,... | collective-permute-start | bytes 73736 | tf_op jit(solution)/shard_map/ppermute | solution.py:472
  7.9 4.3 %collective-permute-start = (f32[48,128]{1,0:T(8,128)S(1)}, f32[48,128]{1,0:T(8,128)S(1)}, u32[]{:S(2)}, u32[]{:S(2)}) collective-permute-start(f32[48,128]{1,0:T(8,128)S(1)} %get-tuple-element.32.mine_ref), channel_id=1, source_target_pairs={{0,1},{1,0},{2,3},{3,2},{4,5},{5,4},{6,7},{7,6},{8,9},{9,8},{10,11... | collective-permute-start | bytes 73736 | tf_op jit(solution)/shard_map/ppermute | solution.py:472

commit v12 on v11

--- a/solution.py
+++ b/solution.py
@@ -5,12 +5,14 @@
 from jax import lax
 from jax.experimental import pallas as pl
 from jax.experimental.pallas import tpu as pltpu
+from jax.sharding import Mesh
 from jax.sharding import PartitionSpec as P
 
 coupling = 0.5
 vmem_grant = 48 * 1024 * 1024
 short_group = 4
 lane_count = 128
+fetch_pieces = 4
 f32 = jnp.float32
 bf16 = jnp.bfloat16
 vmem_spec = pl.BlockSpec(memory_space=pltpu.VMEM)
@@ -133,7 +135,25 @@
             lines.append(
                 jnp.sum(product[probe * elements : (probe + 1) * elements], axis=0, keepdims=True)
             )
-    products_ref[...] = jnp.broadcast_to(as_row(lines, products_ref.shape[-1]), products_ref.shape)
+    products_ref[...] = as_row(lines, products_ref.shape[-1])
+
+
+class PieceCopy:
+    def __init__(self, held, here, arrived):
+        rows = here.shape[-2]
+        count = fetch_pieces if rows % (8 * fetch_pieces) == 0 else 1
+        size = rows // count
+        self.copies = []
+        for piece in range(count):
+            place = (slice(None),) * (len(here.shape) - 2) + (pl.ds(piece * size, size),)
+            whole = count == 1
+            source, target = (held, here) if whole else (held.at[place], here.at[place])
+            self.copies.append(pltpu.make_async_copy(source, target, arrived.at[piece]))
+            self.copies[-1].start()
+
+    def wait(self):
+        for copy in self.copies:
+            copy.wait()
 
 
 def live_column(count_ref, elements):
@@ -152,11 +172,8 @@
         *zip(matrices_hbm[1:], matrix_refs[1:]),
     )
     copies = [
-        pltpu.make_async_copy(held, here, arrived.at[place])
-        for place, (held, here) in enumerate(pairs)
+        PieceCopy(held, here, arrived.at[place]) for place, (held, here) in enumerate(pairs)
     ]
-    for copy in copies:
-        copy.start()
     copies[0].wait()
     copies[1].wait()
     slots_ref = refs["slots"]
@@ -441,7 +458,7 @@
         flops,
         *scalars,
         *(pltpu.with_memory_space_constraint(value, pltpu.HBM) for value in fetched),
-        scratch=scratch + [pltpu.SemaphoreType.DMA((len(fetched),))],
+        scratch=scratch + [pltpu.SemaphoreType.DMA((len(fetched), fetch_pieces))],
     )
 
 
@@ -544,6 +561,14 @@
     return first_pre, second_pre, products
 
 
+def all_rows(row, mesh):
+    if mesh.shape["pair"] == 2:
+        row = row + lax.ppermute(row, "pair", [(0, 1), (1, 0)])
+    count = mesh.size // mesh.shape["pair"]
+    copies = jnp.broadcast_to(row[None], (count,) + row.shape)
+    return lax.all_to_all(copies, ("gx", "gy", "gz"), split_axis=0, concat_axis=0)
+
+
 def per_device(mesh, *arguments):
     rhs, face_index = arguments[0], arguments[4]
     probes, elements, dofs = rhs.shape[3:]
@@ -552,7 +577,7 @@
     shapes = (
         jax.ShapeDtypeStruct((probes * elements, dofs), f32),
         jax.ShapeDtypeStruct((members - 1, 1, face_index.shape[-1]), jnp.int32),
-        jax.ShapeDtypeStruct((mesh.size, 1, lanes), f32),
+        jax.ShapeDtypeStruct((1, lanes), f32),
     )
     near = 1 < members <= short_group and elements <= face_index.shape[-1]
     near = near and elements * dofs < 1 << 24
@@ -566,24 +591,29 @@
         arguments[2],
         first_pre,
         second_pre,
-        lax.all_to_all(products, ("gx", "gy", "gz"), split_axis=0, concat_axis=0),
+        all_rows(products, mesh),
     )
     return result.reshape(rhs.shape)
 
 
 def solution(mesh):
+    outer, inner, length = (mesh.shape[axis] for axis in ("gx", "gy", "gz"))
+    pair = 2 if outer % 2 == 0 else 1
+    devices = mesh.devices.reshape(outer // pair, pair, inner, length)
+    split = Mesh(devices, ("gx", "pair", "gy", "gz"))
+    rows = ("gx", "pair")
     return jax.shard_map(
-        functools.partial(per_device, mesh),
-        mesh=mesh,
+        functools.partial(per_device, split),
+        mesh=split,
         in_specs=(
-            P("gx", "gy", "gz", None, None, None),
-            P("gx", "gy", "gz", None),
-            P("gx", "gy", "gz"),
-            P("gx", "gy", "gz", None),
-            P("gx", "gy", "gz", None, None),
+            P(rows, "gy", "gz", None, None, None),
+            P(rows, "gy", "gz", None),
+            P(rows, "gy", "gz"),
+            P(rows, "gy", "gz", None),
+            P(rows, "gy", "gz", None, None),
             P(),
             P(),
         ),
-        out_specs=P("gx", "gy", "gz", None, None, None),
+        out_specs=P(rows, "gy", "gz", None, None, None),
         check_vma=False,
     )

time: 26.5 us -> 29 us (1.094)
  blocking collectives: 11.2 us -> 12.4 us
  waiting for transfers between devices: 3.39 us -> 4.5 us
    all_to_all x1, blocking collectives: 11.2 us -> 12.4 us  [all_rows(): lax.all_to_all(copies, ('gx', 'gy', 'gz'), split_axis=0, concat_axis=0)]
    ppermute x0 -> x1, waiting for transfers between devices: none -> 1.12 us  [all_rows(): row = row + lax.ppermute(row, 'pair', [(0, 1), (1, 0)])]
  transfers between devices with their start and end apart: 3 -> 4, of which waited for: 1 -> 2; matrix products, arithmetic and copies ran while one was open for 0% -> 0% of each run, Pallas kernels for 0% -> 0%
where the time goes in v12:
time: 29 us; the launch traced here: 28.8 us
  blocking collectives  12.4 us (43%)
  starting transfers between devices  5.68 us (20%)
  Pallas kernels  5.6 us (19%)
  waiting for transfers between devices  4.5 us (16%)
  between operations  0.68 us (2%)
    all_to_all x1, blocking collectives, all_rows(): lax.all_to_all(copies, ('gx', 'gy', 'gz'), split_axis=0, concat_axis=0)  12.4 us
    ppermute x3, starting transfers between devices, near_steps(): lax.ppermute(leaving[step - 1], 'gz', [(source, source ^ step) for source...  5.68 us
    pallas_call x3, Pallas kernels, call(): pl.pallas_call(kernel, out_shape=out_shapes, in_specs=in_specs, out_specs...  5.6 us
    ppermute x3, waiting for transfers between devices, near_steps(): lax.ppermute(leaving[step - 1], 'gz', [(source, source ^ step) for source...  3.39 us
    ppermute x1, waiting for transfers between devices, all_rows(): row = row + lax.ppermute(row, 'pair', [(0, 1), (1, 0)])  1.12 us
  transfers between devices with their start and end apart: 4, of which 2 were waited for; matrix products, arithmetic and copies ran while one was open for 0% of the time, Pallas kernels for 0%

profile of v12, /device:TPU:0, one launch (start us, length us, event | category | flops | bytes accessed | tf_op | source)
XLA Modules:
  0.0 28.8 jit_solution(13481706077448820755)
XLA Ops:
  0.0 2.6 %shard_map.73 = (f32[128,256]{1,0:T(8,128)S(1)}, f32[128,256]{1,0:T(8,128)S(1)}, f32[128,256]{1,0:T(8,128)S(1)}, f32[128,256]{1,0:T(8,128)S(1)}, f32[128,256]{1,...) custom-call(s32[1,1,1,16]{3,2,1,0:T(1,128)} %refs_0_.1, ...), custom_call_target="tpu_custom_call" | custom-call | flops 805306368 | bytes 1048576 | tf_op jit(solution)/shard_map/pallas_call | solution.py:439
  2.6 4.1 %collective-permute-start.1 = (f32[48,128]{1,0:T(8,128)S(1)}, f32[48,128]{1,0:T(8,128)S(1)}, u32[]{:S(2)}, u32[]{:S(2)}) collective-permute-start(f32[48,128]{1,0:T(8,128)S(1)} %get-tuple-element.33), channel_id=1, source_target_pairs={{0,2},{1,3},{2,0},{3,1},{4,6},{5,7},{6,4},{7,5},{8,10},{9,11},{10,... | collective-permute-start | bytes 73736 | tf_op jit(solution)/shard_map/ppermute | solution.py:489
  6.7 1.4 %collective-permute-start.2 = (f32[48,128]{1,0:T(8,128)S(1)}, f32[48,128]{1,0:T(8,128)S(1)}, u32[]{:S(2)}, u32[]{:S(2)}) collective-permute-start(f32[48,128]{1,0:T(8,128)S(1)} %get-tuple-element.34), channel_id=1, source_target_pairs={{0,3},{1,2},{2,1},{3,0},{4,7},{5,6},{6,5},{7,4},{8,11},{9,10},{10,... | collective-permute-start | bytes 73736 | tf_op jit(solution)/shard_map/ppermute | solution.py:489
  8.1 0.2 collective-permute-start
  8.9 0.0 collective-permute-done.1.refs_1_
  9.0 3.4 %collective-permute-done.2.refs_2_ = f32[48,128]{1,0:T(8,128)S(1)} collective-permute-done((f32[48,128]{1,0:T(8,128)S(1)}, f32[48,128]{1,0:T(8,128)S(1)}, u32[]{:S(2)}, u32[]{:S(2)}) %collective-permute-start.2) | collective-permute-done | bytes 24608 | tf_op jit(solution)/shard_map/ppermute | solution.py:489
  12.3 0.0 collective-permute-done.refs_0_
  12.3 2.1 %shard_map.74 = (f32[128,256]{1,0:T(8,128)S(1)}, f32[1,128]{1,0:T(1,128)S(1)}) custom-call(s32[1,1,1]{2,1,0:T(1,128)S(6)} %copy.8.count_ref, f32[128,256]{1,0:T(8,128)S(1)} %get-tuple-element.22.source_ref, f32[128,256]{1,0:T(8,128)S(1)} %get-tuple-element.23.up_ref, f32[128,256]{1,0:T(8,128)S(1)} %get-tuple-element.24.down_ref, ...), custom_call_target="tpu_custom_call" | custom-call | flops 2415919104 | bytes 1048576 | tf_op jit(solution)/shard_map/pallas_call | solution.py:439
  14.4 0.0 collective-permute-start.3
  14.4 1.1 %collective-permute-done.3 = f32[1,128]{1,0:T(1,128)S(1)} collective-permute-done((f32[1,128]{1,0:T(1,128)S(1)}, f32[1,128]{1,0:T(1,128)S(1)}, u32[]{:S(2)}, u32[]{:S(2)}) %collective-permute-start.3) | collective-permute-done | bytes 544 | tf_op jit(solution)/shard_map/ppermute | solution.py:566
  15.5 12.4 %all_to_all.5.parts_ref = f32[16,1,128]{2,1,0:T(1,128)S(1)} all-to-all(f32[16,1,128]{2,1,0:T(1,128)S(1)} %broadcast_in_dim.9), channel_id=1, replica_groups=mesh['gx'=2,'pair'=2,'gy'=2,'gz'=4] {'gx','gy','gz'}, dimensions={0} | all-to-all | bytes 16384 | tf_op jit(solution)/shard_map/all_to_all | solution.py:569
  27.9 0.9 %shard_map.75 = f32[128,256]{1,0:T(8,128)} custom-call(s32[1,1,1]{2,1,0:T(1,128)S(6)} %copy.8.count_ref, f32[128,256]{1,0:T(8,128)S(1)} %get-tuple-element.21.first_ref, f32[128,256]{1,0:T(8,128)S(1)} %get-tuple-element.35.second_ref, f32[16,1,128]{2,1,0:T(1,128)S(1)} %all_to_all.5.parts_ref), custom_call_target="tpu_custom_call" | custom-call | flops 32768 | bytes 1048576 | tf_op jit(solution)/shard_map/pallas_call | solution.py:439
  (2 shorter events, 0.0 us)
Async XLA Ops:
  2.6 6.3 %collective-permute-start.1 = (f32[48,128]{1,0:T(8,128)S(1)}, f32[48,128]{1,0:T(8,128)S(1)}, u32[]{:S(2)}, u32[]{:S(2)}) collective-permute-start(f32[48,128]{1,0:T(8,128)S(1)} %get-tuple-element.33), channel_id=1, source_target_pairs={{0,2},{1,3},{2,0},{3,1},{4,6},{5,7},{6,4},{7,5},{8,10},{9,11},{10,... | collective-permute-start | bytes 73736 | tf_op jit(solution)/shard_map/ppermute | solution.py:489
  6.7 5.6 %collective-permute-start.2 = (f32[48,128]{1,0:T(8,128)S(1)}, f32[48,128]{1,0:T(8,128)S(1)}, u32[]{:S(2)}, u32[]{:S(2)}) collective-permute-start(f32[48,128]{1,0:T(8,128)S(1)} %get-tuple-element.34), channel_id=1, source_target_pairs={{0,3},{1,2},{2,1},{3,0},{4,7},{5,6},{6,5},{7,4},{8,11},{9,10},{10,... | collective-permute-start | bytes 73736 | tf_op jit(solution)/shard_map/ppermute | solution.py:489
  8.1 4.3 %collective-permute-start = (f32[48,128]{1,0:T(8,128)S(1)}, f32[48,128]{1,0:T(8,128)S(1)}, u32[]{:S(2)}, u32[]{:S(2)}) collective-permute-start(f32[48,128]{1,0:T(8,128)S(1)} %get-tuple-element.32.mine_ref), channel_id=1, source_target_pairs={{0,1},{1,0},{2,3},{3,2},{4,5},{5,4},{6,7},{7,6},{8,9},{9,8},{10,11... | collective-permute-start | bytes 73736 | tf_op jit(solution)/shard_map/ppermute | solution.py:489
  14.4 1.1 %collective-permute-start.3 = (f32[1,128]{1,0:T(1,128)S(1)}, f32[1,128]{1,0:T(1,128)S(1)}, u32[]{:S(2)}, u32[]{:S(2)}) collective-permute-start(f32[1,128]{1,0:T(1,128)S(1)} %get-tuple-element.36), channel_id=1, source_target_pairs={{0,8},{8,0},{1,9},{9,1},{2,10},{10,2},{3,11},{11,3},{4,12},{12,4},... | collective-permute-start | bytes 1544 | tf_op jit(solution)/shard_map/ppermute | solution.py:566

commit v13 on v11

--- a/solution.py
+++ b/solution.py
@@ -43,6 +43,14 @@
     )
 
 
+def times_parts_once(rows, mat_high, mat_low):
+    row_high = rows.astype(bf16)
+    return dot(
+        jnp.concatenate([row_high, row_high], axis=1),
+        jnp.concatenate([mat_high, mat_low], axis=0),
+    )
+
+
 def split_index(index, dofs):
     if dofs & (dofs - 1) == 0:
         return lax.shift_right_arithmetic(index, dofs.bit_length() - 1), index & (dofs - 1)
@@ -83,27 +91,33 @@
     return jnp.broadcast_to(jnp.concatenate([column] * probes, axis=0), (probes * column.shape[0], dofs))
 
 
-def take_faces(fields, over_elements, over_dofs):
+def take_faces(parts, over_elements, over_dofs):
     elements = over_elements.shape[0]
     picked = dot(
-        jnp.concatenate(two_parts(fields), axis=1), jnp.concatenate([over_dofs, over_dofs], axis=0)
+        jnp.concatenate(parts, axis=1), jnp.concatenate([over_dofs] * len(parts), axis=0)
     )
     return [
         jnp.sum(jnp.where(over_elements, picked[low : low + elements], 0.0), axis=0, keepdims=True)
-        for low in range(0, fields.shape[0], elements)
+        for low in range(0, picked.shape[0], elements)
     ]
 
 
 def spread_faces(values, over_elements):
+    return jnp.concatenate(
+        [jnp.where(over_elements, value, 0.0).astype(bf16) for value in values], axis=0
+    )
+
+
+def high_low(values):
     highs = [value.astype(bf16).astype(f32) for value in values]
-    lows = [value - high for value, high in zip(values, highs)]
-    return jnp.concatenate(
-        [jnp.where(over_elements, part, 0.0).astype(bf16) for part in highs + lows], axis=0
-    )
+    return highs + [value - high for value, high in zip(values, highs)]
 
 
 def add_faces(spreads, over_dofs):
-    parts = dot_transposed(jnp.concatenate(spreads, axis=1), over_dofs)
+    return dot_transposed(jnp.concatenate(spreads, axis=1), over_dofs)
+
+
+def folded(parts):
     rows = parts.shape[0] // 2
     return parts[:rows] + parts[rows:]
 
@@ -240,7 +254,8 @@
     stiffness = two_parts(k_ref[...])
     base = times_parts(first_pre, *stiffness) * up
     base_ref[...] = base
-    fields = jnp.concatenate([first_pre, times_parts(base, *smoother) * down], axis=0)
+    first_parts = two_parts(first_pre)
+    second_parts = [(times_parts_once(base, *smoother) * down).astype(bf16)]
     for part_ref, part in zip(part_refs, smoother + stiffness):
         part_ref[...] = part
     second_at, index_at, visc_at = message_places(steps, probes)
@@ -248,11 +263,12 @@
         flat_row = slots_ref[step - 1]
         over_elements = hot_elements(flat_row, elements, dofs)
         over_dofs = hot_ref[:, (step - 1) * width : step * width]
-        taken = take_faces(fields, over_elements, over_dofs)
+        first_rows = take_faces(first_parts, over_elements, over_dofs)
+        second_rows = take_faces(second_parts, over_elements, over_dofs)
         for probe in range(probes):
-            write_row(leave_refs[step - 1], second_at + probe, taken[probes + probe])
+            write_row(leave_refs[step - 1], second_at + probe, second_rows[probe])
             for leave_ref in leave_refs:
-                write_row(leave_ref, (step - 1) * probes + probe, taken[probe])
+                write_row(leave_ref, (step - 1) * probes + probe, first_rows[probe])
         for leave_ref in leave_refs:
             write_row(leave_ref, index_at + step - 1, flat_row.astype(f32))
     visc_line = visc_at * (width // lane_count)
@@ -284,15 +300,14 @@
     own_elements = [hot_elements(slots_ref[step], elements, dofs) for step in range(steps)]
 
     def placed_here(values):
-        return add_faces(
-            [spread_faces(values[step], own_elements[step]) for step in range(steps)], hot_ref[...]
-        )
+        spreads = [spread_faces(values[step], own_elements[step]) for step in range(steps)]
+        return add_faces(spreads, hot_ref[...])
 
     up, down = up_ref[...], down_ref[...]
     live = wide(live_column(count_ref, elements).astype(f32), probes, dofs) > 0.0
-    placed = placed_here([inbound_first(0, step) for step in range(1, members)])
+    placed = folded(placed_here([high_low(inbound_first(0, step)) for step in range(1, members)]))
     image = jnp.where(live, base_ref[...] - coupling * placed, 0.0)
-    images, back = [image], []
+    changes, back = [], []
     for member in range(1, members):
         rows_of = [
             read_row(message(member), index_at + step, width).astype(jnp.int32)
@@ -304,10 +319,10 @@
             spread_faces(inbound_first(member, step + 1), over_elements[step])
             for step in range(steps)
         ]
-        images.append(-coupling * add_faces(spreads, jnp.concatenate(over_dofs, axis=1)))
+        changes.append(-coupling * add_faces(spreads, jnp.concatenate(over_dofs, axis=1)))
         back.append((over_elements[member - 1], over_dofs[member - 1]))
-    smooth = times_parts(jnp.concatenate(images, axis=0), p_high_ref[...], p_low_ref[...])
-    second_pre = smooth[:rows] * down
+    second_pre = times_parts(image, p_high_ref[...], p_low_ref[...]) * down
+    changes = times_parts_once(jnp.concatenate(changes, axis=0), p_high_ref[...], p_low_ref[...])
     second_ref[...] = second_pre
     values = []
     visc_line = visc_at * (width // lane_count)
@@ -315,13 +330,14 @@
         sent = message(member)
         visc = as_column(sent[visc_line : visc_line + 1, :elements])
         scale = wide(1.0 / visc, probes, dofs)
-        change = smooth[member * rows : (member + 1) * rows] * scale
-        taken = take_faces(change, *back[member - 1])
+        change = changes[(member - 1) * rows : member * rows] * scale
+        taken = take_faces([change.astype(bf16)], *back[member - 1])
         values.append(
             [taken[probe] + read_row(sent, second_at + probe, width) for probe in range(probes)]
         )
     placed = placed_here(values)
-    second_img = times_parts(second_pre, k_high_ref[...], k_low_ref[...]) * up - coupling * placed
+    second_img = times_parts_once(second_pre, k_high_ref[...], k_low_ref[...])
+    second_img = second_img * up - coupling * placed
     second_img = jnp.where(live, second_img, 0.0)
     source = jnp.where(live, source_ref[...], 0.0)
     inner_products(image, second_img, source, probes, products_ref)
@@ -333,7 +349,8 @@
     me = lax.axis_index("gz")
     for shift in range(1, members):
         flat_row = slots_ref[shift - 1]
-        taken = take_faces(field, hot_elements(flat_row, elements, dofs), hot_dofs(flat_row, dofs))
+        over_elements = hot_elements(flat_row, elements, dofs)
+        taken = take_faces(two_parts(field), over_elements, hot_dofs(flat_row, dofs))
         target = lax.rem(me + shift, members)
         for probe in range(probes):
             leave_ref[target, pl.ds(probe, 1), :] = taken[probe]
@@ -350,8 +367,8 @@
         flat_row = slots_ref[shift - 1]
         came = came_ref[lax.rem(me + shift, members)]
         values = [came[probe : probe + 1, :] for probe in range(probes)]
-        spread = spread_faces(values, hot_elements(flat_row, elements, dofs))
-        total += add_faces([spread], hot_dofs(flat_row, dofs))
+        spread = spread_faces(high_low(values), hot_elements(flat_row, elements, dofs))
+        total += folded(add_faces([spread], hot_dofs(flat_row, dofs)))
     return total
 
 

time: 26.5 us -> 26.3 us (level)
  Pallas kernels: 5.42 us -> 5.14 us
    pallas_call x3, Pallas kernels: 5.42 us -> 5.14 us  [call(): pl.pallas_call(kernel, out_shape=out_shapes, in_specs=in_specs, out_specs...]
where the time goes in v13:
time: 26.3 us; the launch traced here: 26.1 us
  blocking collectives  11.2 us (43%)
  starting transfers between devices  5.68 us (22%)
  Pallas kernels  5.14 us (20%)
  waiting for transfers between devices  3.39 us (13%)
  between operations  0.68 us (3%)
    all_to_all x1, blocking collectives, per_device(): lax.all_to_all(products, ('gx', 'gy', 'gz'), split_axis=0, concat_axis=0)  11.2 us
    ppermute x3, starting transfers between devices, near_steps(): lax.ppermute(leaving[step - 1], 'gz', [(source, source ^ step) for source...  5.68 us
    pallas_call x3, Pallas kernels, call(): pl.pallas_call(kernel, out_shape=out_shapes, in_specs=in_specs, out_specs...  5.14 us
    ppermute x3, waiting for transfers between devices, near_steps(): lax.ppermute(leaving[step - 1], 'gz', [(source, source ^ step) for source...  3.39 us
  transfers between devices with their start and end apart: 3, of which 1 were waited for; matrix products, arithmetic and copies ran while one was open for 0% of the time, Pallas kernels for 0%

profile of v13, /device:TPU:0, one launch (start us, length us, event | category | flops | bytes accessed | tf_op | source)
XLA Modules:
  0.0 26.1 jit_solution(10171952292478712923)
XLA Ops:
  0.0 2.2 %shard_map.73 = (f32[128,256]{1,0:T(8,128)S(1)}, f32[128,256]{1,0:T(8,128)S(1)}, f32[128,256]{1,0:T(8,128)S(1)}, f32[128,256]{1,0:T(8,128)S(1)}, f32[128,256]{1,...) custom-call(s32[1,1,1,16]{3,2,1,0:T(1,128)} %refs_0_.1, ...), custom_call_target="tpu_custom_call" | custom-call | flops 805306368 | bytes 1048576 | tf_op jit(solution)/shard_map/pallas_call | solution.py:439
  2.2 4.1 %collective-permute-start.1 = (f32[48,128]{1,0:T(8,128)S(1)}, f32[48,128]{1,0:T(8,128)S(1)}, u32[]{:S(2)}, u32[]{:S(2)}) collective-permute-start(f32[48,128]{1,0:T(8,128)S(1)} %get-tuple-element.33), channel_id=1, source_target_pairs={{0,2},{1,3},{2,0},{3,1},{4,6},{5,7},{6,4},{7,5},{8,10},{9,11},{10,... | collective-permute-start | bytes 73736 | tf_op jit(solution)/shard_map/ppermute | solution.py:489
  6.3 1.3 %collective-permute-start.2 = (f32[48,128]{1,0:T(8,128)S(1)}, f32[48,128]{1,0:T(8,128)S(1)}, u32[]{:S(2)}, u32[]{:S(2)}) collective-permute-start(f32[48,128]{1,0:T(8,128)S(1)} %get-tuple-element.34), channel_id=1, source_target_pairs={{0,3},{1,2},{2,1},{3,0},{4,7},{5,6},{6,5},{7,4},{8,11},{9,10},{10,... | collective-permute-start | bytes 73736 | tf_op jit(solution)/shard_map/ppermute | solution.py:489
  7.7 0.2 collective-permute-start
  8.5 0.0 collective-permute-done.1.refs_1_
  8.6 3.4 %collective-permute-done.2.refs_2_ = f32[48,128]{1,0:T(8,128)S(1)} collective-permute-done((f32[48,128]{1,0:T(8,128)S(1)}, f32[48,128]{1,0:T(8,128)S(1)}, u32[]{:S(2)}, u32[]{:S(2)}) %collective-permute-start.2) | collective-permute-done | bytes 24608 | tf_op jit(solution)/shard_map/ppermute | solution.py:489
  11.9 0.0 collective-permute-done.refs_0_
  11.9 2.0 %shard_map.74 = (f32[128,256]{1,0:T(8,128)S(1)}, f32[32,1,128]{2,1,0:T(1,128)S(1)}) custom-call(s32[1,1,1]{2,1,0:T(1,128)S(6)} %copy.8.count_ref, f32[128,256]{1,0:T(8,128)S(1)} %get-tuple-element.22.source_ref, f32[128,256]{1,0:T(8,128)S(1)} %get-tuple-element.23.up_ref, f32[128,256]{1,0:T(8,128)S(1)} %get-tuple-element.24.down_ref, ...), custom_call_target="tpu_custom_call" | custom-call | flops 2415919104 | bytes 1048576 | tf_op jit(solution)/shard_map/pallas_call | solution.py:439
  13.9 11.2 %all_to_all.5.parts_ref = f32[32,1,128]{2,1,0:T(1,128)S(1)} all-to-all(f32[32,1,128]{2,1,0:T(1,128)S(1)} %get-tuple-element.36), channel_id=1, replica_groups=mesh['gx'=4,'gy'=2,'gz'=4] {'gx','gy','gz'}, dimensions={0} | all-to-all | bytes 32768 | tf_op jit(solution)/shard_map/all_to_all | solution.py:586
  25.1 1.0 %shard_map.75 = f32[128,256]{1,0:T(8,128)} custom-call(s32[1,1,1]{2,1,0:T(1,128)S(6)} %copy.8.count_ref, f32[128,256]{1,0:T(8,128)S(1)} %get-tuple-element.21.first_ref, f32[128,256]{1,0:T(8,128)S(1)} %get-tuple-element.35.second_ref, f32[32,1,128]{2,1,0:T(1,128)S(1)} %all_to_all.5.parts_ref), custom_call_target="tpu_custom_call" | custom-call | flops 32768 | bytes 1048576 | tf_op jit(solution)/shard_map/pallas_call | solution.py:439
Async XLA Ops:
  2.2 6.3 %collective-permute-start.1 = (f32[48,128]{1,0:T(8,128)S(1)}, f32[48,128]{1,0:T(8,128)S(1)}, u32[]{:S(2)}, u32[]{:S(2)}) collective-permute-start(f32[48,128]{1,0:T(8,128)S(1)} %get-tuple-element.33), channel_id=1, source_target_pairs={{0,2},{1,3},{2,0},{3,1},{4,6},{5,7},{6,4},{7,5},{8,10},{9,11},{10,... | collective-permute-start | bytes 73736 | tf_op jit(solution)/shard_map/ppermute | solution.py:489
  6.3 5.6 %collective-permute-start.2 = (f32[48,128]{1,0:T(8,128)S(1)}, f32[48,128]{1,0:T(8,128)S(1)}, u32[]{:S(2)}, u32[]{:S(2)}) collective-permute-start(f32[48,128]{1,0:T(8,128)S(1)} %get-tuple-element.34), channel_id=1, source_target_pairs={{0,3},{1,2},{2,1},{3,0},{4,7},{5,6},{6,5},{7,4},{8,11},{9,10},{10,... | collective-permute-start | bytes 73736 | tf_op jit(solution)/shard_map/ppermute | solution.py:489
  7.7 4.3 %collective-permute-start = (f32[48,128]{1,0:T(8,128)S(1)}, f32[48,128]{1,0:T(8,128)S(1)}, u32[]{:S(2)}, u32[]{:S(2)}) collective-permute-start(f32[48,128]{1,0:T(8,128)S(1)} %get-tuple-element.32.mine_ref), channel_id=1, source_target_pairs={{0,1},{1,0},{2,3},{3,2},{4,5},{5,4},{6,7},{7,6},{8,9},{9,8},{10,11... | collective-permute-start | bytes 73736 | tf_op jit(solution)/shard_map/ppermute | solution.py:489

commit v14 on v13

--- a/solution.py
+++ b/solution.py
@@ -27,10 +27,6 @@
     return jnp.dot(left, right, preferred_element_type=f32)
 
 
-def dot_transposed(left, right):
-    return lax.dot_general(left, right, (((1,), (1,)), ((), ())), preferred_element_type=f32)
-
-
 def times_matrix(rows, matrix):
     return times_parts(rows, *two_parts(matrix))
 
@@ -79,6 +75,19 @@
     return jnp.where(hit, jnp.ones(shape, bf16), jnp.zeros(shape, bf16))
 
 
+def hot_rows(flat_rows, dofs):
+    shape = (flat_rows[0].shape[1], dofs)
+    spare = [jnp.zeros((8 - len(flat_rows) % 8, shape[0]), jnp.int32)]
+    _, dof = split_index(jnp.concatenate(flat_rows + spare, axis=0), dofs)
+    columns = jnp.transpose(dof.astype(f32)).astype(jnp.int32)
+    lane = lax.broadcasted_iota(jnp.int32, shape, 1).astype(jnp.int16)
+    hits = []
+    for slot in range(len(flat_rows)):
+        column = jnp.broadcast_to(columns[:, slot : slot + 1], shape).astype(jnp.int16)
+        hits.append(jnp.where(lane == column, jnp.ones(shape, bf16), jnp.zeros(shape, bf16)))
+    return jnp.concatenate(hits, axis=0)
+
+
 def as_column(row):
     elements = row.shape[1]
     line = lax.broadcasted_iota(jnp.int32, (elements, elements), 0)
@@ -114,7 +123,7 @@
 
 
 def add_faces(spreads, over_dofs):
-    return dot_transposed(jnp.concatenate(spreads, axis=1), over_dofs)
+    return dot(jnp.concatenate(spreads, axis=1), over_dofs)
 
 
 def folded(parts):
@@ -154,7 +163,7 @@
     return lax.broadcasted_iota(jnp.int32, (elements, 1), 0) < count_ref[0, 0, 0]
 
 
-def begin(refs, partner, count_ref, prepare):
+def begin(refs, partner, count_ref):
     links_hbm, index_hbm, visc_hbm, rhs_hbm, *matrices_hbm = refs["operands"]
     links_ref, index_ref, visc_ref, rhs_ref, *matrix_refs, arrived = refs["scratch"]
     pairs = (
@@ -177,7 +186,6 @@
     me = lax.axis_index("gz")
     for step in range(1, slots_ref.shape[0] + 1):
         slots_ref[step - 1] = slot_of(partner(me, step), links_ref, index_ref)
-    prepare()
     copies[4].wait()
     probes, elements, dofs = rhs_ref.shape[3:]
     live = jnp.ones((elements, 1), f32)
@@ -226,17 +234,12 @@
 
 def near_first_kernel(*refs):
     operands, refs = refs[:6], refs[6:]
-    first_ref, source_ref, up_ref, down_ref, base_ref, slots_ref, hot_ref = refs[:7]
-    part_refs, refs = refs[7:11], refs[11:]
+    first_ref, source_ref, up_ref, down_ref, base_ref, slots_ref = refs[:6]
+    part_refs, refs = refs[6:10], refs[10:]
     steps, _, width = slots_ref.shape
     leave_refs, scratch = refs[:steps], refs[steps:]
     visc_ref, rhs_ref, _, k_ref = scratch[2:6]
     probes, elements, dofs = rhs_ref.shape[3:]
-
-    def prepare():
-        for step in range(steps):
-            hot_ref[:, step * width : (step + 1) * width] = hot_dofs(slots_ref[step], dofs)
-
     first_pre, up, down, smoother = begin(
         {
             "operands": operands,
@@ -249,7 +252,6 @@
         },
         lambda me, step: me ^ step,
         None,
-        prepare,
     )
     stiffness = two_parts(k_ref[...])
     base = times_parts(first_pre, *stiffness) * up
@@ -262,7 +264,7 @@
     for step in range(1, steps + 1):
         flat_row = slots_ref[step - 1]
         over_elements = hot_elements(flat_row, elements, dofs)
-        over_dofs = hot_ref[:, (step - 1) * width : step * width]
+        over_dofs = hot_dofs(flat_row, dofs)
         first_rows = take_faces(first_parts, over_elements, over_dofs)
         second_rows = take_faces(second_parts, over_elements, over_dofs)
         for probe in range(probes):
@@ -277,7 +279,7 @@
 
 
 def near_second_kernel(
-    probes, count_ref, source_ref, up_ref, down_ref, base_ref, slots_ref, hot_ref,
+    probes, count_ref, source_ref, up_ref, down_ref, base_ref, slots_ref,
     p_high_ref, p_low_ref, k_high_ref, k_low_ref, mine_ref, *refs
 ):
     came_refs = refs[:-2]
@@ -297,11 +299,13 @@
             read_row(sent, (step - 1) * probes + probe, width) for probe in range(probes)
         ]
 
-    own_elements = [hot_elements(slots_ref[step], elements, dofs) for step in range(steps)]
+    own_rows = [slots_ref[step] for step in range(steps)]
+    own_elements = [hot_elements(flat_row, elements, dofs) for flat_row in own_rows]
+    own_dofs = hot_rows(own_rows, dofs)
 
     def placed_here(values):
         spreads = [spread_faces(values[step], own_elements[step]) for step in range(steps)]
-        return add_faces(spreads, hot_ref[...])
+        return add_faces(spreads, own_dofs)
 
     up, down = up_ref[...], down_ref[...]
     live = wide(live_column(count_ref, elements).astype(f32), probes, dofs) > 0.0
@@ -314,13 +318,12 @@
             for step in range(steps)
         ]
         over_elements = [hot_elements(flat_row, elements, dofs) for flat_row in rows_of]
-        over_dofs = [hot_dofs(flat_row, dofs) for flat_row in rows_of]
         spreads = [
             spread_faces(inbound_first(member, step + 1), over_elements[step])
             for step in range(steps)
         ]
-        changes.append(-coupling * add_faces(spreads, jnp.concatenate(over_dofs, axis=1)))
-        back.append((over_elements[member - 1], over_dofs[member - 1]))
+        changes.append(-coupling * add_faces(spreads, hot_rows(rows_of, dofs)))
+        back.append((over_elements[member - 1], hot_dofs(rows_of[member - 1], dofs)))
     second_pre = times_parts(image, p_high_ref[...], p_low_ref[...]) * down
     changes = times_parts_once(jnp.concatenate(changes, axis=0), p_high_ref[...], p_low_ref[...])
     second_ref[...] = second_pre
@@ -368,7 +371,7 @@
         came = came_ref[lax.rem(me + shift, members)]
         values = [came[probe : probe + 1, :] for probe in range(probes)]
         spread = spread_faces(high_low(values), hot_elements(flat_row, elements, dofs))
-        total += folded(add_faces([spread], hot_dofs(flat_row, dofs)))
+        total += folded(add_faces([spread], hot_rows([flat_row], dofs)))
     return total
 
 
@@ -389,7 +392,6 @@
         },
         lambda me, step: lax.rem(me + step, members),
         count_ref,
-        lambda: None,
     )
     leave_faces(first_pre, leave_ref.shape[1], slots_ref, leave_ref)
 
@@ -469,12 +471,11 @@
     steps, _, width = slots_shape.shape
     probes = rhs.shape[3]
     flops = 8 * rows * dofs * steps * width
-    hot = jax.ShapeDtypeStruct((dofs, steps * width), bf16)
     message = jax.ShapeDtypeStruct((message_length(steps, probes, width), lane_count), f32)
     part = jax.ShapeDtypeStruct(p_matrix.shape, bf16)
-    first_pre, source, up, down, base, slots, hot_own, *rest = begin_call(
+    first_pre, source, up, down, base, slots, *rest = begin_call(
         near_first_kernel,
-        [field] * 5 + [slots_shape, hot] + [part] * 4 + [message] * steps,
+        [field] * 5 + [slots_shape] + [part] * 4 + [message] * steps,
         2 * flops,
         (),
         neighbours,
@@ -493,7 +494,7 @@
     ]
     second_pre, products = call(
         functools.partial(near_second_kernel, probes),
-        [smem_spec] + [vmem_spec] * (11 + steps),
+        [smem_spec] + [vmem_spec] * (10 + steps),
         [field, products_shape],
         6 * flops,
         counts,
@@ -502,7 +503,6 @@
         down,
         base,
         slots,
-        hot_own,
         *parts,
         leaving[0],
         *came,

time: 26.3 us -> 26.5 us (level)
  no operation moved by 1% of the time
where the time goes in v14:
time: 26.5 us; the launch traced here: 26.3 us
  blocking collectives  11.2 us (42%)
  starting transfers between devices  5.68 us (21%)
  Pallas kernels  5.39 us (20%)
  waiting for transfers between devices  3.39 us (13%)
  between operations  0.68 us (3%)
    all_to_all x1, blocking collectives, per_device(): lax.all_to_all(products, ('gx', 'gy', 'gz'), split_axis=0, concat_axis=0)  11.2 us
    ppermute x3, starting transfers between devices, near_steps(): lax.ppermute(leaving[step - 1], 'gz', [(source, source ^ step) for source...  5.68 us
    pallas_call x3, Pallas kernels, call(): pl.pallas_call(kernel, out_shape=out_shapes, in_specs=in_specs, out_specs...  5.39 us
    ppermute x3, waiting for transfers between devices, near_steps(): lax.ppermute(leaving[step - 1], 'gz', [(source, source ^ step) for source...  3.39 us
  transfers between devices with their start and end apart: 3, of which 1 were waited for; matrix products, arithmetic and copies ran while one was open for 0% of the time, Pallas kernels for 0%

profile of v14, /device:TPU:0, one launch (start us, length us, event | category | flops | bytes accessed | tf_op | source)
XLA Modules:
  0.0 26.3 jit_solution(932472904345102742)
XLA Ops:
  0.0 2.2 %shard_map.73 = (f32[128,256]{1,0:T(8,128)S(1)}, f32[128,256]{1,0:T(8,128)S(1)}, f32[128,256]{1,0:T(8,128)S(1)}, f32[128,256]{1,0:T(8,128)S(1)}, f32[128,256]{1,...) custom-call(s32[1,1,1,16]{3,2,1,0:T(1,128)} %refs_0_.1, ...), custom_call_target="tpu_custom_call" | custom-call | flops 805306368 | bytes 1048576 | tf_op jit(solution)/shard_map/pallas_call | solution.py:441
  2.2 4.1 %collective-permute-start.1 = (f32[48,128]{1,0:T(8,128)S(1)}, f32[48,128]{1,0:T(8,128)S(1)}, u32[]{:S(2)}, u32[]{:S(2)}) collective-permute-start(f32[48,128]{1,0:T(8,128)S(1)} %get-tuple-element.31), channel_id=1, source_target_pairs={{0,2},{1,3},{2,0},{3,1},{4,6},{5,7},{6,4},{7,5},{8,10},{9,11},{10,... | collective-permute-start | bytes 73736 | tf_op jit(solution)/shard_map/ppermute | solution.py:490
  6.3 1.3 %collective-permute-start.2 = (f32[48,128]{1,0:T(8,128)S(1)}, f32[48,128]{1,0:T(8,128)S(1)}, u32[]{:S(2)}, u32[]{:S(2)}) collective-permute-start(f32[48,128]{1,0:T(8,128)S(1)} %get-tuple-element.32), channel_id=1, source_target_pairs={{0,3},{1,2},{2,1},{3,0},{4,7},{5,6},{6,5},{7,4},{8,11},{9,10},{10,... | collective-permute-start | bytes 73736 | tf_op jit(solution)/shard_map/ppermute | solution.py:490
  7.6 0.2 collective-permute-start
  8.5 0.0 collective-permute-done.1.refs_1_
  8.5 3.4 %collective-permute-done.2.refs_2_ = f32[48,128]{1,0:T(8,128)S(1)} collective-permute-done((f32[48,128]{1,0:T(8,128)S(1)}, f32[48,128]{1,0:T(8,128)S(1)}, u32[]{:S(2)}, u32[]{:S(2)}) %collective-permute-start.2) | collective-permute-done | bytes 24608 | tf_op jit(solution)/shard_map/ppermute | solution.py:490
  11.9 0.0 collective-permute-done.refs_0_
  11.9 2.3 %shard_map.74 = (f32[128,256]{1,0:T(8,128)S(1)}, f32[32,1,128]{2,1,0:T(1,128)S(1)}) custom-call(s32[1,1,1]{2,1,0:T(1,128)S(6)} %copy.8.count_ref, f32[128,256]{1,0:T(8,128)S(1)} %get-tuple-element.21.source_ref, f32[128,256]{1,0:T(8,128)S(1)} %get-tuple-element.22.up_ref, f32[128,256]{1,0:T(8,128)S(1)} %get-tuple-element.23.down_ref, ...), custom_call_target="tpu_custom_call" | custom-call | flops 2415919104 | bytes 1048576 | tf_op jit(solution)/shard_map/pallas_call | solution.py:441
  14.2 11.2 %all_to_all.5.parts_ref = f32[32,1,128]{2,1,0:T(1,128)S(1)} all-to-all(f32[32,1,128]{2,1,0:T(1,128)S(1)} %get-tuple-element.34), channel_id=1, replica_groups=mesh['gx'=4,'gy'=2,'gz'=4] {'gx','gy','gz'}, dimensions={0} | all-to-all | bytes 32768 | tf_op jit(solution)/shard_map/all_to_all | solution.py:586
  25.4 1.0 %shard_map.75 = f32[128,256]{1,0:T(8,128)} custom-call(s32[1,1,1]{2,1,0:T(1,128)S(6)} %copy.8.count_ref, f32[128,256]{1,0:T(8,128)S(1)} %get-tuple-element.20.first_ref, f32[128,256]{1,0:T(8,128)S(1)} %get-tuple-element.33.second_ref, f32[32,1,128]{2,1,0:T(1,128)S(1)} %all_to_all.5.parts_ref), custom_call_target="tpu_custom_call" | custom-call | flops 32768 | bytes 1048576 | tf_op jit(solution)/shard_map/pallas_call | solution.py:441
Async XLA Ops:
  2.2 6.3 %collective-permute-start.1 = (f32[48,128]{1,0:T(8,128)S(1)}, f32[48,128]{1,0:T(8,128)S(1)}, u32[]{:S(2)}, u32[]{:S(2)}) collective-permute-start(f32[48,128]{1,0:T(8,128)S(1)} %get-tuple-element.31), channel_id=1, source_target_pairs={{0,2},{1,3},{2,0},{3,1},{4,6},{5,7},{6,4},{7,5},{8,10},{9,11},{10,... | collective-permute-start | bytes 73736 | tf_op jit(solution)/shard_map/ppermute | solution.py:490
  6.3 5.6 %collective-permute-start.2 = (f32[48,128]{1,0:T(8,128)S(1)}, f32[48,128]{1,0:T(8,128)S(1)}, u32[]{:S(2)}, u32[]{:S(2)}) collective-permute-start(f32[48,128]{1,0:T(8,128)S(1)} %get-tuple-element.32), channel_id=1, source_target_pairs={{0,3},{1,2},{2,1},{3,0},{4,7},{5,6},{6,5},{7,4},{8,11},{9,10},{10,... | collective-permute-start | bytes 73736 | tf_op jit(solution)/shard_map/ppermute | solution.py:490
  7.6 4.3 %collective-permute-start = (f32[48,128]{1,0:T(8,128)S(1)}, f32[48,128]{1,0:T(8,128)S(1)}, u32[]{:S(2)}, u32[]{:S(2)}) collective-permute-start(f32[48,128]{1,0:T(8,128)S(1)} %get-tuple-element.30.mine_ref), channel_id=1, source_target_pairs={{0,1},{1,0},{2,3},{3,2},{4,5},{5,4},{6,7},{7,6},{8,9},{9,8},{10,11... | collective-permute-start | bytes 73736 | tf_op jit(solution)/shard_map/ppermute | solution.py:490

commit v15 on v13

--- a/solution.py
+++ b/solution.py
@@ -36,11 +36,10 @@
 
 
 def times_parts(rows, mat_high, mat_low):
+    count = rows.shape[0]
     row_high, row_low = two_parts(rows)
-    return dot(
-        jnp.concatenate([row_high, row_low, row_high], axis=1),
-        jnp.concatenate([mat_high, mat_high, mat_low], axis=0),
-    )
+    both = dot(jnp.concatenate([row_high, row_low], axis=0), mat_high)
+    return both[:count] + (both[count:] + dot(row_high, mat_low))
 
 
 def times_parts_once(rows, mat_high, mat_low):
@@ -91,11 +90,8 @@
     return jnp.broadcast_to(jnp.concatenate([column] * probes, axis=0), (probes * column.shape[0], dofs))
 
 
-def take_faces(parts, over_elements, over_dofs):
+def take_faces(picked, over_elements):
     elements = over_elements.shape[0]
-    picked = dot(
-        jnp.concatenate(parts, axis=1), jnp.concatenate([over_dofs] * len(parts), axis=0)
-    )
     return [
         jnp.sum(jnp.where(over_elements, picked[low : low + elements], 0.0), axis=0, keepdims=True)
         for low in range(0, picked.shape[0], elements)
@@ -115,6 +111,10 @@
 
 def add_faces(spreads, over_dofs):
     return dot_transposed(jnp.concatenate(spreads, axis=1), over_dofs)
+
+
+def add_faces_once(spreads, over_dofs):
+    return jnp.transpose(dot_transposed(over_dofs, jnp.concatenate(spreads, axis=1)))
 
 
 def folded(parts):
@@ -254,8 +254,9 @@
     stiffness = two_parts(k_ref[...])
     base = times_parts(first_pre, *stiffness) * up
     base_ref[...] = base
-    first_parts = two_parts(first_pre)
-    second_parts = [(times_parts_once(base, *smoother) * down).astype(bf16)]
+    second_part = (times_parts_once(base, *smoother) * down).astype(bf16)
+    stacked = jnp.concatenate([*two_parts(first_pre), second_part], axis=0)
+    rows = probes * elements
     for part_ref, part in zip(part_refs, smoother + stiffness):
         part_ref[...] = part
     second_at, index_at, visc_at = message_places(steps, probes)
@@ -263,8 +264,9 @@
         flat_row = slots_ref[step - 1]
         over_elements = hot_elements(flat_row, elements, dofs)
         over_dofs = hot_ref[:, (step - 1) * width : step * width]
-        first_rows = take_faces(first_parts, over_elements, over_dofs)
-        second_rows = take_faces(second_parts, over_elements, over_dofs)
+        picked = dot(stacked, over_dofs)
+        first_rows = take_faces(folded(picked[: 2 * rows]), over_elements)
+        second_rows = take_faces(picked[2 * rows :], over_elements)
         for probe in range(probes):
             write_row(leave_refs[step - 1], second_at + probe, second_rows[probe])
             for leave_ref in leave_refs:
@@ -301,7 +303,8 @@
 
     def placed_here(values):
         spreads = [spread_faces(values[step], own_elements[step]) for step in range(steps)]
-        return add_faces(spreads, hot_ref[...])
+        add = add_faces if len(values[0]) > probes else add_faces_once
+        return add(spreads, hot_ref[...])
 
     up, down = up_ref[...], down_ref[...]
     live = wide(live_column(count_ref, elements).astype(f32), probes, dofs) > 0.0
@@ -319,7 +322,7 @@
             spread_faces(inbound_first(member, step + 1), over_elements[step])
             for step in range(steps)
         ]
-        changes.append(-coupling * add_faces(spreads, jnp.concatenate(over_dofs, axis=1)))
+        changes.append(-coupling * add_faces_once(spreads, jnp.concatenate(over_dofs, axis=1)))
         back.append((over_elements[member - 1], over_dofs[member - 1]))
     second_pre = times_parts(image, p_high_ref[...], p_low_ref[...]) * down
     changes = times_parts_once(jnp.concatenate(changes, axis=0), p_high_ref[...], p_low_ref[...])
@@ -331,7 +334,8 @@
         visc = as_column(sent[visc_line : visc_line + 1, :elements])
         scale = wide(1.0 / visc, probes, dofs)
         change = changes[(member - 1) * rows : member * rows] * scale
-        taken = take_faces([change.astype(bf16)], *back[member - 1])
+        over_elements, over_dofs = back[member - 1]
+        taken = take_faces(dot(change.astype(bf16), over_dofs), over_elements)
         values.append(
             [taken[probe] + read_row(sent, second_at + probe, width) for probe in range(probes)]
         )
@@ -350,7 +354,8 @@
     for shift in range(1, members):
         flat_row = slots_ref[shift - 1]
         over_elements = hot_elements(flat_row, elements, dofs)
-        taken = take_faces(two_parts(field), over_elements, hot_dofs(flat_row, dofs))
+        parts = jnp.concatenate(two_parts(field), axis=0)
+        taken = take_faces(folded(dot(parts, hot_dofs(flat_row, dofs))), over_elements)
         target = lax.rem(me + shift, members)
         for probe in range(probes):
             leave_ref[target, pl.ds(probe, 1), :] = taken[probe]

time: 26.3 us -> 26.3 us (level)
  no operation moved by 1% of the time
where the time goes in v15:
time: 26.3 us; the launch traced here: 26.1 us
  blocking collectives  11.2 us (43%)
  starting transfers between devices  5.68 us (22%)
  Pallas kernels  5.17 us (20%)
  waiting for transfers between devices  3.39 us (13%)
  between operations  0.68 us (3%)
    all_to_all x1, blocking collectives, per_device(): lax.all_to_all(products, ('gx', 'gy', 'gz'), split_axis=0, concat_axis=0)  11.2 us
    ppermute x3, starting transfers between devices, near_steps(): lax.ppermute(leaving[step - 1], 'gz', [(source, source ^ step) for source...  5.68 us
    pallas_call x3, Pallas kernels, call(): pl.pallas_call(kernel, out_shape=out_shapes, in_specs=in_specs, out_specs...  5.17 us
    ppermute x3, waiting for transfers between devices, near_steps(): lax.ppermute(leaving[step - 1], 'gz', [(source, source ^ step) for source...  3.39 us
  transfers between devices with their start and end apart: 3, of which 1 were waited for; matrix products, arithmetic and copies ran while one was open for 0% of the time, Pallas kernels for 0%

profile of v15, /device:TPU:0, one launch (start us, length us, event | category | flops | bytes accessed | tf_op | source)
XLA Modules:
  0.0 26.1 jit_solution(385217178355426183)
XLA Ops:
  0.0 2.2 %shard_map.73 = (f32[128,256]{1,0:T(8,128)S(1)}, f32[128,256]{1,0:T(8,128)S(1)}, f32[128,256]{1,0:T(8,128)S(1)}, f32[128,256]{1,0:T(8,128)S(1)}, f32[128,256]{1,...) custom-call(s32[1,1,1,16]{3,2,1,0:T(1,128)} %refs_0_.1, ...), custom_call_target="tpu_custom_call" | custom-call | flops 805306368 | bytes 1048576 | tf_op jit(solution)/shard_map/pallas_call | solution.py:444
  2.2 4.1 %collective-permute-start.1 = (f32[48,128]{1,0:T(8,128)S(1)}, f32[48,128]{1,0:T(8,128)S(1)}, u32[]{:S(2)}, u32[]{:S(2)}) collective-permute-start(f32[48,128]{1,0:T(8,128)S(1)} %get-tuple-element.33), channel_id=1, source_target_pairs={{0,2},{1,3},{2,0},{3,1},{4,6},{5,7},{6,4},{7,5},{8,10},{9,11},{10,... | collective-permute-start | bytes 73736 | tf_op jit(solution)/shard_map/ppermute | solution.py:494
  6.3 1.3 %collective-permute-start.2 = (f32[48,128]{1,0:T(8,128)S(1)}, f32[48,128]{1,0:T(8,128)S(1)}, u32[]{:S(2)}, u32[]{:S(2)}) collective-permute-start(f32[48,128]{1,0:T(8,128)S(1)} %get-tuple-element.34), channel_id=1, source_target_pairs={{0,3},{1,2},{2,1},{3,0},{4,7},{5,6},{6,5},{7,4},{8,11},{9,10},{10,... | collective-permute-start | bytes 73736 | tf_op jit(solution)/shard_map/ppermute | solution.py:494
  7.6 0.2 collective-permute-start
  8.5 0.0 collective-permute-done.1.refs_1_
  8.5 3.4 %collective-permute-done.2.refs_2_ = f32[48,128]{1,0:T(8,128)S(1)} collective-permute-done((f32[48,128]{1,0:T(8,128)S(1)}, f32[48,128]{1,0:T(8,128)S(1)}, u32[]{:S(2)}, u32[]{:S(2)}) %collective-permute-start.2) | collective-permute-done | bytes 24608 | tf_op jit(solution)/shard_map/ppermute | solution.py:494
  11.9 0.0 collective-permute-done.refs_0_
  11.9 2.1 %shard_map.74 = (f32[128,256]{1,0:T(8,128)S(1)}, f32[32,1,128]{2,1,0:T(1,128)S(1)}) custom-call(s32[1,1,1]{2,1,0:T(1,128)S(6)} %copy.8.count_ref, f32[128,256]{1,0:T(8,128)S(1)} %get-tuple-element.22.source_ref, f32[128,256]{1,0:T(8,128)S(1)} %get-tuple-element.23.up_ref, f32[128,256]{1,0:T(8,128)S(1)} %get-tuple-element.24.down_ref, ...), custom_call_target="tpu_custom_call" | custom-call | flops 2415919104 | bytes 1048576 | tf_op jit(solution)/shard_map/pallas_call | solution.py:444
  14.0 11.2 %all_to_all.5.parts_ref = f32[32,1,128]{2,1,0:T(1,128)S(1)} all-to-all(f32[32,1,128]{2,1,0:T(1,128)S(1)} %get-tuple-element.36), channel_id=1, replica_groups=mesh['gx'=4,'gy'=2,'gz'=4] {'gx','gy','gz'}, dimensions={0} | all-to-all | bytes 32768 | tf_op jit(solution)/shard_map/all_to_all | solution.py:591
  25.2 1.0 %shard_map.75 = f32[128,256]{1,0:T(8,128)} custom-call(s32[1,1,1]{2,1,0:T(1,128)S(6)} %copy.8.count_ref, f32[128,256]{1,0:T(8,128)S(1)} %get-tuple-element.21.first_ref, f32[128,256]{1,0:T(8,128)S(1)} %get-tuple-element.35.second_ref, f32[32,1,128]{2,1,0:T(1,128)S(1)} %all_to_all.5.parts_ref), custom_call_target="tpu_custom_call" | custom-call | flops 32768 | bytes 1048576 | tf_op jit(solution)/shard_map/pallas_call | solution.py:444
Async XLA Ops:
  2.2 6.3 %collective-permute-start.1 = (f32[48,128]{1,0:T(8,128)S(1)}, f32[48,128]{1,0:T(8,128)S(1)}, u32[]{:S(2)}, u32[]{:S(2)}) collective-permute-start(f32[48,128]{1,0:T(8,128)S(1)} %get-tuple-element.33), channel_id=1, source_target_pairs={{0,2},{1,3},{2,0},{3,1},{4,6},{5,7},{6,4},{7,5},{8,10},{9,11},{10,... | collective-permute-start | bytes 73736 | tf_op jit(solution)/shard_map/ppermute | solution.py:494
  6.3 5.6 %collective-permute-start.2 = (f32[48,128]{1,0:T(8,128)S(1)}, f32[48,128]{1,0:T(8,128)S(1)}, u32[]{:S(2)}, u32[]{:S(2)}) collective-permute-start(f32[48,128]{1,0:T(8,128)S(1)} %get-tuple-element.34), channel_id=1, source_target_pairs={{0,3},{1,2},{2,1},{3,0},{4,7},{5,6},{6,5},{7,4},{8,11},{9,10},{10,... | collective-permute-start | bytes 73736 | tf_op jit(solution)/shard_map/ppermute | solution.py:494
  7.6 4.3 %collective-permute-start = (f32[48,128]{1,0:T(8,128)S(1)}, f32[48,128]{1,0:T(8,128)S(1)}, u32[]{:S(2)}, u32[]{:S(2)}) collective-permute-start(f32[48,128]{1,0:T(8,128)S(1)} %get-tuple-element.32.mine_ref), channel_id=1, source_target_pairs={{0,1},{1,0},{2,3},{3,2},{4,5},{5,4},{6,7},{7,6},{8,9},{9,8},{10,11... | collective-permute-start | bytes 73736 | tf_op jit(solution)/shard_map/ppermute | solution.py:494

commit v16 on v15

--- a/solution.py
+++ b/solution.py
@@ -310,11 +310,15 @@
     live = wide(live_column(count_ref, elements).astype(f32), probes, dofs) > 0.0
     placed = folded(placed_here([high_low(inbound_first(0, step)) for step in range(1, members)]))
     image = jnp.where(live, base_ref[...] - coupling * placed, 0.0)
-    changes, back = [], []
+    second_pre = times_parts(image, p_high_ref[...], p_low_ref[...]) * down
+    second_ref[...] = second_pre
+    smoother = jnp.concatenate([p_high_ref[...], p_low_ref[...]], axis=0)
+    visc_line = visc_at * (width // lane_count)
+    values = []
     for member in range(1, members):
+        sent = message(member)
         rows_of = [
-            read_row(message(member), index_at + step, width).astype(jnp.int32)
-            for step in range(steps)
+            read_row(sent, index_at + step, width).astype(jnp.int32) for step in range(steps)
         ]
         over_elements = [hot_elements(flat_row, elements, dofs) for flat_row in rows_of]
         over_dofs = [hot_dofs(flat_row, dofs) for flat_row in rows_of]
@@ -322,20 +326,12 @@
             spread_faces(inbound_first(member, step + 1), over_elements[step])
             for step in range(steps)
         ]
-        changes.append(-coupling * add_faces_once(spreads, jnp.concatenate(over_dofs, axis=1)))
-        back.append((over_elements[member - 1], over_dofs[member - 1]))
-    second_pre = times_parts(image, p_high_ref[...], p_low_ref[...]) * down
-    changes = times_parts_once(jnp.concatenate(changes, axis=0), p_high_ref[...], p_low_ref[...])
-    second_ref[...] = second_pre
-    values = []
-    visc_line = visc_at * (width // lane_count)
-    for member in range(1, members):
-        sent = message(member)
-        visc = as_column(sent[visc_line : visc_line + 1, :elements])
-        scale = wide(1.0 / visc, probes, dofs)
-        change = changes[(member - 1) * rows : member * rows] * scale
-        over_elements, over_dofs = back[member - 1]
-        taken = take_faces(dot(change.astype(bf16), over_dofs), over_elements)
+        scale = wide(-coupling / as_column(sent[visc_line : visc_line + 1, :elements]), probes, dofs)
+        change = add_faces_once(spreads, jnp.concatenate(over_dofs, axis=1)) * scale
+        change = change.astype(bf16)
+        smoother_faces = dot(smoother, over_dofs[member - 1]).astype(bf16)
+        picked = dot(jnp.concatenate([change, change], axis=1), smoother_faces)
+        taken = take_faces(picked, over_elements[member - 1])
         values.append(
             [taken[probe] + read_row(sent, second_at + probe, width) for probe in range(probes)]
         )

time: 26.3 us -> 27 us (1.027)
  Pallas kernels: 5.17 us -> 5.83 us
    pallas_call x3, Pallas kernels: 5.17 us -> 5.83 us  [call(): pl.pallas_call(kernel, out_shape=out_shapes, in_specs=in_specs, out_specs...]
where the time goes in v16:
time: 27 us; the launch traced here: 26.8 us
  blocking collectives  11.2 us (41%)
  Pallas kernels  5.83 us (22%)
  starting transfers between devices  5.68 us (21%)
  waiting for transfers between devices  3.39 us (13%)
  between operations  0.68 us (3%)
    all_to_all x1, blocking collectives, per_device(): lax.all_to_all(products, ('gx', 'gy', 'gz'), split_axis=0, concat_axis=0)  11.2 us
    pallas_call x3, Pallas kernels, call(): pl.pallas_call(kernel, out_shape=out_shapes, in_specs=in_specs, out_specs...  5.83 us
    ppermute x3, starting transfers between devices, near_steps(): lax.ppermute(leaving[step - 1], 'gz', [(source, source ^ step) for source...  5.68 us
    ppermute x3, waiting for transfers between devices, near_steps(): lax.ppermute(leaving[step - 1], 'gz', [(source, source ^ step) for source...  3.39 us
  transfers between devices with their start and end apart: 3, of which 1 were waited for; matrix products, arithmetic and copies ran while one was open for 0% of the time, Pallas kernels for 0%

profile of v16, /device:TPU:0, one launch (start us, length us, event | category | flops | bytes accessed | tf_op | source)
XLA Modules:
  0.0 26.8 jit_solution(17564361230099969999)
XLA Ops:
  0.0 2.2 %shard_map.73 = (f32[128,256]{1,0:T(8,128)S(1)}, f32[128,256]{1,0:T(8,128)S(1)}, f32[128,256]{1,0:T(8,128)S(1)}, f32[128,256]{1,0:T(8,128)S(1)}, f32[128,256]{1,...) custom-call(s32[1,1,1,16]{3,2,1,0:T(1,128)} %refs_0_.1, ...), custom_call_target="tpu_custom_call" | custom-call | flops 805306368 | bytes 1048576 | tf_op jit(solution)/shard_map/pallas_call | solution.py:440
  2.2 4.1 %collective-permute-start.1 = (f32[48,128]{1,0:T(8,128)S(1)}, f32[48,128]{1,0:T(8,128)S(1)}, u32[]{:S(2)}, u32[]{:S(2)}) collective-permute-start(f32[48,128]{1,0:T(8,128)S(1)} %get-tuple-element.33), channel_id=1, source_target_pairs={{0,2},{1,3},{2,0},{3,1},{4,6},{5,7},{6,4},{7,5},{8,10},{9,11},{10,... | collective-permute-start | bytes 73736 | tf_op jit(solution)/shard_map/ppermute | solution.py:490
  6.3 1.3 %collective-permute-start.2 = (f32[48,128]{1,0:T(8,128)S(1)}, f32[48,128]{1,0:T(8,128)S(1)}, u32[]{:S(2)}, u32[]{:S(2)}) collective-permute-start(f32[48,128]{1,0:T(8,128)S(1)} %get-tuple-element.34), channel_id=1, source_target_pairs={{0,3},{1,2},{2,1},{3,0},{4,7},{5,6},{6,5},{7,4},{8,11},{9,10},{10,... | collective-permute-start | bytes 73736 | tf_op jit(solution)/shard_map/ppermute | solution.py:490
  7.6 0.2 collective-permute-start
  8.5 0.0 collective-permute-done.1.refs_1_
  8.5 3.4 %collective-permute-done.2.refs_2_ = f32[48,128]{1,0:T(8,128)S(1)} collective-permute-done((f32[48,128]{1,0:T(8,128)S(1)}, f32[48,128]{1,0:T(8,128)S(1)}, u32[]{:S(2)}, u32[]{:S(2)}) %collective-permute-start.2) | collective-permute-done | bytes 24608 | tf_op jit(solution)/shard_map/ppermute | solution.py:490
  11.9 0.0 collective-permute-done.refs_0_
  11.9 2.7 %shard_map.74 = (f32[128,256]{1,0:T(8,128)S(1)}, f32[32,1,128]{2,1,0:T(1,128)S(1)}) custom-call(s32[1,1,1]{2,1,0:T(1,128)S(6)} %copy.8.count_ref, f32[128,256]{1,0:T(8,128)S(1)} %get-tuple-element.22.source_ref, f32[128,256]{1,0:T(8,128)S(1)} %get-tuple-element.23.up_ref, f32[128,256]{1,0:T(8,128)S(1)} %get-tuple-element.24.down_ref, ...), custom_call_target="tpu_custom_call" | custom-call | flops 2415919104 | bytes 1048576 | tf_op jit(solution)/shard_map/pallas_call | solution.py:440
  14.6 11.2 %all_to_all.5.parts_ref = f32[32,1,128]{2,1,0:T(1,128)S(1)} all-to-all(f32[32,1,128]{2,1,0:T(1,128)S(1)} %get-tuple-element.36), channel_id=1, replica_groups=mesh['gx'=4,'gy'=2,'gz'=4] {'gx','gy','gz'}, dimensions={0} | all-to-all | bytes 32768 | tf_op jit(solution)/shard_map/all_to_all | solution.py:587
  25.8 1.0 %shard_map.75 = f32[128,256]{1,0:T(8,128)} custom-call(s32[1,1,1]{2,1,0:T(1,128)S(6)} %copy.8.count_ref, f32[128,256]{1,0:T(8,128)S(1)} %get-tuple-element.21.first_ref, f32[128,256]{1,0:T(8,128)S(1)} %get-tuple-element.35.second_ref, f32[32,1,128]{2,1,0:T(1,128)S(1)} %all_to_all.5.parts_ref), custom_call_target="tpu_custom_call" | custom-call | flops 32768 | bytes 1048576 | tf_op jit(solution)/shard_map/pallas_call | solution.py:440
Async XLA Ops:
  2.2 6.3 %collective-permute-start.1 = (f32[48,128]{1,0:T(8,128)S(1)}, f32[48,128]{1,0:T(8,128)S(1)}, u32[]{:S(2)}, u32[]{:S(2)}) collective-permute-start(f32[48,128]{1,0:T(8,128)S(1)} %get-tuple-element.33), channel_id=1, source_target_pairs={{0,2},{1,3},{2,0},{3,1},{4,6},{5,7},{6,4},{7,5},{8,10},{9,11},{10,... | collective-permute-start | bytes 73736 | tf_op jit(solution)/shard_map/ppermute | solution.py:490
  6.3 5.6 %collective-permute-start.2 = (f32[48,128]{1,0:T(8,128)S(1)}, f32[48,128]{1,0:T(8,128)S(1)}, u32[]{:S(2)}, u32[]{:S(2)}) collective-permute-start(f32[48,128]{1,0:T(8,128)S(1)} %get-tuple-element.34), channel_id=1, source_target_pairs={{0,3},{1,2},{2,1},{3,0},{4,7},{5,6},{6,5},{7,4},{8,11},{9,10},{10,... | collective-permute-start | bytes 73736 | tf_op jit(solution)/shard_map/ppermute | solution.py:490
  7.6 4.3 %collective-permute-start = (f32[48,128]{1,0:T(8,128)S(1)}, f32[48,128]{1,0:T(8,128)S(1)}, u32[]{:S(2)}, u32[]{:S(2)}) collective-permute-start(f32[48,128]{1,0:T(8,128)S(1)} %get-tuple-element.32.mine_ref), channel_id=1, source_target_pairs={{0,1},{1,0},{2,3},{3,2},{4,5},{5,4},{6,7},{7,6},{8,9},{9,8},{10,11... | collective-permute-start | bytes 73736 | tf_op jit(solution)/shard_map/ppermute | solution.py:490

commit v17 on v15

--- a/solution.py
+++ b/solution.py
@@ -197,9 +197,12 @@
     smoother = two_parts(matrix_refs[0][...])
     first_pre = times_parts(source, *smoother) * down
     refs["first"][...] = first_pre
-    for copy in copies[5:]:
-        copy.wait()
-    return first_pre, up, down, smoother
+
+    def wait_rest():
+        for copy in copies[5:]:
+            copy.wait()
+
+    return first_pre, up, down, smoother, wait_rest
 
 
 def message_places(steps, probes):
@@ -237,7 +240,7 @@
         for step in range(steps):
             hot_ref[:, step * width : (step + 1) * width] = hot_dofs(slots_ref[step], dofs)
 
-    first_pre, up, down, smoother = begin(
+    first_pre, up, down, smoother, wait_rest = begin(
         {
             "operands": operands,
             "scratch": scratch,
@@ -251,28 +254,28 @@
         None,
         prepare,
     )
+    wait_rest()
+    second_at, index_at, visc_at = message_places(steps, probes)
+    slots = [slots_ref[step] for step in range(steps)]
+    over_elements = [hot_elements(flat_row, elements, dofs) for flat_row in slots]
+    over_dofs = [hot_ref[:, step * width : (step + 1) * width] for step in range(steps)]
+    stacked = jnp.concatenate(two_parts(first_pre), axis=0)
+    for step in range(steps):
+        first_rows = take_faces(folded(dot(stacked, over_dofs[step])), over_elements[step])
+        for leave_ref in leave_refs:
+            for probe in range(probes):
+                write_row(leave_ref, step * probes + probe, first_rows[probe])
+            write_row(leave_ref, index_at + step, slots[step].astype(f32))
     stiffness = two_parts(k_ref[...])
     base = times_parts(first_pre, *stiffness) * up
     base_ref[...] = base
     second_part = (times_parts_once(base, *smoother) * down).astype(bf16)
-    stacked = jnp.concatenate([*two_parts(first_pre), second_part], axis=0)
-    rows = probes * elements
+    for step in range(steps):
+        second_rows = take_faces(dot(second_part, over_dofs[step]), over_elements[step])
+        for probe in range(probes):
+            write_row(leave_refs[step], second_at + probe, second_rows[probe])
     for part_ref, part in zip(part_refs, smoother + stiffness):
         part_ref[...] = part
-    second_at, index_at, visc_at = message_places(steps, probes)
-    for step in range(1, steps + 1):
-        flat_row = slots_ref[step - 1]
-        over_elements = hot_elements(flat_row, elements, dofs)
-        over_dofs = hot_ref[:, (step - 1) * width : step * width]
-        picked = dot(stacked, over_dofs)
-        first_rows = take_faces(folded(picked[: 2 * rows]), over_elements)
-        second_rows = take_faces(picked[2 * rows :], over_elements)
-        for probe in range(probes):
-            write_row(leave_refs[step - 1], second_at + probe, second_rows[probe])
-            for leave_ref in leave_refs:
-                write_row(leave_ref, (step - 1) * probes + probe, first_rows[probe])
-        for leave_ref in leave_refs:
-            write_row(leave_ref, index_at + step - 1, flat_row.astype(f32))
     visc_line = visc_at * (width // lane_count)
     for leave_ref in leave_refs:
         leave_ref[visc_line : visc_line + 1, :elements] = visc_ref[0, 0]
@@ -423,11 +426,14 @@
     inner_products(image_ref[...], second_img, source_ref[...], probes, products_ref)
 
 
-def last_kernel(probes, count_ref, first_ref, second_ref, parts_ref, out_ref):
+def last_kernel(
+    probes, count_ref, first_ref, second_ref, parts_ref, out_hbm, out_ref, left
+):
     rows, _ = first_ref.shape
     elements = rows // probes
     total = jnp.sum(parts_ref[...], axis=0)
     live = live_column(count_ref, elements)
+    weights = []
     for probe in range(probes):
         self_one, cross_mid, self_two, load_one, load_two = (
             total[:, place * probes + probe : place * probes + probe + 1] for place in range(5)
@@ -435,17 +441,24 @@
         determinant = self_one * self_two - cross_mid * cross_mid
         weight_one = (self_two * load_one - cross_mid * load_two) / determinant
         weight_two = (self_one * load_two - cross_mid * load_one) / determinant
+        weights.append((weight_one, weight_two))
+    copies = []
+    for probe, (weight_one, weight_two) in enumerate(weights):
         block = pl.ds(probe * elements, elements)
         value = weight_one * first_ref[block, :] + weight_two * second_ref[block, :]
         out_ref[block, :] = jnp.where(live, value, 0.0)
-
-
-def call(kernel, in_specs, out_shapes, flops, *args, scratch=()):
+        copies.append(pltpu.make_async_copy(out_ref.at[block], out_hbm.at[block], left.at[probe]))
+        copies[-1].start()
+    for copy in copies:
+        copy.wait()
+
+
+def call(kernel, in_specs, out_shapes, flops, *args, scratch=(), out_spec=vmem_spec):
     return pl.pallas_call(
         kernel,
         out_shape=out_shapes,
         in_specs=in_specs,
-        out_specs=jax.tree.map(lambda _: vmem_spec, out_shapes),
+        out_specs=jax.tree.map(lambda _: out_spec, out_shapes),
         scratch_shapes=scratch,
         compiler_params=pltpu.CompilerParams(vmem_limit_bytes=vmem_grant),
         cost_estimate=pl.CostEstimate(flops=flops, bytes_accessed=1 << 20, transcendentals=0),
@@ -589,6 +602,8 @@
         first_pre,
         second_pre,
         lax.all_to_all(products, ("gx", "gy", "gz"), split_axis=0, concat_axis=0),
+        scratch=[pltpu.VMEM(shapes[0].shape, f32), pltpu.SemaphoreType.DMA((probes,))],
+        out_spec=hbm_spec,
     )
     return result.reshape(rhs.shape)
 

time: 26.3 us -> 26.3 us (level)
  no operation moved by 1% of the time
where the time goes in v17:
time: 26.3 us; the launch traced here: 26.2 us
  blocking collectives  11.2 us (43%)
  starting transfers between devices  5.68 us (22%)
  Pallas kernels  5.21 us (20%)
  waiting for transfers between devices  3.39 us (13%)
  between operations  0.68 us (3%)
    all_to_all x1, blocking collectives, per_device(): lax.all_to_all(products, ('gx', 'gy', 'gz'), split_axis=0, concat_axis=0)  11.2 us
    ppermute x3, starting transfers between devices, near_steps(): lax.ppermute(leaving[step - 1], 'gz', [(source, source ^ step) for source...  5.68 us
    pallas_call x3, Pallas kernels, call(): pl.pallas_call(kernel, out_shape=out_shapes, in_specs=in_specs, out_specs...  5.21 us
    ppermute x3, waiting for transfers between devices, near_steps(): lax.ppermute(leaving[step - 1], 'gz', [(source, source ^ step) for source...  3.39 us
  transfers between devices with their start and end apart: 3, of which 1 were waited for; matrix products, arithmetic and copies ran while one was open for 0% of the time, Pallas kernels for 0%

profile of v17, /device:TPU:0, one launch (start us, length us, event | category | flops | bytes accessed | tf_op | source)
XLA Modules:
  0.0 26.2 jit_solution(10950692755926473334)
XLA Ops:
  0.0 2.2 %shard_map.73 = (f32[128,256]{1,0:T(8,128)S(1)}, f32[128,256]{1,0:T(8,128)S(1)}, f32[128,256]{1,0:T(8,128)S(1)}, f32[128,256]{1,0:T(8,128)S(1)}, f32[128,256]{1,...) custom-call(s32[1,1,1,16]{3,2,1,0:T(1,128)} %refs_0_.1, ...), custom_call_target="tpu_custom_call" | custom-call | flops 805306368 | bytes 1048576 | tf_op jit(solution)/shard_map/pallas_call | solution.py:457
  2.2 4.1 %collective-permute-start.1 = (f32[48,128]{1,0:T(8,128)S(1)}, f32[48,128]{1,0:T(8,128)S(1)}, u32[]{:S(2)}, u32[]{:S(2)}) collective-permute-start(f32[48,128]{1,0:T(8,128)S(1)} %get-tuple-element.33), channel_id=1, source_target_pairs={{0,2},{1,3},{2,0},{3,1},{4,6},{5,7},{6,4},{7,5},{8,10},{9,11},{10,... | collective-permute-start | bytes 73736 | tf_op jit(solution)/shard_map/ppermute | solution.py:507
  6.3 1.3 %collective-permute-start.2 = (f32[48,128]{1,0:T(8,128)S(1)}, f32[48,128]{1,0:T(8,128)S(1)}, u32[]{:S(2)}, u32[]{:S(2)}) collective-permute-start(f32[48,128]{1,0:T(8,128)S(1)} %get-tuple-element.34), channel_id=1, source_target_pairs={{0,3},{1,2},{2,1},{3,0},{4,7},{5,6},{6,5},{7,4},{8,11},{9,10},{10,... | collective-permute-start | bytes 73736 | tf_op jit(solution)/shard_map/ppermute | solution.py:507
  7.7 0.2 collective-permute-start
  8.5 0.0 collective-permute-done.1.refs_1_
  8.6 3.4 %collective-permute-done.2.refs_2_ = f32[48,128]{1,0:T(8,128)S(1)} collective-permute-done((f32[48,128]{1,0:T(8,128)S(1)}, f32[48,128]{1,0:T(8,128)S(1)}, u32[]{:S(2)}, u32[]{:S(2)}) %collective-permute-start.2) | collective-permute-done | bytes 24608 | tf_op jit(solution)/shard_map/ppermute | solution.py:507
  11.9 0.0 collective-permute-done.refs_0_
  11.9 2.1 %shard_map.74 = (f32[128,256]{1,0:T(8,128)S(1)}, f32[32,1,128]{2,1,0:T(1,128)S(1)}) custom-call(s32[1,1,1]{2,1,0:T(1,128)S(6)} %copy.8.count_ref, f32[128,256]{1,0:T(8,128)S(1)} %get-tuple-element.22.source_ref, f32[128,256]{1,0:T(8,128)S(1)} %get-tuple-element.23.up_ref, f32[128,256]{1,0:T(8,128)S(1)} %get-tuple-element.24.down_ref, ...), custom_call_target="tpu_custom_call" | custom-call | flops 2415919104 | bytes 1048576 | tf_op jit(solution)/shard_map/pallas_call | solution.py:457
  14.0 11.2 %all_to_all.5.parts_ref = f32[32,1,128]{2,1,0:T(1,128)S(1)} all-to-all(f32[32,1,128]{2,1,0:T(1,128)S(1)} %get-tuple-element.36), channel_id=1, replica_groups=mesh['gx'=4,'gy'=2,'gz'=4] {'gx','gy','gz'}, dimensions={0} | all-to-all | bytes 32768 | tf_op jit(solution)/shard_map/all_to_all | solution.py:604
  25.2 1.0 %shard_map.75 = f32[128,256]{1,0:T(8,128)} custom-call(s32[1,1,1]{2,1,0:T(1,128)S(6)} %copy.8.count_ref, f32[128,256]{1,0:T(8,128)S(1)} %get-tuple-element.21.first_ref, f32[128,256]{1,0:T(8,128)S(1)} %get-tuple-element.35.second_ref, f32[32,1,128]{2,1,0:T(1,128)S(1)} %all_to_all.5.parts_ref), custom_call_target="tpu_custom_call" | custom-call | flops 32768 | bytes 1048576 | tf_op jit(solution)/shard_map/pallas_call | solution.py:457
Async XLA Ops:
  2.2 6.3 %collective-permute-start.1 = (f32[48,128]{1,0:T(8,128)S(1)}, f32[48,128]{1,0:T(8,128)S(1)}, u32[]{:S(2)}, u32[]{:S(2)}) collective-permute-start(f32[48,128]{1,0:T(8,128)S(1)} %get-tuple-element.33), channel_id=1, source_target_pairs={{0,2},{1,3},{2,0},{3,1},{4,6},{5,7},{6,4},{7,5},{8,10},{9,11},{10,... | collective-permute-start | bytes 73736 | tf_op jit(solution)/shard_map/ppermute | solution.py:507
  6.3 5.6 %collective-permute-start.2 = (f32[48,128]{1,0:T(8,128)S(1)}, f32[48,128]{1,0:T(8,128)S(1)}, u32[]{:S(2)}, u32[]{:S(2)}) collective-permute-start(f32[48,128]{1,0:T(8,128)S(1)} %get-tuple-element.34), channel_id=1, source_target_pairs={{0,3},{1,2},{2,1},{3,0},{4,7},{5,6},{6,5},{7,4},{8,11},{9,10},{10,... | collective-permute-start | bytes 73736 | tf_op jit(solution)/shard_map/ppermute | solution.py:507
  7.7 4.3 %collective-permute-start = (f32[48,128]{1,0:T(8,128)S(1)}, f32[48,128]{1,0:T(8,128)S(1)}, u32[]{:S(2)}, u32[]{:S(2)}) collective-permute-start(f32[48,128]{1,0:T(8,128)S(1)} %get-tuple-element.32.mine_ref), channel_id=1, source_target_pairs={{0,1},{1,0},{2,3},{3,2},{4,5},{5,4},{6,7},{7,6},{8,9},{9,8},{10,11... | collective-permute-start | bytes 73736 | tf_op jit(solution)/shard_map/ppermute | solution.py:507

commit v18 on v15

--- a/solution.py
+++ b/solution.py
@@ -154,7 +154,7 @@
     return lax.broadcasted_iota(jnp.int32, (elements, 1), 0) < count_ref[0, 0, 0]
 
 
-def begin(refs, partner, count_ref, prepare):
+def begin(refs, partner, count_ref):
     links_hbm, index_hbm, visc_hbm, rhs_hbm, *matrices_hbm = refs["operands"]
     links_ref, index_ref, visc_ref, rhs_ref, *matrix_refs, arrived = refs["scratch"]
     pairs = (
@@ -171,14 +171,8 @@
     ]
     for copy in copies:
         copy.start()
-    copies[0].wait()
-    copies[1].wait()
-    slots_ref = refs["slots"]
-    me = lax.axis_index("gz")
-    for step in range(1, slots_ref.shape[0] + 1):
-        slots_ref[step - 1] = slot_of(partner(me, step), links_ref, index_ref)
-    prepare()
-    copies[4].wait()
+    for copy in copies:
+        copy.wait()
     probes, elements, dofs = rhs_ref.shape[3:]
     live = jnp.ones((elements, 1), f32)
     if count_ref is not None:
@@ -186,20 +180,22 @@
     visc = as_column(visc_ref[0, 0])
     up = wide(live * visc, probes, dofs)
     down = wide(live / visc, probes, dofs)
-    refs["up"][...] = up
-    refs["down"][...] = down
-    copies[2].wait()
     source = rhs_ref[...].reshape(probes * elements, dofs)
     if count_ref is not None:
         source = source * wide(live, probes, dofs)
-    refs["source"][...] = source
-    copies[3].wait()
     smoother = two_parts(matrix_refs[0][...])
     first_pre = times_parts(source, *smoother) * down
+    refs["up"][...] = up
+    refs["down"][...] = down
+    refs["source"][...] = source
     refs["first"][...] = first_pre
-    for copy in copies[5:]:
-        copy.wait()
-    return first_pre, up, down, smoother
+    slots_ref = refs["slots"]
+    me = lax.axis_index("gz")
+    slots = []
+    for step in range(1, slots_ref.shape[0] + 1):
+        slots.append(slot_of(partner(me, step), links_ref, index_ref))
+        slots_ref[step - 1] = slots[-1]
+    return first_pre, up, down, smoother, slots
 
 
 def message_places(steps, probes):
@@ -232,12 +228,7 @@
     leave_refs, scratch = refs[:steps], refs[steps:]
     visc_ref, rhs_ref, _, k_ref = scratch[2:6]
     probes, elements, dofs = rhs_ref.shape[3:]
-
-    def prepare():
-        for step in range(steps):
-            hot_ref[:, step * width : (step + 1) * width] = hot_dofs(slots_ref[step], dofs)
-
-    first_pre, up, down, smoother = begin(
+    first_pre, up, down, smoother, slots = begin(
         {
             "operands": operands,
             "scratch": scratch,
@@ -249,7 +240,6 @@
         },
         lambda me, step: me ^ step,
         None,
-        prepare,
     )
     stiffness = two_parts(k_ref[...])
     base = times_parts(first_pre, *stiffness) * up
@@ -261,9 +251,10 @@
         part_ref[...] = part
     second_at, index_at, visc_at = message_places(steps, probes)
     for step in range(1, steps + 1):
-        flat_row = slots_ref[step - 1]
+        flat_row = slots[step - 1]
         over_elements = hot_elements(flat_row, elements, dofs)
-        over_dofs = hot_ref[:, (step - 1) * width : step * width]
+        over_dofs = hot_dofs(flat_row, dofs)
+        hot_ref[:, (step - 1) * width : step * width] = over_dofs
         picked = dot(stacked, over_dofs)
         first_rows = take_faces(folded(picked[: 2 * rows]), over_elements)
         second_rows = take_faces(picked[2 * rows :], over_elements)
@@ -394,7 +385,6 @@
         },
         lambda me, step: lax.rem(me + step, members),
         count_ref,
-        lambda: None,
     )
     leave_faces(first_pre, leave_ref.shape[1], slots_ref, leave_ref)
 

time: 26.3 us -> 26.3 us (level)
  no operation moved by 1% of the time
where the time goes in v18:
time: 26.3 us; the launch traced here: 26.1 us
  blocking collectives  11.2 us (43%)
  starting transfers between devices  5.68 us (22%)
  Pallas kernels  5.16 us (20%)
  waiting for transfers between devices  3.39 us (13%)
  between operations  0.68 us (3%)
    all_to_all x1, blocking collectives, per_device(): lax.all_to_all(products, ('gx', 'gy', 'gz'), split_axis=0, concat_axis=0)  11.2 us
    ppermute x3, starting transfers between devices, near_steps(): lax.ppermute(leaving[step - 1], 'gz', [(source, source ^ step) for source...  5.68 us
    pallas_call x3, Pallas kernels, call(): pl.pallas_call(kernel, out_shape=out_shapes, in_specs=in_specs, out_specs...  5.16 us
    ppermute x3, waiting for transfers between devices, near_steps(): lax.ppermute(leaving[step - 1], 'gz', [(source, source ^ step) for source...  3.39 us
  transfers between devices with their start and end apart: 3, of which 1 were waited for; matrix products, arithmetic and copies ran while one was open for 0% of the time, Pallas kernels for 0%

profile of v18, /device:TPU:0, one launch (start us, length us, event | category | flops | bytes accessed | tf_op | source)
XLA Modules:
  0.0 26.1 jit_solution(16911874744868006762)
XLA Ops:
  0.0 2.2 %shard_map.73 = (f32[128,256]{1,0:T(8,128)S(1)}, f32[128,256]{1,0:T(8,128)S(1)}, f32[128,256]{1,0:T(8,128)S(1)}, f32[128,256]{1,0:T(8,128)S(1)}, f32[128,256]{1,...) custom-call(s32[1,1,1,16]{3,2,1,0:T(1,128)} %refs_0_.1, ...), custom_call_target="tpu_custom_call" | custom-call | flops 805306368 | bytes 1048576 | tf_op jit(solution)/shard_map/pallas_call | solution.py:434
  2.2 4.1 %collective-permute-start.1 = (f32[48,128]{1,0:T(8,128)S(1)}, f32[48,128]{1,0:T(8,128)S(1)}, u32[]{:S(2)}, u32[]{:S(2)}) collective-permute-start(f32[48,128]{1,0:T(8,128)S(1)} %get-tuple-element.33), channel_id=1, source_target_pairs={{0,2},{1,3},{2,0},{3,1},{4,6},{5,7},{6,4},{7,5},{8,10},{9,11},{10,... | collective-permute-start | bytes 73736 | tf_op jit(solution)/shard_map/ppermute | solution.py:484
  6.3 1.3 %collective-permute-start.2 = (f32[48,128]{1,0:T(8,128)S(1)}, f32[48,128]{1,0:T(8,128)S(1)}, u32[]{:S(2)}, u32[]{:S(2)}) collective-permute-start(f32[48,128]{1,0:T(8,128)S(1)} %get-tuple-element.34), channel_id=1, source_target_pairs={{0,3},{1,2},{2,1},{3,0},{4,7},{5,6},{6,5},{7,4},{8,11},{9,10},{10,... | collective-permute-start | bytes 73736 | tf_op jit(solution)/shard_map/ppermute | solution.py:484
  7.6 0.2 collective-permute-start
  8.5 0.0 collective-permute-done.1.refs_1_
  8.5 3.4 %collective-permute-done.2.refs_2_ = f32[48,128]{1,0:T(8,128)S(1)} collective-permute-done((f32[48,128]{1,0:T(8,128)S(1)}, f32[48,128]{1,0:T(8,128)S(1)}, u32[]{:S(2)}, u32[]{:S(2)}) %collective-permute-start.2) | collective-permute-done | bytes 24608 | tf_op jit(solution)/shard_map/ppermute | solution.py:484
  11.9 0.0 collective-permute-done.refs_0_
  11.9 2.0 %shard_map.74 = (f32[128,256]{1,0:T(8,128)S(1)}, f32[32,1,128]{2,1,0:T(1,128)S(1)}) custom-call(s32[1,1,1]{2,1,0:T(1,128)S(6)} %copy.8.count_ref, f32[128,256]{1,0:T(8,128)S(1)} %get-tuple-element.22.source_ref, f32[128,256]{1,0:T(8,128)S(1)} %get-tuple-element.23.up_ref, f32[128,256]{1,0:T(8,128)S(1)} %get-tuple-element.24.down_ref, ...), custom_call_target="tpu_custom_call" | custom-call | flops 2415919104 | bytes 1048576 | tf_op jit(solution)/shard_map/pallas_call | solution.py:434
  13.9 11.2 %all_to_all.5.parts_ref = f32[32,1,128]{2,1,0:T(1,128)S(1)} all-to-all(f32[32,1,128]{2,1,0:T(1,128)S(1)} %get-tuple-element.36), channel_id=1, replica_groups=mesh['gx'=4,'gy'=2,'gz'=4] {'gx','gy','gz'}, dimensions={0} | all-to-all | bytes 32768 | tf_op jit(solution)/shard_map/all_to_all | solution.py:581
  25.1 1.0 %shard_map.75 = f32[128,256]{1,0:T(8,128)} custom-call(s32[1,1,1]{2,1,0:T(1,128)S(6)} %copy.8.count_ref, f32[128,256]{1,0:T(8,128)S(1)} %get-tuple-element.21.first_ref, f32[128,256]{1,0:T(8,128)S(1)} %get-tuple-element.35.second_ref, f32[32,1,128]{2,1,0:T(1,128)S(1)} %all_to_all.5.parts_ref), custom_call_target="tpu_custom_call" | custom-call | flops 32768 | bytes 1048576 | tf_op jit(solution)/shard_map/pallas_call | solution.py:434
Async XLA Ops:
  2.2 6.3 %collective-permute-start.1 = (f32[48,128]{1,0:T(8,128)S(1)}, f32[48,128]{1,0:T(8,128)S(1)}, u32[]{:S(2)}, u32[]{:S(2)}) collective-permute-start(f32[48,128]{1,0:T(8,128)S(1)} %get-tuple-element.33), channel_id=1, source_target_pairs={{0,2},{1,3},{2,0},{3,1},{4,6},{5,7},{6,4},{7,5},{8,10},{9,11},{10,... | collective-permute-start | bytes 73736 | tf_op jit(solution)/shard_map/ppermute | solution.py:484
  6.3 5.6 %collective-permute-start.2 = (f32[48,128]{1,0:T(8,128)S(1)}, f32[48,128]{1,0:T(8,128)S(1)}, u32[]{:S(2)}, u32[]{:S(2)}) collective-permute-start(f32[48,128]{1,0:T(8,128)S(1)} %get-tuple-element.34), channel_id=1, source_target_pairs={{0,3},{1,2},{2,1},{3,0},{4,7},{5,6},{6,5},{7,4},{8,11},{9,10},{10,... | collective-permute-start | bytes 73736 | tf_op jit(solution)/shard_map/ppermute | solution.py:484
  7.6 4.3 %collective-permute-start = (f32[48,128]{1,0:T(8,128)S(1)}, f32[48,128]{1,0:T(8,128)S(1)}, u32[]{:S(2)}, u32[]{:S(2)}) collective-permute-start(f32[48,128]{1,0:T(8,128)S(1)} %get-tuple-element.32.mine_ref), channel_id=1, source_target_pairs={{0,1},{1,0},{2,3},{3,2},{4,5},{5,4},{6,7},{7,6},{8,9},{9,8},{10,11... | collective-permute-start | bytes 73736 | tf_op jit(solution)/shard_map/ppermute | solution.py:484

commit v19 on v15

--- a/solution.py
+++ b/solution.py
@@ -208,20 +208,20 @@
 
 
 def message_length(steps, probes, width):
-    return -(-(message_places(steps, probes)[2] * (width // lane_count) + 1) // 8) * 8
+    return message_places(steps, probes)[2] * (width // lane_count) + 1
 
 
 def write_row(message_ref, place, row):
     pieces = row.shape[1] // lane_count
     for piece in range(pieces):
-        line = place * pieces + piece
-        message_ref[line : line + 1, :] = row[:, piece * lane_count : (piece + 1) * lane_count]
+        lanes = slice(piece * lane_count, (piece + 1) * lane_count)
+        message_ref[place * pieces + piece] = row[:, lanes]
 
 
 def read_row(message_ref, place, width):
     pieces = width // lane_count
     lines = range(place * pieces, (place + 1) * pieces)
-    return jnp.concatenate([message_ref[line : line + 1, :] for line in lines], axis=1)
+    return jnp.concatenate([message_ref[line] for line in lines], axis=1)
 
 
 def near_first_kernel(*refs):
@@ -275,7 +275,7 @@
             write_row(leave_ref, index_at + step - 1, flat_row.astype(f32))
     visc_line = visc_at * (width // lane_count)
     for leave_ref in leave_refs:
-        leave_ref[visc_line : visc_line + 1, :elements] = visc_ref[0, 0]
+        leave_ref[visc_line, :, :elements] = visc_ref[0, 0]
 
 
 def near_second_kernel(
@@ -331,7 +331,7 @@
     visc_line = visc_at * (width // lane_count)
     for member in range(1, members):
         sent = message(member)
-        visc = as_column(sent[visc_line : visc_line + 1, :elements])
+        visc = as_column(sent[visc_line, :, :elements])
         scale = wide(1.0 / visc, probes, dofs)
         change = changes[(member - 1) * rows : member * rows] * scale
         over_elements, over_dofs = back[member - 1]
@@ -475,7 +475,7 @@
     probes = rhs.shape[3]
     flops = 8 * rows * dofs * steps * width
     hot = jax.ShapeDtypeStruct((dofs, steps * width), bf16)
-    message = jax.ShapeDtypeStruct((message_length(steps, probes, width), lane_count), f32)
+    message = jax.ShapeDtypeStruct((message_length(steps, probes, width), 1, lane_count), f32)
     part = jax.ShapeDtypeStruct(p_matrix.shape, bf16)
     first_pre, source, up, down, base, slots, hot_own, *rest = begin_call(
         near_first_kernel,

time: 26.3 us -> 26.3 us (level)
  no operation moved by 1% of the time
where the time goes in v19:
time: 26.3 us; the launch traced here: 26.1 us
  blocking collectives  11.2 us (43%)
  starting transfers between devices  5.68 us (22%)
  Pallas kernels  5.17 us (20%)
  waiting for transfers between devices  3.37 us (13%)
  between operations  0.68 us (3%)
    all_to_all x1, blocking collectives, per_device(): lax.all_to_all(products, ('gx', 'gy', 'gz'), split_axis=0, concat_axis=0)  11.2 us
    ppermute x3, starting transfers between devices, near_steps(): lax.ppermute(leaving[step - 1], 'gz', [(source, source ^ step) for source...  5.68 us
    pallas_call x3, Pallas kernels, call(): pl.pallas_call(kernel, out_shape=out_shapes, in_specs=in_specs, out_specs...  5.17 us
    ppermute x3, waiting for transfers between devices, near_steps(): lax.ppermute(leaving[step - 1], 'gz', [(source, source ^ step) for source...  3.37 us
  transfers between devices with their start and end apart: 3, of which 1 were waited for; matrix products, arithmetic and copies ran while one was open for 0% of the time, Pallas kernels for 0%

profile of v19, /device:TPU:0, one launch (start us, length us, event | category | flops | bytes accessed | tf_op | source)
XLA Modules:
  0.0 26.1 jit_solution(7047333668697363411)
XLA Ops:
  0.0 2.2 %shard_map.73 = (f32[128,256]{1,0:T(8,128)S(1)}, f32[128,256]{1,0:T(8,128)S(1)}, f32[128,256]{1,0:T(8,128)S(1)}, f32[128,256]{1,0:T(8,128)S(1)}, f32[128,256]{1,...) custom-call(s32[1,1,1,16]{3,2,1,0:T(1,128)} %refs_0_.1, ...), custom_call_target="tpu_custom_call" | custom-call | flops 805306368 | bytes 1048576 | tf_op jit(solution)/shard_map/pallas_call | solution.py:444
  2.2 4.1 %collective-permute-start.1 = (f32[45,1,128]{2,1,0:T(1,128)S(1)}, f32[45,1,128]{2,1,0:T(1,128)S(1)}, u32[]{:S(2)}, u32[]{:S(2)}) collective-permute-start(f32[45,1,128]{2,1,0:T(1,128)S(1)} %get-tuple-element.33), channel_id=1, source_target_pairs={{0,2},{1,3},{2,0},{3,1},{4,6},{5,7},{6,4},{7,5},{8,10},{9,11},{10,... | collective-permute-start | bytes 69128 | tf_op jit(solution)/shard_map/ppermute | solution.py:494
  6.3 1.3 %collective-permute-start.2 = (f32[45,1,128]{2,1,0:T(1,128)S(1)}, f32[45,1,128]{2,1,0:T(1,128)S(1)}, u32[]{:S(2)}, u32[]{:S(2)}) collective-permute-start(f32[45,1,128]{2,1,0:T(1,128)S(1)} %get-tuple-element.34), channel_id=1, source_target_pairs={{0,3},{1,2},{2,1},{3,0},{4,7},{5,6},{6,5},{7,4},{8,11},{9,10},{10,... | collective-permute-start | bytes 69128 | tf_op jit(solution)/shard_map/ppermute | solution.py:494
  7.6 0.2 collective-permute-start
  8.5 0.0 collective-permute-done.1.refs_1_
  8.5 3.4 %collective-permute-done.2.refs_2_ = f32[45,1,128]{2,1,0:T(1,128)S(1)} collective-permute-done((f32[45,1,128]{2,1,0:T(1,128)S(1)}, f32[45,1,128]{2,1,0:T(1,128)S(1)}, u32[]{:S(2)}, u32[]{:S(2)}) %collective-permute-start.2) | collective-permute-done | bytes 23072 | tf_op jit(solution)/shard_map/ppermute | solution.py:494
  11.9 0.0 collective-permute-done.refs_0_
  11.9 2.1 %shard_map.74 = (f32[128,256]{1,0:T(8,128)S(1)}, f32[32,1,128]{2,1,0:T(1,128)S(1)}) custom-call(s32[1,1,1]{2,1,0:T(1,128)S(6)} %copy.8.count_ref, f32[128,256]{1,0:T(8,128)S(1)} %get-tuple-element.22.source_ref, f32[128,256]{1,0:T(8,128)S(1)} %get-tuple-element.23.up_ref, f32[128,256]{1,0:T(8,128)S(1)} %get-tuple-element.24.down_ref, ...), custom_call_target="tpu_custom_call" | custom-call | flops 2415919104 | bytes 1048576 | tf_op jit(solution)/shard_map/pallas_call | solution.py:444
  13.9 11.2 %all_to_all.5.parts_ref = f32[32,1,128]{2,1,0:T(1,128)S(1)} all-to-all(f32[32,1,128]{2,1,0:T(1,128)S(1)} %get-tuple-element.36), channel_id=1, replica_groups=mesh['gx'=4,'gy'=2,'gz'=4] {'gx','gy','gz'}, dimensions={0} | all-to-all | bytes 32768 | tf_op jit(solution)/shard_map/all_to_all | solution.py:591
  25.1 1.0 %shard_map.75 = f32[128,256]{1,0:T(8,128)} custom-call(s32[1,1,1]{2,1,0:T(1,128)S(6)} %copy.8.count_ref, f32[128,256]{1,0:T(8,128)S(1)} %get-tuple-element.21.first_ref, f32[128,256]{1,0:T(8,128)S(1)} %get-tuple-element.35.second_ref, f32[32,1,128]{2,1,0:T(1,128)S(1)} %all_to_all.5.parts_ref), custom_call_target="tpu_custom_call" | custom-call | flops 32768 | bytes 1048576 | tf_op jit(solution)/shard_map/pallas_call | solution.py:444
Async XLA Ops:
  2.2 6.3 %collective-permute-start.1 = (f32[45,1,128]{2,1,0:T(1,128)S(1)}, f32[45,1,128]{2,1,0:T(1,128)S(1)}, u32[]{:S(2)}, u32[]{:S(2)}) collective-permute-start(f32[45,1,128]{2,1,0:T(1,128)S(1)} %get-tuple-element.33), channel_id=1, source_target_pairs={{0,2},{1,3},{2,0},{3,1},{4,6},{5,7},{6,4},{7,5},{8,10},{9,11},{10,... | collective-permute-start | bytes 69128 | tf_op jit(solution)/shard_map/ppermute | solution.py:494
  6.3 5.6 %collective-permute-start.2 = (f32[45,1,128]{2,1,0:T(1,128)S(1)}, f32[45,1,128]{2,1,0:T(1,128)S(1)}, u32[]{:S(2)}, u32[]{:S(2)}) collective-permute-start(f32[45,1,128]{2,1,0:T(1,128)S(1)} %get-tuple-element.34), channel_id=1, source_target_pairs={{0,3},{1,2},{2,1},{3,0},{4,7},{5,6},{6,5},{7,4},{8,11},{9,10},{10,... | collective-permute-start | bytes 69128 | tf_op jit(solution)/shard_map/ppermute | solution.py:494
  7.6 4.3 %collective-permute-start = (f32[45,1,128]{2,1,0:T(1,128)S(1)}, f32[45,1,128]{2,1,0:T(1,128)S(1)}, u32[]{:S(2)}, u32[]{:S(2)}) collective-permute-start(f32[45,1,128]{2,1,0:T(1,128)S(1)} %get-tuple-element.32.mine_ref), channel_id=1, source_target_pairs={{0,1},{1,0},{2,3},{3,2},{4,5},{5,4},{6,7},{7,6},{8,9},{9,8},{10,11... | collective-permute-start | bytes 69128 | tf_op jit(solution)/shard_map/ppermute | solution.py:494

commit v20 on v19

--- a/solution.py
+++ b/solution.py
@@ -490,11 +490,12 @@
         k_matrix,
     )
     parts, leaving = rest[:4], rest[4:]
+    order = [1] + list(range(members - 1, 1, -1))
     came = [
         lax.ppermute(
             leaving[step - 1], "gz", [(source, source ^ step) for source in range(members)]
         )
-        for step in range(1, members)
+        for step in order
     ]
     second_pre, products = call(
         functools.partial(near_second_kernel, probes),
@@ -509,8 +510,8 @@
         slots,
         hot_own,
         *parts,
-        leaving[0],
-        *came,
+        leaving[order[-1] - 1],
+        *(came[order.index(step)] for step in range(1, members)),
     )
     return first_pre, second_pre, products
 

time: 26.3 us -> 26.2 us (level)
  blocking collectives: 11.2 us -> 10.3 us
  waiting for transfers between devices: 3.37 us -> 4.18 us
    all_to_all x1, blocking collectives: 11.2 us -> 10.3 us  [per_device(): lax.all_to_all(products, ('gx', 'gy', 'gz'), split_axis=0, concat_axis=0)]
    ppermute x3, waiting for transfers between devices: 3.37 us -> 4.18 us  [near_steps(): lax.ppermute(leaving[step - 1], 'gz', [(source, source ^ step) for source...]
  transfers between devices with their start and end apart: 3 -> 3, of which waited for: 1 -> 2; matrix products, arithmetic and copies ran while one was open for 0% -> 0% of each run, Pallas kernels for 0% -> 0%
where the time goes in v20:
time: 26.2 us; the launch traced here: 26 us
  blocking collectives  10.3 us (39%)
  starting transfers between devices  5.68 us (22%)
  Pallas kernels  5.16 us (20%)
  waiting for transfers between devices  4.18 us (16%)
  between operations  0.68 us (3%)
    all_to_all x1, blocking collectives, per_device(): lax.all_to_all(products, ('gx', 'gy', 'gz'), split_axis=0, concat_axis=0)  10.3 us
    ppermute x3, starting transfers between devices, near_steps(): lax.ppermute(leaving[step - 1], 'gz', [(source, source ^ step) for source...  5.68 us
    pallas_call x3, Pallas kernels, call(): pl.pallas_call(kernel, out_shape=out_shapes, in_specs=in_specs, out_specs...  5.16 us
    ppermute x3, waiting for transfers between devices, near_steps(): lax.ppermute(leaving[step - 1], 'gz', [(source, source ^ step) for source...  4.18 us
  transfers between devices with their start and end apart: 3, of which 2 were waited for; matrix products, arithmetic and copies ran while one was open for 0% of the time, Pallas kernels for 0%

profile of v20, /device:TPU:0, one launch (start us, length us, event | category | flops | bytes accessed | tf_op | source)
XLA Modules:
  0.0 26.0 jit_solution(5287773607164951967)
XLA Ops:
  0.0 2.2 %shard_map.73 = (f32[128,256]{1,0:T(8,128)S(1)}, f32[128,256]{1,0:T(8,128)S(1)}, f32[128,256]{1,0:T(8,128)S(1)}, f32[128,256]{1,0:T(8,128)S(1)}, f32[128,256]{1,...) custom-call(s32[1,1,1,16]{3,2,1,0:T(1,128)} %refs_0_.1, ...), custom_call_target="tpu_custom_call" | custom-call | flops 805306368 | bytes 1048576 | tf_op jit(solution)/shard_map/pallas_call | solution.py:444
  2.2 3.1 %collective-permute-start = (f32[45,1,128]{2,1,0:T(1,128)S(1)}, f32[45,1,128]{2,1,0:T(1,128)S(1)}, u32[]{:S(2)}, u32[]{:S(2)}) collective-permute-start(f32[45,1,128]{2,1,0:T(1,128)S(1)} %get-tuple-element.33), channel_id=1, source_target_pairs={{0,1},{1,0},{2,3},{3,2},{4,5},{5,4},{6,7},{7,6},{8,9},{9,8},{10,11... | collective-permute-start | bytes 69128 | tf_op jit(solution)/shard_map/ppermute | solution.py:495
  5.3 2.5 %collective-permute-start.2 = (f32[45,1,128]{2,1,0:T(1,128)S(1)}, f32[45,1,128]{2,1,0:T(1,128)S(1)}, u32[]{:S(2)}, u32[]{:S(2)}) collective-permute-start(f32[45,1,128]{2,1,0:T(1,128)S(1)} %get-tuple-element.34), channel_id=1, source_target_pairs={{0,3},{1,2},{2,1},{3,0},{4,7},{5,6},{6,5},{7,4},{8,11},{9,10},{10,... | collective-permute-start | bytes 69128 | tf_op jit(solution)/shard_map/ppermute | solution.py:495
  7.7 0.1 collective-permute-start.1
  8.5 0.0 collective-permute-done.refs_0_
  8.5 2.7 %collective-permute-done.2.refs_2_ = f32[45,1,128]{2,1,0:T(1,128)S(1)} collective-permute-done((f32[45,1,128]{2,1,0:T(1,128)S(1)}, f32[45,1,128]{2,1,0:T(1,128)S(1)}, u32[]{:S(2)}, u32[]{:S(2)}) %collective-permute-start.2) | collective-permute-done | bytes 23072 | tf_op jit(solution)/shard_map/ppermute | solution.py:495
  11.2 1.5 %collective-permute-done.1.refs_1_ = f32[45,1,128]{2,1,0:T(1,128)S(1)} collective-permute-done((f32[45,1,128]{2,1,0:T(1,128)S(1)}, f32[45,1,128]{2,1,0:T(1,128)S(1)}, u32[]{:S(2)}, u32[]{:S(2)}) %collective-permute-start.1) | collective-permute-done | bytes 23072 | tf_op jit(solution)/shard_map/ppermute | solution.py:495
  12.7 2.0 %shard_map.74 = (f32[128,256]{1,0:T(8,128)S(1)}, f32[32,1,128]{2,1,0:T(1,128)S(1)}) custom-call(s32[1,1,1]{2,1,0:T(1,128)S(6)} %copy.8.count_ref, f32[128,256]{1,0:T(8,128)S(1)} %get-tuple-element.22.source_ref, f32[128,256]{1,0:T(8,128)S(1)} %get-tuple-element.23.up_ref, f32[128,256]{1,0:T(8,128)S(1)} %get-tuple-element.24.down_ref, ...), custom_call_target="tpu_custom_call" | custom-call | flops 2415919104 | bytes 1048576 | tf_op jit(solution)/shard_map/pallas_call | solution.py:444
  14.7 10.3 %all_to_all.5.parts_ref = f32[32,1,128]{2,1,0:T(1,128)S(1)} all-to-all(f32[32,1,128]{2,1,0:T(1,128)S(1)} %get-tuple-element.36), channel_id=1, replica_groups=mesh['gx'=4,'gy'=2,'gz'=4] {'gx','gy','gz'}, dimensions={0} | all-to-all | bytes 32768 | tf_op jit(solution)/shard_map/all_to_all | solution.py:592
  25.1 1.0 %shard_map.75 = f32[128,256]{1,0:T(8,128)} custom-call(s32[1,1,1]{2,1,0:T(1,128)S(6)} %copy.8.count_ref, f32[128,256]{1,0:T(8,128)S(1)} %get-tuple-element.21.first_ref, f32[128,256]{1,0:T(8,128)S(1)} %get-tuple-element.35.second_ref, f32[32,1,128]{2,1,0:T(1,128)S(1)} %all_to_all.5.parts_ref), custom_call_target="tpu_custom_call" | custom-call | flops 32768 | bytes 1048576 | tf_op jit(solution)/shard_map/pallas_call | solution.py:444
Async XLA Ops:
  2.2 6.3 %collective-permute-start = (f32[45,1,128]{2,1,0:T(1,128)S(1)}, f32[45,1,128]{2,1,0:T(1,128)S(1)}, u32[]{:S(2)}, u32[]{:S(2)}) collective-permute-start(f32[45,1,128]{2,1,0:T(1,128)S(1)} %get-tuple-element.33), channel_id=1, source_target_pairs={{0,1},{1,0},{2,3},{3,2},{4,5},{5,4},{6,7},{7,6},{8,9},{9,8},{10,11... | collective-permute-start | bytes 69128 | tf_op jit(solution)/shard_map/ppermute | solution.py:495
  5.3 6.0 %collective-permute-start.2 = (f32[45,1,128]{2,1,0:T(1,128)S(1)}, f32[45,1,128]{2,1,0:T(1,128)S(1)}, u32[]{:S(2)}, u32[]{:S(2)}) collective-permute-start(f32[45,1,128]{2,1,0:T(1,128)S(1)} %get-tuple-element.34), channel_id=1, source_target_pairs={{0,3},{1,2},{2,1},{3,0},{4,7},{5,6},{6,5},{7,4},{8,11},{9,10},{10,... | collective-permute-start | bytes 69128 | tf_op jit(solution)/shard_map/ppermute | solution.py:495
  7.7 5.0 %collective-permute-start.1 = (f32[45,1,128]{2,1,0:T(1,128)S(1)}, f32[45,1,128]{2,1,0:T(1,128)S(1)}, u32[]{:S(2)}, u32[]{:S(2)}) collective-permute-start(f32[45,1,128]{2,1,0:T(1,128)S(1)} %get-tuple-element.32.mine_ref), channel_id=1, source_target_pairs={{0,2},{1,3},{2,0},{3,1},{4,6},{5,7},{6,4},{7,5},{8,10},{9,11},{10,... | collective-permute-start | bytes 69128 | tf_op jit(solution)/shard_map/ppermute | solution.py:495

commit v21 on v19

--- a/solution.py
+++ b/solution.py
@@ -588,7 +588,13 @@
         arguments[2],
         first_pre,
         second_pre,
-        lax.all_to_all(products, ("gx", "gy", "gz"), split_axis=0, concat_axis=0),
+        lax.all_to_all(
+            products,
+            ("gx", "gy", "gz"),
+            split_axis=0,
+            concat_axis=0,
+            axis_index_groups=[list(range(mesh.size - 1, -1, -1))],
+        ),
     )
     return result.reshape(rhs.shape)
 

time: 26.3 us -> 26.3 us (level)
  no operation moved by 1% of the time
where the time goes in v21:
time: 26.3 us; the launch traced here: 26.1 us
  blocking collectives  11.2 us (43%)
  starting transfers between devices  5.68 us (22%)
  Pallas kernels  5.17 us (20%)
  waiting for transfers between devices  3.37 us (13%)
  between operations  0.68 us (3%)
    all_to_all x1, blocking collectives, per_device(): lax.all_to_all(products, ('gx', 'gy', 'gz'), split_axis=0, concat_axis=0,...  11.2 us
    ppermute x3, starting transfers between devices, near_steps(): lax.ppermute(leaving[step - 1], 'gz', [(source, source ^ step) for source...  5.68 us
    pallas_call x3, Pallas kernels, call(): pl.pallas_call(kernel, out_shape=out_shapes, in_specs=in_specs, out_specs...  5.17 us
    ppermute x3, waiting for transfers between devices, near_steps(): lax.ppermute(leaving[step - 1], 'gz', [(source, source ^ step) for source...  3.37 us
  transfers between devices with their start and end apart: 3, of which 1 were waited for; matrix products, arithmetic and copies ran while one was open for 0% of the time, Pallas kernels for 0%

profile of v21, /device:TPU:0, one launch (start us, length us, event | category | flops | bytes accessed | tf_op | source)
XLA Modules:
  0.0 26.1 jit_solution(3894933947464349143)
XLA Ops:
  0.0 2.2 %shard_map.73 = (f32[128,256]{1,0:T(8,128)S(1)}, f32[128,256]{1,0:T(8,128)S(1)}, f32[128,256]{1,0:T(8,128)S(1)}, f32[128,256]{1,0:T(8,128)S(1)}, f32[128,256]{1,...) custom-call(s32[1,1,1,16]{3,2,1,0:T(1,128)} %refs_0_.1, ...), custom_call_target="tpu_custom_call" | custom-call | flops 805306368 | bytes 1048576 | tf_op jit(solution)/shard_map/pallas_call | solution.py:444
  2.2 4.1 %collective-permute-start.1 = (f32[45,1,128]{2,1,0:T(1,128)S(1)}, f32[45,1,128]{2,1,0:T(1,128)S(1)}, u32[]{:S(2)}, u32[]{:S(2)}) collective-permute-start(f32[45,1,128]{2,1,0:T(1,128)S(1)} %get-tuple-element.33), channel_id=1, source_target_pairs={{0,2},{1,3},{2,0},{3,1},{4,6},{5,7},{6,4},{7,5},{8,10},{9,11},{10,... | collective-permute-start | bytes 69128 | tf_op jit(solution)/shard_map/ppermute | solution.py:494
  6.3 1.3 %collective-permute-start.2 = (f32[45,1,128]{2,1,0:T(1,128)S(1)}, f32[45,1,128]{2,1,0:T(1,128)S(1)}, u32[]{:S(2)}, u32[]{:S(2)}) collective-permute-start(f32[45,1,128]{2,1,0:T(1,128)S(1)} %get-tuple-element.34), channel_id=1, source_target_pairs={{0,3},{1,2},{2,1},{3,0},{4,7},{5,6},{6,5},{7,4},{8,11},{9,10},{10,... | collective-permute-start | bytes 69128 | tf_op jit(solution)/shard_map/ppermute | solution.py:494
  7.6 0.2 collective-permute-start
  8.5 0.0 collective-permute-done.1.refs_1_
  8.5 3.4 %collective-permute-done.2.refs_2_ = f32[45,1,128]{2,1,0:T(1,128)S(1)} collective-permute-done((f32[45,1,128]{2,1,0:T(1,128)S(1)}, f32[45,1,128]{2,1,0:T(1,128)S(1)}, u32[]{:S(2)}, u32[]{:S(2)}) %collective-permute-start.2) | collective-permute-done | bytes 23072 | tf_op jit(solution)/shard_map/ppermute | solution.py:494
  11.9 0.0 collective-permute-done.refs_0_
  11.9 2.1 %shard_map.74 = (f32[128,256]{1,0:T(8,128)S(1)}, f32[32,1,128]{2,1,0:T(1,128)S(1)}) custom-call(s32[1,1,1]{2,1,0:T(1,128)S(6)} %copy.8.count_ref, f32[128,256]{1,0:T(8,128)S(1)} %get-tuple-element.22.source_ref, f32[128,256]{1,0:T(8,128)S(1)} %get-tuple-element.23.up_ref, f32[128,256]{1,0:T(8,128)S(1)} %get-tuple-element.24.down_ref, ...), custom_call_target="tpu_custom_call" | custom-call | flops 2415919104 | bytes 1048576 | tf_op jit(solution)/shard_map/pallas_call | solution.py:444
  13.9 11.2 %all_to_all.5.parts_ref = f32[32,1,128]{2,1,0:T(1,128)S(1)} all-to-all(f32[32,1,128]{2,1,0:T(1,128)S(1)} %get-tuple-element.36), channel_id=1, replica_groups={{31,30,29,28,27,26,25,24,23,22,21,20,19,18,17,16,15,14,13,12,11,10,9,8,..., dimensions={0} | all-to-all | bytes 32768 | tf_op jit(solution)/shard_map/all_to_all | solution.py:591
  25.2 1.0 %shard_map.75 = f32[128,256]{1,0:T(8,128)} custom-call(s32[1,1,1]{2,1,0:T(1,128)S(6)} %copy.8.count_ref, f32[128,256]{1,0:T(8,128)S(1)} %get-tuple-element.21.first_ref, f32[128,256]{1,0:T(8,128)S(1)} %get-tuple-element.35.second_ref, f32[32,1,128]{2,1,0:T(1,128)S(1)} %all_to_all.5.parts_ref), custom_call_target="tpu_custom_call" | custom-call | flops 32768 | bytes 1048576 | tf_op jit(solution)/shard_map/pallas_call | solution.py:444
Async XLA Ops:
  2.2 6.3 %collective-permute-start.1 = (f32[45,1,128]{2,1,0:T(1,128)S(1)}, f32[45,1,128]{2,1,0:T(1,128)S(1)}, u32[]{:S(2)}, u32[]{:S(2)}) collective-permute-start(f32[45,1,128]{2,1,0:T(1,128)S(1)} %get-tuple-element.33), channel_id=1, source_target_pairs={{0,2},{1,3},{2,0},{3,1},{4,6},{5,7},{6,4},{7,5},{8,10},{9,11},{10,... | collective-permute-start | bytes 69128 | tf_op jit(solution)/shard_map/ppermute | solution.py:494
  6.3 5.6 %collective-permute-start.2 = (f32[45,1,128]{2,1,0:T(1,128)S(1)}, f32[45,1,128]{2,1,0:T(1,128)S(1)}, u32[]{:S(2)}, u32[]{:S(2)}) collective-permute-start(f32[45,1,128]{2,1,0:T(1,128)S(1)} %get-tuple-element.34), channel_id=1, source_target_pairs={{0,3},{1,2},{2,1},{3,0},{4,7},{5,6},{6,5},{7,4},{8,11},{9,10},{10,... | collective-permute-start | bytes 69128 | tf_op jit(solution)/shard_map/ppermute | solution.py:494
  7.6 4.3 %collective-permute-start = (f32[45,1,128]{2,1,0:T(1,128)S(1)}, f32[45,1,128]{2,1,0:T(1,128)S(1)}, u32[]{:S(2)}, u32[]{:S(2)}) collective-permute-start(f32[45,1,128]{2,1,0:T(1,128)S(1)} %get-tuple-element.32.mine_ref), channel_id=1, source_target_pairs={{0,1},{1,0},{2,3},{3,2},{4,5},{5,4},{6,7},{7,6},{8,9},{9,8},{10,11... | collective-permute-start | bytes 69128 | tf_op jit(solution)/shard_map/ppermute | solution.py:494

commit v22 on v19

--- a/solution.py
+++ b/solution.py
@@ -36,10 +36,13 @@
 
 
 def times_parts(rows, mat_high, mat_low):
-    count = rows.shape[0]
-    row_high, row_low = two_parts(rows)
-    both = dot(jnp.concatenate([row_high, row_low], axis=0), mat_high)
-    return both[:count] + (both[count:] + dot(row_high, mat_low))
+    return parts_product(two_parts(rows), (mat_high, mat_low))
+
+
+def parts_product(left, right):
+    count = left[0].shape[0]
+    both = dot(jnp.concatenate(left, axis=0), right[0])
+    return both[:count] + (both[count:] + dot(left[0], right[1]))
 
 
 def times_parts_once(rows, mat_high, mat_low):
@@ -254,7 +257,8 @@
     stiffness = two_parts(k_ref[...])
     base = times_parts(first_pre, *stiffness) * up
     base_ref[...] = base
-    second_part = (times_parts_once(base, *smoother) * down).astype(bf16)
+    both = two_parts(parts_product(stiffness, smoother))
+    second_part = (times_parts_once(first_pre, *both)).astype(bf16)
     stacked = jnp.concatenate([*two_parts(first_pre), second_part], axis=0)
     rows = probes * elements
     for part_ref, part in zip(part_refs, smoother + stiffness):

time: 26.3 us -> 26.6 us (1.011)
  Pallas kernels: 5.17 us -> 5.47 us
    pallas_call x3, Pallas kernels: 5.17 us -> 5.47 us  [call(): pl.pallas_call(kernel, out_shape=out_shapes, in_specs=in_specs, out_specs...]
where the time goes in v22:
time: 26.6 us; the launch traced here: 26.4 us
  blocking collectives  11.2 us (42%)
  starting transfers between devices  5.68 us (21%)
  Pallas kernels  5.47 us (21%)
  waiting for transfers between devices  3.37 us (13%)
  between operations  0.68 us (3%)
    all_to_all x1, blocking collectives, per_device(): lax.all_to_all(products, ('gx', 'gy', 'gz'), split_axis=0, concat_axis=0)  11.2 us
    ppermute x3, starting transfers between devices, near_steps(): lax.ppermute(leaving[step - 1], 'gz', [(source, source ^ step) for source...  5.68 us
    pallas_call x3, Pallas kernels, call(): pl.pallas_call(kernel, out_shape=out_shapes, in_specs=in_specs, out_specs...  5.47 us
    ppermute x3, waiting for transfers between devices, near_steps(): lax.ppermute(leaving[step - 1], 'gz', [(source, source ^ step) for source...  3.37 us
  transfers between devices with their start and end apart: 3, of which 1 were waited for; matrix products, arithmetic and copies ran while one was open for 0% of the time, Pallas kernels for 0%

profile of v22, /device:TPU:0, one launch (start us, length us, event | category | flops | bytes accessed | tf_op | source)
XLA Modules:
  0.0 26.4 jit_solution(16449324815758447721)
XLA Ops:
  0.0 2.5 %shard_map.73 = (f32[128,256]{1,0:T(8,128)S(1)}, f32[128,256]{1,0:T(8,128)S(1)}, f32[128,256]{1,0:T(8,128)S(1)}, f32[128,256]{1,0:T(8,128)S(1)}, f32[128,256]{1,...) custom-call(s32[1,1,1,16]{3,2,1,0:T(1,128)} %refs_0_.1, ...), custom_call_target="tpu_custom_call" | custom-call | flops 805306368 | bytes 1048576 | tf_op jit(solution)/shard_map/pallas_call | solution.py:448
  2.5 4.1 %collective-permute-start.1 = (f32[45,1,128]{2,1,0:T(1,128)S(1)}, f32[45,1,128]{2,1,0:T(1,128)S(1)}, u32[]{:S(2)}, u32[]{:S(2)}) collective-permute-start(f32[45,1,128]{2,1,0:T(1,128)S(1)} %get-tuple-element.33), channel_id=1, source_target_pairs={{0,2},{1,3},{2,0},{3,1},{4,6},{5,7},{6,4},{7,5},{8,10},{9,11},{10,... | collective-permute-start | bytes 69128 | tf_op jit(solution)/shard_map/ppermute | solution.py:498
  6.6 1.3 %collective-permute-start.2 = (f32[45,1,128]{2,1,0:T(1,128)S(1)}, f32[45,1,128]{2,1,0:T(1,128)S(1)}, u32[]{:S(2)}, u32[]{:S(2)}) collective-permute-start(f32[45,1,128]{2,1,0:T(1,128)S(1)} %get-tuple-element.34), channel_id=1, source_target_pairs={{0,3},{1,2},{2,1},{3,0},{4,7},{5,6},{6,5},{7,4},{8,11},{9,10},{10,... | collective-permute-start | bytes 69128 | tf_op jit(solution)/shard_map/ppermute | solution.py:498
  7.9 0.2 collective-permute-start
  8.8 0.0 collective-permute-done.1.refs_1_
  8.8 3.4 %collective-permute-done.2.refs_2_ = f32[45,1,128]{2,1,0:T(1,128)S(1)} collective-permute-done((f32[45,1,128]{2,1,0:T(1,128)S(1)}, f32[45,1,128]{2,1,0:T(1,128)S(1)}, u32[]{:S(2)}, u32[]{:S(2)}) %collective-permute-start.2) | collective-permute-done | bytes 23072 | tf_op jit(solution)/shard_map/ppermute | solution.py:498
  12.2 0.0 collective-permute-done.refs_0_
  12.2 2.0 %shard_map.74 = (f32[128,256]{1,0:T(8,128)S(1)}, f32[32,1,128]{2,1,0:T(1,128)S(1)}) custom-call(s32[1,1,1]{2,1,0:T(1,128)S(6)} %copy.8.count_ref, f32[128,256]{1,0:T(8,128)S(1)} %get-tuple-element.22.source_ref, f32[128,256]{1,0:T(8,128)S(1)} %get-tuple-element.23.up_ref, f32[128,256]{1,0:T(8,128)S(1)} %get-tuple-element.24.down_ref, ...), custom_call_target="tpu_custom_call" | custom-call | flops 2415919104 | bytes 1048576 | tf_op jit(solution)/shard_map/pallas_call | solution.py:448
  14.2 11.2 %all_to_all.5.parts_ref = f32[32,1,128]{2,1,0:T(1,128)S(1)} all-to-all(f32[32,1,128]{2,1,0:T(1,128)S(1)} %get-tuple-element.36), channel_id=1, replica_groups=mesh['gx'=4,'gy'=2,'gz'=4] {'gx','gy','gz'}, dimensions={0} | all-to-all | bytes 32768 | tf_op jit(solution)/shard_map/all_to_all | solution.py:595
  25.4 1.0 %shard_map.75 = f32[128,256]{1,0:T(8,128)} custom-call(s32[1,1,1]{2,1,0:T(1,128)S(6)} %copy.8.count_ref, f32[128,256]{1,0:T(8,128)S(1)} %get-tuple-element.21.first_ref, f32[128,256]{1,0:T(8,128)S(1)} %get-tuple-element.35.second_ref, f32[32,1,128]{2,1,0:T(1,128)S(1)} %all_to_all.5.parts_ref), custom_call_target="tpu_custom_call" | custom-call | flops 32768 | bytes 1048576 | tf_op jit(solution)/shard_map/pallas_call | solution.py:448
Async XLA Ops:
  2.5 6.3 %collective-permute-start.1 = (f32[45,1,128]{2,1,0:T(1,128)S(1)}, f32[45,1,128]{2,1,0:T(1,128)S(1)}, u32[]{:S(2)}, u32[]{:S(2)}) collective-permute-start(f32[45,1,128]{2,1,0:T(1,128)S(1)} %get-tuple-element.33), channel_id=1, source_target_pairs={{0,2},{1,3},{2,0},{3,1},{4,6},{5,7},{6,4},{7,5},{8,10},{9,11},{10,... | collective-permute-start | bytes 69128 | tf_op jit(solution)/shard_map/ppermute | solution.py:498
  6.6 5.6 %collective-permute-start.2 = (f32[45,1,128]{2,1,0:T(1,128)S(1)}, f32[45,1,128]{2,1,0:T(1,128)S(1)}, u32[]{:S(2)}, u32[]{:S(2)}) collective-permute-start(f32[45,1,128]{2,1,0:T(1,128)S(1)} %get-tuple-element.34), channel_id=1, source_target_pairs={{0,3},{1,2},{2,1},{3,0},{4,7},{5,6},{6,5},{7,4},{8,11},{9,10},{10,... | collective-permute-start | bytes 69128 | tf_op jit(solution)/shard_map/ppermute | solution.py:498
  7.9 4.3 %collective-permute-start = (f32[45,1,128]{2,1,0:T(1,128)S(1)}, f32[45,1,128]{2,1,0:T(1,128)S(1)}, u32[]{:S(2)}, u32[]{:S(2)}) collective-permute-start(f32[45,1,128]{2,1,0:T(1,128)S(1)} %get-tuple-element.32.mine_ref), channel_id=1, source_target_pairs={{0,1},{1,0},{2,3},{3,2},{4,5},{5,4},{6,7},{7,6},{8,9},{9,8},{10,11... | collective-permute-start | bytes 69128 | tf_op jit(solution)/shard_map/ppermute | solution.py:498

commit v23 on v19

--- a/solution.py
+++ b/solution.py
@@ -36,10 +36,11 @@
 
 
 def times_parts(rows, mat_high, mat_low):
-    count = rows.shape[0]
     row_high, row_low = two_parts(rows)
-    both = dot(jnp.concatenate([row_high, row_low], axis=0), mat_high)
-    return both[:count] + (both[count:] + dot(row_high, mat_low))
+    return dot(
+        jnp.concatenate([row_high, row_low, row_high], axis=1),
+        jnp.concatenate([mat_high, mat_high, mat_low], axis=0),
+    )
 
 
 def times_parts_once(rows, mat_high, mat_low):
@@ -252,9 +253,9 @@
         prepare,
     )
     stiffness = two_parts(k_ref[...])
-    base = times_parts(first_pre, *stiffness) * up
-    base_ref[...] = base
-    second_part = (times_parts_once(base, *smoother) * down).astype(bf16)
+    product = times_parts(first_pre, *stiffness)
+    base_ref[...] = product * up
+    second_part = times_parts_once(product, *smoother).astype(bf16)
     stacked = jnp.concatenate([*two_parts(first_pre), second_part], axis=0)
     rows = probes * elements
     for part_ref, part in zip(part_refs, smoother + stiffness):

time: 26.3 us -> 26.3 us (level)
  no operation moved by 1% of the time
where the time goes in v23:
time: 26.3 us; the launch traced here: 26.1 us
  blocking collectives  11.2 us (43%)
  starting transfers between devices  5.68 us (22%)
  Pallas kernels  5.17 us (20%)
  waiting for transfers between devices  3.37 us (13%)
  between operations  0.68 us (3%)
    all_to_all x1, blocking collectives, per_device(): lax.all_to_all(products, ('gx', 'gy', 'gz'), split_axis=0, concat_axis=0)  11.2 us
    ppermute x3, starting transfers between devices, near_steps(): lax.ppermute(leaving[step - 1], 'gz', [(source, source ^ step) for source...  5.68 us
    pallas_call x3, Pallas kernels, call(): pl.pallas_call(kernel, out_shape=out_shapes, in_specs=in_specs, out_specs...  5.17 us
    ppermute x3, waiting for transfers between devices, near_steps(): lax.ppermute(leaving[step - 1], 'gz', [(source, source ^ step) for source...  3.37 us
  transfers between devices with their start and end apart: 3, of which 1 were waited for; matrix products, arithmetic and copies ran while one was open for 0% of the time, Pallas kernels for 0%

profile of v23, /device:TPU:0, one launch (start us, length us, event | category | flops | bytes accessed | tf_op | source)
XLA Modules:
  0.0 26.1 jit_solution(11601474053649307450)
XLA Ops:
  0.0 2.2 %shard_map.73 = (f32[128,256]{1,0:T(8,128)S(1)}, f32[128,256]{1,0:T(8,128)S(1)}, f32[128,256]{1,0:T(8,128)S(1)}, f32[128,256]{1,0:T(8,128)S(1)}, f32[128,256]{1,...) custom-call(s32[1,1,1,16]{3,2,1,0:T(1,128)} %refs_0_.1, ...), custom_call_target="tpu_custom_call" | custom-call | flops 805306368 | bytes 1048576 | tf_op jit(solution)/shard_map/pallas_call | solution.py:445
  2.2 4.1 %collective-permute-start.1 = (f32[45,1,128]{2,1,0:T(1,128)S(1)}, f32[45,1,128]{2,1,0:T(1,128)S(1)}, u32[]{:S(2)}, u32[]{:S(2)}) collective-permute-start(f32[45,1,128]{2,1,0:T(1,128)S(1)} %get-tuple-element.33), channel_id=1, source_target_pairs={{0,2},{1,3},{2,0},{3,1},{4,6},{5,7},{6,4},{7,5},{8,10},{9,11},{10,... | collective-permute-start | bytes 69128 | tf_op jit(solution)/shard_map/ppermute | solution.py:495
  6.3 1.4 %collective-permute-start.2 = (f32[45,1,128]{2,1,0:T(1,128)S(1)}, f32[45,1,128]{2,1,0:T(1,128)S(1)}, u32[]{:S(2)}, u32[]{:S(2)}) collective-permute-start(f32[45,1,128]{2,1,0:T(1,128)S(1)} %get-tuple-element.34), channel_id=1, source_target_pairs={{0,3},{1,2},{2,1},{3,0},{4,7},{5,6},{6,5},{7,4},{8,11},{9,10},{10,... | collective-permute-start | bytes 69128 | tf_op jit(solution)/shard_map/ppermute | solution.py:495
  7.6 0.2 collective-permute-start
  8.5 0.0 collective-permute-done.1.refs_1_
  8.5 3.4 %collective-permute-done.2.refs_2_ = f32[45,1,128]{2,1,0:T(1,128)S(1)} collective-permute-done((f32[45,1,128]{2,1,0:T(1,128)S(1)}, f32[45,1,128]{2,1,0:T(1,128)S(1)}, u32[]{:S(2)}, u32[]{:S(2)}) %collective-permute-start.2) | collective-permute-done | bytes 23072 | tf_op jit(solution)/shard_map/ppermute | solution.py:495
  11.9 0.0 collective-permute-done.refs_0_
  11.9 2.0 %shard_map.74 = (f32[128,256]{1,0:T(8,128)S(1)}, f32[32,1,128]{2,1,0:T(1,128)S(1)}) custom-call(s32[1,1,1]{2,1,0:T(1,128)S(6)} %copy.8.count_ref, f32[128,256]{1,0:T(8,128)S(1)} %get-tuple-element.22.source_ref, f32[128,256]{1,0:T(8,128)S(1)} %get-tuple-element.23.up_ref, f32[128,256]{1,0:T(8,128)S(1)} %get-tuple-element.24.down_ref, ...), custom_call_target="tpu_custom_call" | custom-call | flops 2415919104 | bytes 1048576 | tf_op jit(solution)/shard_map/pallas_call | solution.py:445
  13.9 11.2 %all_to_all.5.parts_ref = f32[32,1,128]{2,1,0:T(1,128)S(1)} all-to-all(f32[32,1,128]{2,1,0:T(1,128)S(1)} %get-tuple-element.36), channel_id=1, replica_groups=mesh['gx'=4,'gy'=2,'gz'=4] {'gx','gy','gz'}, dimensions={0} | all-to-all | bytes 32768 | tf_op jit(solution)/shard_map/all_to_all | solution.py:592
  25.1 1.0 %shard_map.75 = f32[128,256]{1,0:T(8,128)} custom-call(s32[1,1,1]{2,1,0:T(1,128)S(6)} %copy.8.count_ref, f32[128,256]{1,0:T(8,128)S(1)} %get-tuple-element.21.first_ref, f32[128,256]{1,0:T(8,128)S(1)} %get-tuple-element.35.second_ref, f32[32,1,128]{2,1,0:T(1,128)S(1)} %all_to_all.5.parts_ref), custom_call_target="tpu_custom_call" | custom-call | flops 32768 | bytes 1048576 | tf_op jit(solution)/shard_map/pallas_call | solution.py:445
Async XLA Ops:
  2.2 6.3 %collective-permute-start.1 = (f32[45,1,128]{2,1,0:T(1,128)S(1)}, f32[45,1,128]{2,1,0:T(1,128)S(1)}, u32[]{:S(2)}, u32[]{:S(2)}) collective-permute-start(f32[45,1,128]{2,1,0:T(1,128)S(1)} %get-tuple-element.33), channel_id=1, source_target_pairs={{0,2},{1,3},{2,0},{3,1},{4,6},{5,7},{6,4},{7,5},{8,10},{9,11},{10,... | collective-permute-start | bytes 69128 | tf_op jit(solution)/shard_map/ppermute | solution.py:495
  6.3 5.6 %collective-permute-start.2 = (f32[45,1,128]{2,1,0:T(1,128)S(1)}, f32[45,1,128]{2,1,0:T(1,128)S(1)}, u32[]{:S(2)}, u32[]{:S(2)}) collective-permute-start(f32[45,1,128]{2,1,0:T(1,128)S(1)} %get-tuple-element.34), channel_id=1, source_target_pairs={{0,3},{1,2},{2,1},{3,0},{4,7},{5,6},{6,5},{7,4},{8,11},{9,10},{10,... | collective-permute-start | bytes 69128 | tf_op jit(solution)/shard_map/ppermute | solution.py:495
  7.6 4.3 %collective-permute-start = (f32[45,1,128]{2,1,0:T(1,128)S(1)}, f32[45,1,128]{2,1,0:T(1,128)S(1)}, u32[]{:S(2)}, u32[]{:S(2)}) collective-permute-start(f32[45,1,128]{2,1,0:T(1,128)S(1)} %get-tuple-element.32.mine_ref), channel_id=1, source_target_pairs={{0,1},{1,0},{2,3},{3,2},{4,5},{5,4},{6,7},{7,6},{8,9},{9,8},{10,11... | collective-permute-start | bytes 69128 | tf_op jit(solution)/shard_map/ppermute | solution.py:495

commit v24 on v19

--- a/solution.py
+++ b/solution.py
@@ -186,13 +186,15 @@
     visc = as_column(visc_ref[0, 0])
     up = wide(live * visc, probes, dofs)
     down = wide(live / visc, probes, dofs)
-    refs["up"][...] = up
-    refs["down"][...] = down
+    if "up" in refs:
+        refs["up"][...] = up
+        refs["down"][...] = down
     copies[2].wait()
     source = rhs_ref[...].reshape(probes * elements, dofs)
     if count_ref is not None:
         source = source * wide(live, probes, dofs)
-    refs["source"][...] = source
+    if "source" in refs:
+        refs["source"][...] = source
     copies[3].wait()
     smoother = two_parts(matrix_refs[0][...])
     first_pre = times_parts(source, *smoother) * down
@@ -226,8 +228,8 @@
 
 def near_first_kernel(*refs):
     operands, refs = refs[:6], refs[6:]
-    first_ref, source_ref, up_ref, down_ref, base_ref, slots_ref, hot_ref = refs[:7]
-    part_refs, refs = refs[7:11], refs[11:]
+    first_ref, base_ref, slots_ref, hot_ref = refs[:4]
+    part_refs, refs = refs[4:8], refs[8:]
     steps, _, width = slots_ref.shape
     leave_refs, scratch = refs[:steps], refs[steps:]
     visc_ref, rhs_ref, _, k_ref = scratch[2:6]
@@ -242,9 +244,6 @@
             "operands": operands,
             "scratch": scratch,
             "slots": slots_ref,
-            "up": up_ref,
-            "down": down_ref,
-            "source": source_ref,
             "first": first_ref,
         },
         lambda me, step: me ^ step,
@@ -279,7 +278,7 @@
 
 
 def near_second_kernel(
-    probes, count_ref, source_ref, up_ref, down_ref, base_ref, slots_ref, hot_ref,
+    probes, count_ref, source_ref, base_ref, slots_ref, hot_ref,
     p_high_ref, p_low_ref, k_high_ref, k_low_ref, mine_ref, *refs
 ):
     came_refs = refs[:-2]
@@ -306,7 +305,9 @@
         add = add_faces if len(values[0]) > probes else add_faces_once
         return add(spreads, hot_ref[...])
 
-    up, down = up_ref[...], down_ref[...]
+    visc_line = visc_at * (width // lane_count)
+    own_visc = as_column(mine_ref[visc_line, :, :elements])
+    up, down = wide(own_visc, probes, dofs), wide(1.0 / own_visc, probes, dofs)
     live = wide(live_column(count_ref, elements).astype(f32), probes, dofs) > 0.0
     placed = folded(placed_here([high_low(inbound_first(0, step)) for step in range(1, members)]))
     image = jnp.where(live, base_ref[...] - coupling * placed, 0.0)
@@ -477,9 +478,9 @@
     hot = jax.ShapeDtypeStruct((dofs, steps * width), bf16)
     message = jax.ShapeDtypeStruct((message_length(steps, probes, width), 1, lane_count), f32)
     part = jax.ShapeDtypeStruct(p_matrix.shape, bf16)
-    first_pre, source, up, down, base, slots, hot_own, *rest = begin_call(
+    first_pre, base, slots, hot_own, *rest = begin_call(
         near_first_kernel,
-        [field] * 5 + [slots_shape, hot] + [part] * 4 + [message] * steps,
+        [field] * 2 + [slots_shape, hot] + [part] * 4 + [message] * steps,
         2 * flops,
         (),
         neighbours,
@@ -498,13 +499,11 @@
     ]
     second_pre, products = call(
         functools.partial(near_second_kernel, probes),
-        [smem_spec] + [vmem_spec] * (11 + steps),
+        [smem_spec] + [vmem_spec] * (9 + steps),
         [field, products_shape],
         6 * flops,
         counts,
-        source,
-        up,
-        down,
+        rhs.reshape(field.shape),
         base,
         slots,
         hot_own,

time: 26.3 us -> 26.3 us (level)
  no operation moved by 1% of the time
where the time goes in v24:
time: 26.3 us; the launch traced here: 26.1 us
  blocking collectives  11.2 us (43%)
  starting transfers between devices  5.68 us (22%)
  Pallas kernels  5.2 us (20%)
  waiting for transfers between devices  3.37 us (13%)
  between operations  0.68 us (3%)
    all_to_all x1, blocking collectives, per_device(): lax.all_to_all(products, ('gx', 'gy', 'gz'), split_axis=0, concat_axis=0)  11.2 us
    ppermute x3, starting transfers between devices, near_steps(): lax.ppermute(leaving[step - 1], 'gz', [(source, source ^ step) for source...  5.68 us
    pallas_call x3, Pallas kernels, call(): pl.pallas_call(kernel, out_shape=out_shapes, in_specs=in_specs, out_specs...  5.2 us
    ppermute x3, waiting for transfers between devices, near_steps(): lax.ppermute(leaving[step - 1], 'gz', [(source, source ^ step) for source...  3.37 us
  transfers between devices with their start and end apart: 3, of which 1 were waited for; matrix products, arithmetic and copies ran while one was open for 0% of the time, Pallas kernels for 0%

profile of v24, /device:TPU:0, one launch (start us, length us, event | category | flops | bytes accessed | tf_op | source)
XLA Modules:
  0.0 26.1 jit_solution(11610386626225590022)
XLA Ops:
  0.0 0.0 copy-start
  0.0 2.2 %shard_map.73 = (f32[128,256]{1,0:T(8,128)S(1)}, f32[128,256]{1,0:T(8,128)S(1)}, s32[3,1,512]{2,1,0:T(1,128)S(1)}, bf16[256,1536]{1,0:T(8,128)(2,1)S(1)}, bf16[2...) custom-call(s32[1,1,1,16]{3,2,1,0:T(1,128)} %refs_0_.1, ...), custom_call_target="tpu_custom_call" | custom-call | flops 805306368 | bytes 1048576 | tf_op jit(solution)/shard_map/pallas_call | solution.py:445
  2.2 4.1 %collective-permute-start.1 = (f32[45,1,128]{2,1,0:T(1,128)S(1)}, f32[45,1,128]{2,1,0:T(1,128)S(1)}, u32[]{:S(2)}, u32[]{:S(2)}) collective-permute-start(f32[45,1,128]{2,1,0:T(1,128)S(1)} %get-tuple-element.27), channel_id=1, source_target_pairs={{0,2},{1,3},{2,0},{3,1},{4,6},{5,7},{6,4},{7,5},{8,10},{9,11},{10,... | collective-permute-start | bytes 69128 | tf_op jit(solution)/shard_map/ppermute | solution.py:495
  6.3 1.3 %collective-permute-start.2 = (f32[45,1,128]{2,1,0:T(1,128)S(1)}, f32[45,1,128]{2,1,0:T(1,128)S(1)}, u32[]{:S(2)}, u32[]{:S(2)}) collective-permute-start(f32[45,1,128]{2,1,0:T(1,128)S(1)} %get-tuple-element.28), channel_id=1, source_target_pairs={{0,3},{1,2},{2,1},{3,0},{4,7},{5,6},{6,5},{7,4},{8,11},{9,10},{10,... | collective-permute-start | bytes 69128 | tf_op jit(solution)/shard_map/ppermute | solution.py:495
  7.7 0.2 collective-permute-start
  8.5 0.0 collective-permute-done.1.refs_1_
  8.6 3.4 %collective-permute-done.2.refs_2_ = f32[45,1,128]{2,1,0:T(1,128)S(1)} collective-permute-done((f32[45,1,128]{2,1,0:T(1,128)S(1)}, f32[45,1,128]{2,1,0:T(1,128)S(1)}, u32[]{:S(2)}, u32[]{:S(2)}) %collective-permute-start.2) | collective-permute-done | bytes 23072 | tf_op jit(solution)/shard_map/ppermute | solution.py:495
  11.9 0.0 collective-permute-done.refs_0_
  11.9 0.0 copy-done
  11.9 2.0 %shard_map.74 = (f32[128,256]{1,0:T(8,128)S(1)}, f32[32,1,128]{2,1,0:T(1,128)S(1)}) custom-call(s32[1,1,1]{2,1,0:T(1,128)S(6)} %copy.8.count_ref, f32[128,256]{1,0:T(8,128)S(1)} %bitcast.2, f32[128,256]{1,0:T(8,128)S(1)} %get-tuple-element.19.base_ref, s32[3,1,512]{2,1,0:T(1,128)S(1)} %get-tuple-element.20.slots_ref, ...), custom_call_target="tpu_custom_call" | custom-call | flops 2415919104 | bytes 1048576 | tf_op jit(solution)/shard_map/pallas_call | solution.py:445
  14.0 11.2 %all_to_all.5.parts_ref = f32[32,1,128]{2,1,0:T(1,128)S(1)} all-to-all(f32[32,1,128]{2,1,0:T(1,128)S(1)} %get-tuple-element.30), channel_id=1, replica_groups=mesh['gx'=4,'gy'=2,'gz'=4] {'gx','gy','gz'}, dimensions={0} | all-to-all | bytes 32768 | tf_op jit(solution)/shard_map/all_to_all | solution.py:590
  25.2 1.0 %shard_map.75 = f32[128,256]{1,0:T(8,128)} custom-call(s32[1,1,1]{2,1,0:T(1,128)S(6)} %copy.8.count_ref, f32[128,256]{1,0:T(8,128)S(1)} %get-tuple-element.18.first_ref, f32[128,256]{1,0:T(8,128)S(1)} %get-tuple-element.29.second_ref, f32[32,1,128]{2,1,0:T(1,128)S(1)} %all_to_all.5.parts_ref), custom_call_target="tpu_custom_call" | custom-call | flops 32768 | bytes 1048576 | tf_op jit(solution)/shard_map/pallas_call | solution.py:445
Async XLA Ops:
  0.0 11.9 %copy-start = (f32[1,1,1,2,64,256]{5,4,3,2,1,0:T(8,128)S(1)}, f32[1,1,1,2,64,256]{5,4,3,2,1,0:T(8,128)}, u32[]{:S(2)}) copy-start(f32[1,1,1,2,64,256]{5,4,3,2,1,0:T(8,128)} %refs_3_.1) | copy-start | bytes 393220
  2.2 6.3 %collective-permute-start.1 = (f32[45,1,128]{2,1,0:T(1,128)S(1)}, f32[45,1,128]{2,1,0:T(1,128)S(1)}, u32[]{:S(2)}, u32[]{:S(2)}) collective-permute-start(f32[45,1,128]{2,1,0:T(1,128)S(1)} %get-tuple-element.27), channel_id=1, source_target_pairs={{0,2},{1,3},{2,0},{3,1},{4,6},{5,7},{6,4},{7,5},{8,10},{9,11},{10,... | collective-permute-start | bytes 69128 | tf_op jit(solution)/shard_map/ppermute | solution.py:495
  6.3 5.6 %collective-permute-start.2 = (f32[45,1,128]{2,1,0:T(1,128)S(1)}, f32[45,1,128]{2,1,0:T(1,128)S(1)}, u32[]{:S(2)}, u32[]{:S(2)}) collective-permute-start(f32[45,1,128]{2,1,0:T(1,128)S(1)} %get-tuple-element.28), channel_id=1, source_target_pairs={{0,3},{1,2},{2,1},{3,0},{4,7},{5,6},{6,5},{7,4},{8,11},{9,10},{10,... | collective-permute-start | bytes 69128 | tf_op jit(solution)/shard_map/ppermute | solution.py:495
  7.7 4.3 %collective-permute-start = (f32[45,1,128]{2,1,0:T(1,128)S(1)}, f32[45,1,128]{2,1,0:T(1,128)S(1)}, u32[]{:S(2)}, u32[]{:S(2)}) collective-permute-start(f32[45,1,128]{2,1,0:T(1,128)S(1)} %get-tuple-element.26.mine_ref), channel_id=1, source_target_pairs={{0,1},{1,0},{2,3},{3,2},{4,5},{5,4},{6,7},{7,6},{8,9},{9,8},{10,11... | collective-permute-start | bytes 69128 | tf_op jit(solution)/shard_map/ppermute | solution.py:495

commit v25 on v19

--- a/solution.py
+++ b/solution.py
@@ -96,6 +96,15 @@
         jnp.sum(jnp.where(over_elements, picked[low : low + elements], 0.0), axis=0, keepdims=True)
         for low in range(0, picked.shape[0], elements)
     ]
+
+
+def side_by_side(field, elements):
+    half = elements // 2
+    blocks = [
+        jnp.concatenate([field[low : low + half], field[low + half : low + elements]], axis=1)
+        for low in range(0, field.shape[0], elements)
+    ]
+    return jnp.concatenate(blocks, axis=0)
 
 
 def spread_faces(values, over_elements):
@@ -255,16 +264,22 @@
     base = times_parts(first_pre, *stiffness) * up
     base_ref[...] = base
     second_part = (times_parts_once(base, *smoother) * down).astype(bf16)
-    stacked = jnp.concatenate([*two_parts(first_pre), second_part], axis=0)
-    rows = probes * elements
+    half = elements // 2
+    fields = [*two_parts(first_pre), second_part]
+    stacked = jnp.concatenate([side_by_side(field, elements) for field in fields], axis=0)
+    rows = probes * half
     for part_ref, part in zip(part_refs, smoother + stiffness):
         part_ref[...] = part
     second_at, index_at, visc_at = message_places(steps, probes)
     for step in range(1, steps + 1):
         flat_row = slots_ref[step - 1]
-        over_elements = hot_elements(flat_row, elements, dofs)
+        element, _ = split_index(flat_row, dofs)
+        lower = element >= half
+        line = lax.broadcasted_iota(jnp.int32, (half, width), 0)
+        over_elements = line == jnp.where(lower, element - half, element)
         over_dofs = hot_ref[:, (step - 1) * width : step * width]
-        picked = dot(stacked, over_dofs)
+        in_lower = over_dofs * lower.astype(f32).astype(bf16)
+        picked = dot(stacked, jnp.concatenate([over_dofs - in_lower, in_lower], axis=0))
         first_rows = take_faces(folded(picked[: 2 * rows]), over_elements)
         second_rows = take_faces(picked[2 * rows :], over_elements)
         for probe in range(probes):
@@ -578,6 +593,8 @@
     )
     near = 1 < members <= short_group and elements <= face_index.shape[-1]
     near = near and elements * dofs < 1 << 24
+    near = near and members & (members - 1) == 0 and elements % 32 == 0
+    near = near and face_index.shape[-1] % lane_count == 0 and elements <= lane_count
     steps = near_steps if near else far_steps
     first_pre, second_pre, products = steps(members, shapes, arguments)
     result = call(

time: 26.3 us -> 26.3 us (level)
  no operation moved by 1% of the time
where the time goes in v25:
time: 26.3 us; the launch traced here: 26.1 us
  blocking collectives  11.2 us (43%)
  starting transfers between devices  5.68 us (22%)
  Pallas kernels  5.22 us (20%)
  waiting for transfers between devices  3.37 us (13%)
  between operations  0.68 us (3%)
    all_to_all x1, blocking collectives, per_device(): lax.all_to_all(products, ('gx', 'gy', 'gz'), split_axis=0, concat_axis=0)  11.2 us
    ppermute x3, starting transfers between devices, near_steps(): lax.ppermute(leaving[step - 1], 'gz', [(source, source ^ step) for source...  5.68 us
    pallas_call x3, Pallas kernels, call(): pl.pallas_call(kernel, out_shape=out_shapes, in_specs=in_specs, out_specs...  5.22 us
    ppermute x3, waiting for transfers between devices, near_steps(): lax.ppermute(leaving[step - 1], 'gz', [(source, source ^ step) for source...  3.37 us
  transfers between devices with their start and end apart: 3, of which 1 were waited for; matrix products, arithmetic and copies ran while one was open for 0% of the time, Pallas kernels for 0%

profile of v25, /device:TPU:0, one launch (start us, length us, event | category | flops | bytes accessed | tf_op | source)
XLA Modules:
  0.0 26.1 jit_solution(4263002631885775937)
XLA Ops:
  0.0 2.2 %shard_map.73 = (f32[128,256]{1,0:T(8,128)S(1)}, f32[128,256]{1,0:T(8,128)S(1)}, f32[128,256]{1,0:T(8,128)S(1)}, f32[128,256]{1,0:T(8,128)S(1)}, f32[128,256]{1,...) custom-call(s32[1,1,1,16]{3,2,1,0:T(1,128)} %refs_0_.1, ...), custom_call_target="tpu_custom_call" | custom-call | flops 805306368 | bytes 1048576 | tf_op jit(solution)/shard_map/pallas_call | solution.py:459
  2.2 4.1 %collective-permute-start.1 = (f32[45,1,128]{2,1,0:T(1,128)S(1)}, f32[45,1,128]{2,1,0:T(1,128)S(1)}, u32[]{:S(2)}, u32[]{:S(2)}) collective-permute-start(f32[45,1,128]{2,1,0:T(1,128)S(1)} %get-tuple-element.33), channel_id=1, source_target_pairs={{0,2},{1,3},{2,0},{3,1},{4,6},{5,7},{6,4},{7,5},{8,10},{9,11},{10,... | collective-permute-start | bytes 69128 | tf_op jit(solution)/shard_map/ppermute | solution.py:509
  6.3 1.3 %collective-permute-start.2 = (f32[45,1,128]{2,1,0:T(1,128)S(1)}, f32[45,1,128]{2,1,0:T(1,128)S(1)}, u32[]{:S(2)}, u32[]{:S(2)}) collective-permute-start(f32[45,1,128]{2,1,0:T(1,128)S(1)} %get-tuple-element.34), channel_id=1, source_target_pairs={{0,3},{1,2},{2,1},{3,0},{4,7},{5,6},{6,5},{7,4},{8,11},{9,10},{10,... | collective-permute-start | bytes 69128 | tf_op jit(solution)/shard_map/ppermute | solution.py:509
  7.7 0.2 collective-permute-start
  8.5 0.0 collective-permute-done.1.refs_1_
  8.6 3.4 %collective-permute-done.2.refs_2_ = f32[45,1,128]{2,1,0:T(1,128)S(1)} collective-permute-done((f32[45,1,128]{2,1,0:T(1,128)S(1)}, f32[45,1,128]{2,1,0:T(1,128)S(1)}, u32[]{:S(2)}, u32[]{:S(2)}) %collective-permute-start.2) | collective-permute-done | bytes 23072 | tf_op jit(solution)/shard_map/ppermute | solution.py:509
  11.9 0.0 collective-permute-done.refs_0_
  11.9 2.1 %shard_map.74 = (f32[128,256]{1,0:T(8,128)S(1)}, f32[32,1,128]{2,1,0:T(1,128)S(1)}) custom-call(s32[1,1,1]{2,1,0:T(1,128)S(6)} %copy.8.count_ref, f32[128,256]{1,0:T(8,128)S(1)} %get-tuple-element.22.source_ref, f32[128,256]{1,0:T(8,128)S(1)} %get-tuple-element.23.up_ref, f32[128,256]{1,0:T(8,128)S(1)} %get-tuple-element.24.down_ref, ...), custom_call_target="tpu_custom_call" | custom-call | flops 2415919104 | bytes 1048576 | tf_op jit(solution)/shard_map/pallas_call | solution.py:459
  14.0 11.2 %all_to_all.5.parts_ref = f32[32,1,128]{2,1,0:T(1,128)S(1)} all-to-all(f32[32,1,128]{2,1,0:T(1,128)S(1)} %get-tuple-element.36), channel_id=1, replica_groups=mesh['gx'=4,'gy'=2,'gz'=4] {'gx','gy','gz'}, dimensions={0} | all-to-all | bytes 32768 | tf_op jit(solution)/shard_map/all_to_all | solution.py:608
  25.2 1.0 %shard_map.75 = f32[128,256]{1,0:T(8,128)} custom-call(s32[1,1,1]{2,1,0:T(1,128)S(6)} %copy.8.count_ref, f32[128,256]{1,0:T(8,128)S(1)} %get-tuple-element.21.first_ref, f32[128,256]{1,0:T(8,128)S(1)} %get-tuple-element.35.second_ref, f32[32,1,128]{2,1,0:T(1,128)S(1)} %all_to_all.5.parts_ref), custom_call_target="tpu_custom_call" | custom-call | flops 32768 | bytes 1048576 | tf_op jit(solution)/shard_map/pallas_call | solution.py:459
Async XLA Ops:
  2.2 6.3 %collective-permute-start.1 = (f32[45,1,128]{2,1,0:T(1,128)S(1)}, f32[45,1,128]{2,1,0:T(1,128)S(1)}, u32[]{:S(2)}, u32[]{:S(2)}) collective-permute-start(f32[45,1,128]{2,1,0:T(1,128)S(1)} %get-tuple-element.33), channel_id=1, source_target_pairs={{0,2},{1,3},{2,0},{3,1},{4,6},{5,7},{6,4},{7,5},{8,10},{9,11},{10,... | collective-permute-start | bytes 69128 | tf_op jit(solution)/shard_map/ppermute | solution.py:509
  6.3 5.6 %collective-permute-start.2 = (f32[45,1,128]{2,1,0:T(1,128)S(1)}, f32[45,1,128]{2,1,0:T(1,128)S(1)}, u32[]{:S(2)}, u32[]{:S(2)}) collective-permute-start(f32[45,1,128]{2,1,0:T(1,128)S(1)} %get-tuple-element.34), channel_id=1, source_target_pairs={{0,3},{1,2},{2,1},{3,0},{4,7},{5,6},{6,5},{7,4},{8,11},{9,10},{10,... | collective-permute-start | bytes 69128 | tf_op jit(solution)/shard_map/ppermute | solution.py:509
  7.7 4.3 %collective-permute-start = (f32[45,1,128]{2,1,0:T(1,128)S(1)}, f32[45,1,128]{2,1,0:T(1,128)S(1)}, u32[]{:S(2)}, u32[]{:S(2)}) collective-permute-start(f32[45,1,128]{2,1,0:T(1,128)S(1)} %get-tuple-element.32.mine_ref), channel_id=1, source_target_pairs={{0,1},{1,0},{2,3},{3,2},{4,5},{5,4},{6,7},{7,6},{8,9},{9,8},{10,11... | collective-permute-start | bytes 69128 | tf_op jit(solution)/shard_map/ppermute | solution.py:509

commit v26 on v19

--- a/solution.py
+++ b/solution.py
@@ -114,7 +114,7 @@
 
 
 def add_faces_once(spreads, over_dofs):
-    return jnp.transpose(dot_transposed(over_dofs, jnp.concatenate(spreads, axis=1)))
+    return add_faces(spreads, over_dofs)
 
 
 def folded(parts):
@@ -578,6 +578,8 @@
     )
     near = 1 < members <= short_group and elements <= face_index.shape[-1]
     near = near and elements * dofs < 1 << 24
+    near = near and members & (members - 1) == 0 and elements <= lane_count
+    near = near and face_index.shape[-1] % lane_count == 0
     steps = near_steps if near else far_steps
     first_pre, second_pre, products = steps(members, shapes, arguments)
     result = call(

time: 26.3 us -> 26.2 us (level)
  no operation moved by 1% of the time
where the time goes in v26:
time: 26.2 us; the launch traced here: 26 us
  blocking collectives  11.2 us (43%)
  starting transfers between devices  5.68 us (22%)
  Pallas kernels  5.09 us (19%)
  waiting for transfers between devices  3.37 us (13%)
  between operations  0.68 us (3%)
    all_to_all x1, blocking collectives, per_device(): lax.all_to_all(products, ('gx', 'gy', 'gz'), split_axis=0, concat_axis=0)  11.2 us
    ppermute x3, starting transfers between devices, near_steps(): lax.ppermute(leaving[step - 1], 'gz', [(source, source ^ step) for source...  5.68 us
    pallas_call x3, Pallas kernels, call(): pl.pallas_call(kernel, out_shape=out_shapes, in_specs=in_specs, out_specs...  5.09 us
    ppermute x3, waiting for transfers between devices, near_steps(): lax.ppermute(leaving[step - 1], 'gz', [(source, source ^ step) for source...  3.37 us
  transfers between devices with their start and end apart: 3, of which 1 were waited for; matrix products, arithmetic and copies ran while one was open for 0% of the time, Pallas kernels for 0%

profile of v26, /device:TPU:0, one launch (start us, length us, event | category | flops | bytes accessed | tf_op | source)
XLA Modules:
  0.0 26.0 jit_solution(15873374295424354371)
XLA Ops:
  0.0 2.2 %shard_map.73 = (f32[128,256]{1,0:T(8,128)S(1)}, f32[128,256]{1,0:T(8,128)S(1)}, f32[128,256]{1,0:T(8,128)S(1)}, f32[128,256]{1,0:T(8,128)S(1)}, f32[128,256]{1,...) custom-call(s32[1,1,1,16]{3,2,1,0:T(1,128)} %refs_0_.1, ...), custom_call_target="tpu_custom_call" | custom-call | flops 805306368 | bytes 1048576 | tf_op jit(solution)/shard_map/pallas_call | solution.py:444
  2.2 4.1 %collective-permute-start.1 = (f32[45,1,128]{2,1,0:T(1,128)S(1)}, f32[45,1,128]{2,1,0:T(1,128)S(1)}, u32[]{:S(2)}, u32[]{:S(2)}) collective-permute-start(f32[45,1,128]{2,1,0:T(1,128)S(1)} %get-tuple-element.33), channel_id=1, source_target_pairs={{0,2},{1,3},{2,0},{3,1},{4,6},{5,7},{6,4},{7,5},{8,10},{9,11},{10,... | collective-permute-start | bytes 69128 | tf_op jit(solution)/shard_map/ppermute | solution.py:494
  6.3 1.3 %collective-permute-start.2 = (f32[45,1,128]{2,1,0:T(1,128)S(1)}, f32[45,1,128]{2,1,0:T(1,128)S(1)}, u32[]{:S(2)}, u32[]{:S(2)}) collective-permute-start(f32[45,1,128]{2,1,0:T(1,128)S(1)} %get-tuple-element.34), channel_id=1, source_target_pairs={{0,3},{1,2},{2,1},{3,0},{4,7},{5,6},{6,5},{7,4},{8,11},{9,10},{10,... | collective-permute-start | bytes 69128 | tf_op jit(solution)/shard_map/ppermute | solution.py:494
  7.6 0.2 collective-permute-start
  8.5 0.0 collective-permute-done.1.refs_1_
  8.5 3.4 %collective-permute-done.2.refs_2_ = f32[45,1,128]{2,1,0:T(1,128)S(1)} collective-permute-done((f32[45,1,128]{2,1,0:T(1,128)S(1)}, f32[45,1,128]{2,1,0:T(1,128)S(1)}, u32[]{:S(2)}, u32[]{:S(2)}) %collective-permute-start.2) | collective-permute-done | bytes 23072 | tf_op jit(solution)/shard_map/ppermute | solution.py:494
  11.9 0.0 collective-permute-done.refs_0_
  11.9 2.0 %shard_map.74 = (f32[128,256]{1,0:T(8,128)S(1)}, f32[32,1,128]{2,1,0:T(1,128)S(1)}) custom-call(s32[1,1,1]{2,1,0:T(1,128)S(6)} %copy.8.count_ref, f32[128,256]{1,0:T(8,128)S(1)} %get-tuple-element.22.source_ref, f32[128,256]{1,0:T(8,128)S(1)} %get-tuple-element.23.up_ref, f32[128,256]{1,0:T(8,128)S(1)} %get-tuple-element.24.down_ref, ...), custom_call_target="tpu_custom_call" | custom-call | flops 2415919104 | bytes 1048576 | tf_op jit(solution)/shard_map/pallas_call | solution.py:444
  13.9 11.2 %all_to_all.5.parts_ref = f32[32,1,128]{2,1,0:T(1,128)S(1)} all-to-all(f32[32,1,128]{2,1,0:T(1,128)S(1)} %get-tuple-element.36), channel_id=1, replica_groups=mesh['gx'=4,'gy'=2,'gz'=4] {'gx','gy','gz'}, dimensions={0} | all-to-all | bytes 32768 | tf_op jit(solution)/shard_map/all_to_all | solution.py:593
  25.1 1.0 %shard_map.75 = f32[128,256]{1,0:T(8,128)} custom-call(s32[1,1,1]{2,1,0:T(1,128)S(6)} %copy.8.count_ref, f32[128,256]{1,0:T(8,128)S(1)} %get-tuple-element.21.first_ref, f32[128,256]{1,0:T(8,128)S(1)} %get-tuple-element.35.second_ref, f32[32,1,128]{2,1,0:T(1,128)S(1)} %all_to_all.5.parts_ref), custom_call_target="tpu_custom_call" | custom-call | flops 32768 | bytes 1048576 | tf_op jit(solution)/shard_map/pallas_call | solution.py:444
Async XLA Ops:
  2.2 6.3 %collective-permute-start.1 = (f32[45,1,128]{2,1,0:T(1,128)S(1)}, f32[45,1,128]{2,1,0:T(1,128)S(1)}, u32[]{:S(2)}, u32[]{:S(2)}) collective-permute-start(f32[45,1,128]{2,1,0:T(1,128)S(1)} %get-tuple-element.33), channel_id=1, source_target_pairs={{0,2},{1,3},{2,0},{3,1},{4,6},{5,7},{6,4},{7,5},{8,10},{9,11},{10,... | collective-permute-start | bytes 69128 | tf_op jit(solution)/shard_map/ppermute | solution.py:494
  6.3 5.6 %collective-permute-start.2 = (f32[45,1,128]{2,1,0:T(1,128)S(1)}, f32[45,1,128]{2,1,0:T(1,128)S(1)}, u32[]{:S(2)}, u32[]{:S(2)}) collective-permute-start(f32[45,1,128]{2,1,0:T(1,128)S(1)} %get-tuple-element.34), channel_id=1, source_target_pairs={{0,3},{1,2},{2,1},{3,0},{4,7},{5,6},{6,5},{7,4},{8,11},{9,10},{10,... | collective-permute-start | bytes 69128 | tf_op jit(solution)/shard_map/ppermute | solution.py:494
  7.6 4.3 %collective-permute-start = (f32[45,1,128]{2,1,0:T(1,128)S(1)}, f32[45,1,128]{2,1,0:T(1,128)S(1)}, u32[]{:S(2)}, u32[]{:S(2)}) collective-permute-start(f32[45,1,128]{2,1,0:T(1,128)S(1)} %get-tuple-element.32.mine_ref), channel_id=1, source_target_pairs={{0,1},{1,0},{2,3},{3,2},{4,5},{5,4},{6,7},{7,6},{8,9},{9,8},{10,11... | collective-permute-start | bytes 69128 | tf_op jit(solution)/shard_map/ppermute | solution.py:494
